TPU v7x, 256 devices: a whole 4x4x8 slice. The times are simulated.
256 devices in a mesh: audio: 16 (over y_lo, x, core), score: 16 (over y_hi, z).
Axes of the slice: x: 4, y: 4 (y_hi: 2, y_lo: 2; y = y_hi * 2 + y_lo), z: 8, core: 2. Of those that a mesh axis runs over, the one named last changes fastest.
Arguments:
- hidden_in: bfloat16 [32768, 1280], P('audio'), may hold values from -6 to 6
- up_weight: bfloat16 [1280, 5120], P(None, 'score'), may hold values from -0.15625 to 0.15625
- down_weight: bfloat16 [5120, 1280], P('score'), may hold values from -0.078125 to 0.078125
- head_weight: bfloat16 [1280, 768], replicated, may hold values from -0.15625 to 0.15625
- score_embed: bfloat16 [32768, 768], P(('audio', 'score')), may hold values from -0.21875 to 0.21875
- pair_index: int32 [16, 2048], P('audio'), may hold values from 0 to 2047, each once within a row
Outputs:
- up_grad: float32 [1280, 5120], P('audio', 'score')
- down_grad: float32 [5120, 1280], P('score', 'audio')
- score_grad: float32 [32768, 768], P(('audio', 'score'))
Inputs may be any that keep to these rules, and one draw needn't show every extreme that they name: Each row of pair_index names every one of the 2048 score rows of its group exactly once.
All inputs are finite; a program needn't handle non-finite values.
Results may differ from a plain program's by a relative error of at most 0.025.
Values may be sent and summed in bfloat16 or wider, within the bound.
No kernel may reach another device: no remote copies, remote signals or barrier semaphores. Data moves between devices by JAX's collectives and lax.ppermute only.
A program may use at most 128 MiB of HBM per device.

v0:
```python
import jax
import jax.numpy as jnp
from jax import lax
from jax.sharding import PartitionSpec as P

logit_scale = 8.0
logit_bias = -3.0
epsilon = 1e-06
gelu_root = 0.7978845608028654
gelu_cubic = 0.044715


def gelu_slope(pre):
    inner = gelu_root * (pre + gelu_cubic * pre * pre * pre)
    tangent = jnp.tanh(inner)
    return 0.5 * (1.0 + tangent) + 0.5 * pre * (1.0 - tangent * tangent) * gelu_root * (
        1.0 + 3.0 * gelu_cubic * pre * pre
    )


def unit_rows(values):
    wide = values.astype(jnp.float32)
    inverse = lax.rsqrt(jnp.sum(wide * wide, axis=-1, keepdims=True) + epsilon)
    return (wide * inverse, inverse)


def unit_backward(unit_wide, inverse, grad_unit):
    inner = jnp.sum(unit_wide * grad_unit, axis=-1, keepdims=True)
    return inverse * (grad_unit - unit_wide * inner)


def pair_coeffs(left, right, partner):
    logits = (
        logit_scale * jnp.einsum("ie,je->ij", left, right, preferred_element_type=jnp.float32)
        + logit_bias
    )
    columns = lax.iota(jnp.int32, right.shape[0])
    sign = jnp.where(partner[:, None] == columns[None, :], 1.0, -1.0)
    return (-logit_scale * sign * jax.nn.sigmoid(-sign * logits)).astype(jnp.bfloat16)


def per_device(hidden_in, up_weight, down_weight, head_weight, score_embed, pair_index):
    group_rows = hidden_in.shape[0]
    row_count = group_rows // lax.axis_size("score")
    own_start = lax.axis_index("score") * row_count
    square_mean = jnp.mean(jnp.square(hidden_in.astype(jnp.float32)), axis=-1, keepdims=True)
    normed = (hidden_in.astype(jnp.float32) * lax.rsqrt(square_mean + epsilon)).astype(jnp.bfloat16)
    pre_act = jnp.dot(normed, up_weight, preferred_element_type=jnp.float32)
    act_out = jax.nn.gelu(pre_act, approximate=True).astype(jnp.bfloat16)
    block = act_out
    mlp_sum = lax.psum_scatter(
        jnp.dot(block, down_weight, preferred_element_type=jnp.float32).astype(jnp.bfloat16),
        "score",
        scatter_dimension=0,
        tiled=True,
    ).astype(jnp.float32)
    own_hidden = lax.dynamic_slice_in_dim(hidden_in, own_start, row_count, 0)
    layer_out = (own_hidden.astype(jnp.float32) + mlp_sum).astype(jnp.bfloat16)
    audio_wide, audio_inverse = unit_rows(
        jnp.dot(layer_out, head_weight, preferred_element_type=jnp.float32)
    )
    audio_unit = audio_wide.astype(jnp.bfloat16)
    score_wide, score_inverse = unit_rows(score_embed)
    score_unit = score_wide.astype(jnp.bfloat16)
    partners = pair_index[0]
    own_partners = lax.dynamic_slice_in_dim(partners, own_start, row_count, 0)
    piece = lax.all_gather(score_unit, "score", axis=0, tiled=True)
    coeffs = pair_coeffs(audio_unit, piece, own_partners)
    total = jnp.dot(coeffs, piece, preferred_element_type=jnp.float32)
    block = coeffs
    grad_score = lax.psum_scatter(
        jnp.einsum("ij,ie->je", block, audio_unit, preferred_element_type=jnp.float32).astype(
            jnp.bfloat16
        ),
        "score",
        scatter_dimension=0,
        tiled=True,
    ).astype(jnp.float32)
    score_grad = unit_backward(score_wide, score_inverse, grad_score)
    grad_embed = unit_backward(audio_wide, audio_inverse, total).astype(jnp.bfloat16)
    grad_layer = jnp.einsum(
        "re,we->rw", grad_embed, head_weight, preferred_element_type=jnp.float32
    ).astype(jnp.bfloat16)
    piece = lax.all_gather(grad_layer, "score", axis=0, tiled=True)
    block = act_out
    down_total = jnp.einsum("rf,rw->fw", block, piece, preferred_element_type=jnp.float32)
    backward = jnp.einsum("rw,fw->rf", piece, down_weight, preferred_element_type=jnp.float32)
    grad_act = backward
    down_part, grad_act = (down_total, grad_act)
    grad_pre = (grad_act * gelu_slope(pre_act)).astype(jnp.bfloat16)
    up_part = jnp.einsum("rw,rf->wf", normed, grad_pre, preferred_element_type=jnp.float32)
    up_grad, down_grad = (
        lax.psum_scatter(
            up_part.astype(jnp.bfloat16), "audio", scatter_dimension=0, tiled=True
        ).astype(jnp.float32),
        lax.psum_scatter(
            down_part.astype(jnp.bfloat16), "audio", scatter_dimension=1, tiled=True
        ).astype(jnp.float32),
    )
    return (up_grad, down_grad, score_grad)


def solution(mesh):
    in_specs = (
        P("audio", None),
        P(None, "score"),
        P("score", None),
        P(),
        P(("audio", "score"), None),
        P("audio", None),
    )
    out_specs = (P("audio", "score"), P("score", "audio"), P(("audio", "score"), None))
    return jax.shard_map(
        per_device, mesh=mesh, in_specs=in_specs, out_specs=out_specs, check_vma=False
    )
```

profile of v0, /device:TPU:1, one launch (start us, length us, event | category | flops | bytes accessed | tf_op | source)
XLA Modules:
  0.0 791.1 jit_solution(7122434601092033182)
XLA Ops:
  7.2 3.7 fusion
  11.4 3.2 fusion.25
  14.7 1.6 copy-done.6
  16.2 4.9 convolution_convert_fusion
  21.2 0.9 copy-done.3
  22.2 0.8 fusion.28
  23.0 0.7 dynamic-slice_bitcast_fusion
  23.7 213.6 %reduce-scatter.5.cloned.1.call-done = bf16[128,1280]{1,0:T(8,128)(2,1)} async-done(((bf16[2048,1280]{1,0:T(8,128)(2,1)}), bf16[128,1280]{1,0:T(8,128)(2,1)}) %reduce-scatter.5.cloned.1.call-update) | async-done | bytes 327696 | tf_op jit(solution)/shard_map/reduce_scatter | solution.py:51
  237.3 1.6 multiply_reduce_fusion.1
  238.9 93.5 %all-gather.3.cloned.1.call-done = bf16[2048,768]{1,0:T(8,128)(2,1)} async-done(((bf16[128,768]{1,0:T(8,128)(2,1)}), bf16[2048,768]{1,0:T(8,128)(2,1)}) %all-gather.3.cloned.1.call-update) | async-done | bytes 3145744 | tf_op jit(solution)/shard_map/all_gather | solution.py:67
  332.4 3.3 fusion.23
  335.7 0.7 multiply_reduce_fusion
  336.4 1.5 convolution_convert_fusion.4
  338.1 2.7 convolution_convert_fusion.1
  341.0 102.1 %all-gather.5.cloned.1.call-done = bf16[2048,1280]{1,0:T(8,128)(2,1)} async-done(((bf16[128,1280]{1,0:T(8,128)(2,1)}), bf16[2048,1280]{1,0:T(8,128)(2,1)}) %all-gather.5.cloned.1.call-update) | async-done | bytes 5242896 | tf_op jit(solution)/shard_map/all_gather | solution.py:84
  443.1 10.8 %convolution_convert_fusion.3 = bf16[1280,320]{1,0:T(8,128)(2,1)} fusion(bf16[2048,1280]{1,0:T(8,128)(2,1)} %param.6, f32[2048]{0:T(1024)S(1)} %add_rsqrt_fusion, bf16[2048,1280]{1,0:T(8,128)(2,1)} %all-gather.5.cloned.1.call-done, bf16[320,1280]{1,0:T(8,128)(2,1)S(1)} %copy-done.5, f32[2048,320]{0,1:T(8,128)} %copy-done.6), kind=kOutput, calls=%fused_computation.11 | convolution fusion | flops 3376168960 | bytes 14753792 | tf_op jit(solution)/shard_map/rw,rf->wf/dot_general | solution.py:91
  454.0 7.2 convolution_convert_fusion.2
  461.3 191.6 %reduce-scatter.11.cloned.1.call-done = bf16[128,768]{1,0:T(8,128)(2,1)} async-done(((bf16[2048,768]{1,0:T(8,128)(2,1)}), bf16[128,768]{1,0:T(8,128)(2,1)}) %reduce-scatter.11.cloned.1.call-update) | async-done | bytes 196624 | tf_op jit(solution)/shard_map/reduce_scatter | solution.py:71
  652.9 1.1 fusion.30
  654.1 1.9 fusion.31
  655.9 62.0 %reduce-scatter.7.cloned.1.call-done = bf16[80,320]{1,0:T(8,128)(2,1)} async-done(((bf16[1280,320]{1,0:T(8,128)(2,1)}), bf16[80,320]{1,0:T(8,128)(2,1)}) %reduce-scatter.7.cloned.1.call-update) | async-done | bytes 51216 | tf_op jit(solution)/shard_map/reduce_scatter | solution.py:93
  718.0 1.5 convert_element_type.76
  719.4 63.4 %reduce-scatter.9.cloned.1.call-done = bf16[320,80]{0,1:T(8,128)(2,1)} async-done(((bf16[320,1280]{0,1:T(8,128)(2,1)}), bf16[320,80]{0,1:T(8,128)(2,1)}) %reduce-scatter.9.cloned.1.call-update) | async-done | bytes 51216 | tf_op jit(solution)/shard_map/reduce_scatter | solution.py:96
  782.8 1.5 convert_element_type.78
  (28 shorter events, 1.1 us)
Async XLA Ops:
  7.2 230.1 %copy-start = (bf16[1280,768]{1,0:T(8,128)(2,1)S(1)}, bf16[1280,768]{1,0:T(8,128)(2,1)}, u32[]{:S(2)}) copy-start(bf16[1280,768]{1,0:T(8,128)(2,1)} %param.9) | copy-start | bytes 5898244
  7.2 230.1 %reduce-scatter.5.cloned.1.call-start = ((), (), s32[]{:S(2)}) async-start(), calls=%async_computation.4 | async-start | bytes 5570560 | tf_op jit(solution)/shard_map/reduce_scatter | solution.py:51
  7.2 4.2 copy-start.1
  11.4 4.8 copy-start.4
  14.6 1.6 copy-start.6
  21.1 0.9 copy-start.3
  21.1 311.3 %all-gather.3.cloned.1.call-start = ((), (), s32[]{:S(2)}) async-start(), calls=%async_computation.5 | async-start | bytes 3342336 | tf_op jit(solution)/shard_map/all_gather | solution.py:67
  23.0 420.1 %all-gather.5.cloned.1.call-start = ((), (), s32[]{:S(2)}) async-start(), calls=%async_computation.6 | async-start | bytes 5570560 | tf_op jit(solution)/shard_map/all_gather | solution.py:84
  332.4 3.3 copy-start.2
  338.0 314.9 %reduce-scatter.11.cloned.1.call-start = ((), (), s32[]{:S(2)}) async-start(), calls=%async_computation.9 | async-start | bytes 3342336 | tf_op jit(solution)/shard_map/reduce_scatter | solution.py:71
  340.8 102.4 %copy-start.5 = (bf16[320,1280]{1,0:T(8,128)(2,1)S(1)}, bf16[320,1280]{1,0:T(8,128)(2,1)}, u32[]{:S(2)}) copy-start(bf16[320,1280]{1,0:T(8,128)(2,1)} %param.8) | copy-start | bytes 2457604
  340.8 377.2 %reduce-scatter.7.cloned.1.call-start = ((), (), s32[]{:S(2)}) async-start(), calls=%async_computation.7 | async-start | bytes 1044480 | tf_op jit(solution)/shard_map/reduce_scatter | solution.py:93
  454.0 328.8 %reduce-scatter.9.cloned.1.call-start = ((), (), s32[]{:S(2)}) async-start(), calls=%async_computation.8 | async-start | bytes 1044480 | tf_op jit(solution)/shard_map/reduce_scatter | solution.py:96
Sparse Core Ops, SparseCore 0:
  21.2 216.0 reduce-scatter.4
  240.8 91.5 all-gather.2
  338.1 104.9 all-gather.4
  447.5 205.3 reduce-scatter.10
  655.3 62.6 reduce-scatter.6
  720.5 62.2 reduce-scatter.8
where the time goes:
time: 794 us; the launch traced here: 791 us
  waiting for transfers between devices  726 us (91%)
  matrix products  36 us (5%)
  between operations  14.2 us (2%)
  other arithmetic  10.6 us (1%)
    reduce_scatter x1, waiting for transfers between devices, per_device(): lax.psum_scatter(jnp.dot(block, down_weight, preferred_element_type=jnp.f...  214 us
    reduce_scatter x1, waiting for transfers between devices, per_device(): lax.psum_scatter(jnp.einsum('ij,ie->je', block, audio_unit, preferred_ele...  192 us
    all_gather x1, waiting for transfers between devices, per_device(): piece = lax.all_gather(grad_layer, 'score', axis=0, tiled=True)  102 us
    all_gather x1, waiting for transfers between devices, per_device(): piece = lax.all_gather(score_unit, 'score', axis=0, tiled=True)  93.5 us
    reduce_scatter x1, waiting for transfers between devices, per_device(): lax.psum_scatter(down_part.astype(jnp.bfloat16), 'audio', scatter_dimensi...  63.4 us
    reduce_scatter x1, waiting for transfers between devices, per_device(): lax.psum_scatter(up_part.astype(jnp.bfloat16), 'audio', scatter_dimension...  62 us
  transfers between devices with their start and end apart: 6, of which 6 were waited for; matrix products, arithmetic and copies ran while one was open for 4% of the time, Pallas kernels for 0%

commit v1 on v0

v1 whole, which is shorter than its diff:
```python
import jax
import jax.numpy as jnp
from jax import lax
from jax.sharding import Mesh, PartitionSpec as P

logit_scale = 8.0
logit_bias = -3.0
epsilon = 1e-06
gelu_root = 0.7978845608028654
gelu_cubic = 0.044715

AUDIO = ("ylo", "x", "core")
SCORE = ("yhi", "z")
f32 = jnp.float32
bf16 = jnp.bfloat16


def dot(left, right, dims):
    return lax.dot_general(left, right, (dims, ((), ())), preferred_element_type=f32)


def gelu_slope(pre):
    inner = gelu_root * (pre + gelu_cubic * pre * pre * pre)
    tangent = jnp.tanh(inner)
    return 0.5 * (1.0 + tangent) + 0.5 * pre * (1.0 - tangent * tangent) * gelu_root * (
        1.0 + 3.0 * gelu_cubic * pre * pre
    )


def unit_rows(values):
    wide = values.astype(f32)
    inverse = lax.rsqrt(jnp.sum(wide * wide, axis=-1, keepdims=True) + epsilon)
    return (wide * inverse, inverse)


def unit_backward(unit_wide, inverse, grad_unit):
    inner = jnp.sum(unit_wide * grad_unit, axis=-1, keepdims=True)
    return inverse * (grad_unit - unit_wide * inner)


def pair_coeffs(left, right, partner, first_column):
    logits = logit_scale * dot(left, right, ((1,), (1,))) + logit_bias
    columns = first_column + lax.iota(jnp.int32, right.shape[0])
    sign = jnp.where(partner[:, None] == columns[None, :], 1.0, -1.0)
    return (-logit_scale * sign * jax.nn.sigmoid(-sign * logits)).astype(bf16)


def swap(value, axis):
    return lax.ppermute(value, axis, [(0, 1), (1, 0)])


def per_device(hidden_in, up_weight, down_weight, head_weight, score_embed, pair_index):
    y_hi, z = lax.axis_index("yhi"), lax.axis_index("z")
    group_rows = hidden_in.shape[0]
    own_rows = group_rows // 8
    half = group_rows // 2
    score_wide, score_inverse = unit_rows(score_embed)
    score_half = lax.all_gather(score_wide.astype(bf16), "z", axis=0, tiled=True)
    down_head = dot(down_weight, head_weight, ((1,), (0,))).astype(bf16)
    square_mean = jnp.mean(jnp.square(hidden_in.astype(f32)), axis=-1, keepdims=True)
    normed = (hidden_in.astype(f32) * lax.rsqrt(square_mean + epsilon)).astype(bf16)
    pre_act = dot(normed, up_weight, ((1,), (0,)))
    act_out = jax.nn.gelu(pre_act, approximate=True).astype(bf16)
    part = dot(act_out, down_head, ((1,), (0,))).astype(bf16)
    summed = lax.psum_scatter(part, "z", scatter_dimension=0, tiled=True)
    own_hidden = lax.dynamic_slice_in_dim(hidden_in, z * own_rows, own_rows, 0)
    own_proj = dot(own_hidden, head_weight, ((1,), (0,)))
    audio_proj = own_proj + (summed.astype(f32) + swap(summed, "yhi").astype(f32))
    audio_wide, audio_inverse = unit_rows(audio_proj)
    audio_unit = audio_wide.astype(bf16)
    partners = lax.dynamic_slice_in_dim(pair_index[0], z * own_rows, own_rows, 0)
    coeffs = pair_coeffs(audio_unit, score_half, partners, y_hi * half)
    grad_audio = dot(coeffs, score_half, ((1,), (0,)))
    grad_audio = grad_audio + swap(grad_audio.astype(bf16), "yhi").astype(f32)
    grad_embed = unit_backward(audio_wide, audio_inverse, grad_audio).astype(bf16)
    grad_all = lax.all_gather(grad_embed, "z", axis=0, tiled=True)
    grad_score = lax.psum_scatter(
        dot(coeffs, audio_unit, ((0,), (0,))).astype(bf16), "z", scatter_dimension=0, tiled=True
    ).astype(f32)
    score_grad = unit_backward(score_wide, score_inverse, grad_score)
    grad_act = dot(grad_all, down_head, ((1,), (1,)))
    grad_pre = (grad_act * gelu_slope(pre_act)).astype(bf16)
    up_part = dot(normed, grad_pre, ((0,), (0,)))
    act_grad = dot(act_out, grad_all, ((0,), (0,))).astype(bf16)
    down_part = dot(head_weight, act_grad, ((1,), (1,)))
    both = jnp.concatenate([up_part.astype(bf16), down_part.astype(bf16)], axis=1)
    both = both.reshape(8, 2, 80, both.shape[1])
    core = lax.axis_index("core")
    keep = lax.dynamic_index_in_dim(both, core, 1, keepdims=False)
    give = lax.dynamic_index_in_dim(both, 1 - core, 1, keepdims=False)
    chip = (keep.astype(f32) + swap(give, "core").astype(f32)).astype(bf16)
    landed = lax.all_to_all(chip, ("ylo", "x"), 0, 0)
    total = jnp.sum(landed.astype(f32), axis=0)
    ff = up_weight.shape[1]
    return (total[:, :ff], total[:, ff:].T, score_grad)


def solution(mesh):
    fine = Mesh(mesh.devices.reshape(2, 4, 2, 2, 8), ("ylo", "x", "core", "yhi", "z"))
    in_specs = (
        P(AUDIO, None),
        P(None, SCORE),
        P(SCORE, None),
        P(),
        P(AUDIO + SCORE, None),
        P(AUDIO, None),
    )
    out_specs = (P(AUDIO, SCORE), P(SCORE, AUDIO), P(AUDIO + SCORE, None))
    return jax.shard_map(
        per_device, mesh=fine, in_specs=in_specs, out_specs=out_specs, check_vma=False
    )
```

time: 794 us -> 223 us (0.28)
  waiting for transfers between devices: 726 us -> 145 us
  starting transfers between devices: 0.43 us -> 11.9 us
    reduce_scatter x4 -> x2, waiting for transfers between devices: 531 us -> 52.2 us  [the longest x1 46.2 us: per_device(): summed = lax.psum_scatter(part, 'z', scatter_dimension=0, tiled=True)]
    all_gather x2, waiting for transfers between devices: 196 us -> 75.7 us  [the longest x1 46.4 us: per_device(): grad_all = lax.all_gather(grad_embed, 'z', axis=0, tiled=True)]
    ppermute x0 -> x3, waiting for transfers between devices: none -> 13 us  [swap(): return lax.ppermute(value, axis, [(0, 1), (1, 0)])]
  transfers between devices with their start and end apart: 6 -> 8, of which waited for: 6 -> 8; matrix products, arithmetic and copies ran while one was open for 4% -> 14% of each run, Pallas kernels for 0% -> 0%
where the time goes in v1:
time: 223 us
  waiting for transfers between devices  145 us (65%)
  matrix products  28.7 us (13%)
  other arithmetic  13.9 us (6%)
  between operations  13.9 us (6%)
  starting transfers between devices  11.9 us (5%)
  local copies, waits for them, and re-layouts  9 us (4%)
    all_gather x1, waiting for transfers between devices, per_device(): grad_all = lax.all_gather(grad_embed, 'z', axis=0, tiled=True)  46.4 us
    reduce_scatter x1, waiting for transfers between devices, per_device(): summed = lax.psum_scatter(part, 'z', scatter_dimension=0, tiled=True)  46.2 us
    all_gather x1, waiting for transfers between devices, per_device(): lax.all_gather(score_wide.astype(bf16), 'z', axis=0, tiled=True)  29.3 us
    dot_general x9, matrix products, dot(): lax.dot_general(left, right, (dims, ((), ())), preferred_element_type=f32)  28.7 us
    ppermute x3, waiting for transfers between devices, swap(): return lax.ppermute(value, axis, [(0, 1), (1, 0)])  13 us
    ppermute x3, starting transfers between devices, swap(): return lax.ppermute(value, axis, [(0, 1), (1, 0)])  6.65 us
    reduce_scatter x1, waiting for transfers between devices, per_device(): lax.psum_scatter(dot(coeffs, audio_unit, ((0,), (0,))).astype(bf16), 'z',...  5.96 us
    all_to_all x1, starting transfers between devices, per_device(): landed = lax.all_to_all(chip, ('ylo', 'x'), 0, 0)  4.89 us
  transfers between devices with their start and end apart: 8, of which 8 were waited for; matrix products, arithmetic and copies ran while one was open for 14% of the time, Pallas kernels for 0%

profile of v1, /device:TPU:1, one launch (start us, length us, event | category | flops | bytes accessed | tf_op | source)
XLA Modules:
  0.0 222.8 jit_solution(16198763368518437809)
XLA Ops:
  7.2 3.7 %fusion = f32[2048]{0:T(1024)S(1)} fusion(bf16[2048,1280]{1,0:T(8,128)(2,1)} %param.6), kind=kLoop, calls=%fused_computation.2 | loop fusion | flops 7862272 | bytes 5251072 | tf_op jit(solution)/shard_map/reduce_sum | solution.py:60
  11.4 3.2 %fusion.18 = f32[2048,320]{0,1:T(8,128)S(1)} fusion(bf16[1280,320]{0,1:T(8,128)(2,1)} %param.7, bf16[2048,1280]{1,0:T(8,128)(2,1)S(1)} %copy-done.1, f32[2048]{0:T(1024)S(1)} %add_rsqrt_fusion), kind=kOutput, calls=%fused_computation.26 | convolution fusion | flops 1685585920 | bytes 8691712 | tf_op jit(solution)/shard_map/dot_general | solution.py:19
  17.0 3.7 %convolution_convert_fusion = bf16[2048,768]{1,0:T(8,128)(2,1)} fusion(bf16[320,768]{1,0:T(8,128)(2,1)S(1)} %convolution_convert_fusion.4, f32[2048,320]{0,1:T(8,128)S(1)} %fusion.18), kind=kOutput, calls=%fused_computation.7 | convolution fusion | flops 1014104064 | bytes 6258688 | tf_op jit(solution)/shard_map/dot_general | solution.py:19
  22.6 46.2 %reduce-scatter.3.cloned.1.call-done = bf16[256,768]{1,0:T(8,128)(2,1)} async-done(((bf16[2048,768]{1,0:T(8,128)(2,1)}), bf16[256,768]{1,0:T(8,128)(2,1)}) %reduce-scatter.3.cloned.1.call-update) | async-done | bytes 393232 | tf_op jit(solution)/shard_map/reduce_scatter | solution.py:65
  68.8 2.8 %collective-permute-start = (bf16[256,768]{1,0:T(8,128)(2,1)}, bf16[256,768]{1,0:T(8,128)(2,1)S(1)}, u32[]{:S(2)}, u32[]{:S(2)}) collective-permute-start(bf16[256,768]{1,0:T(8,128)(2,1)} %reduce-scatter.3.cloned.1.call-done), channel_id=1, source_target_pairs={{0,8},{8,0},{1,9},{9,1},{2,10},{10,2},{3,11},{11,3},{4,12},{12,4},... | collective-permute-start | bytes 1179656 | tf_op jit(solution)/shard_map/ppermute | solution.py:49
  72.4 5.5 %collective-permute-done = bf16[256,768]{1,0:T(8,128)(2,1)S(1)} collective-permute-done((bf16[256,768]{1,0:T(8,128)(2,1)}, bf16[256,768]{1,0:T(8,128)(2,1)S(1)}, u32[]{:S(2)}, u32[]{:S(2)}) %collective-permute-start) | collective-permute-done | bytes 393248 | tf_op jit(solution)/shard_map/ppermute | solution.py:49
  77.9 2.0 multiply_reduce_fusion.1
  79.9 29.3 %all-gather.3.cloned.1.call-done = bf16[1024,768]{1,0:T(8,128)(2,1)} async-done(((bf16[128,768]{1,0:T(8,128)(2,1)}), bf16[1024,768]{1,0:T(8,128)(2,1)}) %all-gather.3.cloned.1.call-update) | async-done | bytes 1572880 | tf_op jit(solution)/shard_map/all_gather | solution.py:58
  109.2 2.4 %fusion.28 = bf16[256,1024]{1,0:T(8,128)(2,1)S(1)} fusion(bf16[1024,768]{1,0:T(8,128)(2,1)} %all-gather.3.cloned.1.call-done, s32[1024]{0:T(1024)S(1)} %iota_add_fusion, s32[256]{0:T(256)S(1)} %bitcast.26, f32[256,768]{1,0:T(8,128)S(1)} %get-tuple-element.6, f32[256]{0:T(256)S(1)} %add_rsqrt_fusion.1), kind=kOutput, calls=%fused_computation.42 | convolution fusion | flops 406192128 | bytes 2889728 | tf_op jit(solution)/shard_map/dot_general | solution.py:19
  112.2 2.8 %collective-permute-start.1 = (bf16[256,768]{1,0:T(8,128)(2,1)S(1)}, bf16[256,768]{1,0:T(8,128)(2,1)S(1)}, u32[]{:S(2)}, u32[]{:S(2)}) collective-permute-start(bf16[256,768]{1,0:T(8,128)(2,1)S(1)} %get-tuple-element.7), channel_id=1, source_target_pairs={{0,8},{8,0},{1,9},{9,1},{2,10},{10,2},{3,11},{11,3},{4,12},{12,4},... | collective-permute-start | bytes 1179656 | tf_op jit(solution)/shard_map/ppermute | solution.py:49
  115.0 5.4 %collective-permute-done.1 = bf16[256,768]{1,0:T(8,128)(2,1)S(1)} collective-permute-done((bf16[256,768]{1,0:T(8,128)(2,1)S(1)}, bf16[256,768]{1,0:T(8,128)(2,1)S(1)}, u32[]{:S(2)}, u32[]{:S(2)}) %collective-permute-start.1) | collective-permute-done | bytes 393248 | tf_op jit(solution)/shard_map/ppermute | solution.py:49
  121.9 1.9 convolution_convert_fusion.3
  123.8 46.4 %all-gather.5.cloned.1.call-done = bf16[2048,768]{1,0:T(8,128)(2,1)} async-done(((bf16[256,768]{1,0:T(8,128)(2,1)}), bf16[2048,768]{1,0:T(8,128)(2,1)}) %all-gather.5.cloned.1.call-update) | async-done | bytes 3145744 | tf_op jit(solution)/shard_map/all_gather | solution.py:76
  170.1 5.3 %fusion.16 = bf16[1280,320]{0,1:T(8,128)(2,1)S(1)} fusion(bf16[1280,768]{1,0:T(8,128)(2,1)S(1)} %copy-done, bf16[2048,768]{1,0:T(8,128)(2,1)} %all-gather.5.cloned.1.call-done, f32[2048,320]{0,1:T(8,128)} %copy-done.5), kind=kOutput, calls=%fused_computation.25 | convolution fusion | flops 1642332160 | bytes 8552448 | tf_op jit(solution)/shard_map/dot_general | solution.py:19
  175.4 8.9 %convolution_convert_fusion.1 = bf16[1280,320]{0,1:T(8,128)(2,1)} fusion(bf16[2048,1280]{1,0:T(8,128)(2,1)} %param.6, f32[2048]{0:T(1024)S(1)} %add_rsqrt_fusion, bf16[2048,768]{1,0:T(8,128)(2,1)} %all-gather.5.cloned.1.call-done, bf16[320,768]{1,0:T(8,128)(2,1)S(1)} %copy-done.7, f32[2048,320]{0,1:T(8,128)} %copy-done.5), kind=kOutput, calls=%fused_computation.10 | convolution fusion | flops 2705080320 | bytes 12328960 | tf_op jit(solution)/shard_map/dot_general | solution.py:19
  184.4 2.4 %pad_maximum_fusion = bf16[1280,640]{0,1:T(8,128)(2,1)} fusion(bf16[1280,320]{0,1:T(8,128)(2,1)S(1)} %fusion.16, bf16[1280,320]{0,1:T(8,128)(2,1)} %convolution_convert_fusion.1), kind=kLoop, calls=%fused_computation.28 | loop fusion | flops 3276800 | bytes 3276800 | tf_op jit(solution)/shard_map/concatenate | solution.py:86
  186.8 3.5 %copy.9 = bf16[1280,640]{1,0:T(8,128)(2,1)} copy(bf16[1280,640]{0,1:T(8,128)(2,1)} %pad_maximum_fusion) | data formatting | bytes 3276800 | tf_op jit(solution)/shard_map/concatenate | solution.py:86
  190.3 1.2 dynamic-slice_bitcast_fusion
  192.5 2.1 collective-permute-done.2
  194.6 2.5 %fusion.20 = bf16[8,80,640]{2,1,0:T(8,128)(2,1)} fusion(bf16[8,80,640]{2,1,0:T(8,128)(2,1)} %collective-permute-done.2, bf16[8,2,80,640]{3,2,1,0:T(8,128)(2,1)} %bitcast.25, s32[]{:T(128)S(6)} %select_n.17), kind=kLoop, calls=%fused_computation.30 | loop fusion | flops 1638400 | bytes 2457604 | tf_op jit(solution)/shard_map/convert_element_type | solution.py:91
  197.1 4.9 %all-to-all-start = ((bf16[8,80,640]{2,1,0:T(8,128)(2,1)}), bf16[8,80,640]{2,1,0:T(8,128)(2,1)S(1)}, u32[]{:S(2)}, u32[]{:S(2)}) async-start(bf16[8,80,640]{2,1,0:T(8,128)(2,1)} %fusion.20), calls=%async_computation.1 | async-start | bytes 1638400 | tf_op jit(solution)/shard_map/all_to_all | solution.py:92
  202.0 6.0 %reduce-scatter.5.cloned.1.call-done = bf16[128,768]{1,0:T(8,128)(2,1)} async-done(((bf16[1024,768]{1,0:T(8,128)(2,1)}), bf16[128,768]{1,0:T(8,128)(2,1)}) %reduce-scatter.5.cloned.1.call-update) | async-done | bytes 196624 | tf_op jit(solution)/shard_map/reduce_scatter | solution.py:77
  209.1 1.9 fusion.37
  211.0 4.4 %all-to-all-done = bf16[8,80,640]{2,1,0:T(8,128)(2,1)S(1)} async-done(((bf16[8,80,640]{2,1,0:T(8,128)(2,1)}), bf16[8,80,640]{2,1,0:T(8,128)(2,1)S(1)}, u32[]{:S(2)}, u32[]{:S(2)}) %all-to-all-start) | async-done | bytes 819232 | tf_op jit(solution)/shard_map/all_to_all | solution.py:92
  (39 shorter events, 10.4 us)
Async XLA Ops:
  7.2 7.5 %copy-start = (bf16[1280,768]{1,0:T(8,128)(2,1)S(1)}, bf16[1280,768]{1,0:T(8,128)(2,1)}, u32[]{:S(2)}) copy-start(bf16[1280,768]{1,0:T(8,128)(2,1)} %param.9) | copy-start | bytes 5898244
  7.2 61.7 %reduce-scatter.3.cloned.1.call-start = ((), (), s32[]{:S(2)}) async-start(), calls=%async_computation.3 | async-start | bytes 3538944 | tf_op jit(solution)/shard_map/reduce_scatter | solution.py:65
  7.2 4.2 %copy-start.1 = (bf16[2048,1280]{1,0:T(8,128)(2,1)S(1)}, bf16[2048,1280]{1,0:T(8,128)(2,1)}, u32[]{:S(2)}) copy-start(bf16[2048,1280]{1,0:T(8,128)(2,1)} %param.6) | copy-start | bytes 15728644
  11.4 3.3 %copy-start.4 = (bf16[320,1280]{1,0:T(8,128)(2,1)S(1)}, bf16[320,1280]{1,0:T(8,128)(2,1)}, u32[]{:S(2)}) copy-start(bf16[320,1280]{1,0:T(8,128)(2,1)} %param.8) | copy-start | bytes 2457604
  14.7 1.5 copy-start.5
  16.2 0.8 copy-start.6
  20.7 0.9 copy-start.2
  20.7 88.5 %all-gather.3.cloned.1.call-start = ((), (), s32[]{:S(2)}) async-start(), calls=%async_computation.4 | async-start | bytes 1769472 | tf_op jit(solution)/shard_map/all_gather | solution.py:58
  22.5 147.6 %all-gather.5.cloned.1.call-start = ((), (), s32[]{:S(2)}) async-start(), calls=%async_computation.5 | async-start | bytes 3538944 | tf_op jit(solution)/shard_map/all_gather | solution.py:76
  68.8 9.1 %collective-permute-start = (bf16[256,768]{1,0:T(8,128)(2,1)}, bf16[256,768]{1,0:T(8,128)(2,1)S(1)}, u32[]{:S(2)}, u32[]{:S(2)}) collective-permute-start(bf16[256,768]{1,0:T(8,128)(2,1)} %reduce-scatter.3.cloned.1.call-done), channel_id=1, source_target_pairs={{0,8},{8,0},{1,9},{9,1},{2,10},{10,2},{3,11},{11,3},{4,12},{12,4},... | collective-permute-start | bytes 1179656 | tf_op jit(solution)/shard_map/ppermute | solution.py:49
  109.2 2.4 %copy-start.3 = (bf16[1024,768]{1,0:T(8,128)(2,1)S(1)}, bf16[1024,768]{1,0:T(8,128)(2,1)}, u32[]{:S(2)}) copy-start(bf16[1024,768]{1,0:T(8,128)(2,1)} %all-gather.3.cloned.1.call-done) | copy-start | bytes 4718596
  112.2 8.2 %collective-permute-start.1 = (bf16[256,768]{1,0:T(8,128)(2,1)S(1)}, bf16[256,768]{1,0:T(8,128)(2,1)S(1)}, u32[]{:S(2)}, u32[]{:S(2)}) collective-permute-start(bf16[256,768]{1,0:T(8,128)(2,1)S(1)} %get-tuple-element.7), channel_id=1, source_target_pairs={{0,8},{8,0},{1,9},{9,1},{2,10},{10,2},{3,11},{11,3},{4,12},{12,4},... | collective-permute-start | bytes 1179656 | tf_op jit(solution)/shard_map/ppermute | solution.py:49
  121.6 86.3 %reduce-scatter.5.cloned.1.call-start = ((), (), s32[]{:S(2)}) async-start(), calls=%async_computation.6 | async-start | bytes 1769472 | tf_op jit(solution)/shard_map/reduce_scatter | solution.py:77
  123.8 51.6 %copy-start.7 = (bf16[320,768]{1,0:T(8,128)(2,1)S(1)}, bf16[320,768]{1,0:T(8,128)(2,1)}, u32[]{:S(2)}) copy-start(bf16[320,768]{1,0:T(8,128)(2,1)} %copy-done.6) | copy-start | bytes 1474564
  191.5 3.1 %collective-permute-start.2 = (bf16[8,80,640]{2,1,0:T(8,128)(2,1)S(1)}, bf16[8,80,640]{2,1,0:T(8,128)(2,1)}, u32[]{:S(2)}, u32[]{:S(2)}) collective-permute-start(bf16[8,80,640]{2,1,0:T(8,128)(2,1)S(1)} %dynamic-slice_bitcast_fusion), channel_id=1, source_target_pairs={{0,16},{16,0},{1,17},{17,1},{2,18},{18,2},{3,19},{19,3},{4,20},{20... | collective-permute-start | bytes 2457608 | tf_op jit(solution)/shard_map/ppermute | solution.py:49
  197.1 18.3 %all-to-all-start = ((bf16[8,80,640]{2,1,0:T(8,128)(2,1)}), bf16[8,80,640]{2,1,0:T(8,128)(2,1)S(1)}, u32[]{:S(2)}, u32[]{:S(2)}) async-start(bf16[8,80,640]{2,1,0:T(8,128)(2,1)} %fusion.20), calls=%async_computation.1 | async-start | bytes 1638400 | tf_op jit(solution)/shard_map/all_to_all | solution.py:92
Sparse Core Ops, SparseCore 0:
  20.8 47.9 reduce-scatter.2
  71.2 37.9 all-gather.2
  121.8 48.3 all-gather.4
  172.6 35.3 reduce-scatter.4

commit v2 on v1

v2 whole, which is shorter than its diff:
```python
import functools

import jax
import jax.numpy as jnp
from jax import lax
from jax.experimental import pallas as pl
from jax.experimental.pallas import tpu as pltpu
from jax.sharding import Mesh, PartitionSpec as P

logit_scale = 8.0
logit_bias = -3.0
epsilon = 1e-06
gelu_root = 0.7978845608028654
gelu_cubic = 0.044715

AUDIO = ("ylo", "x", "core")
SCORE = ("yhi", "z")
RING = 8
VMEM_BYTES = 40 * 1024 * 1024
f32 = jnp.float32
bf16 = jnp.bfloat16


def dot(left, right, dims=((1,), (0,))):
    return lax.dot_general(left, right, (dims, ((), ())), preferred_element_type=f32)


def unit_rows(values):
    wide = values.astype(f32)
    inverse = lax.rsqrt(jnp.sum(wide * wide, axis=-1, keepdims=True) + epsilon)
    return (wide * inverse, inverse)


def unit_backward(unit_wide, inverse, grad_unit):
    inner = jnp.sum(unit_wide * grad_unit, axis=-1, keepdims=True)
    return inverse * (grad_unit - unit_wide * inner)


def pair_coeffs(left, right, partner, first_column):
    logits = logit_scale * dot(left, right, ((1,), (1,))) + logit_bias
    columns = first_column + lax.iota(jnp.int32, right.shape[0])
    sign = jnp.where(partner[:, None] == columns[None, :], 1.0, -1.0)
    return (-logit_scale * sign * jax.nn.sigmoid(-sign * logits)).astype(bf16)


def swap(value, axis):
    return lax.ppermute(value, axis, [(0, 1), (1, 0)])


def shift(value, step):
    return lax.ppermute(value, "z", [(i, (i + step) % RING) for i in range(RING)])


def forward_kernel(index_ref, hidden_ref, up_ref, down_head_ref, part_ref, normed_t_ref, act_t_ref, slope_ref):
    wide = hidden_ref[...].astype(f32)
    square_mean = jnp.mean(wide * wide, axis=-1, keepdims=True)
    normed = wide * lax.rsqrt(square_mean + epsilon)
    normed_t_ref[...] = normed.T.astype(bf16)
    pre = dot(normed.astype(bf16), up_ref[...])
    tangent = jnp.tanh(gelu_root * (pre + gelu_cubic * (pre * pre * pre)))
    act = 0.5 * pre * (1.0 + tangent)
    slope_ref[...] = 0.5 * (1.0 + tangent) + 0.5 * pre * (1.0 - tangent * tangent) * gelu_root * (
        1.0 + 3.0 * gelu_cubic * pre * pre
    )
    act_t_ref[...] = act.T.astype(bf16)
    part_ref[...] = dot(act.astype(bf16), down_head_ref[...]).astype(bf16)


def forward_blocks(offsets, position, hidden_in, up_weight, down_head):
    count = len(offsets)
    rows = hidden_in.shape[0] // RING
    width, ff = up_weight.shape
    embed = down_head.shape[1]
    index = lax.rem(position + jnp.array([o % RING for o in offsets], jnp.int32), RING)
    return pl.pallas_call(
        forward_kernel,
        grid_spec=pltpu.PrefetchScalarGridSpec(
            num_scalar_prefetch=1,
            grid=(count,),
            in_specs=[
                pl.BlockSpec((rows, width), lambda i, index: (index[i], 0)),
                pl.BlockSpec((width, ff), lambda i, index: (0, 0)),
                pl.BlockSpec((ff, embed), lambda i, index: (0, 0)),
            ],
            out_specs=[
                pl.BlockSpec((rows, embed), lambda i, index: (i, 0)),
                pl.BlockSpec((width, rows), lambda i, index: (0, i)),
                pl.BlockSpec((ff, rows), lambda i, index: (0, i)),
                pl.BlockSpec((rows, ff), lambda i, index: (i, 0)),
            ],
        ),
        out_shape=[
            jax.ShapeDtypeStruct((count * rows, embed), bf16),
            jax.ShapeDtypeStruct((width, count * rows), bf16),
            jax.ShapeDtypeStruct((ff, count * rows), bf16),
            jax.ShapeDtypeStruct((count * rows, ff), f32),
        ],
        compiler_params=pltpu.CompilerParams(vmem_limit_bytes=VMEM_BYTES),
        cost_estimate=pl.CostEstimate(
            flops=2 * count * rows * ff * (width + embed),
            bytes_accessed=2 * count * rows * (2 * width + embed + 3 * ff) + 2 * ff * (width + embed),
            transcendentals=count * rows * ff,
        ),
    )(index, hidden_in, up_weight, down_head)


def backward_kernel(pieces, first, last, *refs):
    grads = refs[:pieces]
    down_head_ref, normed_t_ref, act_t_ref, slope_ref = refs[pieces : pieces + 4]
    rest = refs[pieces + 4 :]
    if not first:
        up_in, act_in = rest[:2]
        rest = rest[2:]
    if last:
        core_ref, head_ref, keep_ref, give_ref, up_acc, act_acc = rest
    else:
        up_acc, act_acc = rest
    tile = 256
    start = 0
    grad_pre = []
    for grad_ref in grads:
        count = grad_ref.shape[0]
        grad_act = dot(grad_ref[...], down_head_ref[...], ((1,), (1,)))
        grad_pre.append((grad_act * slope_ref[start : start + count, :]).astype(bf16))
        start += count
    start = 0
    act_sum = None
    for grad_ref in grads:
        count = grad_ref.shape[0]
        term = dot(act_t_ref[:, start : start + count], grad_ref[...])
        act_sum = term if act_sum is None else act_sum + term
        start += count
    if not first:
        act_sum = act_sum + act_in[...]
    act_acc[...] = act_sum
    grad_pre = jnp.concatenate(grad_pre, axis=0) if len(grad_pre) > 1 else grad_pre[0]

    for m in range(0, up_acc.shape[0], tile):
        up_sum = dot(normed_t_ref[m : m + tile, :], grad_pre)
        if not first:
            up_sum = up_sum + up_in[m : m + tile, :]
        up_acc[m : m + tile, :] = up_sum
    if last:
        core = core_ref[0]
        ff = up_acc.shape[1]
        act_grad = act_acc[...].astype(bf16)
        act_acc_rows = keep_ref.shape[1]
        for half, out_ref in ((core, keep_ref), (1 - core, give_ref)):
            for chip in range(keep_ref.shape[0]):
                at = pl.multiple_of((2 * chip + half) * act_acc_rows, act_acc_rows)
                out_ref[chip, :, :ff] = up_acc[pl.ds(at, act_acc_rows), :].astype(bf16)
        for m in range(0, up_acc.shape[0], tile):
            up_acc[m : m + tile, :] = dot(head_ref[m : m + tile, :], act_grad, ((1,), (1,)))
        for half, out_ref in ((core, keep_ref), (1 - core, give_ref)):
            for chip in range(keep_ref.shape[0]):
                at = pl.multiple_of((2 * chip + half) * act_acc_rows, act_acc_rows)
                out_ref[chip, :, ff:] = up_acc[pl.ds(at, act_acc_rows), :].astype(bf16)


def backward_blocks(grads, saved, down_head, sums, last=None):
    _, normed_t, act_t, slope = saved
    width, rows = normed_t.shape
    ff, embed = down_head.shape
    args = list(grads) + [down_head, normed_t, act_t, slope]
    specs = [pl.BlockSpec(memory_space=pltpu.VMEM)] * len(args)
    aliases = {}
    if sums is not None:
        if last is None:
            aliases = {len(args): 0, len(args) + 1: 1}
        args += list(sums)
        specs += [pl.BlockSpec(memory_space=pltpu.VMEM)] * 2
    flops = 2 * rows * ff * (2 * embed + width)
    if last is None:
        shapes = [jax.ShapeDtypeStruct((width, ff), f32), jax.ShapeDtypeStruct((ff, embed), f32)]
        scratch = []
    else:
        args += list(last)
        specs += [pl.BlockSpec(memory_space=pltpu.SMEM), pl.BlockSpec(memory_space=pltpu.VMEM)]
        shapes = [jax.ShapeDtypeStruct((8, width // 16, 2 * ff), bf16)] * 2
        scratch = [pltpu.VMEM((width, ff), f32), pltpu.VMEM((ff, embed), f32)]
        flops += 2 * width * ff * embed
    return pl.pallas_call(
        functools.partial(backward_kernel, len(grads), sums is None, last is not None),
        in_specs=specs,
        out_specs=[pl.BlockSpec(memory_space=pltpu.VMEM)] * 2,
        out_shape=shapes,
        scratch_shapes=scratch,
        input_output_aliases=aliases,
        compiler_params=pltpu.CompilerParams(vmem_limit_bytes=VMEM_BYTES),
        cost_estimate=pl.CostEstimate(
            flops=flops, bytes_accessed=8 * 1024 * 1024, transcendentals=0
        ),
    )(*args)


def add(left, right):
    return (left.astype(f32) + right.astype(f32)).astype(bf16)


def per_device(hidden_in, up_weight, down_weight, head_weight, score_embed, pair_index):
    y_hi, z, core = lax.axis_index("yhi"), lax.axis_index("z"), lax.axis_index("core")
    own_rows = hidden_in.shape[0] // RING
    cut = own_rows // 2
    group_half = hidden_in.shape[0] // 2
    score_wide, score_inverse = unit_rows(score_embed)
    score_half = lax.all_gather(score_wide.astype(bf16), "z", axis=0, tiled=True)
    down_head = dot(down_weight, head_weight).astype(bf16)
    saved = {
        0: None,
    }
    run = lambda *offsets: forward_blocks(offsets, z, hidden_in, up_weight, down_head)
    saved[4] = run(4)
    part = saved[4][0]
    fore, back = shift(part[:cut], 1), shift(part[cut:], -1)
    saved[3] = run(3, -3)
    ahead, behind = saved[3][0][:own_rows], saved[3][0][own_rows:]
    fore = jnp.concatenate([add(fore, ahead[:cut]), ahead[cut:]], axis=0)
    back = jnp.concatenate([behind[:cut], add(back, behind[cut:])], axis=0)
    for step in (2, 1):
        fore, back = shift(fore, 1), shift(back, -1)
        saved[step] = run(step, -step)
        fore = add(fore, saved[step][0][:own_rows])
        back = add(back, saved[step][0][own_rows:])
    fore, back = shift(fore, 1), shift(back, -1)
    saved[0] = run(0)
    summed = (fore.astype(f32) + back.astype(f32) + saved[0][0].astype(f32)).astype(bf16)
    own_hidden = lax.dynamic_slice_in_dim(hidden_in, z * own_rows, own_rows, 0)
    own_proj = dot(own_hidden, head_weight)
    audio_proj = own_proj + (summed.astype(f32) + swap(summed, "yhi").astype(f32))
    audio_wide, audio_inverse = unit_rows(audio_proj)
    audio_unit = audio_wide.astype(bf16)
    partners = lax.dynamic_slice_in_dim(pair_index[0], z * own_rows, own_rows, 0)
    coeffs = pair_coeffs(audio_unit, score_half, partners, y_hi * group_half)
    grad_audio = dot(coeffs, score_half)
    grad_audio = grad_audio + swap(grad_audio.astype(bf16), "yhi").astype(f32)
    grad_embed = unit_backward(audio_wide, audio_inverse, grad_audio).astype(bf16)
    grad_score = lax.psum_scatter(
        dot(coeffs, audio_unit, ((0,), (0,))).astype(bf16), "z", scatter_dimension=0, tiled=True
    ).astype(f32)
    score_grad = unit_backward(score_wide, score_inverse, grad_score)
    sums = backward_blocks([grad_embed], saved[0], down_head, None)
    fore = back = grad_embed
    for step in (1, 2, 3):
        fore, back = shift(fore, 1), shift(back, -1)
        sums = backward_blocks([back, fore], saved[step], down_head, sums)
    fore, back = shift(fore[:cut], 1), shift(back[cut:], -1)
    keep, give = backward_blocks(
        [fore, back], saved[4], down_head, sums, (core.astype(jnp.int32)[None], head_weight)
    )
    chip = add(keep, swap(give, "core"))
    landed = lax.all_to_all(chip, ("ylo", "x"), 0, 0)
    total = jnp.sum(landed.astype(f32), axis=0)
    ff = up_weight.shape[1]
    return (total[:, :ff], total[:, ff:].T, score_grad)


def solution(mesh):
    fine = Mesh(mesh.devices.reshape(2, 4, 2, 2, RING), ("ylo", "x", "core", "yhi", "z"))
    in_specs = (
        P(AUDIO, None),
        P(None, SCORE),
        P(SCORE, None),
        P(),
        P(AUDIO + SCORE, None),
        P(AUDIO, None),
    )
    out_specs = (P(AUDIO, SCORE), P(SCORE, AUDIO), P(AUDIO + SCORE, None))
    return jax.shard_map(
        per_device, mesh=fine, in_specs=in_specs, out_specs=out_specs, check_vma=False
    )
```

time: 223 us -> 196 us (0.88)
  waiting for transfers between devices: 145 us -> 69.1 us
  starting transfers between devices: 11.9 us -> 50.9 us
  Pallas kernels: 0 us -> 22.4 us
  matrix products: 28.7 us -> 8.73 us
  local copies, waits for them, and re-layouts: 9 us -> 20.5 us
  other arithmetic: 13.9 us -> 9.3 us
    ppermute x0 -> x16, waiting for transfers between devices: none -> 46.6 us  [shift(): lax.ppermute(value, 'z', [(i, (i + step) % RING) for i in range(RING)])]
    all_gather x1 -> x0, waiting for transfers between devices: 46.4 us -> none  [per_device(): grad_all = lax.all_gather(grad_embed, 'z', axis=0, tiled=True)]
    reduce_scatter x1 -> x0, waiting for transfers between devices: 46.2 us -> none  [per_device(): summed = lax.psum_scatter(part, 'z', scatter_dimension=0, tiled=True)]
    all_gather x1, waiting for transfers between devices: 29.3 us -> 0.02 us  [per_device(): lax.all_gather(score_wide.astype(bf16), 'z', axis=0, tiled=True)]
    ppermute x0 -> x16, starting transfers between devices: none -> 28.6 us  [shift(): lax.ppermute(value, 'z', [(i, (i + step) % RING) for i in range(RING)])]
    pallas_call x0 -> x10, Pallas kernels: none -> 22.4 us  [the longest x5 11.4 us: forward_blocks(): pl.pallas_call(forward_kernel, grid_spec=pltpu.PrefetchScalarGridSpec(num...]
    dot_general x9 -> x5, matrix products: 28.7 us -> 8.73 us  [dot(): lax.dot_general(left, right, (dims, ((), ())), preferred_element_type=f32)]
    unnamed x16 -> x95, local copies, waits for them, and re-layouts: 2.8 us -> 18.1 us
  transfers between devices with their start and end apart: 8 -> 22, of which waited for: 8 -> 14; matrix products, arithmetic and copies ran while one was open for 14% -> 7% of each run, Pallas kernels for 0% -> 11%
where the time goes in v2:
time: 196 us
  waiting for transfers between devices  69.1 us (35%)
  starting transfers between devices  50.9 us (26%)
  Pallas kernels  22.4 us (11%)
  local copies, waits for them, and re-layouts  20.5 us (10%)
  between operations  14.7 us (8%)
  other arithmetic  9.3 us (5%)
  matrix products  8.73 us (4%)
    ppermute x16, waiting for transfers between devices, shift(): lax.ppermute(value, 'z', [(i, (i + step) % RING) for i in range(RING)])  46.6 us
    ppermute x16, starting transfers between devices, shift(): lax.ppermute(value, 'z', [(i, (i + step) % RING) for i in range(RING)])  28.6 us
    unnamed x95, local copies, waits for them, and re-layouts  18.1 us
    ppermute x3, starting transfers between devices, swap(): return lax.ppermute(value, axis, [(0, 1), (1, 0)])  17.1 us
    ppermute x3, waiting for transfers between devices, swap(): return lax.ppermute(value, axis, [(0, 1), (1, 0)])  12 us
    pallas_call x5, Pallas kernels, forward_blocks(): pl.pallas_call(forward_kernel, grid_spec=pltpu.PrefetchScalarGridSpec(num...  11.4 us
    pallas_call x5, Pallas kernels, backward_blocks(): pl.pallas_call(functools.partial(backward_kernel, len(grads), sums is Non...  11 us
    all_to_all x1, waiting for transfers between devices, per_device(): landed = lax.all_to_all(chip, ('ylo', 'x'), 0, 0)  10.4 us
  transfers between devices with their start and end apart: 22, of which 14 were waited for; matrix products, arithmetic and copies ran while one was open for 7% of the time, Pallas kernels for 11%

profile of v2, /device:TPU:1, one launch (start us, length us, event | category | flops | bytes accessed | tf_op | source)
XLA Modules:
  0.0 195.6 jit_solution(4298622621441169996)
XLA Ops:
  17.1 4.0 %collective-permute-start.4 = (bf16[128,768]{1,0:T(8,128)(2,1)S(1)}, bf16[128,768]{1,0:T(8,128)(2,1)S(1)}, u32[]{:S(2)}, u32[]{:S(2)}) collective-permute-start(bf16[128,768]{1,0:T(8,128)(2,1)S(1)} %get-tuple-element.74), channel_id=1, source_target_pairs={{0,7},{1,0},{2,1},{3,2},{4,3},{5,4},{6,5},{7,6},{8,15},{9,8},{10,9... | collective-permute-start | bytes 589832 | tf_op jit(solution)/shard_map/ppermute | solution.py:51
  21.2 3.0 %shard_map.131 = (bf16[512,768]{1,0:T(8,128)(2,1)S(1)}, bf16[1280,512]{1,0:T(8,128)(2,1)S(1)}, bf16[320,512]{1,0:T(8,128)(2,1)S(1)}, f32[512,320]{1,0:T(8,128)S(1)}) custom-call(s32[2]{0:T(128)S(1)} %compare_select_fusion.4.index_ref, bf16[2048,1280]{1,0:T(8,128)(2,1)S(1)} %copy-done.1, bf16[1280,320]{1,0:T(8,128)(2,1)S(1)} %copy.20.up_ref, ...), custom_call_target="tpu_custom_call" | custom-call | flops 671088640 | bytes 5701632 | tf_op jit(solution)/shard_map/pallas_call | solution.py:75
  32.6 3.0 %shard_map.132 = (bf16[512,768]{1,0:T(8,128)(2,1)S(1)}, bf16[1280,512]{1,0:T(8,128)(2,1)S(1)}, bf16[320,512]{1,0:T(8,128)(2,1)S(1)}, f32[512,320]{1,0:T(8,128)S(1)}) custom-call(s32[2]{0:T(128)S(1)} %get-tuple-element.80.index_ref, bf16[2048,1280]{1,0:T(8,128)(2,1)S(1)} %copy-done.2, bf16[1280,320]{1,0:T(8,128)(2,1)S(1)} %copy.20.up_ref, ...), custom_call_target="tpu_custom_call" | custom-call | flops 671088640 | bytes 5701632 | tf_op jit(solution)/shard_map/pallas_call | solution.py:75
  36.7 2.7 %collective-permute-done.1 = bf16[256,768]{1,0:T(8,128)(2,1)S(1)} collective-permute-done((bf16[256,768]{1,0:T(8,128)(2,1)}, bf16[256,768]{1,0:T(8,128)(2,1)S(1)}, u32[]{:S(2)}, u32[]{:S(2)}) %collective-permute-start.1) | collective-permute-done | bytes 393248 | tf_op jit(solution)/shard_map/ppermute | solution.py:51
  42.4 3.0 %shard_map.133 = (bf16[512,768]{1,0:T(8,128)(2,1)S(1)}, bf16[1280,512]{1,0:T(8,128)(2,1)S(1)}, bf16[320,512]{1,0:T(8,128)(2,1)S(1)}, f32[512,320]{1,0:T(8,128)S(1)}) custom-call(s32[2]{0:T(128)S(1)} %get-tuple-element.79.index_ref, bf16[2048,1280]{1,0:T(8,128)(2,1)S(1)} %copy-done.2, bf16[1280,320]{1,0:T(8,128)(2,1)S(1)} %copy.20.up_ref, ...), custom_call_target="tpu_custom_call" | custom-call | flops 671088640 | bytes 5701632 | tf_op jit(solution)/shard_map/pallas_call | solution.py:75
  47.5 3.1 %collective-permute-done.2 = bf16[256,768]{1,0:T(8,128)(2,1)S(1)} collective-permute-done((bf16[256,768]{1,0:T(8,128)(2,1)S(1)}, bf16[256,768]{1,0:T(8,128)(2,1)S(1)}, u32[]{:S(2)}, u32[]{:S(2)}) %collective-permute-start.2) | collective-permute-done | bytes 393248 | tf_op jit(solution)/shard_map/ppermute | solution.py:51
  50.6 4.2 %collective-permute-done.6 = bf16[256,768]{1,0:T(8,128)(2,1)S(1)} collective-permute-done((bf16[256,768]{1,0:T(8,128)(2,1)S(1)}, bf16[256,768]{1,0:T(8,128)(2,1)S(1)}, u32[]{:S(2)}, u32[]{:S(2)}) %collective-permute-start.6) | collective-permute-done | bytes 393248 | tf_op jit(solution)/shard_map/ppermute | solution.py:51
  55.1 3.8 %collective-permute-start.7 = (bf16[256,768]{1,0:T(8,128)(2,1)S(1)}, bf16[256,768]{1,0:T(8,128)(2,1)}, u32[]{:S(2)}, u32[]{:S(2)}) collective-permute-start(bf16[256,768]{1,0:T(8,128)(2,1)S(1)} %get-tuple-element.66), channel_id=1, source_target_pairs={{0,7},{1,0},{2,1},{3,2},{4,3},{5,4},{6,5},{7,6},{8,15},{9,8},{10,9... | collective-permute-start | bytes 1179656 | tf_op jit(solution)/shard_map/ppermute | solution.py:51
  62.6 11.1 %collective-permute-done.3 = bf16[256,768]{1,0:T(8,128)(2,1)S(1)} collective-permute-done((bf16[256,768]{1,0:T(8,128)(2,1)S(1)}, bf16[256,768]{1,0:T(8,128)(2,1)S(1)}, u32[]{:S(2)}, u32[]{:S(2)}) %collective-permute-start.3) | collective-permute-done | bytes 393248 | tf_op jit(solution)/shard_map/ppermute | solution.py:51
  74.8 3.5 %collective-permute-start.8 = (bf16[256,768]{1,0:T(8,128)(2,1)S(1)}, bf16[256,768]{1,0:T(8,128)(2,1)S(1)}, u32[]{:S(2)}, u32[]{:S(2)}) collective-permute-start(bf16[256,768]{1,0:T(8,128)(2,1)S(1)} %add_convert_fusion.1), channel_id=1, source_target_pairs={{0,8},{8,0},{1,9},{9,1},{2,10},{10,2},{3,11},{11,3},{4,12},{12,4},... | collective-permute-start | bytes 1179656 | tf_op jit(solution)/shard_map/ppermute | solution.py:47
  79.7 5.6 %collective-permute-done.8 = bf16[256,768]{1,0:T(8,128)(2,1)S(1)} collective-permute-done((bf16[256,768]{1,0:T(8,128)(2,1)S(1)}, bf16[256,768]{1,0:T(8,128)(2,1)S(1)}, u32[]{:S(2)}, u32[]{:S(2)}) %collective-permute-start.8) | collective-permute-done | bytes 393248 | tf_op jit(solution)/shard_map/ppermute | solution.py:47
  89.3 2.9 %collective-permute-start.9 = (bf16[256,768]{1,0:T(8,128)(2,1)}, bf16[256,768]{1,0:T(8,128)(2,1)S(1)}, u32[]{:S(2)}, u32[]{:S(2)}) collective-permute-start(bf16[256,768]{1,0:T(8,128)(2,1)} %get-tuple-element.77), channel_id=1, source_target_pairs={{0,8},{8,0},{1,9},{9,1},{2,10},{10,2},{3,11},{11,3},{4,12},{12,4},... | collective-permute-start | bytes 1179656 | tf_op jit(solution)/shard_map/ppermute | solution.py:47
  94.0 4.5 %collective-permute-done.9 = bf16[256,768]{1,0:T(8,128)(2,1)S(1)} collective-permute-done((bf16[256,768]{1,0:T(8,128)(2,1)}, bf16[256,768]{1,0:T(8,128)(2,1)S(1)}, u32[]{:S(2)}, u32[]{:S(2)}) %collective-permute-start.9) | collective-permute-done | bytes 393248 | tf_op jit(solution)/shard_map/ppermute | solution.py:47
  103.5 8.3 %collective-permute-done.10.refs_1_ = bf16[256,768]{1,0:T(8,128)(2,1)S(1)} collective-permute-done((bf16[256,768]{1,0:T(8,128)(2,1)S(1)}, bf16[256,768]{1,0:T(8,128)(2,1)S(1)}, u32[]{:S(2)}, u32[]{:S(2)}) %collective-permute-start.10) | collective-permute-done | bytes 393248 | tf_op jit(solution)/shard_map/ppermute | solution.py:51
  113.6 3.5 %collective-permute-start.15 = (bf16[256,768]{1,0:T(8,128)(2,1)S(1)}, bf16[256,768]{1,0:T(8,128)(2,1)}, u32[]{:S(2)}, u32[]{:S(2)}) collective-permute-start(bf16[256,768]{1,0:T(8,128)(2,1)S(1)} %collective-permute-done.14.refs_0_), channel_id=1, source_target_pairs={{0,7},{1,0},{2,1},{3,2},{4,3},{5,4},{6,5},{7,6},{8,15},{9,8},{10,9... | collective-permute-start | bytes 1179656 | tf_op jit(solution)/shard_map/ppermute | solution.py:51
  117.8 11.1 %collective-permute-done.11.refs_1_ = bf16[256,768]{1,0:T(8,128)(2,1)} collective-permute-done((bf16[256,768]{1,0:T(8,128)(2,1)S(1)}, bf16[256,768]{1,0:T(8,128)(2,1)}, u32[]{:S(2)}, u32[]{:S(2)}) %collective-permute-start.11) | collective-permute-done | bytes 393248 | tf_op jit(solution)/shard_map/ppermute | solution.py:51
  129.3 3.5 %collective-permute-start.16 = (bf16[256,768]{1,0:T(8,128)(2,1)}, bf16[256,768]{1,0:T(8,128)(2,1)}, u32[]{:S(2)}, u32[]{:S(2)}) collective-permute-start(bf16[256,768]{1,0:T(8,128)(2,1)} %collective-permute-done.15.refs_0_), channel_id=1, source_target_pairs={{0,7},{1,0},{2,1},{3,2},{4,3},{5,4},{6,5},{7,6},{8,15},{9,8},{10,9... | collective-permute-start | bytes 1179656 | tf_op jit(solution)/shard_map/ppermute | solution.py:51
  136.8 3.5 %collective-permute-done.12.refs_1_ = bf16[256,768]{1,0:T(8,128)(2,1)S(1)} collective-permute-done((bf16[256,768]{1,0:T(8,128)(2,1)}, bf16[256,768]{1,0:T(8,128)(2,1)S(1)}, u32[]{:S(2)}, u32[]{:S(2)}) %collective-permute-start.12) | collective-permute-done | bytes 393248 | tf_op jit(solution)/shard_map/ppermute | solution.py:51
  141.3 3.0 %collective-permute-start.17 = (bf16[128,768]{1,0:T(8,128)(2,1)S(1)}, bf16[128,768]{1,0:T(8,128)(2,1)S(1)}, u32[]{:S(2)}, u32[]{:S(2)}) collective-permute-start(bf16[128,768]{1,0:T(8,128)(2,1)S(1)} %slice.63), channel_id=1, source_target_pairs={{0,7},{1,0},{2,1},{3,2},{4,3},{5,4},{6,5},{7,6},{8,15},{9,8},{10,9... | collective-permute-start | bytes 589832 | tf_op jit(solution)/shard_map/ppermute | solution.py:51
  147.0 3.0 %shard_map.137 = (f32[1280,320]{1,0:T(8,128)S(1)}, f32[320,768]{1,0:T(8,128)S(1)}) custom-call(bf16[256,768]{1,0:T(8,128)(2,1)} %collective-permute-done.15.refs_0_, bf16[256,768]{1,0:T(8,128)(2,1)} %collective-permute-done.11.refs_1_, ...), custom_call_target="tpu_custom_call", output_to_operand_aliasing={{0}: (6, {}), {1}: (7, {})} | custom-call | flops 922746880 | bytes 8388608 | tf_op jit(solution)/shard_map/pallas_call | solution.py:182
  150.1 2.9 %shard_map.138 = (f32[1280,320]{1,0:T(8,128)S(1)}, f32[320,768]{1,0:T(8,128)S(1)}) custom-call(bf16[256,768]{1,0:T(8,128)(2,1)} %collective-permute-done.16.refs_0_, bf16[256,768]{1,0:T(8,128)(2,1)S(1)} %collective-permute-done.12.refs_1_, ...), custom_call_target="tpu_custom_call", output_to_operand_aliasing={{0}: (6, {}), {1}: (7, {})} | custom-call | flops 922746880 | bytes 8388608 | tf_op jit(solution)/shard_map/pallas_call | solution.py:182
  155.6 10.7 %collective-permute-start.18 = (bf16[8,80,640]{2,1,0:T(8,128)(2,1)S(1)}, bf16[8,80,640]{2,1,0:T(8,128)(2,1)S(1)}, u32[]{:S(2)}, u32[]{:S(2)}) collective-permute-start(bf16[8,80,640]{2,1,0:T(8,128)(2,1)S(1)} %get-tuple-element.62), channel_id=1, source_target_pairs={{0,16},{16,0},{1,17},{17,1},{2,18},{18,2},{3,19},{19,3},{4,20},{20... | collective-permute-start | bytes 2457608 | tf_op jit(solution)/shard_map/ppermute | solution.py:47
  169.4 5.1 %all-to-all-start = ((bf16[8,80,640]{2,1,0:T(8,128)(2,1)}), bf16[8,80,640]{2,1,0:T(8,128)(2,1)S(1)}, u32[]{:S(2)}, u32[]{:S(2)}) async-start(bf16[8,80,640]{2,1,0:T(8,128)(2,1)} %add_convert_fusion), calls=%async_computation | async-start | bytes 1638400 | tf_op jit(solution)/shard_map/all_to_all | solution.py:251
  177.6 10.4 %all-to-all-done = bf16[8,80,640]{2,1,0:T(8,128)(2,1)S(1)} async-done(((bf16[8,80,640]{2,1,0:T(8,128)(2,1)}), bf16[8,80,640]{2,1,0:T(8,128)(2,1)S(1)}, u32[]{:S(2)}, u32[]{:S(2)}) %all-to-all-start) | async-done | bytes 819232 | tf_op jit(solution)/shard_map/all_to_all | solution.py:251
  (158 shorter events, 61.6 us)
Async XLA Ops:
  7.2 78.4 %all-gather.2.cloned.1.call-start = ((), (), s32[]{:S(2)}) async-start(), calls=%async_computation.2 | async-start | bytes 1769472 | tf_op jit(solution)/shard_map/all_gather | solution.py:206
  14.6 11.1 %collective-permute-start = (bf16[128,768]{1,0:T(8,128)(2,1)S(1)}, bf16[128,768]{1,0:T(8,128)(2,1)S(1)}, u32[]{:S(2)}, u32[]{:S(2)}) collective-permute-start(bf16[128,768]{1,0:T(8,128)(2,1)S(1)} %get-tuple-element.73), channel_id=1, source_target_pairs={{0,1},{1,2},{2,3},{3,4},{4,5},{5,6},{6,7},{7,0},{8,9},{9,10},{10,1... | collective-permute-start | bytes 589832 | tf_op jit(solution)/shard_map/ppermute | solution.py:51
  17.1 8.6 %collective-permute-start.4 = (bf16[128,768]{1,0:T(8,128)(2,1)S(1)}, bf16[128,768]{1,0:T(8,128)(2,1)S(1)}, u32[]{:S(2)}, u32[]{:S(2)}) collective-permute-start(bf16[128,768]{1,0:T(8,128)(2,1)S(1)} %get-tuple-element.74), channel_id=1, source_target_pairs={{0,7},{1,0},{2,1},{3,2},{4,3},{5,4},{6,5},{7,6},{8,15},{9,8},{10,9... | collective-permute-start | bytes 589832 | tf_op jit(solution)/shard_map/ppermute | solution.py:51
  25.8 10.9 %collective-permute-start.5 = (bf16[256,768]{1,0:T(8,128)(2,1)S(1)}, bf16[256,768]{1,0:T(8,128)(2,1)S(1)}, u32[]{:S(2)}, u32[]{:S(2)}) collective-permute-start(bf16[256,768]{1,0:T(8,128)(2,1)S(1)} %pad_maximum_fusion.1), channel_id=1, source_target_pairs={{0,7},{1,0},{2,1},{3,2},{4,3},{5,4},{6,5},{7,6},{8,15},{9,8},{10,9... | collective-permute-start | bytes 1179656 | tf_op jit(solution)/shard_map/ppermute | solution.py:51
  29.1 10.3 %collective-permute-start.1 = (bf16[256,768]{1,0:T(8,128)(2,1)}, bf16[256,768]{1,0:T(8,128)(2,1)S(1)}, u32[]{:S(2)}, u32[]{:S(2)}) collective-permute-start(bf16[256,768]{1,0:T(8,128)(2,1)} %pad_maximum_fusion), channel_id=1, source_target_pairs={{0,1},{1,2},{2,3},{3,4},{4,5},{5,6},{6,7},{7,0},{8,9},{9,10},{10,1... | collective-permute-start | bytes 1179656 | tf_op jit(solution)/shard_map/ppermute | solution.py:51
  30.0 144.5 %reduce-scatter.2.cloned.1.call-start = ((), (), s32[]{:S(2)}) async-start(), calls=%async_computation.3 | async-start | bytes 1769472 | tf_op jit(solution)/shard_map/reduce_scatter | solution.py:237
  39.6 11.0 %collective-permute-start.2 = (bf16[256,768]{1,0:T(8,128)(2,1)S(1)}, bf16[256,768]{1,0:T(8,128)(2,1)S(1)}, u32[]{:S(2)}, u32[]{:S(2)}) collective-permute-start(bf16[256,768]{1,0:T(8,128)(2,1)S(1)} %get-tuple-element.67), channel_id=1, source_target_pairs={{0,1},{1,2},{2,3},{3,4},{4,5},{5,6},{6,7},{7,0},{8,9},{9,10},{10,1... | collective-permute-start | bytes 1179656 | tf_op jit(solution)/shard_map/ppermute | solution.py:51
  39.7 15.1 %collective-permute-start.6 = (bf16[256,768]{1,0:T(8,128)(2,1)S(1)}, bf16[256,768]{1,0:T(8,128)(2,1)S(1)}, u32[]{:S(2)}, u32[]{:S(2)}) collective-permute-start(bf16[256,768]{1,0:T(8,128)(2,1)S(1)} %get-tuple-element.68), channel_id=1, source_target_pairs={{0,7},{1,0},{2,1},{3,2},{4,3},{5,4},{6,5},{7,6},{8,15},{9,8},{10,9... | collective-permute-start | bytes 1179656 | tf_op jit(solution)/shard_map/ppermute | solution.py:51
  55.0 18.7 %collective-permute-start.3 = (bf16[256,768]{1,0:T(8,128)(2,1)S(1)}, bf16[256,768]{1,0:T(8,128)(2,1)S(1)}, u32[]{:S(2)}, u32[]{:S(2)}) collective-permute-start(bf16[256,768]{1,0:T(8,128)(2,1)S(1)} %get-tuple-element.65), channel_id=1, source_target_pairs={{0,1},{1,2},{2,3},{3,4},{4,5},{5,6},{6,7},{7,0},{8,9},{9,10},{10,1... | collective-permute-start | bytes 1179656 | tf_op jit(solution)/shard_map/ppermute | solution.py:51
  55.1 18.6 %collective-permute-start.7 = (bf16[256,768]{1,0:T(8,128)(2,1)S(1)}, bf16[256,768]{1,0:T(8,128)(2,1)}, u32[]{:S(2)}, u32[]{:S(2)}) collective-permute-start(bf16[256,768]{1,0:T(8,128)(2,1)S(1)} %get-tuple-element.66), channel_id=1, source_target_pairs={{0,7},{1,0},{2,1},{3,2},{4,3},{5,4},{6,5},{7,6},{8,15},{9,8},{10,9... | collective-permute-start | bytes 1179656 | tf_op jit(solution)/shard_map/ppermute | solution.py:51
  61.3 17.6 %copy-start.4 = (bf16[1280,768]{1,0:T(8,128)(2,1)S(1)}, bf16[1280,768]{1,0:T(8,128)(2,1)}, u32[]{:S(2)}) copy-start(bf16[1280,768]{1,0:T(8,128)(2,1)} %refs_9_.1) | copy-start | bytes 5898244
  74.8 10.5 %collective-permute-start.8 = (bf16[256,768]{1,0:T(8,128)(2,1)S(1)}, bf16[256,768]{1,0:T(8,128)(2,1)S(1)}, u32[]{:S(2)}, u32[]{:S(2)}) collective-permute-start(bf16[256,768]{1,0:T(8,128)(2,1)S(1)} %add_convert_fusion.1), channel_id=1, source_target_pairs={{0,8},{8,0},{1,9},{9,1},{2,10},{10,2},{3,11},{11,3},{4,12},{12,4},... | collective-permute-start | bytes 1179656 | tf_op jit(solution)/shard_map/ppermute | solution.py:47
  89.3 9.2 %collective-permute-start.9 = (bf16[256,768]{1,0:T(8,128)(2,1)}, bf16[256,768]{1,0:T(8,128)(2,1)S(1)}, u32[]{:S(2)}, u32[]{:S(2)}) collective-permute-start(bf16[256,768]{1,0:T(8,128)(2,1)} %get-tuple-element.77), channel_id=1, source_target_pairs={{0,8},{8,0},{1,9},{9,1},{2,10},{10,2},{3,11},{11,3},{4,12},{12,4},... | collective-permute-start | bytes 1179656 | tf_op jit(solution)/shard_map/ppermute | solution.py:47
  100.7 43.5 %copy-start.11 = (bf16[1280,512]{1,0:T(8,128)(2,1)S(1)}, bf16[1280,512]{1,0:T(8,128)(2,1)}, u32[]{:S(2)}) copy-start(bf16[1280,512]{1,0:T(8,128)(2,1)} %copy-done.10) | copy-start | bytes 3932164
  100.7 11.1 %collective-permute-start.10 = (bf16[256,768]{1,0:T(8,128)(2,1)S(1)}, bf16[256,768]{1,0:T(8,128)(2,1)S(1)}, u32[]{:S(2)}, u32[]{:S(2)}) collective-permute-start(bf16[256,768]{1,0:T(8,128)(2,1)S(1)} %multiply_convert_fusion.refs_0_), channel_id=1, source_target_pairs={{0,1},{1,2},{2,3},{3,4},{4,5},{5,6},{6,7},{7,0},{8,9},{9,10},{10,1... | collective-permute-start | bytes 1179656 | tf_op jit(solution)/shard_map/ppermute | solution.py:51
  100.8 12.8 %collective-permute-start.14 = (bf16[256,768]{1,0:T(8,128)(2,1)S(1)}, bf16[256,768]{1,0:T(8,128)(2,1)S(1)}, u32[]{:S(2)}, u32[]{:S(2)}) collective-permute-start(bf16[256,768]{1,0:T(8,128)(2,1)S(1)} %multiply_convert_fusion.refs_0_), channel_id=1, source_target_pairs={{0,7},{1,0},{2,1},{3,2},{4,3},{5,4},{6,5},{7,6},{8,15},{9,8},{10,9... | collective-permute-start | bytes 1179656 | tf_op jit(solution)/shard_map/ppermute | solution.py:51
  111.8 17.1 %collective-permute-start.11 = (bf16[256,768]{1,0:T(8,128)(2,1)S(1)}, bf16[256,768]{1,0:T(8,128)(2,1)}, u32[]{:S(2)}, u32[]{:S(2)}) collective-permute-start(bf16[256,768]{1,0:T(8,128)(2,1)S(1)} %collective-permute-done.10.refs_1_), channel_id=1, source_target_pairs={{0,1},{1,2},{2,3},{3,4},{4,5},{5,6},{6,7},{7,0},{8,9},{9,10},{10,1... | collective-permute-start | bytes 1179656 | tf_op jit(solution)/shard_map/ppermute | solution.py:51
  113.6 15.7 %collective-permute-start.15 = (bf16[256,768]{1,0:T(8,128)(2,1)S(1)}, bf16[256,768]{1,0:T(8,128)(2,1)}, u32[]{:S(2)}, u32[]{:S(2)}) collective-permute-start(bf16[256,768]{1,0:T(8,128)(2,1)S(1)} %collective-permute-done.14.refs_0_), channel_id=1, source_target_pairs={{0,7},{1,0},{2,1},{3,2},{4,3},{5,4},{6,5},{7,6},{8,15},{9,8},{10,9... | collective-permute-start | bytes 1179656 | tf_op jit(solution)/shard_map/ppermute | solution.py:51
  128.9 11.3 %collective-permute-start.12 = (bf16[256,768]{1,0:T(8,128)(2,1)}, bf16[256,768]{1,0:T(8,128)(2,1)S(1)}, u32[]{:S(2)}, u32[]{:S(2)}) collective-permute-start(bf16[256,768]{1,0:T(8,128)(2,1)} %collective-permute-done.11.refs_1_), channel_id=1, source_target_pairs={{0,1},{1,2},{2,3},{3,4},{4,5},{5,6},{6,7},{7,0},{8,9},{9,10},{10,1... | collective-permute-start | bytes 1179656 | tf_op jit(solution)/shard_map/ppermute | solution.py:51
  129.3 11.0 %collective-permute-start.16 = (bf16[256,768]{1,0:T(8,128)(2,1)}, bf16[256,768]{1,0:T(8,128)(2,1)}, u32[]{:S(2)}, u32[]{:S(2)}) collective-permute-start(bf16[256,768]{1,0:T(8,128)(2,1)} %collective-permute-done.15.refs_0_), channel_id=1, source_target_pairs={{0,7},{1,0},{2,1},{3,2},{4,3},{5,4},{6,5},{7,6},{8,15},{9,8},{10,9... | collective-permute-start | bytes 1179656 | tf_op jit(solution)/shard_map/ppermute | solution.py:51
  140.2 12.7 %collective-permute-start.13 = (bf16[128,768]{1,0:T(8,128)(2,1)S(1)}, bf16[128,768]{1,0:T(8,128)(2,1)S(1)}, u32[]{:S(2)}, u32[]{:S(2)}) collective-permute-start(bf16[128,768]{1,0:T(8,128)(2,1)S(1)} %slice.62), channel_id=1, source_target_pairs={{0,1},{1,2},{2,3},{3,4},{4,5},{5,6},{6,7},{7,0},{8,9},{9,10},{10,1... | collective-permute-start | bytes 589832 | tf_op jit(solution)/shard_map/ppermute | solution.py:51
  141.3 11.7 %collective-permute-start.17 = (bf16[128,768]{1,0:T(8,128)(2,1)S(1)}, bf16[128,768]{1,0:T(8,128)(2,1)S(1)}, u32[]{:S(2)}, u32[]{:S(2)}) collective-permute-start(bf16[128,768]{1,0:T(8,128)(2,1)S(1)} %slice.63), channel_id=1, source_target_pairs={{0,7},{1,0},{2,1},{3,2},{4,3},{5,4},{6,5},{7,6},{8,15},{9,8},{10,9... | collective-permute-start | bytes 589832 | tf_op jit(solution)/shard_map/ppermute | solution.py:51
  155.6 12.7 %collective-permute-start.18 = (bf16[8,80,640]{2,1,0:T(8,128)(2,1)S(1)}, bf16[8,80,640]{2,1,0:T(8,128)(2,1)S(1)}, u32[]{:S(2)}, u32[]{:S(2)}) collective-permute-start(bf16[8,80,640]{2,1,0:T(8,128)(2,1)S(1)} %get-tuple-element.62), channel_id=1, source_target_pairs={{0,16},{16,0},{1,17},{17,1},{2,18},{18,2},{3,19},{19,3},{4,20},{20... | collective-permute-start | bytes 2457608 | tf_op jit(solution)/shard_map/ppermute | solution.py:47
  169.4 18.5 %all-to-all-start = ((bf16[8,80,640]{2,1,0:T(8,128)(2,1)}), bf16[8,80,640]{2,1,0:T(8,128)(2,1)S(1)}, u32[]{:S(2)}, u32[]{:S(2)}) async-start(bf16[8,80,640]{2,1,0:T(8,128)(2,1)} %add_convert_fusion), calls=%async_computation | async-start | bytes 1638400 | tf_op jit(solution)/shard_map/all_to_all | solution.py:251
  (45 other events, 198.8 us)
Sparse Core Ops, SparseCore 0:
  30.2 43.2 all-gather.1
  94.1 40.1 reduce-scatter.1

commit v3 on v2

--- a/solution.py
+++ b/solution.py
@@ -16,7 +16,7 @@
 AUDIO = ("ylo", "x", "core")
 SCORE = ("yhi", "z")
 RING = 8
-VMEM_BYTES = 40 * 1024 * 1024
+VMEM_BYTES = 20 * 1024 * 1024
 f32 = jnp.float32
 bf16 = jnp.bfloat16
 
@@ -56,7 +56,7 @@
     square_mean = jnp.mean(wide * wide, axis=-1, keepdims=True)
     normed = wide * lax.rsqrt(square_mean + epsilon)
     normed_t_ref[...] = normed.T.astype(bf16)
-    pre = dot(normed.astype(bf16), up_ref[...])
+    pre = dot(normed.astype(bf16), up_ref[...], ((1,), (1,)))
     tangent = jnp.tanh(gelu_root * (pre + gelu_cubic * (pre * pre * pre)))
     act = 0.5 * pre * (1.0 + tangent)
     slope_ref[...] = 0.5 * (1.0 + tangent) + 0.5 * pre * (1.0 - tangent * tangent) * gelu_root * (
@@ -66,10 +66,10 @@
     part_ref[...] = dot(act.astype(bf16), down_head_ref[...]).astype(bf16)
 
 
-def forward_blocks(offsets, position, hidden_in, up_weight, down_head):
+def forward_blocks(offsets, position, hidden_in, up_t, down_head):
     count = len(offsets)
     rows = hidden_in.shape[0] // RING
-    width, ff = up_weight.shape
+    ff, width = up_t.shape
     embed = down_head.shape[1]
     index = lax.rem(position + jnp.array([o % RING for o in offsets], jnp.int32), RING)
     return pl.pallas_call(
@@ -79,7 +79,7 @@
             grid=(count,),
             in_specs=[
                 pl.BlockSpec((rows, width), lambda i, index: (index[i], 0)),
-                pl.BlockSpec((width, ff), lambda i, index: (0, 0)),
+                pl.BlockSpec((ff, width), lambda i, index: (0, 0)),
                 pl.BlockSpec((ff, embed), lambda i, index: (0, 0)),
             ],
             out_specs=[
@@ -101,7 +101,7 @@
             bytes_accessed=2 * count * rows * (2 * width + embed + 3 * ff) + 2 * ff * (width + embed),
             transcendentals=count * rows * ff,
         ),
-    )(index, hidden_in, up_weight, down_head)
+    )(index, hidden_in, up_t, down_head)
 
 
 def backward_kernel(pieces, first, last, *refs):
@@ -205,10 +205,9 @@
     score_wide, score_inverse = unit_rows(score_embed)
     score_half = lax.all_gather(score_wide.astype(bf16), "z", axis=0, tiled=True)
     down_head = dot(down_weight, head_weight).astype(bf16)
-    saved = {
-        0: None,
-    }
-    run = lambda *offsets: forward_blocks(offsets, z, hidden_in, up_weight, down_head)
+    saved = {}
+    up_t = up_weight.T
+    run = lambda *offsets: forward_blocks(offsets, z, hidden_in, up_t, down_head)
     saved[4] = run(4)
     part = saved[4][0]
     fore, back = shift(part[:cut], 1), shift(part[cut:], -1)
@@ -234,19 +233,25 @@
     grad_audio = dot(coeffs, score_half)
     grad_audio = grad_audio + swap(grad_audio.astype(bf16), "yhi").astype(f32)
     grad_embed = unit_backward(audio_wide, audio_inverse, grad_audio).astype(bf16)
-    grad_score = lax.psum_scatter(
-        dot(coeffs, audio_unit, ((0,), (0,))).astype(bf16), "z", scatter_dimension=0, tiled=True
-    ).astype(f32)
-    score_grad = unit_backward(score_wide, score_inverse, grad_score)
-    sums = backward_blocks([grad_embed], saved[0], down_head, None)
+    score_part = dot(coeffs, audio_unit, ((0,), (0,))).astype(bf16)
     fore = back = grad_embed
-    for step in (1, 2, 3):
-        fore, back = shift(fore, 1), shift(back, -1)
-        sums = backward_blocks([back, fore], saved[step], down_head, sums)
-    fore, back = shift(fore[:cut], 1), shift(back[cut:], -1)
+    arrived, saved_at = [grad_embed], 0
+    sums = None
+    for step in (1, 2, 3, 4):
+        if step < 4:
+            fore, back = shift(fore, 1), shift(back, -1)
+        else:
+            fore, back = shift(fore[:cut], 1), shift(back[cut:], -1)
+        sums = backward_blocks(arrived, saved[saved_at], down_head, sums)
+        fore, back, sums = lax.optimization_barrier((fore, back, sums))
+        if step == 2:
+            fore, back, score_part = lax.optimization_barrier((fore, back, score_part))
+            grad_score = lax.psum_scatter(score_part, "z", scatter_dimension=0, tiled=True)
+        arrived, saved_at = [back, fore], step
     keep, give = backward_blocks(
         [fore, back], saved[4], down_head, sums, (core.astype(jnp.int32)[None], head_weight)
     )
+    score_grad = unit_backward(score_wide, score_inverse, grad_score.astype(f32))
     chip = add(keep, swap(give, "core"))
     landed = lax.all_to_all(chip, ("ylo", "x"), 0, 0)
     total = jnp.sum(landed.astype(f32), axis=0)

time: 196 us -> 188 us (0.959)
  waiting for transfers between devices: 69.1 us -> 42.1 us
  blocking collectives: 0 us -> 18.6 us
  local copies, waits for them, and re-layouts: 20.5 us -> 33.9 us
  starting transfers between devices: 50.9 us -> 37.9 us
    all_to_all x0 -> x1, blocking collectives: none -> 18.6 us  [per_device(): landed = lax.all_to_all(chip, ('ylo', 'x'), 0, 0)]
    ppermute x16, waiting for transfers between devices: 46.6 us -> 28.2 us  [shift(): lax.ppermute(value, 'z', [(i, (i + step) % RING) for i in range(RING)])]
    unnamed x95 -> x106, local copies, waits for them, and re-layouts: 18.1 us -> 31 us
    all_to_all x1 -> x0, waiting for transfers between devices: 10.4 us -> none  [per_device(): landed = lax.all_to_all(chip, ('ylo', 'x'), 0, 0)]
    all_to_all x1 -> x0, starting transfers between devices: 5.14 us -> none  [per_device(): landed = lax.all_to_all(chip, ('ylo', 'x'), 0, 0)]
    ppermute x16, starting transfers between devices: 28.6 us -> 23.9 us  [shift(): lax.ppermute(value, 'z', [(i, (i + step) % RING) for i in range(RING)])]
    ppermute x3, starting transfers between devices: 17.1 us -> 14 us  [swap(): return lax.ppermute(value, axis, [(0, 1), (1, 0)])]
  transfers between devices with their start and end apart: 22 -> 21, of which waited for: 14 -> 10; matrix products, arithmetic and copies ran while one was open for 7% -> 5% of each run, Pallas kernels for 11% -> 12%
where the time goes in v3:
time: 188 us; the launch traced here: 186 us
  waiting for transfers between devices  42.1 us (22%)
  starting transfers between devices  37.9 us (20%)
  local copies, waits for them, and re-layouts  33.9 us (18%)
  Pallas kernels  22.5 us (12%)
  blocking collectives  18.6 us (10%)
  between operations  14.6 us (8%)
  other arithmetic  8.37 us (4%)
  matrix products  8.13 us (4%)
    unnamed x106, local copies, waits for them, and re-layouts  31 us
    ppermute x16, waiting for transfers between devices, shift(): lax.ppermute(value, 'z', [(i, (i + step) % RING) for i in range(RING)])  28.2 us
    ppermute x16, starting transfers between devices, shift(): lax.ppermute(value, 'z', [(i, (i + step) % RING) for i in range(RING)])  23.9 us
    all_to_all x1, blocking collectives, per_device(): landed = lax.all_to_all(chip, ('ylo', 'x'), 0, 0)  18.6 us
    ppermute x3, starting transfers between devices, swap(): return lax.ppermute(value, axis, [(0, 1), (1, 0)])  14 us
    ppermute x3, waiting for transfers between devices, swap(): return lax.ppermute(value, axis, [(0, 1), (1, 0)])  13.8 us
    pallas_call x5, Pallas kernels, backward_blocks(): pl.pallas_call(functools.partial(backward_kernel, len(grads), sums is Non...  11.7 us
    pallas_call x5, Pallas kernels, forward_blocks(): pl.pallas_call(forward_kernel, grid_spec=pltpu.PrefetchScalarGridSpec(num...  10.8 us
  transfers between devices with their start and end apart: 21, of which 10 were waited for; matrix products, arithmetic and copies ran while one was open for 5% of the time, Pallas kernels for 12%

profile of v3, /device:TPU:1, one launch (start us, length us, event | category | flops | bytes accessed | tf_op | source)
XLA Modules:
  0.0 186.2 jit_solution(4055795704091970584)
XLA Ops:
  14.2 2.5 %collective-permute-start = (bf16[128,768]{1,0:T(8,128)(2,1)S(1)}, bf16[128,768]{1,0:T(8,128)(2,1)S(1)}, u32[]{:S(2)}, u32[]{:S(2)}) collective-permute-start(bf16[128,768]{1,0:T(8,128)(2,1)S(1)} %get-tuple-element.111), channel_id=1, source_target_pairs={{0,1},{1,2},{2,3},{3,4},{4,5},{5,6},{6,7},{7,0},{8,9},{9,10},{10,1... | collective-permute-start | bytes 589832 | tf_op jit(solution)/shard_map/ppermute | solution.py:51
  16.7 4.0 %collective-permute-start.4 = (bf16[128,768]{1,0:T(8,128)(2,1)S(1)}, bf16[128,768]{1,0:T(8,128)(2,1)S(1)}, u32[]{:S(2)}, u32[]{:S(2)}) collective-permute-start(bf16[128,768]{1,0:T(8,128)(2,1)S(1)} %get-tuple-element.112), channel_id=1, source_target_pairs={{0,7},{1,0},{2,1},{3,2},{4,3},{5,4},{6,5},{7,6},{8,15},{9,8},{10,9... | collective-permute-start | bytes 589832 | tf_op jit(solution)/shard_map/ppermute | solution.py:51
  20.9 2.9 %shard_map.131 = (bf16[512,768]{1,0:T(8,128)(2,1)S(1)}, bf16[1280,512]{1,0:T(8,128)(2,1)S(1)}, bf16[320,512]{1,0:T(8,128)(2,1)S(1)}, f32[512,320]{1,0:T(8,128)S(1)}) custom-call(s32[2]{0:T(128)S(1)} %compare_select_fusion.4.index_ref, bf16[2048,1280]{1,0:T(8,128)(2,1)S(1)} %copy-done.1, bf16[320,1280]{1,0:T(8,128)(2,1)S(1)} %bitcast.14, ...), custom_call_target="tpu_custom_call" | custom-call | flops 671088640 | bytes 5701632 | tf_op jit(solution)/shard_map/pallas_call | solution.py:75
  32.2 2.9 %shard_map.132 = (bf16[512,768]{1,0:T(8,128)(2,1)S(1)}, bf16[1280,512]{1,0:T(8,128)(2,1)S(1)}, bf16[320,512]{1,0:T(8,128)(2,1)S(1)}, f32[512,320]{1,0:T(8,128)S(1)}) custom-call(s32[2]{0:T(128)S(1)} %get-tuple-element.118.index_ref, bf16[2048,1280]{1,0:T(8,128)(2,1)S(1)} %copy-done.2, bf16[320,1280]{1,0:T(8,128)(2,1)S(1)} %bitcast.15, ...), custom_call_target="tpu_custom_call" | custom-call | flops 671088640 | bytes 5701632 | tf_op jit(solution)/shard_map/pallas_call | solution.py:75
  36.1 2.9 %collective-permute-done.1 = bf16[256,768]{1,0:T(8,128)(2,1)S(1)} collective-permute-done((bf16[256,768]{1,0:T(8,128)(2,1)}, bf16[256,768]{1,0:T(8,128)(2,1)S(1)}, u32[]{:S(2)}, u32[]{:S(2)}) %collective-permute-start.1) | collective-permute-done | bytes 393248 | tf_op jit(solution)/shard_map/ppermute | solution.py:51
  39.3 2.7 %collective-permute-start.6 = (bf16[256,768]{1,0:T(8,128)(2,1)S(1)}, bf16[256,768]{1,0:T(8,128)(2,1)S(1)}, u32[]{:S(2)}, u32[]{:S(2)}) collective-permute-start(bf16[256,768]{1,0:T(8,128)(2,1)S(1)} %get-tuple-element.106), channel_id=1, source_target_pairs={{0,7},{1,0},{2,1},{3,2},{4,3},{5,4},{6,5},{7,6},{8,15},{9,8},{10,9... | collective-permute-start | bytes 1179656 | tf_op jit(solution)/shard_map/ppermute | solution.py:51
  42.0 2.9 %shard_map.133 = (bf16[512,768]{1,0:T(8,128)(2,1)S(1)}, bf16[1280,512]{1,0:T(8,128)(2,1)S(1)}, bf16[320,512]{1,0:T(8,128)(2,1)S(1)}, f32[512,320]{1,0:T(8,128)S(1)}) custom-call(s32[2]{0:T(128)S(1)} %get-tuple-element.117.index_ref, bf16[2048,1280]{1,0:T(8,128)(2,1)S(1)} %copy-done.2, bf16[320,1280]{1,0:T(8,128)(2,1)S(1)} %bitcast.16, ...), custom_call_target="tpu_custom_call" | custom-call | flops 671088640 | bytes 5701632 | tf_op jit(solution)/shard_map/pallas_call | solution.py:75
  46.8 3.4 %collective-permute-done.2 = bf16[256,768]{1,0:T(8,128)(2,1)S(1)} collective-permute-done((bf16[256,768]{1,0:T(8,128)(2,1)S(1)}, bf16[256,768]{1,0:T(8,128)(2,1)S(1)}, u32[]{:S(2)}, u32[]{:S(2)}) %collective-permute-start.2) | collective-permute-done | bytes 393248 | tf_op jit(solution)/shard_map/ppermute | solution.py:51
  50.2 4.2 %collective-permute-done.6 = bf16[256,768]{1,0:T(8,128)(2,1)S(1)} collective-permute-done((bf16[256,768]{1,0:T(8,128)(2,1)S(1)}, bf16[256,768]{1,0:T(8,128)(2,1)S(1)}, u32[]{:S(2)}, u32[]{:S(2)}) %collective-permute-start.6) | collective-permute-done | bytes 393248 | tf_op jit(solution)/shard_map/ppermute | solution.py:51
  55.5 3.5 %collective-permute-start.7 = (bf16[256,768]{1,0:T(8,128)(2,1)}, bf16[256,768]{1,0:T(8,128)(2,1)}, u32[]{:S(2)}, u32[]{:S(2)}) collective-permute-start(bf16[256,768]{1,0:T(8,128)(2,1)} %get-tuple-element.104), channel_id=1, source_target_pairs={{0,7},{1,0},{2,1},{3,2},{4,3},{5,4},{6,5},{7,6},{8,15},{9,8},{10,9... | collective-permute-start | bytes 1179656 | tf_op jit(solution)/shard_map/ppermute | solution.py:51
  59.0 2.5 %copy-done.3 = bf16[2048,1280]{1,0:T(8,128)(2,1)S(1)} copy-done((bf16[2048,1280]{1,0:T(8,128)(2,1)S(1)}, bf16[2048,1280]{1,0:T(8,128)(2,1)}, u32[]{:S(2)}) %copy-start.3) | copy-done | bytes 5242904
  62.7 11.6 %collective-permute-done.3 = bf16[256,768]{1,0:T(8,128)(2,1)} collective-permute-done((bf16[256,768]{1,0:T(8,128)(2,1)}, bf16[256,768]{1,0:T(8,128)(2,1)}, u32[]{:S(2)}, u32[]{:S(2)}) %collective-permute-start.3) | collective-permute-done | bytes 393248 | tf_op jit(solution)/shard_map/ppermute | solution.py:51
  75.5 2.9 %collective-permute-start.8 = (bf16[256,768]{1,0:T(8,128)(2,1)S(1)}, bf16[256,768]{1,0:T(8,128)(2,1)S(1)}, u32[]{:S(2)}, u32[]{:S(2)}) collective-permute-start(bf16[256,768]{1,0:T(8,128)(2,1)S(1)} %add_convert_fusion.1), channel_id=1, source_target_pairs={{0,8},{8,0},{1,9},{9,1},{2,10},{10,2},{3,11},{11,3},{4,12},{12,4},... | collective-permute-start | bytes 1179656 | tf_op jit(solution)/shard_map/ppermute | solution.py:47
  79.8 5.7 %collective-permute-done.8 = bf16[256,768]{1,0:T(8,128)(2,1)S(1)} collective-permute-done((bf16[256,768]{1,0:T(8,128)(2,1)S(1)}, bf16[256,768]{1,0:T(8,128)(2,1)S(1)}, u32[]{:S(2)}, u32[]{:S(2)}) %collective-permute-start.8) | collective-permute-done | bytes 393248 | tf_op jit(solution)/shard_map/ppermute | solution.py:47
  85.8 2.5 %fusion.7 = bf16[256,1024]{1,0:T(8,128)(2,1)S(1)} fusion(bf16[1024,768]{1,0:T(8,128)(2,1)} %all-gather.2.cloned.1.call-done, s32[1024]{0:T(1024)S(1)} %iota_add_fusion, s32[256]{0:T(256)S(1)} %bitcast.18, f32[256,768]{1,0:T(8,128)S(1)} %get-tuple-element.102, f32[256]{0:T(256)S(1)} %add_rsqrt_fusion), kind=kOutput, calls=%fused_computation.13 | convolution fusion | flops 406192128 | bytes 2889728 | tf_op jit(solution)/shard_map/dot_general | solution.py:25
  89.0 2.9 %collective-permute-start.9 = (bf16[256,768]{1,0:T(8,128)(2,1)S(1)}, bf16[256,768]{1,0:T(8,128)(2,1)S(1)}, u32[]{:S(2)}, u32[]{:S(2)}) collective-permute-start(bf16[256,768]{1,0:T(8,128)(2,1)S(1)} %get-tuple-element.115), channel_id=1, source_target_pairs={{0,8},{8,0},{1,9},{9,1},{2,10},{10,2},{3,11},{11,3},{4,12},{12,4},... | collective-permute-start | bytes 1179656 | tf_op jit(solution)/shard_map/ppermute | solution.py:47
  91.9 6.2 %collective-permute-done.9 = bf16[256,768]{1,0:T(8,128)(2,1)S(1)} collective-permute-done((bf16[256,768]{1,0:T(8,128)(2,1)S(1)}, bf16[256,768]{1,0:T(8,128)(2,1)S(1)}, u32[]{:S(2)}, u32[]{:S(2)}) %collective-permute-start.9) | collective-permute-done | bytes 393248 | tf_op jit(solution)/shard_map/ppermute | solution.py:47
  101.9 3.4 %collective-permute-done.11.refs_0_ = bf16[256,768]{1,0:T(8,128)(2,1)} collective-permute-done((bf16[256,768]{1,0:T(8,128)(2,1)S(1)}, bf16[256,768]{1,0:T(8,128)(2,1)}, u32[]{:S(2)}, u32[]{:S(2)}) %collective-permute-start.11) | collective-permute-done | bytes 393248 | tf_op jit(solution)/shard_map/ppermute | solution.py:51
  115.8 2.8 %shard_map.136 = (f32[1280,320]{1,0:T(8,128)S(1)}, f32[320,768]{1,0:T(8,128)S(1)}) custom-call(bf16[256,768]{1,0:T(8,128)(2,1)} %collective-permute-done.11.refs_0_, bf16[256,768]{1,0:T(8,128)(2,1)} %collective-permute-done.10.refs_1_, ...), custom_call_target="tpu_custom_call", output_to_operand_aliasing={{0}: (6, {}), {1}: (7, {})} | custom-call | flops 922746880 | bytes 8388608 | tf_op jit(solution)/shard_map/pallas_call | solution.py:182
  119.7 2.7 %collective-permute-start.15 = (bf16[256,768]{1,0:T(8,128)(2,1)}, bf16[256,768]{1,0:T(8,128)(2,1)S(1)}, u32[]{:S(2)}, u32[]{:S(2)}) collective-permute-start(bf16[256,768]{1,0:T(8,128)(2,1)} %collective-permute-done.13.refs_0_), channel_id=1, source_target_pairs={{0,7},{1,0},{2,1},{3,2},{4,3},{5,4},{6,5},{7,6},{8,15},{9,8},{10,9... | collective-permute-start | bytes 1179656 | tf_op jit(solution)/shard_map/ppermute | solution.py:51
  127.0 2.8 %shard_map.137 = (f32[1280,320]{1,0:T(8,128)S(1)}, f32[320,768]{1,0:T(8,128)S(1)}) custom-call(bf16[256,768]{1,0:T(8,128)(2,1)} %collective-permute-done.13.refs_0_, bf16[256,768]{1,0:T(8,128)(2,1)} %collective-permute-done.12.refs_1_, ...), custom_call_target="tpu_custom_call", output_to_operand_aliasing={{0}: (6, {}), {1}: (7, {})} | custom-call | flops 922746880 | bytes 8388608 | tf_op jit(solution)/shard_map/pallas_call | solution.py:182
  143.0 3.5 %shard_map.139 = (bf16[8,80,640]{2,1,0:T(8,128)(2,1)S(1)}, bf16[8,80,640]{2,1,0:T(8,128)(2,1)S(1)}) custom-call(bf16[128,768]{1,0:T(8,128)(2,1)} %collective-permute-done.16.refs_0_, bf16[128,768]{1,0:T(8,128)(2,1)S(1)} %collective-permute-done.17.refs_1_, bf16[320,768]{1,0:T(8,128)(2,1)S(1)} %convolution_convert_fusion.1.down_head_ref.refs_1_.refs_2_, ...), custom_call_target="tpu_custom_call" | custom-call | flops 1090519040 | bytes 8388608 | tf_op jit(solution)/shard_map/pallas_call | solution.py:182
  146.5 8.2 %collective-permute-start.18 = (bf16[8,80,640]{2,1,0:T(8,128)(2,1)S(1)}, bf16[8,80,640]{2,1,0:T(8,128)(2,1)S(1)}, u32[]{:S(2)}, u32[]{:S(2)}) collective-permute-start(bf16[8,80,640]{2,1,0:T(8,128)(2,1)S(1)} %get-tuple-element.99), channel_id=1, source_target_pairs={{0,16},{16,0},{1,17},{17,1},{2,18},{18,2},{3,19},{19,3},{4,20},{20... | collective-permute-start | bytes 2457608 | tf_op jit(solution)/shard_map/ppermute | solution.py:47
  156.8 18.6 %all_to_all.5 = bf16[8,80,640]{2,1,0:T(8,128)(2,1)S(1)} all-to-all(bf16[8,80,640]{2,1,0:T(8,128)(2,1)S(1)} %add_convert_fusion), channel_id=1, replica_groups=mesh['ylo'=2,'x'=4,'core'=2,'yhi'=2,'z'=8] {'ylo','x'}, dimensions={0} | all-to-all | bytes 1638400 | tf_op jit(solution)/shard_map/all_to_all | solution.py:256
  (168 shorter events, 63.5 us)
Async XLA Ops:
  7.2 78.6 %all-gather.2.cloned.1.call-start = ((), (), s32[]{:S(2)}) async-start(), calls=%async_computation.2 | async-start | bytes 1769472 | tf_op jit(solution)/shard_map/all_gather | solution.py:206
  14.2 11.1 %collective-permute-start = (bf16[128,768]{1,0:T(8,128)(2,1)S(1)}, bf16[128,768]{1,0:T(8,128)(2,1)S(1)}, u32[]{:S(2)}, u32[]{:S(2)}) collective-permute-start(bf16[128,768]{1,0:T(8,128)(2,1)S(1)} %get-tuple-element.111), channel_id=1, source_target_pairs={{0,1},{1,2},{2,3},{3,4},{4,5},{5,6},{6,7},{7,0},{8,9},{9,10},{10,1... | collective-permute-start | bytes 589832 | tf_op jit(solution)/shard_map/ppermute | solution.py:51
  16.7 8.6 %collective-permute-start.4 = (bf16[128,768]{1,0:T(8,128)(2,1)S(1)}, bf16[128,768]{1,0:T(8,128)(2,1)S(1)}, u32[]{:S(2)}, u32[]{:S(2)}) collective-permute-start(bf16[128,768]{1,0:T(8,128)(2,1)S(1)} %get-tuple-element.112), channel_id=1, source_target_pairs={{0,7},{1,0},{2,1},{3,2},{4,3},{5,4},{6,5},{7,6},{8,15},{9,8},{10,9... | collective-permute-start | bytes 589832 | tf_op jit(solution)/shard_map/ppermute | solution.py:51
  25.4 10.7 %collective-permute-start.5 = (bf16[256,768]{1,0:T(8,128)(2,1)S(1)}, bf16[256,768]{1,0:T(8,128)(2,1)S(1)}, u32[]{:S(2)}, u32[]{:S(2)}) collective-permute-start(bf16[256,768]{1,0:T(8,128)(2,1)S(1)} %pad_maximum_fusion.1), channel_id=1, source_target_pairs={{0,7},{1,0},{2,1},{3,2},{4,3},{5,4},{6,5},{7,6},{8,15},{9,8},{10,9... | collective-permute-start | bytes 1179656 | tf_op jit(solution)/shard_map/ppermute | solution.py:51
  28.7 10.3 %collective-permute-start.1 = (bf16[256,768]{1,0:T(8,128)(2,1)}, bf16[256,768]{1,0:T(8,128)(2,1)S(1)}, u32[]{:S(2)}, u32[]{:S(2)}) collective-permute-start(bf16[256,768]{1,0:T(8,128)(2,1)} %pad_maximum_fusion), channel_id=1, source_target_pairs={{0,1},{1,2},{2,3},{3,4},{4,5},{5,6},{6,7},{7,0},{8,9},{9,10},{10,1... | collective-permute-start | bytes 1179656 | tf_op jit(solution)/shard_map/ppermute | solution.py:51
  29.6 146.7 %reduce-scatter.2.cloned.1.call-start = ((), (), s32[]{:S(2)}) async-start(), calls=%async_computation.3 | async-start | bytes 1769472 | tf_op jit(solution)/shard_map/reduce_scatter | solution.py:249
  39.2 11.0 %collective-permute-start.2 = (bf16[256,768]{1,0:T(8,128)(2,1)S(1)}, bf16[256,768]{1,0:T(8,128)(2,1)S(1)}, u32[]{:S(2)}, u32[]{:S(2)}) collective-permute-start(bf16[256,768]{1,0:T(8,128)(2,1)S(1)} %get-tuple-element.105), channel_id=1, source_target_pairs={{0,1},{1,2},{2,3},{3,4},{4,5},{5,6},{6,7},{7,0},{8,9},{9,10},{10,1... | collective-permute-start | bytes 1179656 | tf_op jit(solution)/shard_map/ppermute | solution.py:51
  39.3 15.1 %collective-permute-start.6 = (bf16[256,768]{1,0:T(8,128)(2,1)S(1)}, bf16[256,768]{1,0:T(8,128)(2,1)S(1)}, u32[]{:S(2)}, u32[]{:S(2)}) collective-permute-start(bf16[256,768]{1,0:T(8,128)(2,1)S(1)} %get-tuple-element.106), channel_id=1, source_target_pairs={{0,7},{1,0},{2,1},{3,2},{4,3},{5,4},{6,5},{7,6},{8,15},{9,8},{10,9... | collective-permute-start | bytes 1179656 | tf_op jit(solution)/shard_map/ppermute | solution.py:51
  55.5 18.8 %collective-permute-start.3 = (bf16[256,768]{1,0:T(8,128)(2,1)}, bf16[256,768]{1,0:T(8,128)(2,1)}, u32[]{:S(2)}, u32[]{:S(2)}) collective-permute-start(bf16[256,768]{1,0:T(8,128)(2,1)} %get-tuple-element.103), channel_id=1, source_target_pairs={{0,1},{1,2},{2,3},{3,4},{4,5},{5,6},{6,7},{7,0},{8,9},{9,10},{10,1... | collective-permute-start | bytes 1179656 | tf_op jit(solution)/shard_map/ppermute | solution.py:51
  55.5 18.8 %collective-permute-start.7 = (bf16[256,768]{1,0:T(8,128)(2,1)}, bf16[256,768]{1,0:T(8,128)(2,1)}, u32[]{:S(2)}, u32[]{:S(2)}) collective-permute-start(bf16[256,768]{1,0:T(8,128)(2,1)} %get-tuple-element.104), channel_id=1, source_target_pairs={{0,7},{1,0},{2,1},{3,2},{4,3},{5,4},{6,5},{7,6},{8,15},{9,8},{10,9... | collective-permute-start | bytes 1179656 | tf_op jit(solution)/shard_map/ppermute | solution.py:51
  61.5 17.6 %copy-start.11 = (bf16[1280,768]{1,0:T(8,128)(2,1)S(1)}, bf16[1280,768]{1,0:T(8,128)(2,1)}, u32[]{:S(2)}) copy-start(bf16[1280,768]{1,0:T(8,128)(2,1)} %refs_9_.1) | copy-start | bytes 5898244
  62.6 17.2 %copy-start.29 = (bf16[1280,256]{1,0:T(8,128)(2,1)}, bf16[1280,256]{1,0:T(8,128)(2,1)S(1)}, u32[]{:S(2)}) copy-start(bf16[1280,256]{1,0:T(8,128)(2,1)S(1)} %get-tuple-element.57.refs_2_) | copy-start | bytes 1966084
  75.5 10.0 %collective-permute-start.8 = (bf16[256,768]{1,0:T(8,128)(2,1)S(1)}, bf16[256,768]{1,0:T(8,128)(2,1)S(1)}, u32[]{:S(2)}, u32[]{:S(2)}) collective-permute-start(bf16[256,768]{1,0:T(8,128)(2,1)S(1)} %add_convert_fusion.1), channel_id=1, source_target_pairs={{0,8},{8,0},{1,9},{9,1},{2,10},{10,2},{3,11},{11,3},{4,12},{12,4},... | collective-permute-start | bytes 1179656 | tf_op jit(solution)/shard_map/ppermute | solution.py:47
  89.0 9.1 %collective-permute-start.9 = (bf16[256,768]{1,0:T(8,128)(2,1)S(1)}, bf16[256,768]{1,0:T(8,128)(2,1)S(1)}, u32[]{:S(2)}, u32[]{:S(2)}) collective-permute-start(bf16[256,768]{1,0:T(8,128)(2,1)S(1)} %get-tuple-element.115), channel_id=1, source_target_pairs={{0,8},{8,0},{1,9},{9,1},{2,10},{10,2},{3,11},{11,3},{4,12},{12,4},... | collective-permute-start | bytes 1179656 | tf_op jit(solution)/shard_map/ppermute | solution.py:47
  98.5 6.8 %collective-permute-start.11 = (bf16[256,768]{1,0:T(8,128)(2,1)S(1)}, bf16[256,768]{1,0:T(8,128)(2,1)}, u32[]{:S(2)}, u32[]{:S(2)}) collective-permute-start(bf16[256,768]{1,0:T(8,128)(2,1)S(1)} %multiply_convert_fusion.refs_0_), channel_id=1, source_target_pairs={{0,7},{1,0},{2,1},{3,2},{4,3},{5,4},{6,5},{7,6},{8,15},{9,8},{10,9... | collective-permute-start | bytes 1179656 | tf_op jit(solution)/shard_map/ppermute | solution.py:51
  98.6 8.0 %collective-permute-start.10 = (bf16[256,768]{1,0:T(8,128)(2,1)S(1)}, bf16[256,768]{1,0:T(8,128)(2,1)}, u32[]{:S(2)}, u32[]{:S(2)}) collective-permute-start(bf16[256,768]{1,0:T(8,128)(2,1)S(1)} %multiply_convert_fusion.refs_0_), channel_id=1, source_target_pairs={{0,1},{1,2},{2,3},{3,4},{4,5},{5,6},{6,7},{7,0},{8,9},{9,10},{10,1... | collective-permute-start | bytes 1179656 | tf_op jit(solution)/shard_map/ppermute | solution.py:51
  106.6 13.0 %collective-permute-start.12 = (bf16[256,768]{1,0:T(8,128)(2,1)}, bf16[256,768]{1,0:T(8,128)(2,1)}, u32[]{:S(2)}, u32[]{:S(2)}) collective-permute-start(bf16[256,768]{1,0:T(8,128)(2,1)} %collective-permute-done.10.refs_1_), channel_id=1, source_target_pairs={{0,1},{1,2},{2,3},{3,4},{4,5},{5,6},{6,7},{7,0},{8,9},{9,10},{10,1... | collective-permute-start | bytes 1179656 | tf_op jit(solution)/shard_map/ppermute | solution.py:51
  107.1 12.5 %collective-permute-start.13 = (bf16[256,768]{1,0:T(8,128)(2,1)}, bf16[256,768]{1,0:T(8,128)(2,1)}, u32[]{:S(2)}, u32[]{:S(2)}) collective-permute-start(bf16[256,768]{1,0:T(8,128)(2,1)} %collective-permute-done.11.refs_0_), channel_id=1, source_target_pairs={{0,7},{1,0},{2,1},{3,2},{4,3},{5,4},{6,5},{7,6},{8,15},{9,8},{10,9... | collective-permute-start | bytes 1179656 | tf_op jit(solution)/shard_map/ppermute | solution.py:51
  119.6 11.2 %collective-permute-start.14 = (bf16[256,768]{1,0:T(8,128)(2,1)}, bf16[256,768]{1,0:T(8,128)(2,1)S(1)}, u32[]{:S(2)}, u32[]{:S(2)}) collective-permute-start(bf16[256,768]{1,0:T(8,128)(2,1)} %collective-permute-done.12.refs_1_), channel_id=1, source_target_pairs={{0,1},{1,2},{2,3},{3,4},{4,5},{5,6},{6,7},{7,0},{8,9},{9,10},{10,1... | collective-permute-start | bytes 1179656 | tf_op jit(solution)/shard_map/ppermute | solution.py:51
  119.7 11.1 %collective-permute-start.15 = (bf16[256,768]{1,0:T(8,128)(2,1)}, bf16[256,768]{1,0:T(8,128)(2,1)S(1)}, u32[]{:S(2)}, u32[]{:S(2)}) collective-permute-start(bf16[256,768]{1,0:T(8,128)(2,1)} %collective-permute-done.13.refs_0_), channel_id=1, source_target_pairs={{0,7},{1,0},{2,1},{3,2},{4,3},{5,4},{6,5},{7,6},{8,15},{9,8},{10,9... | collective-permute-start | bytes 1179656 | tf_op jit(solution)/shard_map/ppermute | solution.py:51
  133.1 9.8 %collective-permute-start.17 = (bf16[128,768]{1,0:T(8,128)(2,1)}, bf16[128,768]{1,0:T(8,128)(2,1)S(1)}, u32[]{:S(2)}, u32[]{:S(2)}) collective-permute-start(bf16[128,768]{1,0:T(8,128)(2,1)} %slice.59), channel_id=1, source_target_pairs={{0,7},{1,0},{2,1},{3,2},{4,3},{5,4},{6,5},{7,6},{8,15},{9,8},{10,9... | collective-permute-start | bytes 589832 | tf_op jit(solution)/shard_map/ppermute | solution.py:51
  133.1 9.9 %collective-permute-start.16 = (bf16[128,768]{1,0:T(8,128)(2,1)}, bf16[128,768]{1,0:T(8,128)(2,1)}, u32[]{:S(2)}, u32[]{:S(2)}) collective-permute-start(bf16[128,768]{1,0:T(8,128)(2,1)} %slice.58), channel_id=1, source_target_pairs={{0,1},{1,2},{2,3},{3,4},{4,5},{5,6},{6,7},{7,0},{8,9},{9,10},{10,1... | collective-permute-start | bytes 589832 | tf_op jit(solution)/shard_map/ppermute | solution.py:51
  146.5 10.1 %collective-permute-start.18 = (bf16[8,80,640]{2,1,0:T(8,128)(2,1)S(1)}, bf16[8,80,640]{2,1,0:T(8,128)(2,1)S(1)}, u32[]{:S(2)}, u32[]{:S(2)}) collective-permute-start(bf16[8,80,640]{2,1,0:T(8,128)(2,1)S(1)} %get-tuple-element.99), channel_id=1, source_target_pairs={{0,16},{16,0},{1,17},{17,1},{2,18},{18,2},{3,19},{19,3},{4,20},{20... | collective-permute-start | bytes 2457608 | tf_op jit(solution)/shard_map/ppermute | solution.py:47
  156.8 19.5 %copy-start.48 = (bf16[128,768]{1,0:T(8,128)(2,1)S(1)}, bf16[128,768]{1,0:T(8,128)(2,1)}, u32[]{:S(2)}) copy-start(bf16[128,768]{1,0:T(8,128)(2,1)} %param.15) | copy-start | bytes 589828
  (50 other events, 162.8 us)
Sparse Core Ops, SparseCore 0:
  29.7 42.8 all-gather.1
  119.8 43.5 reduce-scatter.1

commit v4 on v3

v4 whole, which is shorter than its diff:
```python
import functools

import jax
import jax.numpy as jnp
from jax import lax
from jax.experimental import pallas as pl
from jax.experimental.pallas import tpu as pltpu
from jax.sharding import Mesh, PartitionSpec as P

logit_scale = 8.0
logit_bias = -3.0
epsilon = 1e-06
gelu_root = 0.7978845608028654
gelu_cubic = 0.044715

AUDIO = ("ylo", "x", "core")
SCORE = ("yhi", "z")
RING = 8
VMEM_BYTES = 56 * 1024 * 1024
f32 = jnp.float32
bf16 = jnp.bfloat16


def dot(left, right, dims=((1,), (0,))):
    return lax.dot_general(left, right, (dims, ((), ())), preferred_element_type=f32)


def unit_rows(values):
    wide = values.astype(f32)
    inverse = lax.rsqrt(jnp.sum(wide * wide, axis=-1, keepdims=True) + epsilon)
    return (wide * inverse, inverse)


def unit_backward(unit_wide, inverse, grad_unit):
    inner = jnp.sum(unit_wide * grad_unit, axis=-1, keepdims=True)
    return inverse * (grad_unit - unit_wide * inner)


def pair_coeffs(left, right, partner, first_column):
    logits = logit_scale * dot(left, right, ((1,), (1,))) + logit_bias
    columns = first_column + lax.iota(jnp.int32, right.shape[0])
    sign = jnp.where(partner[:, None] == columns[None, :], 1.0, -1.0)
    return (-logit_scale * sign * jax.nn.sigmoid(-sign * logits)).astype(bf16)


def swap(value, axis):
    return lax.ppermute(value, axis, [(0, 1), (1, 0)])


def shift(value, step):
    perm = [(i, (i + step) % RING) for i in range(RING)]
    perm += [(RING + i, RING + (i - step) % RING) for i in range(RING)]
    return lax.ppermute(value, ("core", "z"), perm)


def forward_kernel(first, index_ref, hidden_ref, up_ref, *refs):
    if first:
        down_ref, head_ref, part_ref, normed_t_ref, act_t_ref, slope_ref, down_head_ref = refs
        down_head_ref[...] = dot(down_ref[...], head_ref[...]).astype(bf16)
    else:
        down_head_ref, part_ref, normed_t_ref, act_t_ref, slope_ref = refs
    wide = hidden_ref[...].astype(f32)
    square_mean = jnp.mean(wide * wide, axis=-1, keepdims=True)
    normed = (wide * lax.rsqrt(square_mean + epsilon)).astype(bf16)
    pre = dot(normed, up_ref[...], ((1,), (1,)))
    tangent = jnp.tanh(gelu_root * (pre + gelu_cubic * (pre * pre * pre)))
    act = (0.5 * pre * (1.0 + tangent)).astype(bf16)
    part_ref[...] = dot(act, down_head_ref[...]).astype(bf16)
    slope = 0.5 * (1.0 + tangent) + 0.5 * pre * (1.0 - tangent * tangent) * gelu_root * (
        1.0 + 3.0 * gelu_cubic * pre * pre
    )
    slope_ref[...] = slope.astype(bf16)
    normed_t_ref[...] = normed.T
    act_t_ref[...] = act.T


def forward_blocks(offsets, place, direction, hidden_in, up_t, *weights):
    count = len(offsets)
    first = len(weights) == 2
    rows = hidden_in.shape[0] // RING
    ff, width = up_t.shape
    embed = weights[-1].shape[1]
    index = lax.rem(place + direction * jnp.array(offsets, jnp.int32) + RING, RING)
    weight_specs = [pl.BlockSpec(w.shape, lambda i, index: (0, 0)) for w in weights]
    extra_specs = [pl.BlockSpec((ff, embed), lambda i, index: (0, 0))] if first else []
    extra_shapes = [jax.ShapeDtypeStruct((ff, embed), bf16)] if first else []
    return pl.pallas_call(
        functools.partial(forward_kernel, first),
        grid_spec=pltpu.PrefetchScalarGridSpec(
            num_scalar_prefetch=1,
            grid=(count,),
            in_specs=[
                pl.BlockSpec((rows, width), lambda i, index: (index[i], 0)),
                pl.BlockSpec((ff, width), lambda i, index: (0, 0)),
            ]
            + weight_specs,
            out_specs=[
                pl.BlockSpec((rows, embed), lambda i, index: (i, 0)),
                pl.BlockSpec((width, rows), lambda i, index: (0, i)),
                pl.BlockSpec((ff, rows), lambda i, index: (0, i)),
                pl.BlockSpec((rows, ff), lambda i, index: (i, 0)),
            ]
            + extra_specs,
        ),
        out_shape=[
            jax.ShapeDtypeStruct((count * rows, embed), bf16),
            jax.ShapeDtypeStruct((width, count * rows), bf16),
            jax.ShapeDtypeStruct((ff, count * rows), bf16),
            jax.ShapeDtypeStruct((count * rows, ff), bf16),
        ]
        + extra_shapes,
        compiler_params=pltpu.CompilerParams(vmem_limit_bytes=VMEM_BYTES),
        cost_estimate=pl.CostEstimate(
            flops=2 * count * rows * ff * (width + embed),
            bytes_accessed=2 * count * rows * (2 * width + embed + 2 * ff) + 2 * ff * (width + embed),
            transcendentals=count * rows * ff,
        ),
    )(index, hidden_in, up_t, *weights)


def backward_kernel(count, first, last, *refs):
    grads = [ref[...] for ref in refs[:count]]
    down_head_ref = refs[count]
    refs = refs[count + 1 :]
    saved = []
    taken = 0
    while taken < count:
        saved.append([ref[...] for ref in refs[:3]])
        taken += saved[-1][2].shape[0] // grads[0].shape[0]
        refs = refs[3:]
    join = lambda parts, axis: jnp.concatenate(parts, axis=axis) if len(parts) > 1 else parts[0]
    grad = join(grads, 0)
    normed_t, act_t, slope = (join([kept[i] for kept in saved], axis) for i, axis in ((0, 1), (1, 1), (2, 0)))
    if not first:
        up_in, act_in = refs[:2]
        refs = refs[2:]
    if last:
        core_ref, head_ref, keep_ref, give_ref, up_acc = refs
    else:
        up_acc, act_acc = refs
    tile = 256
    width, ff = up_acc.shape
    grad_act = dot(grad, down_head_ref[...], ((1,), (1,)))
    grad_pre = (grad_act * slope.astype(f32)).astype(bf16)
    act_sum = dot(act_t, grad)
    if not first:
        act_sum = act_sum + act_in[...]
    if not last:
        act_acc[...] = act_sum
    for m in range(0, width, tile):
        up_sum = dot(normed_t[m : m + tile, :], grad_pre)
        if not first:
            up_sum = up_sum + up_in[m : m + tile, :]
        up_acc[m : m + tile, :] = up_sum
    if last:
        core = core_ref[0]
        act_grad = act_sum.astype(bf16)
        rows = keep_ref.shape[1]
        for side in range(2):
            for half, out_ref in ((core, keep_ref), (1 - core, give_ref)):
                for chip in range(keep_ref.shape[0]):
                    at = pl.multiple_of((2 * chip + half) * rows, rows)
                    out_ref[chip, :, side * ff : (side + 1) * ff] = up_acc[pl.ds(at, rows), :].astype(bf16)
            if side == 0:
                for m in range(0, width, tile):
                    up_acc[m : m + tile, :] = dot(head_ref[m : m + tile, :], act_grad, ((1,), (1,)))


def backward_blocks(grads, saved, down_head, sums, last=None):
    whole = pl.BlockSpec(memory_space=pltpu.VMEM)
    args = list(grads) + [down_head] + [array for kept in saved for array in kept]
    aliases = {}
    if sums is not None:
        if last is None:
            aliases = {len(args): 0, len(args) + 1: 1}
        args += list(sums)
    specs = [whole] * len(args)
    ff, embed = down_head.shape
    rows, width = sum(grad.shape[0] for grad in grads), saved[0][0].shape[0]
    flops = 2 * rows * ff * (2 * embed + width)
    if last is None:
        shapes = [jax.ShapeDtypeStruct((width, ff), f32), jax.ShapeDtypeStruct((ff, embed), f32)]
        scratch = []
    else:
        args += list(last)
        specs += [pl.BlockSpec(memory_space=pltpu.SMEM), whole]
        shapes = [jax.ShapeDtypeStruct((8, width // 16, 2 * ff), bf16)] * 2
        scratch = [pltpu.VMEM((width, ff), f32)]
        flops += 2 * width * ff * embed
    return pl.pallas_call(
        functools.partial(backward_kernel, len(grads), sums is None, last is not None),
        in_specs=specs,
        out_specs=[whole] * 2,
        out_shape=shapes,
        scratch_shapes=scratch,
        input_output_aliases=aliases,
        compiler_params=pltpu.CompilerParams(vmem_limit_bytes=VMEM_BYTES),
        cost_estimate=pl.CostEstimate(flops=flops, bytes_accessed=8 * 1024 * 1024, transcendentals=0),
    )(*args)


def total_of(*terms):
    return sum(term.astype(f32) for term in terms)


def per_device(hidden_in, up_weight, down_weight, head_weight, score_embed, pair_index):
    y_hi, z, core = (lax.axis_index(name).astype(jnp.int32) for name in ("yhi", "z", "core"))
    rows = hidden_in.shape[0] // RING
    group_half = hidden_in.shape[0] // 2
    direction = 1 - 2 * core
    up_t = up_weight.T
    part, *kept, down_head = forward_blocks((4,), z, direction, hidden_in, up_t, down_weight, head_weight)
    saved = {4: kept}
    fore = shift(part, 1)
    score_wide, score_inverse = unit_rows(score_embed)
    score_unit, up_t = lax.optimization_barrier((score_wide.astype(bf16), up_t))
    score_half = lax.all_gather(score_unit, "z", axis=0, tiled=True)
    back = None
    for step in (3, 2, 1):
        part, *saved[step] = forward_blocks((step, -step), z, direction, hidden_in, up_t, down_head)
        fore = total_of(fore, part[:rows]).astype(bf16)
        back = part[rows:] if back is None else total_of(back, part[rows:]).astype(bf16)
        fore, back = shift(fore, 1), shift(back, -1)
    part, *saved[0] = forward_blocks((0,), z, direction, hidden_in, up_t, down_head)
    own_hidden = lax.dynamic_slice_in_dim(hidden_in, z * rows, rows, 0)
    own_proj = dot(own_hidden, head_weight)
    summed = total_of(part, fore, back).astype(bf16)
    audio_proj = own_proj + total_of(summed, swap(summed, "yhi"))
    audio_wide, audio_inverse = unit_rows(audio_proj)
    audio_unit = audio_wide.astype(bf16)
    partners = lax.dynamic_slice_in_dim(pair_index[0], z * rows, rows, 0)
    coeffs = pair_coeffs(audio_unit, score_half, partners, y_hi * group_half)
    grad_audio = dot(coeffs, score_half)
    grad_audio = grad_audio + swap(grad_audio.astype(bf16), "yhi").astype(f32)
    grad_embed = unit_backward(audio_wide, audio_inverse, grad_audio).astype(bf16)
    score_part = dot(coeffs, audio_unit, ((0,), (0,))).astype(bf16)
    fore, back = shift(grad_embed, 1), shift(grad_embed, -1)
    grads, kept, sums = [grad_embed, back, fore], [saved[0], saved[1]], None
    for step in (2, 3, 4):
        fore, back = shift(fore, 1), shift(back, -1) if step < 4 else None
        sums = backward_blocks(grads, kept, down_head, sums)
        if step == 2:
            fore, back, sums, score_part = lax.optimization_barrier((fore, back, sums, score_part))
            grad_score = lax.psum_scatter(score_part, "z", scatter_dimension=0, tiled=True)
        elif step == 3:
            fore, back, sums = lax.optimization_barrier((fore, back, sums))
        else:
            fore, sums = lax.optimization_barrier((fore, sums))
        grads, kept = [back, fore], [saved[step]]
    keep, give = backward_blocks([fore], [saved[4]], down_head, sums, (core[None], head_weight))
    chip = total_of(keep, swap(give, "core")).astype(bf16)
    landed = lax.all_to_all(chip, ("ylo", "x"), 0, 0)
    total = jnp.sum(landed.astype(f32), axis=0)
    ff = up_weight.shape[1]
    score_grad = unit_backward(score_wide, score_inverse, grad_score.astype(f32))
    return (total[:, :ff], total[:, ff:].T, score_grad)


def solution(mesh):
    fine = Mesh(mesh.devices.reshape(2, 4, 2, 2, RING), ("ylo", "x", "core", "yhi", "z"))
    in_specs = (
        P(AUDIO, None),
        P(None, SCORE),
        P(SCORE, None),
        P(),
        P(AUDIO + SCORE, None),
        P(AUDIO, None),
    )
    out_specs = (P(AUDIO, SCORE), P(SCORE, AUDIO), P(AUDIO + SCORE, None))
    return jax.shard_map(
        per_device, mesh=fine, in_specs=in_specs, out_specs=out_specs, check_vma=False
    )
```

time: 188 us -> 194 us (1.032)
  local copies, waits for them, and re-layouts: 33.9 us -> 3.02 us
  Pallas kernels: 22.5 us -> 48 us
  waiting for transfers between devices: 42.1 us -> 60.5 us
  starting transfers between devices: 37.9 us -> 31.1 us
  other arithmetic: 8.37 us -> 12.1 us
    unnamed x106 -> x30, local copies, waits for them, and re-layouts: 31 us -> 1.23 us
    ppermute x16 -> x14, waiting for transfers between devices: 28.2 us -> 43.1 us  [shift(): return lax.ppermute(value, ('core', 'z'), perm)]
    pallas_call x5, Pallas kernels: 10.8 us -> 24.5 us  [forward_blocks(): pl.pallas_call(functools.partial(forward_kernel, first), grid_spec=pltpu....]
    pallas_call x5 -> x4, Pallas kernels: 11.7 us -> 23.5 us  [backward_blocks(): pl.pallas_call(functools.partial(backward_kernel, len(grads), sums is Non...]
    ppermute x3, starting transfers between devices: 14 us -> 9.91 us  [swap(): return lax.ppermute(value, axis, [(0, 1), (1, 0)])]
    ppermute x3, waiting for transfers between devices: 13.8 us -> 17.4 us  [swap(): return lax.ppermute(value, axis, [(0, 1), (1, 0)])]
    convert_element_type x6, other arithmetic: 3.62 us -> 7.14 us  [the longest x3 3.81 us: per_device(): fore = total_of(fore, part[:rows]).astype(bf16)]
    ppermute x16 -> x14, starting transfers between devices: 23.9 us -> 21.1 us  [shift(): return lax.ppermute(value, ('core', 'z'), perm)]
  transfers between devices with their start and end apart: 21 -> 19, of which waited for: 10 -> 13; matrix products, arithmetic and copies ran while one was open for 5% -> 7% of each run, Pallas kernels for 12% -> 22%
where the time goes in v4:
time: 194 us; the launch traced here: 193 us
  waiting for transfers between devices  60.5 us (31%)
  Pallas kernels  48 us (25%)
  starting transfers between devices  31.1 us (16%)
  blocking collectives  17.8 us (9%)
  between operations  14.3 us (7%)
  other arithmetic  12.1 us (6%)
  matrix products  6.53 us (3%)
  local copies, waits for them, and re-layouts  3.02 us (2%)
    ppermute x14, waiting for transfers between devices, shift(): return lax.ppermute(value, ('core', 'z'), perm)  43.1 us
    pallas_call x5, Pallas kernels, forward_blocks(): pl.pallas_call(functools.partial(forward_kernel, first), grid_spec=pltpu....  24.5 us
    pallas_call x4, Pallas kernels, backward_blocks(): pl.pallas_call(functools.partial(backward_kernel, len(grads), sums is Non...  23.5 us
    ppermute x14, starting transfers between devices, shift(): return lax.ppermute(value, ('core', 'z'), perm)  21.1 us
    all_to_all x1, blocking collectives, per_device(): landed = lax.all_to_all(chip, ('ylo', 'x'), 0, 0)  17.8 us
    ppermute x3, waiting for transfers between devices, swap(): return lax.ppermute(value, axis, [(0, 1), (1, 0)])  17.4 us
    ppermute x3, starting transfers between devices, swap(): return lax.ppermute(value, axis, [(0, 1), (1, 0)])  9.91 us
    dot_general x4, matrix products, dot(): lax.dot_general(left, right, (dims, ((), ())), preferred_element_type=f32)  6.53 us
  transfers between devices with their start and end apart: 19, of which 13 were waited for; matrix products, arithmetic and copies ran while one was open for 7% of the time, Pallas kernels for 22%

profile of v4, /device:TPU:1, one launch (start us, length us, event | category | flops | bytes accessed | tf_op | source)
XLA Modules:
  0.0 193.4 jit_solution(15467415787317311373)
XLA Ops:
  7.3 4.9 %shard_map.130 = (bf16[256,768]{1,0:T(8,128)(2,1)}, bf16[1280,256]{1,0:T(8,128)(2,1)}, bf16[320,256]{1,0:T(8,128)(2,1)}, bf16[256,320]{1,0:T(8,128)(2,1)}, bf16[320,768]{1,0:T(8,128)(2,1)}) custom-call(s32[1]{0:T(128)S(6)} %rem.78.index_ref, bf16[2048,1280]{1,0:T(8,128)(2,1)} %hidden_ref.9, bf16[320,1280]{1,0:T(8,128)(2,1)} %bitcast.12, ...), custom_call_target="tpu_custom_call" | custom-call | flops 335544320 | bytes 3342336 | tf_op jit(solution)/shard_map/pallas_call | solution.py:87
  12.1 6.4 %collective-permute-start = (bf16[256,768]{1,0:T(8,128)(2,1)}, bf16[256,768]{1,0:T(8,128)(2,1)S(1)}, u32[]{:S(2)}, u32[]{:S(2)}) collective-permute-start(bf16[256,768]{1,0:T(8,128)(2,1)} %get-tuple-element.49), channel_id=1, source_target_pairs={{0,1},{1,2},{2,3},{3,4},{4,5},{5,6},{6,7},{7,0},{16,23},{17,16},{1... | collective-permute-start | bytes 1179656 | tf_op jit(solution)/shard_map/ppermute | solution.py:53
  20.0 5.4 %shard_map.132 = (bf16[512,768]{1,0:T(8,128)(2,1)}, bf16[1280,512]{1,0:T(8,128)(2,1)}, bf16[320,512]{1,0:T(8,128)(2,1)}, bf16[512,320]{1,0:T(8,128)(2,1)}) custom-call(s32[2]{0:T(128)} %compare_select_fusion.4.index_ref, bf16[2048,1280]{1,0:T(8,128)(2,1)} %hidden_ref.9, bf16[320,1280]{1,0:T(8,128)(2,1)} %bitcast.13, ...), custom_call_target="tpu_custom_call" | custom-call | flops 671088640 | bytes 5373952 | tf_op jit(solution)/shard_map/pallas_call | solution.py:87
  27.6 2.7 %collective-permute-start.1 = (bf16[256,768]{1,0:T(8,128)(2,1)S(1)}, bf16[256,768]{1,0:T(8,128)(2,1)S(1)}, u32[]{:S(2)}, u32[]{:S(2)}) collective-permute-start(bf16[256,768]{1,0:T(8,128)(2,1)S(1)} %add_convert_fusion.6), channel_id=1, source_target_pairs={{0,1},{1,2},{2,3},{3,4},{4,5},{5,6},{6,7},{7,0},{16,23},{17,16},{1... | collective-permute-start | bytes 1179656 | tf_op jit(solution)/shard_map/ppermute | solution.py:53
  30.9 5.3 %shard_map.133 = (bf16[512,768]{1,0:T(8,128)(2,1)}, bf16[1280,512]{1,0:T(8,128)(2,1)}, bf16[320,512]{1,0:T(8,128)(2,1)}, bf16[512,320]{1,0:T(8,128)(2,1)}) custom-call(s32[2]{0:T(128)} %get-tuple-element.100.index_ref, bf16[2048,1280]{1,0:T(8,128)(2,1)} %hidden_ref.9, bf16[320,1280]{1,0:T(8,128)(2,1)} %bitcast.14, ...), custom_call_target="tpu_custom_call" | custom-call | flops 671088640 | bytes 5373952 | tf_op jit(solution)/shard_map/pallas_call | solution.py:87
  37.9 3.2 %collective-permute-start.2 = (bf16[256,768]{1,0:T(8,128)(2,1)S(1)}, bf16[256,768]{1,0:T(8,128)(2,1)S(1)}, u32[]{:S(2)}, u32[]{:S(2)}) collective-permute-start(bf16[256,768]{1,0:T(8,128)(2,1)S(1)} %get-tuple-element.93), channel_id=1, source_target_pairs={{0,1},{1,2},{2,3},{3,4},{4,5},{5,6},{6,7},{7,0},{16,23},{17,16},{1... | collective-permute-start | bytes 1179656 | tf_op jit(solution)/shard_map/ppermute | solution.py:53
  41.1 5.4 %shard_map.134 = (bf16[512,768]{1,0:T(8,128)(2,1)}, bf16[1280,512]{1,0:T(8,128)(2,1)}, bf16[320,512]{1,0:T(8,128)(2,1)}, bf16[512,320]{1,0:T(8,128)(2,1)}) custom-call(s32[2]{0:T(128)} %get-tuple-element.99.index_ref, bf16[2048,1280]{1,0:T(8,128)(2,1)} %hidden_ref.9, bf16[320,1280]{1,0:T(8,128)(2,1)} %bitcast.15, ...), custom_call_target="tpu_custom_call" | custom-call | flops 671088640 | bytes 5373952 | tf_op jit(solution)/shard_map/pallas_call | solution.py:87
  46.5 5.0 %collective-permute-done.2 = bf16[256,768]{1,0:T(8,128)(2,1)S(1)} collective-permute-done((bf16[256,768]{1,0:T(8,128)(2,1)S(1)}, bf16[256,768]{1,0:T(8,128)(2,1)S(1)}, u32[]{:S(2)}, u32[]{:S(2)}) %collective-permute-start.2) | collective-permute-done | bytes 393248 | tf_op jit(solution)/shard_map/ppermute | solution.py:53
  51.5 9.7 %collective-permute-done.5 = bf16[256,768]{1,0:T(8,128)(2,1)S(1)} collective-permute-done((bf16[256,768]{1,0:T(8,128)(2,1)S(1)}, bf16[256,768]{1,0:T(8,128)(2,1)S(1)}, u32[]{:S(2)}, u32[]{:S(2)}) %collective-permute-start.5) | collective-permute-done | bytes 393248 | tf_op jit(solution)/shard_map/ppermute | solution.py:53
  64.1 3.6 %shard_map.131 = (bf16[256,768]{1,0:T(8,128)(2,1)}, bf16[1280,256]{1,0:T(8,128)(2,1)}, bf16[320,256]{1,0:T(8,128)(2,1)}, bf16[256,320]{1,0:T(8,128)(2,1)}) custom-call(s32[1]{0:T(128)S(6)} %rem.72.index_ref, bf16[2048,1280]{1,0:T(8,128)(2,1)} %hidden_ref.9, bf16[320,1280]{1,0:T(8,128)(2,1)} %bitcast.16, ...), custom_call_target="tpu_custom_call" | custom-call | flops 335544320 | bytes 3342336 | tf_op jit(solution)/shard_map/pallas_call | solution.py:87
  67.8 9.0 %collective-permute-done.3 = bf16[256,768]{1,0:T(8,128)(2,1)S(1)} collective-permute-done((bf16[256,768]{1,0:T(8,128)(2,1)S(1)}, bf16[256,768]{1,0:T(8,128)(2,1)S(1)}, u32[]{:S(2)}, u32[]{:S(2)}) %collective-permute-start.3) | collective-permute-done | bytes 393248 | tf_op jit(solution)/shard_map/ppermute | solution.py:53
  78.3 2.8 %collective-permute-start.7 = (bf16[256,768]{1,0:T(8,128)(2,1)S(1)}, bf16[256,768]{1,0:T(8,128)(2,1)S(1)}, u32[]{:S(2)}, u32[]{:S(2)}) collective-permute-start(bf16[256,768]{1,0:T(8,128)(2,1)S(1)} %add_convert_fusion.1), channel_id=1, source_target_pairs={{0,8},{8,0},{1,9},{9,1},{2,10},{10,2},{3,11},{11,3},{4,12},{12,4},... | collective-permute-start | bytes 1179656 | tf_op jit(solution)/shard_map/ppermute | solution.py:47
  82.9 7.1 %collective-permute-done.7 = bf16[256,768]{1,0:T(8,128)(2,1)S(1)} collective-permute-done((bf16[256,768]{1,0:T(8,128)(2,1)S(1)}, bf16[256,768]{1,0:T(8,128)(2,1)S(1)}, u32[]{:S(2)}, u32[]{:S(2)}) %collective-permute-start.7) | collective-permute-done | bytes 393248 | tf_op jit(solution)/shard_map/ppermute | solution.py:47
  95.9 8.1 %collective-permute-done.8 = bf16[256,768]{1,0:T(8,128)(2,1)S(1)} collective-permute-done((bf16[256,768]{1,0:T(8,128)(2,1)S(1)}, bf16[256,768]{1,0:T(8,128)(2,1)S(1)}, u32[]{:S(2)}, u32[]{:S(2)}) %collective-permute-start.8) | collective-permute-done | bytes 393248 | tf_op jit(solution)/shard_map/ppermute | solution.py:47
  106.0 5.8 %collective-permute-done.9.refs_2_ = bf16[256,768]{1,0:T(8,128)(2,1)S(1)} collective-permute-done((bf16[256,768]{1,0:T(8,128)(2,1)S(1)}, bf16[256,768]{1,0:T(8,128)(2,1)S(1)}, u32[]{:S(2)}, u32[]{:S(2)}) %collective-permute-start.9) | collective-permute-done | bytes 393248 | tf_op jit(solution)/shard_map/ppermute | solution.py:53
  117.0 5.8 %shard_map.135 = (f32[1280,320]{1,0:T(8,128)}, f32[320,768]{1,0:T(8,128)}) custom-call(bf16[256,768]{1,0:T(8,128)(2,1)} %copy-done.8, bf16[256,768]{1,0:T(8,128)(2,1)} %copy-done.14, bf16[256,768]{1,0:T(8,128)(2,1)} %copy-done.13, bf16[320,768]{1,0:T(8,128)(2,1)} %get-tuple-element.47.refs_0_.refs_3_.refs_2_.refs_1_, ...), custom_call_target="tpu_custom_call" | custom-call | flops 1384120320 | bytes 8388608 | tf_op jit(solution)/shard_map/pallas_call | solution.py:190
  124.0 3.6 %collective-permute-start.13 = (bf16[256,768]{1,0:T(8,128)(2,1)S(1)}, bf16[256,768]{1,0:T(8,128)(2,1)S(1)}, u32[]{:S(2)}, u32[]{:S(2)}) collective-permute-start(bf16[256,768]{1,0:T(8,128)(2,1)S(1)} %collective-permute-done.10.refs_1_), channel_id=1, source_target_pairs={{0,1},{1,2},{2,3},{3,4},{4,5},{5,6},{6,7},{7,0},{16,23},{17,16},{1... | collective-permute-start | bytes 1179656 | tf_op jit(solution)/shard_map/ppermute | solution.py:53
  127.6 5.6 %shard_map.136 = (f32[1280,320]{1,0:T(8,128)}, f32[320,768]{1,0:T(8,128)}) custom-call(bf16[256,768]{1,0:T(8,128)(2,1)} %copy-done.5, bf16[256,768]{1,0:T(8,128)(2,1)} %copy-done.4, bf16[320,768]{1,0:T(8,128)(2,1)} %get-tuple-element.47.refs_0_.refs_3_.refs_2_.refs_1_, ...), custom_call_target="tpu_custom_call", output_to_operand_aliasing={{0}: (6, {}), {1}: (7, {})} | custom-call | flops 922746880 | bytes 8388608 | tf_op jit(solution)/shard_map/pallas_call | solution.py:190
  133.2 4.6 %collective-permute-done.14.refs_0_ = bf16[256,768]{1,0:T(8,128)(2,1)S(1)} collective-permute-done((bf16[256,768]{1,0:T(8,128)(2,1)S(1)}, bf16[256,768]{1,0:T(8,128)(2,1)S(1)}, u32[]{:S(2)}, u32[]{:S(2)}) %collective-permute-start.14) | collective-permute-done | bytes 393248 | tf_op jit(solution)/shard_map/ppermute | solution.py:53
  138.5 5.7 %shard_map.137 = (f32[1280,320]{1,0:T(8,128)}, f32[320,768]{1,0:T(8,128)}) custom-call(bf16[256,768]{1,0:T(8,128)(2,1)} %copy-done.7, bf16[256,768]{1,0:T(8,128)(2,1)} %copy-done.6, bf16[320,768]{1,0:T(8,128)(2,1)} %get-tuple-element.47.refs_0_.refs_3_.refs_2_.refs_1_, ...), custom_call_target="tpu_custom_call", output_to_operand_aliasing={{0}: (6, {}), {1}: (7, {})} | custom-call | flops 922746880 | bytes 8388608 | tf_op jit(solution)/shard_map/pallas_call | solution.py:190
  144.1 5.4 %collective-permute-done.15.refs_0_ = bf16[256,768]{1,0:T(8,128)(2,1)S(1)} collective-permute-done((bf16[256,768]{1,0:T(8,128)(2,1)S(1)}, bf16[256,768]{1,0:T(8,128)(2,1)S(1)}, u32[]{:S(2)}, u32[]{:S(2)}) %collective-permute-start.15) | collective-permute-done | bytes 393248 | tf_op jit(solution)/shard_map/ppermute | solution.py:53
  150.2 6.5 %shard_map.138 = (bf16[8,80,640]{2,1,0:T(8,128)(2,1)}, bf16[8,80,640]{2,1,0:T(8,128)(2,1)}) custom-call(bf16[256,768]{1,0:T(8,128)(2,1)} %copy-done.9, bf16[320,768]{1,0:T(8,128)(2,1)} %get-tuple-element.47.refs_0_.refs_3_.refs_2_.refs_1_, bf16[1280,256]{1,0:T(8,128)(2,1)} %get-tuple-element.81.refs_2_, bf16[320,256]{1,0:T(8,128)(2,1)} %get-tuple-element.82.refs_3_, ...), custom_call_target="tpu_custom_call" | custom-call | flops 1090519040 | bytes 8388608 | tf_op jit(solution)/shard_map/pallas_call | solution.py:190
  156.7 4.6 %collective-permute-start.16 = (bf16[8,80,640]{2,1,0:T(8,128)(2,1)}, bf16[8,80,640]{2,1,0:T(8,128)(2,1)S(1)}, u32[]{:S(2)}, u32[]{:S(2)}) collective-permute-start(bf16[8,80,640]{2,1,0:T(8,128)(2,1)} %get-tuple-element.87), channel_id=1, source_target_pairs={{0,16},{16,0},{1,17},{17,1},{2,18},{18,2},{3,19},{19,3},{4,20},{20... | collective-permute-start | bytes 2457608 | tf_op jit(solution)/shard_map/ppermute | solution.py:47
  164.8 17.8 %all_to_all.5 = bf16[8,80,640]{2,1,0:T(8,128)(2,1)S(1)} all-to-all(bf16[8,80,640]{2,1,0:T(8,128)(2,1)S(1)} %add_convert_fusion), channel_id=1, replica_groups=mesh['ylo'=2,'x'=4,'core'=2,'yhi'=2,'z'=8] {'ylo','x'}, dimensions={0} | all-to-all | bytes 1638400 | tf_op jit(solution)/shard_map/all_to_all | solution.py:252
  (81 shorter events, 35.2 us)
Async XLA Ops:
  7.2 74.0 %copy-start = (s32[1,2048]{1,0:T(1,128)S(1)}, s32[1,2048]{1,0:T(1,128)}, u32[]{:S(2)}) copy-start(s32[1,2048]{1,0:T(1,128)} %param.16) | copy-start | bytes 24580
  7.2 83.2 %all-gather.2.cloned.1.call-start = ((), (), s32[]{:S(2)}) async-start(), calls=%async_computation.2 | async-start | bytes 1769472 | tf_op jit(solution)/shard_map/all_gather | solution.py:217
  7.2 11.3 %copy-start.2 = (bf16[128,768]{1,0:T(8,128)(2,1)S(1)}, bf16[128,768]{1,0:T(8,128)(2,1)}, u32[]{:S(2)}) copy-start(bf16[128,768]{1,0:T(8,128)(2,1)} %param.15) | copy-start | bytes 589828
  7.2 12.2 %copy-start.12 = (s32[2]{0:T(128)S(1)}, s32[2]{0:T(128)}, u32[]{:S(2)}) copy-start(s32[2]{0:T(128)} %constant.74.clone) | copy-start | bytes 28
  12.1 14.3 %collective-permute-start = (bf16[256,768]{1,0:T(8,128)(2,1)}, bf16[256,768]{1,0:T(8,128)(2,1)S(1)}, u32[]{:S(2)}, u32[]{:S(2)}) collective-permute-start(bf16[256,768]{1,0:T(8,128)(2,1)} %get-tuple-element.49), channel_id=1, source_target_pairs={{0,1},{1,2},{2,3},{3,4},{4,5},{5,6},{6,7},{7,0},{16,23},{17,16},{1... | collective-permute-start | bytes 1179656 | tf_op jit(solution)/shard_map/ppermute | solution.py:53
  26.4 9.8 %collective-permute-start.4 = (bf16[256,768]{1,0:T(8,128)(2,1)S(1)}, bf16[256,768]{1,0:T(8,128)(2,1)S(1)}, u32[]{:S(2)}, u32[]{:S(2)}) collective-permute-start(bf16[256,768]{1,0:T(8,128)(2,1)S(1)} %slice.27), channel_id=1, source_target_pairs={{0,7},{1,0},{2,1},{3,2},{4,3},{5,4},{6,5},{7,6},{16,17},{17,18},{1... | collective-permute-start | bytes 1179656 | tf_op jit(solution)/shard_map/ppermute | solution.py:53
  27.6 8.9 %collective-permute-start.1 = (bf16[256,768]{1,0:T(8,128)(2,1)S(1)}, bf16[256,768]{1,0:T(8,128)(2,1)S(1)}, u32[]{:S(2)}, u32[]{:S(2)}) collective-permute-start(bf16[256,768]{1,0:T(8,128)(2,1)S(1)} %add_convert_fusion.6), channel_id=1, source_target_pairs={{0,1},{1,2},{2,3},{3,4},{4,5},{5,6},{6,7},{7,0},{16,23},{17,16},{1... | collective-permute-start | bytes 1179656 | tf_op jit(solution)/shard_map/ppermute | solution.py:53
  30.4 153.2 %reduce-scatter.2.cloned.1.call-start = ((), (), s32[]{:S(2)}) async-start(), calls=%async_computation.3 | async-start | bytes 1769472 | tf_op jit(solution)/shard_map/reduce_scatter | solution.py:244
  37.9 13.6 %collective-permute-start.2 = (bf16[256,768]{1,0:T(8,128)(2,1)S(1)}, bf16[256,768]{1,0:T(8,128)(2,1)S(1)}, u32[]{:S(2)}, u32[]{:S(2)}) collective-permute-start(bf16[256,768]{1,0:T(8,128)(2,1)S(1)} %get-tuple-element.93), channel_id=1, source_target_pairs={{0,1},{1,2},{2,3},{3,4},{4,5},{5,6},{6,7},{7,0},{16,23},{17,16},{1... | collective-permute-start | bytes 1179656 | tf_op jit(solution)/shard_map/ppermute | solution.py:53
  41.1 20.2 %collective-permute-start.5 = (bf16[256,768]{1,0:T(8,128)(2,1)S(1)}, bf16[256,768]{1,0:T(8,128)(2,1)S(1)}, u32[]{:S(2)}, u32[]{:S(2)}) collective-permute-start(bf16[256,768]{1,0:T(8,128)(2,1)S(1)} %get-tuple-element.94), channel_id=1, source_target_pairs={{0,7},{1,0},{2,1},{3,2},{4,3},{5,4},{6,5},{7,6},{16,17},{17,18},{1... | collective-permute-start | bytes 1179656 | tf_op jit(solution)/shard_map/ppermute | solution.py:53
  62.6 14.2 %collective-permute-start.3 = (bf16[256,768]{1,0:T(8,128)(2,1)S(1)}, bf16[256,768]{1,0:T(8,128)(2,1)S(1)}, u32[]{:S(2)}, u32[]{:S(2)}) collective-permute-start(bf16[256,768]{1,0:T(8,128)(2,1)S(1)} %get-tuple-element.91), channel_id=1, source_target_pairs={{0,1},{1,2},{2,3},{3,4},{4,5},{5,6},{6,7},{7,0},{16,23},{17,16},{1... | collective-permute-start | bytes 1179656 | tf_op jit(solution)/shard_map/ppermute | solution.py:53
  62.7 14.5 %collective-permute-start.6 = (bf16[256,768]{1,0:T(8,128)(2,1)S(1)}, bf16[256,768]{1,0:T(8,128)(2,1)S(1)}, u32[]{:S(2)}, u32[]{:S(2)}) collective-permute-start(bf16[256,768]{1,0:T(8,128)(2,1)S(1)} %get-tuple-element.92), channel_id=1, source_target_pairs={{0,7},{1,0},{2,1},{3,2},{4,3},{5,4},{6,5},{7,6},{16,17},{17,18},{1... | collective-permute-start | bytes 1179656 | tf_op jit(solution)/shard_map/ppermute | solution.py:53
  64.1 17.0 %copy-start.1 = (bf16[1280,768]{1,0:T(8,128)(2,1)S(1)}, bf16[1280,768]{1,0:T(8,128)(2,1)}, u32[]{:S(2)}) copy-start(bf16[1280,768]{1,0:T(8,128)(2,1)} %refs_8_.1) | copy-start | bytes 5898244
  78.3 11.7 %collective-permute-start.7 = (bf16[256,768]{1,0:T(8,128)(2,1)S(1)}, bf16[256,768]{1,0:T(8,128)(2,1)S(1)}, u32[]{:S(2)}, u32[]{:S(2)}) collective-permute-start(bf16[256,768]{1,0:T(8,128)(2,1)S(1)} %add_convert_fusion.1), channel_id=1, source_target_pairs={{0,8},{8,0},{1,9},{9,1},{2,10},{10,2},{3,11},{11,3},{4,12},{12,4},... | collective-permute-start | bytes 1179656 | tf_op jit(solution)/shard_map/ppermute | solution.py:47
  93.3 10.6 %collective-permute-start.8 = (bf16[256,768]{1,0:T(8,128)(2,1)S(1)}, bf16[256,768]{1,0:T(8,128)(2,1)S(1)}, u32[]{:S(2)}, u32[]{:S(2)}) collective-permute-start(bf16[256,768]{1,0:T(8,128)(2,1)S(1)} %get-tuple-element.97), channel_id=1, source_target_pairs={{0,8},{8,0},{1,9},{9,1},{2,10},{10,2},{3,11},{11,3},{4,12},{12,4},... | collective-permute-start | bytes 1179656 | tf_op jit(solution)/shard_map/ppermute | solution.py:47
  104.4 12.6 %copy-start.8 = (bf16[256,768]{1,0:T(8,128)(2,1)}, bf16[256,768]{1,0:T(8,128)(2,1)S(1)}, u32[]{:S(2)}) copy-start(bf16[256,768]{1,0:T(8,128)(2,1)S(1)} %multiply_convert_fusion.refs_0_) | copy-start | bytes 1179652
  104.4 7.4 %collective-permute-start.9 = (bf16[256,768]{1,0:T(8,128)(2,1)S(1)}, bf16[256,768]{1,0:T(8,128)(2,1)S(1)}, u32[]{:S(2)}, u32[]{:S(2)}) collective-permute-start(bf16[256,768]{1,0:T(8,128)(2,1)S(1)} %multiply_convert_fusion.refs_0_), channel_id=1, source_target_pairs={{0,1},{1,2},{2,3},{3,4},{4,5},{5,6},{6,7},{7,0},{16,23},{17,16},{1... | collective-permute-start | bytes 1179656 | tf_op jit(solution)/shard_map/ppermute | solution.py:53
  104.5 9.5 %collective-permute-start.11 = (bf16[256,768]{1,0:T(8,128)(2,1)S(1)}, bf16[256,768]{1,0:T(8,128)(2,1)S(1)}, u32[]{:S(2)}, u32[]{:S(2)}) collective-permute-start(bf16[256,768]{1,0:T(8,128)(2,1)S(1)} %multiply_convert_fusion.refs_0_), channel_id=1, source_target_pairs={{0,7},{1,0},{2,1},{3,2},{4,3},{5,4},{6,5},{7,6},{16,17},{17,18},{1... | collective-permute-start | bytes 1179656 | tf_op jit(solution)/shard_map/ppermute | solution.py:53
  111.8 11.0 %collective-permute-start.10 = (bf16[256,768]{1,0:T(8,128)(2,1)S(1)}, bf16[256,768]{1,0:T(8,128)(2,1)S(1)}, u32[]{:S(2)}, u32[]{:S(2)}) collective-permute-start(bf16[256,768]{1,0:T(8,128)(2,1)S(1)} %collective-permute-done.9.refs_2_), channel_id=1, source_target_pairs={{0,1},{1,2},{2,3},{3,4},{4,5},{5,6},{6,7},{7,0},{16,23},{17,16},{1... | collective-permute-start | bytes 1179656 | tf_op jit(solution)/shard_map/ppermute | solution.py:53
  114.0 10.0 %collective-permute-start.12 = (bf16[256,768]{1,0:T(8,128)(2,1)S(1)}, bf16[256,768]{1,0:T(8,128)(2,1)S(1)}, u32[]{:S(2)}, u32[]{:S(2)}) collective-permute-start(bf16[256,768]{1,0:T(8,128)(2,1)S(1)} %collective-permute-done.11.refs_1_), channel_id=1, source_target_pairs={{0,7},{1,0},{2,1},{3,2},{4,3},{5,4},{6,5},{7,6},{16,17},{17,18},{1... | collective-permute-start | bytes 1179656 | tf_op jit(solution)/shard_map/ppermute | solution.py:53
  124.0 9.2 %collective-permute-start.13 = (bf16[256,768]{1,0:T(8,128)(2,1)S(1)}, bf16[256,768]{1,0:T(8,128)(2,1)S(1)}, u32[]{:S(2)}, u32[]{:S(2)}) collective-permute-start(bf16[256,768]{1,0:T(8,128)(2,1)S(1)} %collective-permute-done.10.refs_1_), channel_id=1, source_target_pairs={{0,1},{1,2},{2,3},{3,4},{4,5},{5,6},{6,7},{7,0},{16,23},{17,16},{1... | collective-permute-start | bytes 1179656 | tf_op jit(solution)/shard_map/ppermute | solution.py:53
  127.6 10.2 %collective-permute-start.14 = (bf16[256,768]{1,0:T(8,128)(2,1)S(1)}, bf16[256,768]{1,0:T(8,128)(2,1)S(1)}, u32[]{:S(2)}, u32[]{:S(2)}) collective-permute-start(bf16[256,768]{1,0:T(8,128)(2,1)S(1)} %collective-permute-done.12.refs_0_), channel_id=1, source_target_pairs={{0,7},{1,0},{2,1},{3,2},{4,3},{5,4},{6,5},{7,6},{16,17},{17,18},{1... | collective-permute-start | bytes 1179656 | tf_op jit(solution)/shard_map/ppermute | solution.py:53
  137.7 11.8 %collective-permute-start.15 = (bf16[256,768]{1,0:T(8,128)(2,1)S(1)}, bf16[256,768]{1,0:T(8,128)(2,1)S(1)}, u32[]{:S(2)}, u32[]{:S(2)}) collective-permute-start(bf16[256,768]{1,0:T(8,128)(2,1)S(1)} %collective-permute-done.13.refs_1_), channel_id=1, source_target_pairs={{0,1},{1,2},{2,3},{3,4},{4,5},{5,6},{6,7},{7,0},{16,23},{17,16},{1... | collective-permute-start | bytes 1179656 | tf_op jit(solution)/shard_map/ppermute | solution.py:53
  156.7 6.7 %collective-permute-start.16 = (bf16[8,80,640]{2,1,0:T(8,128)(2,1)}, bf16[8,80,640]{2,1,0:T(8,128)(2,1)S(1)}, u32[]{:S(2)}, u32[]{:S(2)}) collective-permute-start(bf16[8,80,640]{2,1,0:T(8,128)(2,1)} %get-tuple-element.87), channel_id=1, source_target_pairs={{0,16},{16,0},{1,17},{17,1},{2,18},{18,2},{3,19},{19,3},{4,20},{20... | collective-permute-start | bytes 2457608 | tf_op jit(solution)/shard_map/ppermute | solution.py:47
  (10 other events, 35.5 us)
Sparse Core Ops, SparseCore 0:
  30.5 40.7 all-gather.1
  124.1 40.7 reduce-scatter.1

commit v5 on v1

v5 whole, which is shorter than its diff:
```python
import functools

import jax
import jax.numpy as jnp
from jax import lax
from jax.experimental import pallas as pl
from jax.experimental.pallas import tpu as pltpu
from jax.sharding import Mesh, PartitionSpec as P

logit_scale = 8.0
logit_bias = -3.0
epsilon = 1e-06
gelu_root = 0.7978845608028654
gelu_cubic = 0.044715

AUDIO = ("ylo", "x", "core")
SCORE = ("yhi", "z")
RING = 8
VMEM_BYTES = 56 * 1024 * 1024
f32 = jnp.float32
bf16 = jnp.bfloat16


def dot(left, right, dims=((1,), (0,))):
    return lax.dot_general(left, right, (dims, ((), ())), preferred_element_type=f32)


def unit_rows(values):
    wide = values.astype(f32)
    inverse = lax.rsqrt(jnp.sum(wide * wide, axis=-1, keepdims=True) + epsilon)
    return (wide * inverse, inverse)


def unit_backward(unit_wide, inverse, grad_unit):
    inner = jnp.sum(unit_wide * grad_unit, axis=-1, keepdims=True)
    return inverse * (grad_unit - unit_wide * inner)


def pair_coeffs(left, right, partner, first_column):
    logits = logit_scale * dot(left, right, ((1,), (1,))) + logit_bias
    columns = first_column + lax.iota(jnp.int32, right.shape[0])
    sign = jnp.where(partner[:, None] == columns[None, :], 1.0, -1.0)
    return (-logit_scale * sign * jax.nn.sigmoid(-sign * logits)).astype(bf16)


def swap(value, axis):
    return lax.ppermute(value, axis, [(0, 1), (1, 0)])


def shift(value, step):
    perm = [(i, (i + step) % RING) for i in range(RING)]
    perm += [(RING + i, RING + (i - step) % RING) for i in range(RING)]
    return lax.ppermute(value, ("core", "z"), perm)


def forward_kernel(count, index_ref, *refs):
    hidden = [ref[...] for ref in refs[:count]]
    up_ref, down_head_ref, part_ref, normed_t_ref, act_t_ref, slope_ref = refs[count:]
    rows = hidden[0].shape[0]
    wide = (jnp.concatenate(hidden, axis=0) if count > 1 else hidden[0]).astype(f32)
    square_mean = jnp.mean(wide * wide, axis=-1, keepdims=True)
    normed = (wide * lax.rsqrt(square_mean + epsilon)).astype(bf16)
    part = None
    for side in range(2):
        pre = dot(normed, up_ref[side], ((1,), (1,)))
        tangent = jnp.tanh(gelu_root * (pre + gelu_cubic * (pre * pre * pre)))
        act = (0.5 * pre * (1.0 + tangent)).astype(bf16)
        term = dot(act, down_head_ref[side])
        part = term if part is None else part + term
        slope = 0.5 * (1.0 + tangent) + 0.5 * pre * (1.0 - tangent * tangent) * gelu_root * (
            1.0 + 3.0 * gelu_cubic * pre * pre
        )
        slope = slope.astype(bf16)
        act_t = act.T
        for i in range(count):
            slope_ref[i, side] = slope[i * rows : (i + 1) * rows, :]
            act_t_ref[i, side] = act_t[:, i * rows : (i + 1) * rows]
    part_ref[...] = part.astype(bf16)
    normed_t = normed.T
    for i in range(count):
        normed_t_ref[i] = normed_t[:, i * rows : (i + 1) * rows]


def forward_blocks(offsets, half, place, direction, hidden_in, up_pair, down_head):
    count = len(offsets)
    rows = hidden_in.shape[0] // (2 * RING)
    _, ff, width = up_pair.shape
    embed = down_head.shape[2]
    index = half * RING + lax.rem(place + direction * jnp.array(offsets, jnp.int32) + RING, RING)
    out = pl.pallas_call(
        functools.partial(forward_kernel, count),
        grid_spec=pltpu.PrefetchScalarGridSpec(
            num_scalar_prefetch=1,
            grid=(1,),
            in_specs=[pl.BlockSpec((rows, width), lambda i, index, at=at: (index[at], 0)) for at in range(count)]
            + [
                pl.BlockSpec((2, ff, width), lambda i, index: (0, 0, 0)),
                pl.BlockSpec((2, ff, embed), lambda i, index: (0, 0, 0)),
            ],
            out_specs=[
                pl.BlockSpec((count * rows, embed), lambda i, index: (0, 0)),
                pl.BlockSpec((count, width, rows), lambda i, index: (0, 0, 0)),
                pl.BlockSpec((count, 2, ff, rows), lambda i, index: (0, 0, 0, 0)),
                pl.BlockSpec((count, 2, rows, ff), lambda i, index: (0, 0, 0, 0)),
            ],
        ),
        out_shape=[
            jax.ShapeDtypeStruct((count * rows, embed), bf16),
            jax.ShapeDtypeStruct((count, width, rows), bf16),
            jax.ShapeDtypeStruct((count, 2, ff, rows), bf16),
            jax.ShapeDtypeStruct((count, 2, rows, ff), bf16),
        ],
        compiler_params=pltpu.CompilerParams(vmem_limit_bytes=VMEM_BYTES),
        cost_estimate=pl.CostEstimate(
            flops=4 * count * rows * ff * (width + embed),
            bytes_accessed=2 * count * rows * (2 * width + embed + 4 * ff) + 4 * ff * (width + embed),
            transcendentals=2 * count * rows * ff,
        ),
    )(index, *([hidden_in] * count), up_pair, down_head)
    return [out[0][at * rows : (at + 1) * rows] for at in range(count)], out[1:]


def backward_kernel(count, first, last, *refs):
    join = lambda parts, axis: jnp.concatenate(parts, axis=axis) if count > 1 else parts[0]
    grad = join([ref[...] for ref in refs[:count]], 0)
    kept = refs[count : 4 * count]
    normed_t = join([ref[0] for ref in kept[0::3]], 1)
    down_head_ref = refs[4 * count]
    refs = refs[4 * count + 1 :]
    if not first:
        up_in, act_in = refs[:2]
        refs = refs[2:]
    if last:
        place_ref, head_ref, keep_ref, give_ref, up_acc = refs
        core, half = place_ref[0], place_ref[1]
    else:
        up_acc, act_acc = refs
    tile = 256
    _, width, ff = up_acc.shape
    for side in range(2):
        act_t = join([ref[0, side] for ref in kept[1::3]], 1)
        slope = join([ref[0, side] for ref in kept[2::3]], 0)
        grad_act = dot(grad, down_head_ref[side], ((1,), (1,)))
        grad_pre = (grad_act * slope.astype(f32)).astype(bf16)
        act_sum = dot(act_t, grad)
        if not first:
            act_sum = act_sum + act_in[side]
        if not last:
            act_acc[side] = act_sum
        for m in range(0, width, tile):
            up_sum = dot(normed_t[m : m + tile, :], grad_pre)
            if not first:
                up_sum = up_sum + up_in[side, m : m + tile, :]
            up_acc[side, m : m + tile, :] = up_sum
        if last:
            act_grad = act_sum.astype(bf16)
            rows = keep_ref.shape[1]
            slot = lax.rem(half + side, 2)
            for part in range(2):
                for which, out_ref in ((core, keep_ref), (1 - core, give_ref)):
                    for chip in range(keep_ref.shape[0] // 2):
                        at = pl.multiple_of((2 * chip + which) * rows, rows)
                        out_ref[2 * chip + slot, :, part * ff : (part + 1) * ff] = up_acc[
                            side, pl.ds(at, rows), :
                        ].astype(bf16)
                if part == 0:
                    for m in range(0, width, tile):
                        up_acc[side, m : m + tile, :] = dot(head_ref[m : m + tile, :], act_grad, ((1,), (1,)))


def backward_blocks(items, down_head, sums, last=None):
    whole = pl.BlockSpec(memory_space=pltpu.VMEM)
    args = [grad for grad, _, _ in items]
    specs = [whole] * len(items)
    for _, saved, at in items:
        for array in saved:
            args.append(array)
            zeros = (0,) * (array.ndim - 1)
            specs.append(pl.BlockSpec((1,) + array.shape[1:], lambda i, at=at, zeros=zeros: (at,) + zeros))
    _, ff, embed = down_head.shape
    rows, width = items[0][0].shape[0], items[0][1][0].shape[1]
    args.append(down_head)
    specs.append(whole)
    aliases = {}
    if sums is not None:
        if last is None:
            aliases = {len(args): 0, len(args) + 1: 1}
        args += list(sums)
        specs += [whole] * 2
    flops = 4 * len(items) * rows * ff * (2 * embed + width)
    if last is None:
        shapes = [jax.ShapeDtypeStruct((2, width, ff), f32), jax.ShapeDtypeStruct((2, ff, embed), f32)]
        scratch = []
    else:
        args += list(last)
        specs += [pl.BlockSpec(memory_space=pltpu.SMEM), whole]
        shapes = [jax.ShapeDtypeStruct((16, width // 16, 2 * ff), bf16)] * 2
        scratch = [pltpu.VMEM((2, width, ff), f32)]
        flops += 4 * width * ff * embed
    return pl.pallas_call(
        functools.partial(backward_kernel, len(items), sums is None, last is not None),
        grid=(1,),
        in_specs=specs,
        out_specs=[whole] * 2,
        out_shape=shapes,
        scratch_shapes=scratch,
        input_output_aliases=aliases,
        compiler_params=pltpu.CompilerParams(vmem_limit_bytes=VMEM_BYTES),
        cost_estimate=pl.CostEstimate(flops=flops, bytes_accessed=12 * 1024 * 1024, transcendentals=0),
    )(*args)


def total_of(*terms):
    return sum(term.astype(f32) for term in terms)


def from_partner(value, core):
    cut = value.shape[0] // 2
    mine = swap(lax.dynamic_slice_in_dim(value, core * cut, cut, 0), "yhi")
    other = swap(mine, "core")
    halves = [jnp.where(core == 0, mine, other), jnp.where(core == 0, other, mine)]
    return jnp.concatenate([value] + halves, axis=0).reshape((2,) + value.shape)


def per_device(hidden_in, up_weight, down_weight, head_weight, score_embed, pair_index):
    y_hi, z, core = (lax.axis_index(name).astype(jnp.int32) for name in ("yhi", "z", "core"))
    rows = hidden_in.shape[0] // (2 * RING)
    group_half = RING * rows
    direction = 1 - 2 * core
    up_pair = from_partner(up_weight.T, core)
    score_wide, score_inverse = unit_rows(score_embed)
    down_head, score_unit = lax.optimization_barrier(
        (dot(down_weight, head_weight).astype(bf16), score_wide.astype(bf16))
    )
    score_half = lax.all_gather(score_unit, "z", axis=0, tiled=True)
    down_head = from_partner(down_head, core)
    saved, parts = {}, {}

    def forward(*offsets):
        found, arrays = forward_blocks(offsets, y_hi, z, direction, hidden_in, up_pair, down_head)
        for at, offset in enumerate(offsets):
            parts[offset] = found[at]
            saved[offset] = (arrays, at)

    forward(4)
    fore, back = shift(parts[4], 1), None
    forward(3, -3)
    for step in (3, 2, 1):
        fore = total_of(fore, parts[step]).astype(bf16)
        back = parts[-step] if back is None else total_of(back, parts[-step]).astype(bf16)
        fore, back = shift(fore, 1), shift(back, -1)
        if step == 3:
            forward(2, -2, 1, -1, 0)
    own_start = y_hi * group_half + z * rows
    own_hidden = lax.dynamic_slice_in_dim(hidden_in, own_start, rows, 0)
    own_proj = dot(own_hidden, head_weight)
    audio_wide, audio_inverse = unit_rows(own_proj + total_of(parts[0], fore, back))
    audio_own = audio_wide.astype(bf16)
    audio_unit = jnp.concatenate([audio_own, swap(audio_own, "yhi")], axis=0)
    far_start = (1 - y_hi) * group_half + z * rows
    partners = jnp.concatenate(
        [lax.dynamic_slice_in_dim(pair_index[0], start, rows, 0) for start in (own_start, far_start)]
    )
    coeffs = pair_coeffs(audio_unit, score_half, partners, y_hi * group_half)
    grad_audio = dot(coeffs, score_half)
    grad_audio = grad_audio[:rows] + swap(grad_audio[rows:].astype(bf16), "yhi").astype(f32)
    grad_embed = unit_backward(audio_wide, audio_inverse, grad_audio).astype(bf16)
    score_part = dot(coeffs, audio_unit, ((0,), (0,))).astype(bf16)
    item = lambda grad, offset: (grad,) + saved[offset]
    items = [item(grad_embed, 0)]
    fore = back = grad_embed
    for step in (1, 2):
        fore, back = shift(fore, 1), shift(back, -1)
        items += [item(back, step), item(fore, -step)]
    fore, back, score_part = lax.optimization_barrier((fore, back, score_part))
    grad_score = lax.psum_scatter(score_part, "z", scatter_dimension=0, tiled=True)
    fore, back = shift(fore, 1), shift(back, -1)
    sums = backward_blocks(items, down_head, None)
    fore, back, sums = lax.optimization_barrier((fore, back, sums))
    items = [item(back, 3), item(fore, -3), item(shift(fore, 1), 4)]
    place = jnp.stack([core, y_hi])
    keep, give = backward_blocks(items, down_head, sums, (place, head_weight))
    chip = total_of(keep, swap(give, "core")).astype(bf16)
    landed = lax.all_to_all(chip, ("ylo", "x", "yhi"), 0, 0)
    total = jnp.sum(landed.astype(f32), axis=0)
    ff = up_weight.shape[1]
    score_grad = unit_backward(score_wide, score_inverse, grad_score.astype(f32))
    return (total[:, :ff], total[:, ff:].T, score_grad)


def solution(mesh):
    fine = Mesh(mesh.devices.reshape(2, 4, 2, 2, RING), ("ylo", "x", "core", "yhi", "z"))
    in_specs = (
        P(AUDIO, None),
        P(None, SCORE),
        P(SCORE, None),
        P(),
        P(AUDIO + SCORE, None),
        P(AUDIO, None),
    )
    out_specs = (P(AUDIO, SCORE), P(SCORE, AUDIO), P(AUDIO + SCORE, None))
    return jax.shard_map(
        per_device, mesh=fine, in_specs=in_specs, out_specs=out_specs, check_vma=False
    )
```

time: 223 us -> 203 us (0.910)
  waiting for transfers between devices: 145 us -> 64.3 us
  starting transfers between devices: 11.9 us -> 54.3 us
  Pallas kernels: 0 us -> 37.7 us
  matrix products: 28.7 us -> 8.55 us
  local copies, waits for them, and re-layouts: 9 us -> 3.2 us
  other arithmetic: 13.9 us -> 19.1 us
    all_gather x2 -> x1, waiting for transfers between devices: 75.7 us -> 0.01 us  [per_device(): score_half = lax.all_gather(score_unit, 'z', axis=0, tiled=True)]
    reduce_scatter x2 -> x1, waiting for transfers between devices: 52.2 us -> 3.29 us  [per_device(): lax.psum_scatter(score_part, 'z', scatter_dimension=0, tiled=True)]
    pallas_call x0 -> x5, Pallas kernels: none -> 37.7 us  [the longest x2 19.6 us: backward_blocks(): pl.pallas_call(functools.partial(backward_kernel, len(items), sums is Non...]
    ppermute x0 -> x14, starting transfers between devices: none -> 25 us  [shift(): return lax.ppermute(value, ('core', 'z'), perm)]
    ppermute x0 -> x14, waiting for transfers between devices: none -> 23.9 us  [shift(): return lax.ppermute(value, ('core', 'z'), perm)]
    dot_general x9 -> x5, matrix products: 28.7 us -> 8.55 us  [dot(): lax.dot_general(left, right, (dims, ((), ())), preferred_element_type=f32)]
    ppermute x3 -> x7, starting transfers between devices: 6.65 us -> 22.4 us  [swap(): return lax.ppermute(value, axis, [(0, 1), (1, 0)])]
    all_to_all x1, waiting for transfers between devices: 4.43 us -> 19 us  [per_device(): landed = lax.all_to_all(chip, ('ylo', 'x', 'yhi'), 0, 0)]
  transfers between devices with their start and end apart: 8 -> 24, of which waited for: 8 -> 16; matrix products, arithmetic and copies ran while one was open for 14% -> 10% of each run, Pallas kernels for 0% -> 19%
where the time goes in v5:
time: 203 us; the launch traced here: 201 us
  waiting for transfers between devices  64.3 us (32%)
  starting transfers between devices  54.3 us (27%)
  Pallas kernels  37.7 us (19%)
  other arithmetic  19.1 us (9%)
  between operations  14.3 us (7%)
  matrix products  8.55 us (4%)
  local copies, waits for them, and re-layouts  3.2 us (2%)
    ppermute x14, starting transfers between devices, shift(): return lax.ppermute(value, ('core', 'z'), perm)  25 us
    ppermute x14, waiting for transfers between devices, shift(): return lax.ppermute(value, ('core', 'z'), perm)  23.9 us
    ppermute x7, starting transfers between devices, swap(): return lax.ppermute(value, axis, [(0, 1), (1, 0)])  22.4 us
    pallas_call x2, Pallas kernels, backward_blocks(): pl.pallas_call(functools.partial(backward_kernel, len(items), sums is Non...  19.6 us
    all_to_all x1, waiting for transfers between devices, per_device(): landed = lax.all_to_all(chip, ('ylo', 'x', 'yhi'), 0, 0)  19 us
    pallas_call x3, Pallas kernels, forward_blocks(): pl.pallas_call(functools.partial(forward_kernel, count), grid_spec=pltpu....  18.1 us
    ppermute x7, waiting for transfers between devices, swap(): return lax.ppermute(value, axis, [(0, 1), (1, 0)])  18 us
    dot_general x5, matrix products, dot(): lax.dot_general(left, right, (dims, ((), ())), preferred_element_type=f32)  8.55 us
  transfers between devices with their start and end apart: 24, of which 16 were waited for; matrix products, arithmetic and copies ran while one was open for 10% of the time, Pallas kernels for 19%

profile of v5, /device:TPU:1, one launch (start us, length us, event | category | flops | bytes accessed | tf_op | source)
XLA Modules:
  0.0 201.4 jit_solution(12540917015939178281)
XLA Ops:
  12.5 3.8 %collective-permute-start.2 = (bf16[160,768]{1,0:T(8,128)(2,1)S(1)}, bf16[160,768]{1,0:T(8,128)(2,1)S(1)}, u32[]{:S(2)}, u32[]{:S(2)}) collective-permute-start(bf16[160,768]{1,0:T(8,128)(2,1)S(1)} %constant_dynamic-slice_fusion.2), channel_id=1, source_target_pairs={{0,8},{8,0},{1,9},{9,1},{2,10},{10,2},{3,11},{11,3},{4,12},{12,4},... | collective-permute-start | bytes 737288 | tf_op jit(solution)/shard_map/ppermute | solution.py:47
  16.5 4.5 %collective-permute-done.2 = bf16[160,768]{1,0:T(8,128)(2,1)S(1)} collective-permute-done((bf16[160,768]{1,0:T(8,128)(2,1)S(1)}, bf16[160,768]{1,0:T(8,128)(2,1)S(1)}, u32[]{:S(2)}, u32[]{:S(2)}) %collective-permute-start.2) | collective-permute-done | bytes 245792 | tf_op jit(solution)/shard_map/ppermute | solution.py:47
  21.0 5.1 %collective-permute-start.3 = (bf16[160,768]{1,0:T(8,128)(2,1)S(1)}, bf16[160,768]{1,0:T(8,128)(2,1)S(1)}, u32[]{:S(2)}, u32[]{:S(2)}) collective-permute-start(bf16[160,768]{1,0:T(8,128)(2,1)S(1)} %collective-permute-done.2), channel_id=1, source_target_pairs={{0,16},{16,0},{1,17},{17,1},{2,18},{18,2},{3,19},{19,3},{4,20},{20... | collective-permute-start | bytes 737288 | tf_op jit(solution)/shard_map/ppermute | solution.py:47
  26.0 3.7 %collective-permute-done = bf16[160,1280]{1,0:T(8,128)(2,1)S(1)} collective-permute-done((bf16[160,1280]{1,0:T(8,128)(2,1)S(1)}, bf16[160,1280]{1,0:T(8,128)(2,1)S(1)}, u32[]{:S(2)}, u32[]{:S(2)}) %collective-permute-start) | collective-permute-done | bytes 409632 | tf_op jit(solution)/shard_map/ppermute | solution.py:47
  35.1 3.8 %shard_map.113 = (bf16[128,768]{1,0:T(8,128)(2,1)}, bf16[1,1280,128]{2,1,0:T(8,128)(2,1)}, bf16[1,2,320,128]{3,2,1,0:T(8,128)(2,1)}, bf16[1,2,128,320]{3,2,1,0:T(8,128)(2,1)}) custom-call(s32[1]{0:T(128)S(6)} %add.142.index_ref, bf16[2048,1280]{1,0:T(8,128)(2,1)} %refs_1_.3, bf16[2,320,1280]{2,1,0:T(8,128)(2,1)} %bitcast.27, bf16[2,320,768]{2,1,0:T(8,128)(2,1)} %bitcast.22), custom_call_target="tpu_custom_call" | custom-call | flops 335544320 | bytes 3801088 | tf_op jit(solution)/shard_map/pallas_call | solution.py:90
  38.9 5.3 %collective-permute-start.4 = (bf16[128,768]{1,0:T(8,128)(2,1)}, bf16[128,768]{1,0:T(8,128)(2,1)S(1)}, u32[]{:S(2)}, u32[]{:S(2)}) collective-permute-start(bf16[128,768]{1,0:T(8,128)(2,1)} %get-tuple-element.30), channel_id=1, source_target_pairs={{0,1},{1,2},{2,3},{3,4},{4,5},{5,6},{6,7},{7,0},{16,23},{17,16},{1... | collective-permute-start | bytes 589832 | tf_op jit(solution)/shard_map/ppermute | solution.py:53
  44.7 5.4 %shard_map.114 = (bf16[256,768]{1,0:T(8,128)(2,1)}, bf16[2,1280,128]{2,1,0:T(8,128)(2,1)}, bf16[2,2,320,128]{3,2,1,0:T(8,128)(2,1)}, bf16[2,2,128,320]{3,2,1,0:T(8,128)(2,1)}) custom-call(s32[2]{0:T(128)} %fusion.21.index_ref, bf16[2048,1280]{1,0:T(8,128)(2,1)} %refs_1_.3, bf16[2048,1280]{1,0:T(8,128)(2,1)} %refs_1_.3, bf16[2,320,1280]{2,1,0:T(8,128)(2,1)} %bitcast.28, ...), custom_call_target="tpu_custom_call" | custom-call | flops 671088640 | bytes 4980736 | tf_op jit(solution)/shard_map/pallas_call | solution.py:90
  55.4 8.9 %shard_map.112 = (bf16[640,768]{1,0:T(8,128)(2,1)}, bf16[5,1280,128]{2,1,0:T(8,128)(2,1)}, bf16[5,2,320,128]{3,2,1,0:T(8,128)(2,1)}, bf16[5,2,128,320]{3,2,1,0:T(8,128)(2,1)}) custom-call(s32[5]{0:T(128)} %fusion.19.index_ref, bf16[2048,1280]{1,0:T(8,128)(2,1)} %refs_1_.3, bf16[2048,1280]{1,0:T(8,128)(2,1)} %refs_1_.3, bf16[2048,1280]{1,0:T(8,128)(2,1)} %refs_1_.3, ...), custom_call_target="tpu_custom_call" | custom-call | flops 1677721600 | bytes 8519680 | tf_op jit(solution)/shard_map/pallas_call | solution.py:90
  67.3 8.9 %collective-permute-done.6 = bf16[128,768]{1,0:T(8,128)(2,1)S(1)} collective-permute-done((bf16[128,768]{1,0:T(8,128)(2,1)S(1)}, bf16[128,768]{1,0:T(8,128)(2,1)S(1)}, u32[]{:S(2)}, u32[]{:S(2)}) %collective-permute-start.6) | collective-permute-done | bytes 196640 | tf_op jit(solution)/shard_map/ppermute | solution.py:53
  86.7 3.0 %collective-permute-start.11 = (bf16[128,768]{1,0:T(8,128)(2,1)S(1)}, bf16[128,768]{1,0:T(8,128)(2,1)S(1)}, u32[]{:S(2)}, u32[]{:S(2)}) collective-permute-start(bf16[128,768]{1,0:T(8,128)(2,1)S(1)} %multiply_convert_fusion.1), channel_id=1, source_target_pairs={{0,8},{8,0},{1,9},{9,1},{2,10},{10,2},{3,11},{11,3},{4,12},{12,4},... | collective-permute-start | bytes 589832 | tf_op jit(solution)/shard_map/ppermute | solution.py:47
  89.7 3.1 %collective-permute-done.11 = bf16[128,768]{1,0:T(8,128)(2,1)S(1)} collective-permute-done((bf16[128,768]{1,0:T(8,128)(2,1)S(1)}, bf16[128,768]{1,0:T(8,128)(2,1)S(1)}, u32[]{:S(2)}, u32[]{:S(2)}) %collective-permute-start.11) | collective-permute-done | bytes 196640 | tf_op jit(solution)/shard_map/ppermute | solution.py:47
  95.8 3.0 %collective-permute-start.12 = (bf16[128,768]{1,0:T(8,128)(2,1)S(1)}, bf16[128,768]{1,0:T(8,128)(2,1)S(1)}, u32[]{:S(2)}, u32[]{:S(2)}) collective-permute-start(bf16[128,768]{1,0:T(8,128)(2,1)S(1)} %slice.62), channel_id=1, source_target_pairs={{0,8},{8,0},{1,9},{9,1},{2,10},{10,2},{3,11},{11,3},{4,12},{12,4},... | collective-permute-start | bytes 589832 | tf_op jit(solution)/shard_map/ppermute | solution.py:47
  98.7 3.2 %collective-permute-done.12 = bf16[128,768]{1,0:T(8,128)(2,1)S(1)} collective-permute-done((bf16[128,768]{1,0:T(8,128)(2,1)S(1)}, bf16[128,768]{1,0:T(8,128)(2,1)S(1)}, u32[]{:S(2)}, u32[]{:S(2)}) %collective-permute-start.12) | collective-permute-done | bytes 196640 | tf_op jit(solution)/shard_map/ppermute | solution.py:47
  102.3 6.6 %collective-permute-start.13 = (bf16[128,768]{1,0:T(8,128)(2,1)S(1)}, bf16[128,768]{1,0:T(8,128)(2,1)S(1)}, u32[]{:S(2)}, u32[]{:S(2)}) collective-permute-start(bf16[128,768]{1,0:T(8,128)(2,1)S(1)} %multiply_convert_fusion.refs_0_), channel_id=1, source_target_pairs={{0,1},{1,2},{2,3},{3,4},{4,5},{5,6},{6,7},{7,0},{16,23},{17,16},{1... | collective-permute-start | bytes 589832 | tf_op jit(solution)/shard_map/ppermute | solution.py:53
  111.5 3.1 %collective-permute-start.14 = (bf16[128,768]{1,0:T(8,128)(2,1)S(1)}, bf16[128,768]{1,0:T(8,128)(2,1)S(1)}, u32[]{:S(2)}, u32[]{:S(2)}) collective-permute-start(bf16[128,768]{1,0:T(8,128)(2,1)S(1)} %collective-permute-done.13.refs_2_), channel_id=1, source_target_pairs={{0,1},{1,2},{2,3},{3,4},{4,5},{5,6},{6,7},{7,0},{16,23},{17,16},{1... | collective-permute-start | bytes 589832 | tf_op jit(solution)/shard_map/ppermute | solution.py:53
  117.5 6.1 %collective-permute-done.16.refs_3_ = bf16[128,768]{1,0:T(8,128)(2,1)S(1)} collective-permute-done((bf16[128,768]{1,0:T(8,128)(2,1)S(1)}, bf16[128,768]{1,0:T(8,128)(2,1)S(1)}, u32[]{:S(2)}, u32[]{:S(2)}) %collective-permute-start.16) | collective-permute-done | bytes 196640 | tf_op jit(solution)/shard_map/ppermute | solution.py:53
  125.2 8.4 %shard_map.115 = (f32[2,1280,320]{2,1,0:T(8,128)}, f32[2,320,768]{2,1,0:T(8,128)}) custom-call(bf16[128,768]{1,0:T(8,128)(2,1)} %copy-done.5, bf16[128,768]{1,0:T(8,128)(2,1)} %copy-done.7, bf16[128,768]{1,0:T(8,128)(2,1)} %copy-done.6, bf16[128,768]{1,0:T(8,128)(2,1)} %copy-done.9, bf16[128,768]{1,0:T(8,128)(2,1)} %copy-done.8, ...), custom_call_target="tpu_custom_call" | custom-call | flops 2306867200 | bytes 12582912 | tf_op jit(solution)/shard_map/pallas_call | solution.py:200
  138.9 11.2 %shard_map.116 = (bf16[16,80,640]{2,1,0:T(8,128)(2,1)}, bf16[16,80,640]{2,1,0:T(8,128)(2,1)}) custom-call(bf16[128,768]{1,0:T(8,128)(2,1)} %copy-done.11, bf16[128,768]{1,0:T(8,128)(2,1)} %copy-done.10, bf16[128,768]{1,0:T(8,128)(2,1)} %copy-done.12, bf16[2,1280,128]{2,1,0:T(8,128)(2,1)} %get-tuple-element.42.refs_3_.refs_6_, ...), custom_call_target="tpu_custom_call" | custom-call | flops 2642411520 | bytes 12582912 | tf_op jit(solution)/shard_map/pallas_call | solution.py:200
  150.1 4.9 %collective-permute-start.20 = (bf16[16,80,640]{2,1,0:T(8,128)(2,1)}, bf16[16,80,640]{2,1,0:T(8,128)(2,1)S(1)}, u32[]{:S(2)}, u32[]{:S(2)}) collective-permute-start(bf16[16,80,640]{2,1,0:T(8,128)(2,1)} %get-tuple-element.51), channel_id=1, source_target_pairs={{0,16},{16,0},{1,17},{17,1},{2,18},{18,2},{3,19},{19,3},{4,20},{20... | collective-permute-start | bytes 4915208 | tf_op jit(solution)/shard_map/ppermute | solution.py:47
  155.0 3.3 %collective-permute-done.20 = bf16[16,80,640]{2,1,0:T(8,128)(2,1)S(1)} collective-permute-done((bf16[16,80,640]{2,1,0:T(8,128)(2,1)}, bf16[16,80,640]{2,1,0:T(8,128)(2,1)S(1)}, u32[]{:S(2)}, u32[]{:S(2)}) %collective-permute-start.20) | collective-permute-done | bytes 1638432 | tf_op jit(solution)/shard_map/ppermute | solution.py:47
  158.4 3.1 %add_convert_fusion = bf16[16,80,640]{2,1,0:T(8,128)(2,1)} fusion(bf16[16,80,640]{2,1,0:T(8,128)(2,1)S(1)} %collective-permute-done.20, bf16[16,80,640]{2,1,0:T(8,128)(2,1)} %get-tuple-element.50), kind=kLoop, calls=%fused_computation.1 | loop fusion | flops 3276800 | bytes 4915200 | tf_op jit(solution)/shard_map/convert_element_type | solution.py:283
  161.5 6.8 %all-to-all-start = ((bf16[16,80,640]{2,1,0:T(8,128)(2,1)}), bf16[16,80,640]{2,1,0:T(8,128)(2,1)S(1)}, u32[]{:S(2)}, u32[]{:S(2)}) async-start(bf16[16,80,640]{2,1,0:T(8,128)(2,1)} %add_convert_fusion), calls=%async_computation | async-start | bytes 3276800 | tf_op jit(solution)/shard_map/all_to_all | solution.py:284
  168.3 3.3 %reduce-scatter.2.cloned.1.call-done = bf16[128,768]{1,0:T(8,128)(2,1)} async-done(((bf16[1024,768]{1,0:T(8,128)(2,1)}), bf16[128,768]{1,0:T(8,128)(2,1)}) %reduce-scatter.2.cloned.1.call-update) | async-done | bytes 196624 | tf_op jit(solution)/shard_map/reduce_scatter | solution.py:276
  174.6 19.0 %all-to-all-done = bf16[16,80,640]{2,1,0:T(8,128)(2,1)S(1)} async-done(((bf16[16,80,640]{2,1,0:T(8,128)(2,1)}), bf16[16,80,640]{2,1,0:T(8,128)(2,1)S(1)}, u32[]{:S(2)}, u32[]{:S(2)}) %all-to-all-start) | async-done | bytes 1638432 | tf_op jit(solution)/shard_map/all_to_all | solution.py:284
  (96 shorter events, 49.6 us)
Async XLA Ops:
  7.2 85.6 %all-gather.2.cloned.1.call-start = ((), (), s32[]{:S(2)}) async-start(), calls=%async_computation.2 | async-start | bytes 1769472 | tf_op jit(solution)/shard_map/all_gather | solution.py:235
  12.5 8.4 %collective-permute-start.2 = (bf16[160,768]{1,0:T(8,128)(2,1)S(1)}, bf16[160,768]{1,0:T(8,128)(2,1)S(1)}, u32[]{:S(2)}, u32[]{:S(2)}) collective-permute-start(bf16[160,768]{1,0:T(8,128)(2,1)S(1)} %constant_dynamic-slice_fusion.2), channel_id=1, source_target_pairs={{0,8},{8,0},{1,9},{9,1},{2,10},{10,2},{3,11},{11,3},{4,12},{12,4},... | collective-permute-start | bytes 737288 | tf_op jit(solution)/shard_map/ppermute | solution.py:47
  16.4 13.4 %collective-permute-start = (bf16[160,1280]{1,0:T(8,128)(2,1)S(1)}, bf16[160,1280]{1,0:T(8,128)(2,1)S(1)}, u32[]{:S(2)}, u32[]{:S(2)}) collective-permute-start(bf16[160,1280]{1,0:T(8,128)(2,1)S(1)} %dynamic-slice_bitcast_fusion), channel_id=1, source_target_pairs={{0,8},{8,0},{1,9},{9,1},{2,10},{10,2},{3,11},{11,3},{4,12},{12,4},... | collective-permute-start | bytes 1228808 | tf_op jit(solution)/shard_map/ppermute | solution.py:47
  21.0 11.5 %collective-permute-start.3 = (bf16[160,768]{1,0:T(8,128)(2,1)S(1)}, bf16[160,768]{1,0:T(8,128)(2,1)S(1)}, u32[]{:S(2)}, u32[]{:S(2)}) collective-permute-start(bf16[160,768]{1,0:T(8,128)(2,1)S(1)} %collective-permute-done.2), channel_id=1, source_target_pairs={{0,16},{16,0},{1,17},{17,1},{2,18},{18,2},{3,19},{19,3},{4,20},{20... | collective-permute-start | bytes 737288 | tf_op jit(solution)/shard_map/ppermute | solution.py:47
  29.8 4.0 %collective-permute-start.1 = (bf16[160,1280]{1,0:T(8,128)(2,1)S(1)}, bf16[160,1280]{1,0:T(8,128)(2,1)S(1)}, u32[]{:S(2)}, u32[]{:S(2)}) collective-permute-start(bf16[160,1280]{1,0:T(8,128)(2,1)S(1)} %collective-permute-done), channel_id=1, source_target_pairs={{0,16},{16,0},{1,17},{17,1},{2,18},{18,2},{3,19},{19,3},{4,20},{20... | collective-permute-start | bytes 1228808 | tf_op jit(solution)/shard_map/ppermute | solution.py:47
  32.4 139.2 %reduce-scatter.2.cloned.1.call-start = ((), (), s32[]{:S(2)}) async-start(), calls=%async_computation.3 | async-start | bytes 1769472 | tf_op jit(solution)/shard_map/reduce_scatter | solution.py:276
  38.9 12.3 %collective-permute-start.4 = (bf16[128,768]{1,0:T(8,128)(2,1)}, bf16[128,768]{1,0:T(8,128)(2,1)S(1)}, u32[]{:S(2)}, u32[]{:S(2)}) collective-permute-start(bf16[128,768]{1,0:T(8,128)(2,1)} %get-tuple-element.30), channel_id=1, source_target_pairs={{0,1},{1,2},{2,3},{3,4},{4,5},{5,6},{6,7},{7,0},{16,23},{17,16},{1... | collective-permute-start | bytes 589832 | tf_op jit(solution)/shard_map/ppermute | solution.py:53
  51.1 13.3 %collective-permute-start.8 = (bf16[128,768]{1,0:T(8,128)(2,1)S(1)}, bf16[128,768]{1,0:T(8,128)(2,1)S(1)}, u32[]{:S(2)}, u32[]{:S(2)}) collective-permute-start(bf16[128,768]{1,0:T(8,128)(2,1)S(1)} %slice.38), channel_id=1, source_target_pairs={{0,7},{1,0},{2,1},{3,2},{4,3},{5,4},{6,5},{7,6},{16,17},{17,18},{1... | collective-permute-start | bytes 589832 | tf_op jit(solution)/shard_map/ppermute | solution.py:53
  52.2 12.2 %collective-permute-start.5 = (bf16[128,768]{1,0:T(8,128)(2,1)S(1)}, bf16[128,768]{1,0:T(8,128)(2,1)S(1)}, u32[]{:S(2)}, u32[]{:S(2)}) collective-permute-start(bf16[128,768]{1,0:T(8,128)(2,1)S(1)} %add_convert_fusion.5), channel_id=1, source_target_pairs={{0,1},{1,2},{2,3},{3,4},{4,5},{5,6},{6,7},{7,0},{16,23},{17,16},{1... | collective-permute-start | bytes 589832 | tf_op jit(solution)/shard_map/ppermute | solution.py:53
  65.6 10.7 %collective-permute-start.6 = (bf16[128,768]{1,0:T(8,128)(2,1)S(1)}, bf16[128,768]{1,0:T(8,128)(2,1)S(1)}, u32[]{:S(2)}, u32[]{:S(2)}) collective-permute-start(bf16[128,768]{1,0:T(8,128)(2,1)S(1)} %get-tuple-element.57), channel_id=1, source_target_pairs={{0,1},{1,2},{2,3},{3,4},{4,5},{5,6},{6,7},{7,0},{16,23},{17,16},{1... | collective-permute-start | bytes 589832 | tf_op jit(solution)/shard_map/ppermute | solution.py:53
  66.1 10.3 %collective-permute-start.9 = (bf16[128,768]{1,0:T(8,128)(2,1)S(1)}, bf16[128,768]{1,0:T(8,128)(2,1)}, u32[]{:S(2)}, u32[]{:S(2)}) collective-permute-start(bf16[128,768]{1,0:T(8,128)(2,1)S(1)} %get-tuple-element.58), channel_id=1, source_target_pairs={{0,7},{1,0},{2,1},{3,2},{4,3},{5,4},{6,5},{7,6},{16,17},{17,18},{1... | collective-permute-start | bytes 589832 | tf_op jit(solution)/shard_map/ppermute | solution.py:53
  78.4 5.9 %collective-permute-start.10 = (bf16[128,768]{1,0:T(8,128)(2,1)}, bf16[128,768]{1,0:T(8,128)(2,1)S(1)}, u32[]{:S(2)}, u32[]{:S(2)}) collective-permute-start(bf16[128,768]{1,0:T(8,128)(2,1)} %get-tuple-element.56), channel_id=1, source_target_pairs={{0,7},{1,0},{2,1},{3,2},{4,3},{5,4},{6,5},{7,6},{16,17},{17,18},{1... | collective-permute-start | bytes 589832 | tf_op jit(solution)/shard_map/ppermute | solution.py:53
  78.4 7.0 %collective-permute-start.7 = (bf16[128,768]{1,0:T(8,128)(2,1)}, bf16[128,768]{1,0:T(8,128)(2,1)}, u32[]{:S(2)}, u32[]{:S(2)}) collective-permute-start(bf16[128,768]{1,0:T(8,128)(2,1)} %get-tuple-element.55), channel_id=1, source_target_pairs={{0,1},{1,2},{2,3},{3,4},{4,5},{5,6},{6,7},{7,0},{16,23},{17,16},{1... | collective-permute-start | bytes 589832 | tf_op jit(solution)/shard_map/ppermute | solution.py:53
  86.7 6.1 %collective-permute-start.11 = (bf16[128,768]{1,0:T(8,128)(2,1)S(1)}, bf16[128,768]{1,0:T(8,128)(2,1)S(1)}, u32[]{:S(2)}, u32[]{:S(2)}) collective-permute-start(bf16[128,768]{1,0:T(8,128)(2,1)S(1)} %multiply_convert_fusion.1), channel_id=1, source_target_pairs={{0,8},{8,0},{1,9},{9,1},{2,10},{10,2},{3,11},{11,3},{4,12},{12,4},... | collective-permute-start | bytes 589832 | tf_op jit(solution)/shard_map/ppermute | solution.py:47
  95.8 6.1 %collective-permute-start.12 = (bf16[128,768]{1,0:T(8,128)(2,1)S(1)}, bf16[128,768]{1,0:T(8,128)(2,1)S(1)}, u32[]{:S(2)}, u32[]{:S(2)}) collective-permute-start(bf16[128,768]{1,0:T(8,128)(2,1)S(1)} %slice.62), channel_id=1, source_target_pairs={{0,8},{8,0},{1,9},{9,1},{2,10},{10,2},{3,11},{11,3},{4,12},{12,4},... | collective-permute-start | bytes 589832 | tf_op jit(solution)/shard_map/ppermute | solution.py:47
  102.3 9.2 %collective-permute-start.13 = (bf16[128,768]{1,0:T(8,128)(2,1)S(1)}, bf16[128,768]{1,0:T(8,128)(2,1)S(1)}, u32[]{:S(2)}, u32[]{:S(2)}) collective-permute-start(bf16[128,768]{1,0:T(8,128)(2,1)S(1)} %multiply_convert_fusion.refs_0_), channel_id=1, source_target_pairs={{0,1},{1,2},{2,3},{3,4},{4,5},{5,6},{6,7},{7,0},{16,23},{17,16},{1... | collective-permute-start | bytes 589832 | tf_op jit(solution)/shard_map/ppermute | solution.py:53
  108.8 6.9 %collective-permute-start.15 = (bf16[128,768]{1,0:T(8,128)(2,1)S(1)}, bf16[128,768]{1,0:T(8,128)(2,1)S(1)}, u32[]{:S(2)}, u32[]{:S(2)}) collective-permute-start(bf16[128,768]{1,0:T(8,128)(2,1)S(1)} %multiply_convert_fusion.refs_0_), channel_id=1, source_target_pairs={{0,7},{1,0},{2,1},{3,2},{4,3},{5,4},{6,5},{7,6},{16,17},{17,18},{1... | collective-permute-start | bytes 589832 | tf_op jit(solution)/shard_map/ppermute | solution.py:53
  111.5 6.1 %collective-permute-start.14 = (bf16[128,768]{1,0:T(8,128)(2,1)S(1)}, bf16[128,768]{1,0:T(8,128)(2,1)S(1)}, u32[]{:S(2)}, u32[]{:S(2)}) collective-permute-start(bf16[128,768]{1,0:T(8,128)(2,1)S(1)} %collective-permute-done.13.refs_2_), channel_id=1, source_target_pairs={{0,1},{1,2},{2,3},{3,4},{4,5},{5,6},{6,7},{7,0},{16,23},{17,16},{1... | collective-permute-start | bytes 589832 | tf_op jit(solution)/shard_map/ppermute | solution.py:53
  115.7 7.9 %collective-permute-start.16 = (bf16[128,768]{1,0:T(8,128)(2,1)S(1)}, bf16[128,768]{1,0:T(8,128)(2,1)S(1)}, u32[]{:S(2)}, u32[]{:S(2)}) collective-permute-start(bf16[128,768]{1,0:T(8,128)(2,1)S(1)} %collective-permute-done.15.refs_1_), channel_id=1, source_target_pairs={{0,7},{1,0},{2,1},{3,2},{4,3},{5,4},{6,5},{7,6},{16,17},{17,18},{1... | collective-permute-start | bytes 589832 | tf_op jit(solution)/shard_map/ppermute | solution.py:53
  123.7 9.9 %collective-permute-start.17 = (bf16[128,768]{1,0:T(8,128)(2,1)S(1)}, bf16[128,768]{1,0:T(8,128)(2,1)S(1)}, u32[]{:S(2)}, u32[]{:S(2)}) collective-permute-start(bf16[128,768]{1,0:T(8,128)(2,1)S(1)} %collective-permute-done.14.refs_4_), channel_id=1, source_target_pairs={{0,1},{1,2},{2,3},{3,4},{4,5},{5,6},{6,7},{7,0},{16,23},{17,16},{1... | collective-permute-start | bytes 589832 | tf_op jit(solution)/shard_map/ppermute | solution.py:53
  123.7 9.9 %collective-permute-start.18 = (bf16[128,768]{1,0:T(8,128)(2,1)S(1)}, bf16[128,768]{1,0:T(8,128)(2,1)S(1)}, u32[]{:S(2)}, u32[]{:S(2)}) collective-permute-start(bf16[128,768]{1,0:T(8,128)(2,1)S(1)} %collective-permute-done.16.refs_3_), channel_id=1, source_target_pairs={{0,7},{1,0},{2,1},{3,2},{4,3},{5,4},{6,5},{7,6},{16,17},{17,18},{1... | collective-permute-start | bytes 589832 | tf_op jit(solution)/shard_map/ppermute | solution.py:53
  133.6 4.6 %collective-permute-start.19 = (bf16[128,768]{1,0:T(8,128)(2,1)S(1)}, bf16[128,768]{1,0:T(8,128)(2,1)S(1)}, u32[]{:S(2)}, u32[]{:S(2)}) collective-permute-start(bf16[128,768]{1,0:T(8,128)(2,1)S(1)} %collective-permute-done.17.refs_1_), channel_id=1, source_target_pairs={{0,1},{1,2},{2,3},{3,4},{4,5},{5,6},{6,7},{7,0},{16,23},{17,16},{1... | collective-permute-start | bytes 589832 | tf_op jit(solution)/shard_map/ppermute | solution.py:53
  150.1 8.3 %collective-permute-start.20 = (bf16[16,80,640]{2,1,0:T(8,128)(2,1)}, bf16[16,80,640]{2,1,0:T(8,128)(2,1)S(1)}, u32[]{:S(2)}, u32[]{:S(2)}) collective-permute-start(bf16[16,80,640]{2,1,0:T(8,128)(2,1)} %get-tuple-element.51), channel_id=1, source_target_pairs={{0,16},{16,0},{1,17},{17,1},{2,18},{18,2},{3,19},{19,3},{4,20},{20... | collective-permute-start | bytes 4915208 | tf_op jit(solution)/shard_map/ppermute | solution.py:47
  161.5 32.1 %all-to-all-start = ((bf16[16,80,640]{2,1,0:T(8,128)(2,1)}), bf16[16,80,640]{2,1,0:T(8,128)(2,1)S(1)}, u32[]{:S(2)}, u32[]{:S(2)}) async-start(bf16[16,80,640]{2,1,0:T(8,128)(2,1)} %add_convert_fusion), calls=%async_computation | async-start | bytes 3276800 | tf_op jit(solution)/shard_map/all_to_all | solution.py:284
  (15 other events, 122.7 us)
Sparse Core Ops, SparseCore 0:
  32.5 42.9 all-gather.1
  135.6 35.8 reduce-scatter.1

commit v6 on v4

v6 whole, which is shorter than its diff:
```python
import functools

import jax
import jax.numpy as jnp
from jax import lax
from jax.experimental import pallas as pl
from jax.experimental.pallas import tpu as pltpu
from jax.sharding import Mesh, PartitionSpec as P

logit_scale = 8.0
logit_bias = -3.0
epsilon = 1e-06
gelu_root = 0.7978845608028654
gelu_cubic = 0.044715

AUDIO = ("ylo", "x", "core")
SCORE = ("yhi", "z")
RING = 8
VMEM_BYTES = 56 * 1024 * 1024
f32 = jnp.float32
bf16 = jnp.bfloat16


def dot(left, right, dims=((1,), (0,))):
    return lax.dot_general(left, right, (dims, ((), ())), preferred_element_type=f32)


def unit_rows(values):
    wide = values.astype(f32)
    inverse = lax.rsqrt(jnp.sum(wide * wide, axis=-1, keepdims=True) + epsilon)
    return (wide * inverse, inverse)


def unit_backward(unit_wide, inverse, grad_unit):
    inner = jnp.sum(unit_wide * grad_unit, axis=-1, keepdims=True)
    return inverse * (grad_unit - unit_wide * inner)


def pair_coeffs(left, right, partner, first_column):
    logits = logit_scale * dot(left, right, ((1,), (1,))) + logit_bias
    columns = first_column + lax.iota(jnp.int32, right.shape[0])
    sign = jnp.where(partner[:, None] == columns[None, :], 1.0, -1.0)
    return (-logit_scale * sign * jax.nn.sigmoid(-sign * logits)).astype(bf16)


def swap(value, axis):
    return lax.ppermute(value, axis, [(0, 1), (1, 0)])


def shift(value, step):
    perm = [(i, (i + step) % RING) for i in range(RING)]
    perm += [(RING + i, RING + (i - step) % RING) for i in range(RING)]
    return lax.ppermute(value, ("core", "z"), perm)


GROUPS = (
    (((1, 4),), ((1, 3), (1, -3)), ((0, 4),)),
    (((1, 2), (1, -2)), ((0, 3), (0, -3))),
    (((1, 1), (1, -1), (1, 0)), ((0, 2), (0, -2))),
    (((0, 1), (0, -1), (0, 0)),),
)
MEMBERS = tuple(tuple(block for piece in group for block in piece) for group in GROUPS)
BLOCKS = tuple(block for members in MEMBERS for block in members)


def block_index(half, place, direction):
    halves = jnp.array([block[0] for block in BLOCKS], jnp.int32)
    offsets = jnp.array([block[1] for block in BLOCKS], jnp.int32)
    return lax.rem(half + halves, 2) * RING + lax.rem(place + direction * offsets + RING, RING)


def forward_kernel(pieces, first, index_ref, *refs):
    count = sum(pieces)
    hidden = [ref[...] for ref in refs[:count]]
    refs = refs[count:]
    if first:
        up_ref, down_ref, head_ref = refs[:3]
        down_head_ref = refs[-1]
        down_head_ref[...] = dot(down_ref[...], head_ref[...]).astype(bf16)
        refs = refs[3:-1]
    else:
        up_ref, down_head_ref = refs[:2]
        refs = refs[2:]
    part_refs = refs[: len(pieces)]
    normed_t_ref, act_t_ref, slope_ref = refs[len(pieces) :]
    rows = hidden[0].shape[0]
    wide = jnp.concatenate(hidden, axis=0).astype(f32)
    square_mean = jnp.mean(wide * wide, axis=-1, keepdims=True)
    normed = (wide * lax.rsqrt(square_mean + epsilon)).astype(bf16)
    pre = dot(normed, up_ref[...], ((1,), (1,)))
    tangent = jnp.tanh(gelu_root * (pre + gelu_cubic * (pre * pre * pre)))
    act = (0.5 * pre * (1.0 + tangent)).astype(bf16)
    part = dot(act, down_head_ref[...]).astype(bf16)
    at = 0
    for size, part_ref in zip(pieces, part_refs):
        part_ref[...] = part[at * rows : (at + size) * rows, :]
        at += size
    slope = 0.5 * (1.0 + tangent) + 0.5 * pre * (1.0 - tangent * tangent) * gelu_root * (
        1.0 + 3.0 * gelu_cubic * pre * pre
    )
    slope = slope.astype(bf16)
    normed_t, act_t = normed.T, act.T
    for i in range(count):
        span = slice(i * rows, (i + 1) * rows)
        slope_ref[i] = slope[span, :]
        normed_t_ref[i] = normed_t[:, span]
        act_t_ref[i] = act_t[:, span]


def forward_blocks(group, index, hidden_in, up_t, *weights):
    pieces = tuple(len(piece) for piece in GROUPS[group])
    count = sum(pieces)
    start = sum(len(members) for members in MEMBERS[:group])
    first = len(weights) == 2
    rows = hidden_in.shape[0] // (2 * RING)
    ff, width = up_t.shape
    embed = weights[-1].shape[1]
    flat = lambda i, index: (0, 0)
    cube = lambda i, index: (0, 0, 0)
    shapes = [jax.ShapeDtypeStruct((size * rows, embed), bf16) for size in pieces]
    shapes += [jax.ShapeDtypeStruct((count,) + dims, bf16) for dims in ((width, rows), (ff, rows), (rows, ff))]
    shapes += [jax.ShapeDtypeStruct((ff, embed), bf16)] if first else []
    out = pl.pallas_call(
        functools.partial(forward_kernel, pieces, first),
        grid_spec=pltpu.PrefetchScalarGridSpec(
            num_scalar_prefetch=1,
            grid=(1,),
            in_specs=[
                pl.BlockSpec((rows, width), lambda i, index, at=start + at: (index[at], 0)) for at in range(count)
            ]
            + [pl.BlockSpec(w.shape, flat) for w in (up_t,) + weights],
            out_specs=[pl.BlockSpec(shape.shape, cube if len(shape.shape) == 3 else flat) for shape in shapes],
        ),
        out_shape=shapes,
        compiler_params=pltpu.CompilerParams(vmem_limit_bytes=VMEM_BYTES),
        cost_estimate=pl.CostEstimate(
            flops=2 * count * rows * ff * (width + embed),
            bytes_accessed=2 * count * rows * (2 * width + embed + 2 * ff) + 2 * ff * (width + embed),
            transcendentals=count * rows * ff,
        ),
    )(index, *([hidden_in] * count), up_t, *weights)
    parts, kept = out[: len(pieces)], out[len(pieces) : len(pieces) + 3]
    return parts, kept, out[-1]


def backward_kernel(count, blocks, first, last, *refs):
    join = lambda parts, axis: jnp.concatenate(parts, axis=axis) if len(parts) > 1 else parts[0]
    grad = join([ref[...] for ref in refs[:count]], 0)
    kept = refs[count : count + 3 * blocks]
    normed_t, act_t, slope = (join([ref[0] for ref in kept[i::3]], axis) for i, axis in ((0, 1), (1, 1), (2, 0)))
    refs = refs[count + 3 * blocks :]
    down_head_ref, refs = refs[0], refs[1:]
    if not first:
        up_in, act_in = refs[:2]
        refs = refs[2:]
    if last:
        core_ref, head_ref, keep_ref, give_ref, up_acc = refs
    else:
        up_acc, act_acc = refs
    tile = 256
    width, ff = up_acc.shape
    grad_act = dot(grad, down_head_ref[...], ((1,), (1,)))
    grad_pre = (grad_act * slope.astype(f32)).astype(bf16)
    act_sum = dot(act_t, grad)
    if not first:
        act_sum = act_sum + act_in[...]
    if not last:
        act_acc[...] = act_sum
    for m in range(0, width, tile):
        up_sum = dot(normed_t[m : m + tile, :], grad_pre)
        if not first:
            up_sum = up_sum + up_in[m : m + tile, :]
        up_acc[m : m + tile, :] = up_sum
    if last:
        core = core_ref[0]
        act_grad = act_sum.astype(bf16)
        rows = keep_ref.shape[1]
        for side in range(2):
            for half, out_ref in ((core, keep_ref), (1 - core, give_ref)):
                for chip in range(keep_ref.shape[0]):
                    at = pl.multiple_of((2 * chip + half) * rows, rows)
                    out_ref[chip, :, side * ff : (side + 1) * ff] = up_acc[pl.ds(at, rows), :].astype(bf16)
            if side == 0:
                for m in range(0, width, tile):
                    up_acc[m : m + tile, :] = dot(head_ref[m : m + tile, :], act_grad, ((1,), (1,)))


def backward_blocks(items, down_head, sums, last=None):
    whole = pl.BlockSpec(memory_space=pltpu.VMEM)
    args = [grad for grad, _ in items]
    specs = [whole] * len(items)
    places = [place for _, blocks in items for place in blocks]
    for kept, at in places:
        for array in kept:
            args.append(array)
            specs.append(pl.BlockSpec((1,) + array.shape[1:], lambda i, at=at: (at, 0, 0)))
    ff, embed = down_head.shape
    rows, width = sum(grad.shape[0] for grad, _ in items), places[0][0][0].shape[1]
    args.append(down_head)
    specs.append(whole)
    aliases = {}
    if sums is not None:
        if last is None:
            aliases = {len(args): 0, len(args) + 1: 1}
        args += list(sums)
        specs += [whole] * 2
    flops = 2 * rows * ff * (2 * embed + width)
    if last is None:
        shapes = [jax.ShapeDtypeStruct((width, ff), f32), jax.ShapeDtypeStruct((ff, embed), f32)]
        scratch = []
    else:
        args += list(last)
        specs += [pl.BlockSpec(memory_space=pltpu.SMEM), whole]
        shapes = [jax.ShapeDtypeStruct((8, width // 16, 2 * ff), bf16)] * 2
        scratch = [pltpu.VMEM((width, ff), f32)]
        flops += 2 * width * ff * embed
    return pl.pallas_call(
        functools.partial(backward_kernel, len(items), len(places), sums is None, last is not None),
        grid=(1,),
        in_specs=specs,
        out_specs=[whole] * 2,
        out_shape=shapes,
        scratch_shapes=scratch,
        input_output_aliases=aliases,
        compiler_params=pltpu.CompilerParams(vmem_limit_bytes=VMEM_BYTES),
        cost_estimate=pl.CostEstimate(flops=flops, bytes_accessed=8 * 1024 * 1024, transcendentals=0),
    )(*args)


def total_of(*terms):
    return sum(term.astype(f32) for term in terms)


def per_device(hidden_in, up_weight, down_weight, head_weight, score_embed, pair_index):
    y_hi, z, core = (lax.axis_index(name).astype(jnp.int32) for name in ("yhi", "z", "core"))
    rows = hidden_in.shape[0] // (2 * RING)
    group_half = RING * rows
    index = block_index(y_hi, z, 1 - 2 * core)
    up_t = up_weight.T
    saved = {}

    def forward(group, *weights):
        parts, kept, down_head = forward_blocks(group, index, hidden_in, up_t, *weights)
        for at, block in enumerate(MEMBERS[group]):
            saved[block] = (kept, at)
        return parts, down_head

    (other4, other3, own4), down_head = forward(0, down_weight, head_weight)
    came4, came3 = swap(other4, "yhi"), swap(other3, "yhi")
    score_wide, score_inverse = unit_rows(score_embed)
    score_unit, up_t = lax.optimization_barrier((score_wide.astype(bf16), up_t))
    score_half = lax.all_gather(score_unit, "z", axis=0, tiled=True)
    (other2, own3), _ = forward(1, down_head)
    came2 = swap(other2, "yhi")
    fore = shift(total_of(own4, came4).astype(bf16), 1)
    (other1, own2), _ = forward(2, down_head)
    came1 = swap(other1, "yhi")
    fore = shift(total_of(own3[:rows], came3[:rows], fore).astype(bf16), 1)
    back = shift(total_of(own3[rows:], came3[rows:]).astype(bf16), -1)
    (own1,), _ = forward(3, down_head)
    for own, came in ((own2, came2), (own1, came1)):
        fore = shift(total_of(own[:rows], came[:rows], fore).astype(bf16), 1)
        back = shift(total_of(own[rows : 2 * rows], came[rows : 2 * rows], back).astype(bf16), -1)
    own_start = y_hi * group_half + z * rows
    own_hidden = lax.dynamic_slice_in_dim(hidden_in, own_start, rows, 0)
    own_proj = dot(own_hidden, head_weight)
    audio_wide, audio_inverse = unit_rows(own_proj + total_of(own1[2 * rows :], came1[2 * rows :], fore, back))
    audio_own = audio_wide.astype(bf16)
    audio_unit = jnp.concatenate([audio_own, swap(audio_own, "yhi")], axis=0)
    far_start = (1 - y_hi) * group_half + z * rows
    partners = jnp.concatenate(
        [lax.dynamic_slice_in_dim(pair_index[0], start, rows, 0) for start in (own_start, far_start)]
    )
    coeffs = pair_coeffs(audio_unit, score_half, partners, y_hi * group_half)
    grad_audio = dot(coeffs, score_half)
    grad_audio = grad_audio[:rows] + swap(grad_audio[rows:].astype(bf16), "yhi").astype(f32)
    grad_embed = unit_backward(audio_wide, audio_inverse, grad_audio).astype(bf16)
    score_part = dot(coeffs, audio_unit, ((0,), (0,))).astype(bf16)
    item = lambda grad, *blocks: (grad, [saved[block] for block in blocks])
    pair = lambda step, half: ((half, step), (half, -step))
    both = lambda up, down: jnp.concatenate([up, down], axis=0)
    crossed0 = swap(grad_embed, "yhi")
    fore, back = shift(grad_embed, 1), shift(grad_embed, -1)
    fore, back, crossed0, score_part = lax.optimization_barrier((fore, back, crossed0, score_part))
    grad_score = lax.psum_scatter(score_part, "z", scatter_dimension=0, tiled=True)
    ring1 = both(back, fore)
    crossed1 = swap(ring1, "yhi")
    fore, back = shift(fore, 1), shift(back, -1)
    ring2 = both(back, fore)
    crossed2 = swap(ring2, "yhi")
    fore, back = shift(fore, 1), shift(back, -1)
    items = [item(grad_embed, (0, 0)), item(crossed0, (1, 0)), item(ring1, *pair(1, 0)), item(crossed1, *pair(1, 1))]
    sums = backward_blocks(items + [item(ring2, *pair(2, 0))], down_head, None)
    fore, back, sums = lax.optimization_barrier((fore, back, sums))
    ring3 = both(back, fore)
    crossed3 = swap(ring3, "yhi")
    ring4 = shift(fore, 1)
    crossed4 = swap(ring4, "yhi")
    items = [item(ring3, *pair(3, 0)), item(crossed2, *pair(2, 1)), item(ring4, (0, 4))]
    sums = backward_blocks(items, down_head, sums)
    crossed4, sums = lax.optimization_barrier((crossed4, sums))
    items = [item(crossed3, *pair(3, 1)), item(crossed4, (1, 4))]
    keep, give = backward_blocks(items, down_head, sums, (core[None], head_weight))
    chip = total_of(keep, swap(give, "core")).astype(bf16)
    landed = lax.all_to_all(chip, ("ylo", "x"), 0, 0)
    total = jnp.sum(landed.astype(f32), axis=0)
    ff = up_weight.shape[1]
    score_grad = unit_backward(score_wide, score_inverse, grad_score.astype(f32))
    return (total[:, :ff], total[:, ff:].T, score_grad)


def solution(mesh):
    fine = Mesh(mesh.devices.reshape(2, 4, 2, 2, RING), ("ylo", "x", "core", "yhi", "z"))
    in_specs = (
        P(AUDIO, None),
        P(None, SCORE),
        P(SCORE, None),
        P(),
        P(AUDIO + SCORE, None),
        P(AUDIO, None),
    )
    out_specs = (P(AUDIO, SCORE), P(SCORE, AUDIO), P(AUDIO + SCORE, None))
    return jax.shard_map(
        per_device, mesh=fine, in_specs=in_specs, out_specs=out_specs, check_vma=False
    )
```

time: 194 us -> 188 us (0.969)
  waiting for transfers between devices: 60.5 us -> 37.4 us
  starting transfers between devices: 31.1 us -> 51.4 us
  Pallas kernels: 48 us -> 44.1 us
    ppermute x14, waiting for transfers between devices: 43.1 us -> 20.8 us  [shift(): return lax.ppermute(value, ('core', 'z'), perm)]
    ppermute x3 -> x12, starting transfers between devices: 9.91 us -> 30.6 us  [swap(): return lax.ppermute(value, axis, [(0, 1), (1, 0)])]
    pallas_call x9 -> x7, Pallas kernels: 48 us -> 44.1 us  [the longest x4 23.6 us: forward_blocks(): pl.pallas_call(functools.partial(forward_kernel, pieces, first), grid_spe...]
    ppermute x3 -> x12, waiting for transfers between devices: 17.4 us -> 16.5 us  [swap(): return lax.ppermute(value, axis, [(0, 1), (1, 0)])]
    convert_element_type x4 -> x5, other arithmetic: 4.98 us -> 4.55 us  [the longest x2 2.33 us: per_device(): fore = shift(total_of(own[:rows], came[:rows], fore).astype(bf16), 1)]
  transfers between devices with their start and end apart: 19 -> 28, of which waited for: 13 -> 16; matrix products, arithmetic and copies ran while one was open for 7% -> 7% of each run, Pallas kernels for 22% -> 20%
where the time goes in v6:
time: 188 us; the launch traced here: 187 us
  starting transfers between devices  51.4 us (27%)
  Pallas kernels  44.1 us (23%)
  waiting for transfers between devices  37.4 us (20%)
  blocking collectives  17.4 us (9%)
  between operations  14.3 us (8%)
  other arithmetic  12.7 us (7%)
  matrix products  6.14 us (3%)
  local copies, waits for them, and re-layouts  3.86 us (2%)
    ppermute x12, starting transfers between devices, swap(): return lax.ppermute(value, axis, [(0, 1), (1, 0)])  30.6 us
    pallas_call x4, Pallas kernels, forward_blocks(): pl.pallas_call(functools.partial(forward_kernel, pieces, first), grid_spe...  23.6 us
    ppermute x14, waiting for transfers between devices, shift(): return lax.ppermute(value, ('core', 'z'), perm)  20.8 us
    ppermute x14, starting transfers between devices, shift(): return lax.ppermute(value, ('core', 'z'), perm)  20.7 us
    pallas_call x3, Pallas kernels, backward_blocks(): pl.pallas_call(functools.partial(backward_kernel, len(items), len(places)...  20.5 us
    all_to_all x1, blocking collectives, per_device(): landed = lax.all_to_all(chip, ('ylo', 'x'), 0, 0)  17.4 us
    ppermute x12, waiting for transfers between devices, swap(): return lax.ppermute(value, axis, [(0, 1), (1, 0)])  16.5 us
    dot_general x4, matrix products, dot(): lax.dot_general(left, right, (dims, ((), ())), preferred_element_type=f32)  6.14 us
  transfers between devices with their start and end apart: 28, of which 16 were waited for; matrix products, arithmetic and copies ran while one was open for 7% of the time, Pallas kernels for 20%

profile of v6, /device:TPU:1, one launch (start us, length us, event | category | flops | bytes accessed | tf_op | source)
XLA Modules:
  0.0 187.3 jit_solution(4083802416620337861)
XLA Ops:
  8.4 6.7 %shard_map.103 = (bf16[128,768]{1,0:T(8,128)(2,1)}, bf16[256,768]{1,0:T(8,128)(2,1)}, bf16[128,768]{1,0:T(8,128)(2,1)}, bf16[4,1280,128]{2,1,0:T(8,128)(2,1)}, b...) custom-call(s32[16]{0:T(128)} %fusion.18.index_ref, ...), custom_call_target="tpu_custom_call" | custom-call | flops 671088640 | bytes 5373952 | tf_op jit(solution)/shard_map/pallas_call | solution.py:123
  15.1 3.7 %collective-permute-start.3 = (bf16[128,768]{1,0:T(8,128)(2,1)}, bf16[128,768]{1,0:T(8,128)(2,1)S(1)}, u32[]{:S(2)}, u32[]{:S(2)}) collective-permute-start(bf16[128,768]{1,0:T(8,128)(2,1)} %get-tuple-element.52), channel_id=1, source_target_pairs={{0,8},{8,0},{1,9},{9,1},{2,10},{10,2},{3,11},{11,3},{4,12},{12,4},... | collective-permute-start | bytes 589832 | tf_op jit(solution)/shard_map/ppermute | solution.py:47
  20.0 2.8 %collective-permute-done.3 = bf16[128,768]{1,0:T(8,128)(2,1)S(1)} collective-permute-done((bf16[128,768]{1,0:T(8,128)(2,1)}, bf16[128,768]{1,0:T(8,128)(2,1)S(1)}, u32[]{:S(2)}, u32[]{:S(2)}) %collective-permute-start.3) | collective-permute-done | bytes 196640 | tf_op jit(solution)/shard_map/ppermute | solution.py:47
  23.7 6.3 %collective-permute-start.4 = (bf16[128,768]{1,0:T(8,128)(2,1)S(1)}, bf16[128,768]{1,0:T(8,128)(2,1)S(1)}, u32[]{:S(2)}, u32[]{:S(2)}) collective-permute-start(bf16[128,768]{1,0:T(8,128)(2,1)S(1)} %add_convert_fusion.7), channel_id=1, source_target_pairs={{0,1},{1,2},{2,3},{3,4},{4,5},{5,6},{6,7},{7,0},{16,23},{17,16},{1... | collective-permute-start | bytes 589832 | tf_op jit(solution)/shard_map/ppermute | solution.py:53
  30.1 5.6 %shard_map.106 = (bf16[256,768]{1,0:T(8,128)(2,1)}, bf16[256,768]{1,0:T(8,128)(2,1)}, bf16[4,1280,128]{2,1,0:T(8,128)(2,1)}, bf16[4,320,128]{2,1,0:T(8,128)(2,1)}, bf16[4,128,320]{2,1,0:T(8,128)(2,1)}) custom-call(s32[16]{0:T(128)} %fusion.18.index_ref, bf16[2048,1280]{1,0:T(8,128)(2,1)} %refs_3_.5, bf16[2048,1280]{1,0:T(8,128)(2,1)} %refs_3_.5, ...), custom_call_target="tpu_custom_call" | custom-call | flops 671088640 | bytes 5373952 | tf_op jit(solution)/shard_map/pallas_call | solution.py:123
  35.7 2.9 %collective-permute-start.1 = (bf16[256,768]{1,0:T(8,128)(2,1)}, bf16[256,768]{1,0:T(8,128)(2,1)S(1)}, u32[]{:S(2)}, u32[]{:S(2)}) collective-permute-start(bf16[256,768]{1,0:T(8,128)(2,1)} %get-tuple-element.48), channel_id=1, source_target_pairs={{0,8},{8,0},{1,9},{9,1},{2,10},{10,2},{3,11},{11,3},{4,12},{12,4},... | collective-permute-start | bytes 1179656 | tf_op jit(solution)/shard_map/ppermute | solution.py:47
  41.3 6.4 %shard_map.105 = (bf16[384,768]{1,0:T(8,128)(2,1)}, bf16[256,768]{1,0:T(8,128)(2,1)}, bf16[5,1280,128]{2,1,0:T(8,128)(2,1)}, bf16[5,320,128]{2,1,0:T(8,128)(2,1)}, bf16[5,128,320]{2,1,0:T(8,128)(2,1)}) custom-call(s32[16]{0:T(128)} %fusion.18.index_ref, bf16[2048,1280]{1,0:T(8,128)(2,1)} %refs_3_.5, bf16[2048,1280]{1,0:T(8,128)(2,1)} %refs_3_.5, ...), custom_call_target="tpu_custom_call" | custom-call | flops 838860800 | bytes 6389760 | tf_op jit(solution)/shard_map/pallas_call | solution.py:123
  49.4 3.1 %collective-permute-done.8 = bf16[128,768]{1,0:T(8,128)(2,1)S(1)} collective-permute-done((bf16[128,768]{1,0:T(8,128)(2,1)S(1)}, bf16[128,768]{1,0:T(8,128)(2,1)S(1)}, u32[]{:S(2)}, u32[]{:S(2)}) %collective-permute-start.8) | collective-permute-done | bytes 196640 | tf_op jit(solution)/shard_map/ppermute | solution.py:53
  55.2 4.9 %shard_map.104 = (bf16[384,768]{1,0:T(8,128)(2,1)}, bf16[3,1280,128]{2,1,0:T(8,128)(2,1)}, bf16[3,320,128]{2,1,0:T(8,128)(2,1)}, bf16[3,128,320]{2,1,0:T(8,128)(2,1)}) custom-call(s32[16]{0:T(128)} %fusion.18.index_ref, bf16[2048,1280]{1,0:T(8,128)(2,1)} %refs_3_.5, bf16[2048,1280]{1,0:T(8,128)(2,1)} %refs_3_.5, bf16[2048,1280]{1,0:T(8,128)(2,1)} %refs_3_.5, ...), custom_call_target="tpu_custom_call" | custom-call | flops 503316480 | bytes 4358144 | tf_op jit(solution)/shard_map/pallas_call | solution.py:123
  69.1 3.6 %collective-permute-done.10 = bf16[128,768]{1,0:T(8,128)(2,1)S(1)} collective-permute-done((bf16[128,768]{1,0:T(8,128)(2,1)S(1)}, bf16[128,768]{1,0:T(8,128)(2,1)S(1)}, u32[]{:S(2)}, u32[]{:S(2)}) %collective-permute-start.10) | collective-permute-done | bytes 196640 | tf_op jit(solution)/shard_map/ppermute | solution.py:53
  76.2 4.2 %collective-permute-done.11 = bf16[128,768]{1,0:T(8,128)(2,1)S(1)} collective-permute-done((bf16[128,768]{1,0:T(8,128)(2,1)S(1)}, bf16[128,768]{1,0:T(8,128)(2,1)S(1)}, u32[]{:S(2)}, u32[]{:S(2)}) %collective-permute-start.11) | collective-permute-done | bytes 196640 | tf_op jit(solution)/shard_map/ppermute | solution.py:47
  80.5 2.3 %fusion.7 = bf16[256,1024]{1,0:T(8,128)(2,1)S(1)} fusion(bf16[1024,768]{1,0:T(8,128)(2,1)} %all-gather.2.cloned.1.call-done, s32[1024]{0:T(1024)S(1)} %iota_add_fusion, s32[256]{0:T(256)S(1)} %pad_add_fusion, bf16[128,768]{1,0:T(8,128)(2,1)S(1)} %collective-permute-done.11, bf16[128,768]{1,0:T(8,128)(2,1)S(1)} %multiply_convert_fusion.1), kind=kOutput, calls=%fused_computation.13 | convolution fusion | flops 406585344 | bytes 2495488 | tf_op jit(solution)/shard_map/dot_general | solution.py:25
  83.4 2.5 %collective-permute-start.12 = (bf16[128,768]{1,0:T(8,128)(2,1)S(1)}, bf16[128,768]{1,0:T(8,128)(2,1)S(1)}, u32[]{:S(2)}, u32[]{:S(2)}) collective-permute-start(bf16[128,768]{1,0:T(8,128)(2,1)S(1)} %slice.105), channel_id=1, source_target_pairs={{0,8},{8,0},{1,9},{9,1},{2,10},{10,2},{3,11},{11,3},{4,12},{12,4},... | collective-permute-start | bytes 589832 | tf_op jit(solution)/shard_map/ppermute | solution.py:47
  86.0 3.6 %collective-permute-done.12 = bf16[128,768]{1,0:T(8,128)(2,1)S(1)} collective-permute-done((bf16[128,768]{1,0:T(8,128)(2,1)S(1)}, bf16[128,768]{1,0:T(8,128)(2,1)S(1)}, u32[]{:S(2)}, u32[]{:S(2)}) %collective-permute-start.12) | collective-permute-done | bytes 196640 | tf_op jit(solution)/shard_map/ppermute | solution.py:47
  89.9 2.5 %collective-permute-start.15 = (bf16[128,768]{1,0:T(8,128)(2,1)S(1)}, bf16[128,768]{1,0:T(8,128)(2,1)S(1)}, u32[]{:S(2)}, u32[]{:S(2)}) collective-permute-start(bf16[128,768]{1,0:T(8,128)(2,1)S(1)} %multiply_convert_fusion.refs_0_), channel_id=1, source_target_pairs={{0,8},{8,0},{1,9},{9,1},{2,10},{10,2},{3,11},{11,3},{4,12},{12,4},... | collective-permute-start | bytes 589832 | tf_op jit(solution)/shard_map/ppermute | solution.py:47
  99.1 2.7 %collective-permute-start.16 = (bf16[128,768]{1,0:T(8,128)(2,1)S(1)}, bf16[128,768]{1,0:T(8,128)(2,1)S(1)}, u32[]{:S(2)}, u32[]{:S(2)}) collective-permute-start(bf16[128,768]{1,0:T(8,128)(2,1)S(1)} %collective-permute-done.13), channel_id=1, source_target_pairs={{0,1},{1,2},{2,3},{3,4},{4,5},{5,6},{6,7},{7,0},{16,23},{17,16},{1... | collective-permute-start | bytes 589832 | tf_op jit(solution)/shard_map/ppermute | solution.py:53
  102.0 2.5 %collective-permute-done.16 = bf16[128,768]{1,0:T(8,128)(2,1)S(1)} collective-permute-done((bf16[128,768]{1,0:T(8,128)(2,1)S(1)}, bf16[128,768]{1,0:T(8,128)(2,1)S(1)}, u32[]{:S(2)}, u32[]{:S(2)}) %collective-permute-start.16) | collective-permute-done | bytes 196640 | tf_op jit(solution)/shard_map/ppermute | solution.py:53
  104.5 3.1 %collective-permute-start.17 = (bf16[128,768]{1,0:T(8,128)(2,1)S(1)}, bf16[128,768]{1,0:T(8,128)(2,1)S(1)}, u32[]{:S(2)}, u32[]{:S(2)}) collective-permute-start(bf16[128,768]{1,0:T(8,128)(2,1)S(1)} %collective-permute-done.16), channel_id=1, source_target_pairs={{0,1},{1,2},{2,3},{3,4},{4,5},{5,6},{6,7},{7,0},{16,23},{17,16},{1... | collective-permute-start | bytes 589832 | tf_op jit(solution)/shard_map/ppermute | solution.py:53
  110.9 7.0 %shard_map.107 = (f32[1280,320]{1,0:T(8,128)}, f32[320,768]{1,0:T(8,128)}) custom-call(bf16[128,768]{1,0:T(8,128)(2,1)} %copy-done.6, bf16[128,768]{1,0:T(8,128)(2,1)} %copy-done.10, bf16[256,768]{1,0:T(8,128)(2,1)} %copy-done.3, bf16[256,768]{1,0:T(8,128)(2,1)} %copy-done.9, bf16[256,768]{1,0:T(8,128)(2,1)} %copy-done.5, ...), custom_call_target="tpu_custom_call" | custom-call | flops 1845493760 | bytes 8388608 | tf_op jit(solution)/shard_map/pallas_call | solution.py:217
  121.4 6.2 %collective-permute-done.22.refs_2_ = bf16[128,768]{1,0:T(8,128)(2,1)S(1)} collective-permute-done((bf16[128,768]{1,0:T(8,128)(2,1)S(1)}, bf16[128,768]{1,0:T(8,128)(2,1)S(1)}, u32[]{:S(2)}, u32[]{:S(2)}) %collective-permute-start.22) | collective-permute-done | bytes 196640 | tf_op jit(solution)/shard_map/ppermute | solution.py:53
  129.4 6.4 %shard_map.108 = (f32[1280,320]{1,0:T(8,128)}, f32[320,768]{1,0:T(8,128)}) custom-call(bf16[256,768]{1,0:T(8,128)(2,1)} %copy-done.4, bf16[256,768]{1,0:T(8,128)(2,1)} %copy-done.8, bf16[128,768]{1,0:T(8,128)(2,1)} %copy-done.11, ...), custom_call_target="tpu_custom_call", output_to_operand_aliasing={{0}: (19, {}), {1}: (20, {})} | custom-call | flops 1153433600 | bytes 8388608 | tf_op jit(solution)/shard_map/pallas_call | solution.py:217
  136.6 7.2 %shard_map.109 = (bf16[8,80,640]{2,1,0:T(8,128)(2,1)}, bf16[8,80,640]{2,1,0:T(8,128)(2,1)}) custom-call(bf16[256,768]{1,0:T(8,128)(2,1)} %copy-done.7, bf16[128,768]{1,0:T(8,128)(2,1)} %copy-done.12, bf16[4,1280,128]{2,1,0:T(8,128)(2,1)} %get-tuple-element.70.refs_15_.refs_2_.refs_5_.refs_8_, ...), custom_call_target="tpu_custom_call" | custom-call | flops 1321205760 | bytes 8388608 | tf_op jit(solution)/shard_map/pallas_call | solution.py:217
  143.8 11.9 %collective-permute-start.25 = (bf16[8,80,640]{2,1,0:T(8,128)(2,1)}, bf16[8,80,640]{2,1,0:T(8,128)(2,1)S(1)}, u32[]{:S(2)}, u32[]{:S(2)}) collective-permute-start(bf16[8,80,640]{2,1,0:T(8,128)(2,1)} %get-tuple-element.81), channel_id=1, source_target_pairs={{0,16},{16,0},{1,17},{17,1},{2,18},{18,2},{3,19},{19,3},{4,20},{20... | collective-permute-start | bytes 2457608 | tf_op jit(solution)/shard_map/ppermute | solution.py:47
  159.2 17.4 %all_to_all.5 = bf16[8,80,640]{2,1,0:T(8,128)(2,1)S(1)} all-to-all(bf16[8,80,640]{2,1,0:T(8,128)(2,1)S(1)} %add_convert_fusion), channel_id=1, replica_groups=mesh['ylo'=2,'x'=4,'core'=2,'yhi'=2,'z'=8] {'ylo','x'}, dimensions={0} | all-to-all | bytes 1638400 | tf_op jit(solution)/shard_map/all_to_all | solution.py:305
  (100 shorter events, 47.4 us)
Async XLA Ops:
  7.2 73.3 %all-gather.2.cloned.1.call-start = ((), (), s32[]{:S(2)}) async-start(), calls=%async_computation.2 | async-start | bytes 1769472 | tf_op jit(solution)/shard_map/all_gather | solution.py:252
  15.1 7.6 %collective-permute-start.3 = (bf16[128,768]{1,0:T(8,128)(2,1)}, bf16[128,768]{1,0:T(8,128)(2,1)S(1)}, u32[]{:S(2)}, u32[]{:S(2)}) collective-permute-start(bf16[128,768]{1,0:T(8,128)(2,1)} %get-tuple-element.52), channel_id=1, source_target_pairs={{0,8},{8,0},{1,9},{9,1},{2,10},{10,2},{3,11},{11,3},{4,12},{12,4},... | collective-permute-start | bytes 589832 | tf_op jit(solution)/shard_map/ppermute | solution.py:47
  19.8 157.6 %reduce-scatter.2.cloned.1.call-start = ((), (), s32[]{:S(2)}) async-start(), calls=%async_computation.3 | async-start | bytes 1769472 | tf_op jit(solution)/shard_map/reduce_scatter | solution.py:285
  19.9 18.7 %collective-permute-start.2 = (bf16[256,768]{1,0:T(8,128)(2,1)}, bf16[256,768]{1,0:T(8,128)(2,1)S(1)}, u32[]{:S(2)}, u32[]{:S(2)}) collective-permute-start(bf16[256,768]{1,0:T(8,128)(2,1)} %get-tuple-element.50), channel_id=1, source_target_pairs={{0,8},{8,0},{1,9},{9,1},{2,10},{10,2},{3,11},{11,3},{4,12},{12,4},... | collective-permute-start | bytes 1179656 | tf_op jit(solution)/shard_map/ppermute | solution.py:47
  23.7 14.9 %collective-permute-start.4 = (bf16[128,768]{1,0:T(8,128)(2,1)S(1)}, bf16[128,768]{1,0:T(8,128)(2,1)S(1)}, u32[]{:S(2)}, u32[]{:S(2)}) collective-permute-start(bf16[128,768]{1,0:T(8,128)(2,1)S(1)} %add_convert_fusion.7), channel_id=1, source_target_pairs={{0,1},{1,2},{2,3},{3,4},{4,5},{5,6},{6,7},{7,0},{16,23},{17,16},{1... | collective-permute-start | bytes 589832 | tf_op jit(solution)/shard_map/ppermute | solution.py:53
  35.7 12.4 %collective-permute-start.1 = (bf16[256,768]{1,0:T(8,128)(2,1)}, bf16[256,768]{1,0:T(8,128)(2,1)S(1)}, u32[]{:S(2)}, u32[]{:S(2)}) collective-permute-start(bf16[256,768]{1,0:T(8,128)(2,1)} %get-tuple-element.48), channel_id=1, source_target_pairs={{0,8},{8,0},{1,9},{9,1},{2,10},{10,2},{3,11},{11,3},{4,12},{12,4},... | collective-permute-start | bytes 1179656 | tf_op jit(solution)/shard_map/ppermute | solution.py:47
  39.7 9.7 %collective-permute-start.5 = (bf16[128,768]{1,0:T(8,128)(2,1)S(1)}, bf16[128,768]{1,0:T(8,128)(2,1)S(1)}, u32[]{:S(2)}, u32[]{:S(2)}) collective-permute-start(bf16[128,768]{1,0:T(8,128)(2,1)S(1)} %get-tuple-element.89), channel_id=1, source_target_pairs={{0,1},{1,2},{2,3},{3,4},{4,5},{5,6},{6,7},{7,0},{16,23},{17,16},{1... | collective-permute-start | bytes 589832 | tf_op jit(solution)/shard_map/ppermute | solution.py:53
  40.6 11.9 %collective-permute-start.8 = (bf16[128,768]{1,0:T(8,128)(2,1)S(1)}, bf16[128,768]{1,0:T(8,128)(2,1)S(1)}, u32[]{:S(2)}, u32[]{:S(2)}) collective-permute-start(bf16[128,768]{1,0:T(8,128)(2,1)S(1)} %get-tuple-element.90), channel_id=1, source_target_pairs={{0,7},{1,0},{2,1},{3,2},{4,3},{5,4},{6,5},{7,6},{16,17},{17,18},{1... | collective-permute-start | bytes 589832 | tf_op jit(solution)/shard_map/ppermute | solution.py:53
  47.7 14.7 %collective-permute-start = (bf16[384,768]{1,0:T(8,128)(2,1)}, bf16[384,768]{1,0:T(8,128)(2,1)S(1)}, u32[]{:S(2)}, u32[]{:S(2)}) collective-permute-start(bf16[384,768]{1,0:T(8,128)(2,1)} %get-tuple-element.46), channel_id=1, source_target_pairs={{0,8},{8,0},{1,9},{9,1},{2,10},{10,2},{3,11},{11,3},{4,12},{12,4},... | collective-permute-start | bytes 1769480 | tf_op jit(solution)/shard_map/ppermute | solution.py:47
  53.6 9.1 %collective-permute-start.6 = (bf16[128,768]{1,0:T(8,128)(2,1)S(1)}, bf16[128,768]{1,0:T(8,128)(2,1)S(1)}, u32[]{:S(2)}, u32[]{:S(2)}) collective-permute-start(bf16[128,768]{1,0:T(8,128)(2,1)S(1)} %get-tuple-element.87), channel_id=1, source_target_pairs={{0,1},{1,2},{2,3},{3,4},{4,5},{5,6},{6,7},{7,0},{16,23},{17,16},{1... | collective-permute-start | bytes 589832 | tf_op jit(solution)/shard_map/ppermute | solution.py:53
  53.7 9.6 %collective-permute-start.9 = (bf16[128,768]{1,0:T(8,128)(2,1)S(1)}, bf16[128,768]{1,0:T(8,128)(2,1)S(1)}, u32[]{:S(2)}, u32[]{:S(2)}) collective-permute-start(bf16[128,768]{1,0:T(8,128)(2,1)S(1)} %get-tuple-element.88), channel_id=1, source_target_pairs={{0,7},{1,0},{2,1},{3,2},{4,3},{5,4},{6,5},{7,6},{16,17},{17,18},{1... | collective-permute-start | bytes 589832 | tf_op jit(solution)/shard_map/ppermute | solution.py:53
  65.7 7.0 %collective-permute-start.10 = (bf16[128,768]{1,0:T(8,128)(2,1)S(1)}, bf16[128,768]{1,0:T(8,128)(2,1)S(1)}, u32[]{:S(2)}, u32[]{:S(2)}) collective-permute-start(bf16[128,768]{1,0:T(8,128)(2,1)S(1)} %get-tuple-element.86), channel_id=1, source_target_pairs={{0,7},{1,0},{2,1},{3,2},{4,3},{5,4},{6,5},{7,6},{16,17},{17,18},{1... | collective-permute-start | bytes 589832 | tf_op jit(solution)/shard_map/ppermute | solution.py:53
  74.0 6.5 %collective-permute-start.11 = (bf16[128,768]{1,0:T(8,128)(2,1)S(1)}, bf16[128,768]{1,0:T(8,128)(2,1)S(1)}, u32[]{:S(2)}, u32[]{:S(2)}) collective-permute-start(bf16[128,768]{1,0:T(8,128)(2,1)S(1)} %multiply_convert_fusion.1), channel_id=1, source_target_pairs={{0,8},{8,0},{1,9},{9,1},{2,10},{10,2},{3,11},{11,3},{4,12},{12,4},... | collective-permute-start | bytes 589832 | tf_op jit(solution)/shard_map/ppermute | solution.py:47
  83.4 6.1 %collective-permute-start.12 = (bf16[128,768]{1,0:T(8,128)(2,1)S(1)}, bf16[128,768]{1,0:T(8,128)(2,1)S(1)}, u32[]{:S(2)}, u32[]{:S(2)}) collective-permute-start(bf16[128,768]{1,0:T(8,128)(2,1)S(1)} %slice.105), channel_id=1, source_target_pairs={{0,8},{8,0},{1,9},{9,1},{2,10},{10,2},{3,11},{11,3},{4,12},{12,4},... | collective-permute-start | bytes 589832 | tf_op jit(solution)/shard_map/ppermute | solution.py:47
  89.9 7.0 %collective-permute-start.15 = (bf16[128,768]{1,0:T(8,128)(2,1)S(1)}, bf16[128,768]{1,0:T(8,128)(2,1)S(1)}, u32[]{:S(2)}, u32[]{:S(2)}) collective-permute-start(bf16[128,768]{1,0:T(8,128)(2,1)S(1)} %multiply_convert_fusion.refs_0_), channel_id=1, source_target_pairs={{0,8},{8,0},{1,9},{9,1},{2,10},{10,2},{3,11},{11,3},{4,12},{12,4},... | collective-permute-start | bytes 589832 | tf_op jit(solution)/shard_map/ppermute | solution.py:47
  99.1 8.5 %collective-permute-start.18 = (bf16[128,768]{1,0:T(8,128)(2,1)S(1)}, bf16[128,768]{1,0:T(8,128)(2,1)S(1)}, u32[]{:S(2)}, u32[]{:S(2)}) collective-permute-start(bf16[128,768]{1,0:T(8,128)(2,1)S(1)} %collective-permute-done.14), channel_id=1, source_target_pairs={{0,7},{1,0},{2,1},{3,2},{4,3},{5,4},{6,5},{7,6},{16,17},{17,18},{1... | collective-permute-start | bytes 589832 | tf_op jit(solution)/shard_map/ppermute | solution.py:53
  101.9 8.2 %collective-permute-start.20 = (bf16[256,768]{1,0:T(8,128)(2,1)S(1)}, bf16[256,768]{1,0:T(8,128)(2,1)S(1)}, u32[]{:S(2)}, u32[]{:S(2)}) collective-permute-start(bf16[256,768]{1,0:T(8,128)(2,1)S(1)} %constant_dynamic-update-slice_fusion.refs_2_), channel_id=1, source_target_pairs={{0,8},{8,0},{1,9},{9,1},{2,10},{10,2},{3,11},{11,3},{4,12},{12,4},... | collective-permute-start | bytes 1179656 | tf_op jit(solution)/shard_map/ppermute | solution.py:47
  104.5 13.4 %collective-permute-start.17 = (bf16[128,768]{1,0:T(8,128)(2,1)S(1)}, bf16[128,768]{1,0:T(8,128)(2,1)S(1)}, u32[]{:S(2)}, u32[]{:S(2)}) collective-permute-start(bf16[128,768]{1,0:T(8,128)(2,1)S(1)} %collective-permute-done.16), channel_id=1, source_target_pairs={{0,1},{1,2},{2,3},{3,4},{4,5},{5,6},{6,7},{7,0},{16,23},{17,16},{1... | collective-permute-start | bytes 589832 | tf_op jit(solution)/shard_map/ppermute | solution.py:53
  107.6 10.3 %collective-permute-start.19 = (bf16[128,768]{1,0:T(8,128)(2,1)S(1)}, bf16[128,768]{1,0:T(8,128)(2,1)S(1)}, u32[]{:S(2)}, u32[]{:S(2)}) collective-permute-start(bf16[128,768]{1,0:T(8,128)(2,1)S(1)} %collective-permute-done.18), channel_id=1, source_target_pairs={{0,7},{1,0},{2,1},{3,2},{4,3},{5,4},{6,5},{7,6},{16,17},{17,18},{1... | collective-permute-start | bytes 589832 | tf_op jit(solution)/shard_map/ppermute | solution.py:53
  107.7 21.0 %collective-permute-start.24 = (bf16[256,768]{1,0:T(8,128)(2,1)S(1)}, bf16[256,768]{1,0:T(8,128)(2,1)S(1)}, u32[]{:S(2)}, u32[]{:S(2)}) collective-permute-start(bf16[256,768]{1,0:T(8,128)(2,1)S(1)} %constant_dynamic-update-slice_fusion.2.refs_4_), channel_id=1, source_target_pairs={{0,8},{8,0},{1,9},{9,1},{2,10},{10,2},{3,11},{11,3},{4,12},{12,4},... | collective-permute-start | bytes 1179656 | tf_op jit(solution)/shard_map/ppermute | solution.py:47
  117.9 9.7 %collective-permute-start.22 = (bf16[128,768]{1,0:T(8,128)(2,1)S(1)}, bf16[128,768]{1,0:T(8,128)(2,1)S(1)}, u32[]{:S(2)}, u32[]{:S(2)}) collective-permute-start(bf16[128,768]{1,0:T(8,128)(2,1)S(1)} %collective-permute-done.17), channel_id=1, source_target_pairs={{0,1},{1,2},{2,3},{3,4},{4,5},{5,6},{6,7},{7,0},{16,23},{17,16},{1... | collective-permute-start | bytes 589832 | tf_op jit(solution)/shard_map/ppermute | solution.py:53
  119.2 16.6 %collective-permute-start.21 = (bf16[256,768]{1,0:T(8,128)(2,1)S(1)}, bf16[256,768]{1,0:T(8,128)(2,1)S(1)}, u32[]{:S(2)}, u32[]{:S(2)}) collective-permute-start(bf16[256,768]{1,0:T(8,128)(2,1)S(1)} %constant_dynamic-update-slice_fusion.4.refs_0_), channel_id=1, source_target_pairs={{0,8},{8,0},{1,9},{9,1},{2,10},{10,2},{3,11},{11,3},{4,12},{12,4},... | collective-permute-start | bytes 1179656 | tf_op jit(solution)/shard_map/ppermute | solution.py:47
  127.6 8.2 %collective-permute-start.23 = (bf16[128,768]{1,0:T(8,128)(2,1)S(1)}, bf16[128,768]{1,0:T(8,128)(2,1)S(1)}, u32[]{:S(2)}, u32[]{:S(2)}) collective-permute-start(bf16[128,768]{1,0:T(8,128)(2,1)S(1)} %collective-permute-done.22.refs_2_), channel_id=1, source_target_pairs={{0,8},{8,0},{1,9},{9,1},{2,10},{10,2},{3,11},{11,3},{4,12},{12,4},... | collective-permute-start | bytes 589832 | tf_op jit(solution)/shard_map/ppermute | solution.py:47
  143.8 14.0 %collective-permute-start.25 = (bf16[8,80,640]{2,1,0:T(8,128)(2,1)}, bf16[8,80,640]{2,1,0:T(8,128)(2,1)S(1)}, u32[]{:S(2)}, u32[]{:S(2)}) collective-permute-start(bf16[8,80,640]{2,1,0:T(8,128)(2,1)} %get-tuple-element.81), channel_id=1, source_target_pairs={{0,16},{16,0},{1,17},{17,1},{2,18},{18,2},{3,19},{19,3},{4,20},{20... | collective-permute-start | bytes 2457608 | tf_op jit(solution)/shard_map/ppermute | solution.py:47
  (17 other events, 94.0 us)
Sparse Core Ops, SparseCore 0:
  19.9 40.0 all-gather.1
  102.2 42.2 reduce-scatter.1

commit v7 on v6

--- a/solution.py
+++ b/solution.py
@@ -60,16 +60,24 @@
     (((0, 1), (0, -1), (0, 0)),),
 )
 MEMBERS = tuple(tuple(block for piece in group for block in piece) for group in GROUPS)
-BLOCKS = tuple(block for members in MEMBERS for block in members)
-
-
-def block_index(half, place, direction):
-    halves = jnp.array([block[0] for block in BLOCKS], jnp.int32)
-    offsets = jnp.array([block[1] for block in BLOCKS], jnp.int32)
-    return lax.rem(half + halves, 2) * RING + lax.rem(place + direction * offsets + RING, RING)
-
-
-def forward_kernel(pieces, first, index_ref, *refs):
+
+
+def packed_place(half, place, core):
+    return (half * (2 * RING) + place * 2 + core)[None]
+
+
+def block_map(block):
+    half, offset = block
+
+    def index_map(i, packed):
+        own_half, place, core = packed[0] // (2 * RING), packed[0] // 2 % RING, packed[0] % 2
+        along = lax.rem(place + (1 - 2 * core) * offset + RING, RING)
+        return lax.rem(own_half + half, 2) * RING + along, 0
+
+    return index_map
+
+
+def forward_kernel(pieces, first, packed_ref, *refs):
     count = sum(pieces)
     hidden = [ref[...] for ref in refs[:count]]
     refs = refs[count:]
@@ -82,11 +90,12 @@
         up_ref, down_head_ref = refs[:2]
         refs = refs[2:]
     part_refs = refs[: len(pieces)]
-    normed_t_ref, act_t_ref, slope_ref = refs[len(pieces) :]
+    act_t_ref, slope_ref = refs[len(pieces) :]
     rows = hidden[0].shape[0]
     wide = jnp.concatenate(hidden, axis=0).astype(f32)
     square_mean = jnp.mean(wide * wide, axis=-1, keepdims=True)
-    normed = (wide * lax.rsqrt(square_mean + epsilon)).astype(bf16)
+    inverse = lax.rsqrt(square_mean + epsilon)
+    normed = (wide * inverse).astype(bf16)
     pre = dot(normed, up_ref[...], ((1,), (1,)))
     tangent = jnp.tanh(gelu_root * (pre + gelu_cubic * (pre * pre * pre)))
     act = (0.5 * pre * (1.0 + tangent)).astype(bf16)
@@ -98,36 +107,32 @@
     slope = 0.5 * (1.0 + tangent) + 0.5 * pre * (1.0 - tangent * tangent) * gelu_root * (
         1.0 + 3.0 * gelu_cubic * pre * pre
     )
-    slope = slope.astype(bf16)
-    normed_t, act_t = normed.T, act.T
+    slope = (inverse * slope).astype(bf16)
+    act_t = act.T
     for i in range(count):
         span = slice(i * rows, (i + 1) * rows)
         slope_ref[i] = slope[span, :]
-        normed_t_ref[i] = normed_t[:, span]
         act_t_ref[i] = act_t[:, span]
 
 
-def forward_blocks(group, index, hidden_in, up_t, *weights):
+def forward_blocks(group, packed, hidden_in, up_t, *weights):
     pieces = tuple(len(piece) for piece in GROUPS[group])
     count = sum(pieces)
-    start = sum(len(members) for members in MEMBERS[:group])
     first = len(weights) == 2
     rows = hidden_in.shape[0] // (2 * RING)
     ff, width = up_t.shape
     embed = weights[-1].shape[1]
-    flat = lambda i, index: (0, 0)
-    cube = lambda i, index: (0, 0, 0)
+    flat = lambda i, packed: (0, 0)
+    cube = lambda i, packed: (0, 0, 0)
     shapes = [jax.ShapeDtypeStruct((size * rows, embed), bf16) for size in pieces]
-    shapes += [jax.ShapeDtypeStruct((count,) + dims, bf16) for dims in ((width, rows), (ff, rows), (rows, ff))]
+    shapes += [jax.ShapeDtypeStruct((count,) + dims, bf16) for dims in ((ff, rows), (rows, ff))]
     shapes += [jax.ShapeDtypeStruct((ff, embed), bf16)] if first else []
     out = pl.pallas_call(
         functools.partial(forward_kernel, pieces, first),
         grid_spec=pltpu.PrefetchScalarGridSpec(
             num_scalar_prefetch=1,
             grid=(1,),
-            in_specs=[
-                pl.BlockSpec((rows, width), lambda i, index, at=start + at: (index[at], 0)) for at in range(count)
-            ]
+            in_specs=[pl.BlockSpec((rows, width), block_map(block)) for block in MEMBERS[group]]
             + [pl.BlockSpec(w.shape, flat) for w in (up_t,) + weights],
             out_specs=[pl.BlockSpec(shape.shape, cube if len(shape.shape) == 3 else flat) for shape in shapes],
         ),
@@ -135,96 +140,103 @@
         compiler_params=pltpu.CompilerParams(vmem_limit_bytes=VMEM_BYTES),
         cost_estimate=pl.CostEstimate(
             flops=2 * count * rows * ff * (width + embed),
-            bytes_accessed=2 * count * rows * (2 * width + embed + 2 * ff) + 2 * ff * (width + embed),
+            bytes_accessed=2 * count * rows * (width + embed + 2 * ff) + 2 * ff * (width + embed),
             transcendentals=count * rows * ff,
         ),
-    )(index, *([hidden_in] * count), up_t, *weights)
-    parts, kept = out[: len(pieces)], out[len(pieces) : len(pieces) + 3]
+    )(packed, *([hidden_in] * count), up_t, *weights)
+    parts, kept = out[: len(pieces)], out[len(pieces) : len(pieces) + 2]
     return parts, kept, out[-1]
 
 
-def backward_kernel(count, blocks, first, last, *refs):
+def backward_kernel(count, blocks, first, last, packed_ref, *refs):
     join = lambda parts, axis: jnp.concatenate(parts, axis=axis) if len(parts) > 1 else parts[0]
     grad = join([ref[...] for ref in refs[:count]], 0)
     kept = refs[count : count + 3 * blocks]
-    normed_t, act_t, slope = (join([ref[0] for ref in kept[i::3]], axis) for i, axis in ((0, 1), (1, 1), (2, 0)))
+    hidden = join([ref[...] for ref in kept[0::3]], 0)
+    act_t, slope = join([ref[0] for ref in kept[1::3]], 1), join([ref[0] for ref in kept[2::3]], 0)
     refs = refs[count + 3 * blocks :]
     down_head_ref, refs = refs[0], refs[1:]
     if not first:
         up_in, act_in = refs[:2]
         refs = refs[2:]
-    if last:
-        core_ref, head_ref, keep_ref, give_ref, up_acc = refs
-    else:
-        up_acc, act_acc = refs
     tile = 256
-    width, ff = up_acc.shape
     grad_act = dot(grad, down_head_ref[...], ((1,), (1,)))
-    grad_pre = (grad_act * slope.astype(f32)).astype(bf16)
+    grad_pre_t = (grad_act * slope.astype(f32)).astype(bf16).T
     act_sum = dot(act_t, grad)
     if not first:
         act_sum = act_sum + act_in[...]
-    if not last:
+    if last:
+        head_ref, keep_ref, give_ref, total = refs
+    else:
+        up_acc, act_acc = refs
         act_acc[...] = act_sum
+    width, ff = hidden.shape[1], act_sum.shape[0]
     for m in range(0, width, tile):
-        up_sum = dot(normed_t[m : m + tile, :], grad_pre)
+        up_sum = dot(grad_pre_t, hidden[:, m : m + tile])
         if not first:
-            up_sum = up_sum + up_in[m : m + tile, :]
-        up_acc[m : m + tile, :] = up_sum
+            up_sum = up_sum + up_in[:, m : m + tile]
+        if last:
+            total[m : m + tile, :] = up_sum.T
+        else:
+            up_acc[:, m : m + tile] = up_sum
     if last:
-        core = core_ref[0]
+        core = packed_ref[0] % 2
         act_grad = act_sum.astype(bf16)
         rows = keep_ref.shape[1]
         for side in range(2):
             for half, out_ref in ((core, keep_ref), (1 - core, give_ref)):
                 for chip in range(keep_ref.shape[0]):
                     at = pl.multiple_of((2 * chip + half) * rows, rows)
-                    out_ref[chip, :, side * ff : (side + 1) * ff] = up_acc[pl.ds(at, rows), :].astype(bf16)
+                    out_ref[chip, :, side * ff : (side + 1) * ff] = total[pl.ds(at, rows), :].astype(bf16)
             if side == 0:
                 for m in range(0, width, tile):
-                    up_acc[m : m + tile, :] = dot(head_ref[m : m + tile, :], act_grad, ((1,), (1,)))
-
-
-def backward_blocks(items, down_head, sums, last=None):
+                    total[m : m + tile, :] = dot(head_ref[m : m + tile, :], act_grad, ((1,), (1,)))
+
+
+def backward_blocks(items, packed, hidden_in, down_head, sums, head_weight=None):
+    last = head_weight is not None
     whole = pl.BlockSpec(memory_space=pltpu.VMEM)
     args = [grad for grad, _ in items]
     specs = [whole] * len(items)
     places = [place for _, blocks in items for place in blocks]
-    for kept, at in places:
+    rows, width = hidden_in.shape[0] // (2 * RING), hidden_in.shape[1]
+    for block, kept, at in places:
+        args.append(hidden_in)
+        specs.append(pl.BlockSpec((rows, width), block_map(block)))
         for array in kept:
             args.append(array)
-            specs.append(pl.BlockSpec((1,) + array.shape[1:], lambda i, at=at: (at, 0, 0)))
+            specs.append(pl.BlockSpec((1,) + array.shape[1:], lambda i, packed, at=at: (at, 0, 0)))
     ff, embed = down_head.shape
-    rows, width = sum(grad.shape[0] for grad, _ in items), places[0][0][0].shape[1]
     args.append(down_head)
-    specs.append(whole)
     aliases = {}
     if sums is not None:
-        if last is None:
-            aliases = {len(args): 0, len(args) + 1: 1}
+        if not last:
+            aliases = {len(args) + 1: 0, len(args) + 2: 1}
         args += list(sums)
-        specs += [whole] * 2
-    flops = 2 * rows * ff * (2 * embed + width)
-    if last is None:
-        shapes = [jax.ShapeDtypeStruct((width, ff), f32), jax.ShapeDtypeStruct((ff, embed), f32)]
-        scratch = []
-    else:
-        args += list(last)
-        specs += [pl.BlockSpec(memory_space=pltpu.SMEM), whole]
+    flops = 2 * len(places) * rows * ff * (2 * embed + width)
+    if last:
+        args.append(head_weight)
         shapes = [jax.ShapeDtypeStruct((8, width // 16, 2 * ff), bf16)] * 2
         scratch = [pltpu.VMEM((width, ff), f32)]
         flops += 2 * width * ff * embed
+    else:
+        shapes = [jax.ShapeDtypeStruct((ff, width), f32), jax.ShapeDtypeStruct((ff, embed), f32)]
+        scratch = []
+    specs += [whole] * (len(args) - len(specs))
     return pl.pallas_call(
-        functools.partial(backward_kernel, len(items), len(places), sums is None, last is not None),
-        grid=(1,),
-        in_specs=specs,
-        out_specs=[whole] * 2,
+        functools.partial(backward_kernel, len(items), len(places), sums is None, last),
+        grid_spec=pltpu.PrefetchScalarGridSpec(
+            num_scalar_prefetch=1,
+            grid=(1,),
+            in_specs=specs,
+            out_specs=[whole] * 2,
+            scratch_shapes=scratch,
+        ),
         out_shape=shapes,
-        scratch_shapes=scratch,
         input_output_aliases=aliases,
         compiler_params=pltpu.CompilerParams(vmem_limit_bytes=VMEM_BYTES),
         cost_estimate=pl.CostEstimate(flops=flops, bytes_accessed=8 * 1024 * 1024, transcendentals=0),
-    )(*args)
+    )(packed, *args)
 
 
 def total_of(*terms):
@@ -235,14 +247,14 @@
     y_hi, z, core = (lax.axis_index(name).astype(jnp.int32) for name in ("yhi", "z", "core"))
     rows = hidden_in.shape[0] // (2 * RING)
     group_half = RING * rows
-    index = block_index(y_hi, z, 1 - 2 * core)
+    packed = packed_place(y_hi, z, core)
     up_t = up_weight.T
     saved = {}
 
     def forward(group, *weights):
-        parts, kept, down_head = forward_blocks(group, index, hidden_in, up_t, *weights)
+        parts, kept, down_head = forward_blocks(group, packed, hidden_in, up_t, *weights)
         for at, block in enumerate(MEMBERS[group]):
-            saved[block] = (kept, at)
+            saved[block] = (block, kept, at)
         return parts, down_head
 
     (other4, other3, own4), down_head = forward(0, down_weight, head_weight)
@@ -289,23 +301,24 @@
     ring2 = both(back, fore)
     crossed2 = swap(ring2, "yhi")
     fore, back = shift(fore, 1), shift(back, -1)
-    items = [item(grad_embed, (0, 0)), item(crossed0, (1, 0)), item(ring1, *pair(1, 0)), item(crossed1, *pair(1, 1))]
-    sums = backward_blocks(items + [item(ring2, *pair(2, 0))], down_head, None)
-    fore, back, sums = lax.optimization_barrier((fore, back, sums))
+    backward = lambda items, sums, *head: backward_blocks(items, packed, hidden_in, down_head, sums, *head)
+    sums = backward([item(grad_embed, (0, 0)), item(crossed0, (1, 0)), item(ring1, *pair(1, 0))], None)
+    fore, back, crossed1, sums = lax.optimization_barrier((fore, back, crossed1, sums))
+    ring4 = shift(fore, 1)
     ring3 = both(back, fore)
     crossed3 = swap(ring3, "yhi")
-    ring4 = shift(fore, 1)
+    sums = backward([item(crossed1, *pair(1, 1)), item(ring2, *pair(2, 0))], sums)
+    ring4, sums = lax.optimization_barrier((ring4, sums))
     crossed4 = swap(ring4, "yhi")
-    items = [item(ring3, *pair(3, 0)), item(crossed2, *pair(2, 1)), item(ring4, (0, 4))]
-    sums = backward_blocks(items, down_head, sums)
+    sums = backward([item(ring3, *pair(3, 0)), item(crossed2, *pair(2, 1)), item(ring4, (0, 4))], sums)
     crossed4, sums = lax.optimization_barrier((crossed4, sums))
-    items = [item(crossed3, *pair(3, 1)), item(crossed4, (1, 4))]
-    keep, give = backward_blocks(items, down_head, sums, (core[None], head_weight))
+    keep, give = backward([item(crossed3, *pair(3, 1)), item(crossed4, (1, 4))], sums, head_weight)
     chip = total_of(keep, swap(give, "core")).astype(bf16)
+    score_grad = unit_backward(score_wide, score_inverse, grad_score.astype(f32))
+    chip, score_grad = lax.optimization_barrier((chip, score_grad))
     landed = lax.all_to_all(chip, ("ylo", "x"), 0, 0)
     total = jnp.sum(landed.astype(f32), axis=0)
     ff = up_weight.shape[1]
-    score_grad = unit_backward(score_wide, score_inverse, grad_score.astype(f32))
     return (total[:, :ff], total[:, ff:].T, score_grad)
 
 

time: 188 us -> 184 us (0.979)
  starting transfers between devices: 51.4 us -> 48.8 us
  Pallas kernels: 44.1 us -> 42.1 us
    pallas_call x4, Pallas kernels: 23.6 us -> 19.1 us  [forward_blocks(): pl.pallas_call(functools.partial(forward_kernel, pieces, first), grid_spe...]
    ppermute x12, starting transfers between devices: 30.6 us -> 26.6 us  [swap(): return lax.ppermute(value, axis, [(0, 1), (1, 0)])]
    ppermute x14, waiting for transfers between devices: 20.8 us -> 23.8 us  [shift(): return lax.ppermute(value, ('core', 'z'), perm)]
    pallas_call x3 -> x4, Pallas kernels: 20.5 us -> 23 us  [backward_blocks(): pl.pallas_call(functools.partial(backward_kernel, len(items), len(places)...]
where the time goes in v7:
time: 184 us; the launch traced here: 183 us
  starting transfers between devices  48.8 us (27%)
  Pallas kernels  42.1 us (23%)
  waiting for transfers between devices  38.9 us (21%)
  blocking collectives  17.6 us (10%)
  between operations  14.3 us (8%)
  other arithmetic  11.4 us (6%)
  matrix products  6.09 us (3%)
  local copies, waits for them, and re-layouts  3.77 us (2%)
    ppermute x12, starting transfers between devices, swap(): return lax.ppermute(value, axis, [(0, 1), (1, 0)])  26.6 us
    ppermute x14, waiting for transfers between devices, shift(): return lax.ppermute(value, ('core', 'z'), perm)  23.8 us
    pallas_call x4, Pallas kernels, backward_blocks(): pl.pallas_call(functools.partial(backward_kernel, len(items), len(places)...  23 us
    ppermute x14, starting transfers between devices, shift(): return lax.ppermute(value, ('core', 'z'), perm)  22.1 us
    pallas_call x4, Pallas kernels, forward_blocks(): pl.pallas_call(functools.partial(forward_kernel, pieces, first), grid_spe...  19.1 us
    all_to_all x1, blocking collectives, per_device(): landed = lax.all_to_all(chip, ('ylo', 'x'), 0, 0)  17.6 us
    ppermute x12, waiting for transfers between devices, swap(): return lax.ppermute(value, axis, [(0, 1), (1, 0)])  15 us
    dot_general x4, matrix products, dot(): lax.dot_general(left, right, (dims, ((), ())), preferred_element_type=f32)  6.09 us
  transfers between devices with their start and end apart: 28, of which 16 were waited for; matrix products, arithmetic and copies ran while one was open for 7% of the time, Pallas kernels for 20%

profile of v7, /device:TPU:1, one launch (start us, length us, event | category | flops | bytes accessed | tf_op | source)
XLA Modules:
  0.0 183.0 jit_solution(4785634578419132171)
XLA Ops:
  7.2 5.6 %shard_map.85 = (bf16[128,768]{1,0:T(8,128)(2,1)}, bf16[256,768]{1,0:T(8,128)(2,1)}, bf16[128,768]{1,0:T(8,128)(2,1)}, bf16[4,320,128]{2,1,0:T(8,128)(2,1)}, bf1...) custom-call(s32[1]{0:T(128)} %bitcast.packed_ref, bf16[2048,1280]{1,0:T(8,128)(2,1)} %refs_8_.3, ...), custom_call_target="tpu_custom_call" | custom-call | flops 671088640 | bytes 4063232 | tf_op jit(solution)/shard_map/pallas_call | solution.py:130
  12.9 3.7 %collective-permute-start.3 = (bf16[128,768]{1,0:T(8,128)(2,1)}, bf16[128,768]{1,0:T(8,128)(2,1)S(1)}, u32[]{:S(2)}, u32[]{:S(2)}) collective-permute-start(bf16[128,768]{1,0:T(8,128)(2,1)} %get-tuple-element.56), channel_id=1, source_target_pairs={{0,8},{8,0},{1,9},{9,1},{2,10},{10,2},{3,11},{11,3},{4,12},{12,4},... | collective-permute-start | bytes 589832 | tf_op jit(solution)/shard_map/ppermute | solution.py:47
  17.7 2.8 %collective-permute-done.3 = bf16[128,768]{1,0:T(8,128)(2,1)S(1)} collective-permute-done((bf16[128,768]{1,0:T(8,128)(2,1)}, bf16[128,768]{1,0:T(8,128)(2,1)S(1)}, u32[]{:S(2)}, u32[]{:S(2)}) %collective-permute-start.3) | collective-permute-done | bytes 196640 | tf_op jit(solution)/shard_map/ppermute | solution.py:47
  21.5 6.3 %collective-permute-start.4 = (bf16[128,768]{1,0:T(8,128)(2,1)S(1)}, bf16[128,768]{1,0:T(8,128)(2,1)S(1)}, u32[]{:S(2)}, u32[]{:S(2)}) collective-permute-start(bf16[128,768]{1,0:T(8,128)(2,1)S(1)} %add_convert_fusion.7), channel_id=1, source_target_pairs={{0,1},{1,2},{2,3},{3,4},{4,5},{5,6},{6,7},{7,0},{16,23},{17,16},{1... | collective-permute-start | bytes 589832 | tf_op jit(solution)/shard_map/ppermute | solution.py:53
  27.8 4.4 %shard_map.88 = (bf16[256,768]{1,0:T(8,128)(2,1)}, bf16[256,768]{1,0:T(8,128)(2,1)}, bf16[4,320,128]{2,1,0:T(8,128)(2,1)}, bf16[4,128,320]{2,1,0:T(8,128)(2,1)}) custom-call(s32[1]{0:T(128)} %bitcast.packed_ref, bf16[2048,1280]{1,0:T(8,128)(2,1)} %refs_8_.3, bf16[2048,1280]{1,0:T(8,128)(2,1)} %refs_8_.3, bf16[2048,1280]{1,0:T(8,128)(2,1)} %refs_8_.3, ...), custom_call_target="tpu_custom_call" | custom-call | flops 671088640 | bytes 4063232 | tf_op jit(solution)/shard_map/pallas_call | solution.py:130
  32.2 2.9 %collective-permute-start.1 = (bf16[256,768]{1,0:T(8,128)(2,1)}, bf16[256,768]{1,0:T(8,128)(2,1)S(1)}, u32[]{:S(2)}, u32[]{:S(2)}) collective-permute-start(bf16[256,768]{1,0:T(8,128)(2,1)} %get-tuple-element.52), channel_id=1, source_target_pairs={{0,8},{8,0},{1,9},{9,1},{2,10},{10,2},{3,11},{11,3},{4,12},{12,4},... | collective-permute-start | bytes 1179656 | tf_op jit(solution)/shard_map/ppermute | solution.py:47
  37.8 5.0 %shard_map.87 = (bf16[384,768]{1,0:T(8,128)(2,1)}, bf16[256,768]{1,0:T(8,128)(2,1)}, bf16[5,320,128]{2,1,0:T(8,128)(2,1)}, bf16[5,128,320]{2,1,0:T(8,128)(2,1)}) custom-call(s32[1]{0:T(128)} %bitcast.packed_ref, bf16[2048,1280]{1,0:T(8,128)(2,1)} %refs_8_.3, bf16[2048,1280]{1,0:T(8,128)(2,1)} %refs_8_.3, bf16[2048,1280]{1,0:T(8,128)(2,1)} %refs_8_.3, ...), custom_call_target="tpu_custom_call" | custom-call | flops 838860800 | bytes 4751360 | tf_op jit(solution)/shard_map/pallas_call | solution.py:130
  46.2 2.8 %collective-permute-done.8 = bf16[128,768]{1,0:T(8,128)(2,1)S(1)} collective-permute-done((bf16[128,768]{1,0:T(8,128)(2,1)S(1)}, bf16[128,768]{1,0:T(8,128)(2,1)S(1)}, u32[]{:S(2)}, u32[]{:S(2)}) %collective-permute-start.8) | collective-permute-done | bytes 196640 | tf_op jit(solution)/shard_map/ppermute | solution.py:53
  51.7 4.1 %shard_map.86 = (bf16[384,768]{1,0:T(8,128)(2,1)}, bf16[3,320,128]{2,1,0:T(8,128)(2,1)}, bf16[3,128,320]{2,1,0:T(8,128)(2,1)}) custom-call(s32[1]{0:T(128)} %bitcast.packed_ref, bf16[2048,1280]{1,0:T(8,128)(2,1)} %refs_8_.3, bf16[2048,1280]{1,0:T(8,128)(2,1)} %refs_8_.3, bf16[2048,1280]{1,0:T(8,128)(2,1)} %refs_8_.3, bf16[320,1280]{1,0:T(8,128)(2,1)} %bitcast.16, ...), custom_call_target="tpu_custom_call" | custom-call | flops 503316480 | bytes 3375104 | tf_op jit(solution)/shard_map/pallas_call | solution.py:130
  57.4 2.8 %collective-permute-done.6 = bf16[128,768]{1,0:T(8,128)(2,1)S(1)} collective-permute-done((bf16[128,768]{1,0:T(8,128)(2,1)S(1)}, bf16[128,768]{1,0:T(8,128)(2,1)S(1)}, u32[]{:S(2)}, u32[]{:S(2)}) %collective-permute-start.6) | collective-permute-done | bytes 196640 | tf_op jit(solution)/shard_map/ppermute | solution.py:53
  73.8 3.6 %collective-permute-done.11 = bf16[128,768]{1,0:T(8,128)(2,1)S(1)} collective-permute-done((bf16[128,768]{1,0:T(8,128)(2,1)S(1)}, bf16[128,768]{1,0:T(8,128)(2,1)S(1)}, u32[]{:S(2)}, u32[]{:S(2)}) %collective-permute-start.11) | collective-permute-done | bytes 196640 | tf_op jit(solution)/shard_map/ppermute | solution.py:47
  82.8 3.6 %collective-permute-done.12 = bf16[128,768]{1,0:T(8,128)(2,1)S(1)} collective-permute-done((bf16[128,768]{1,0:T(8,128)(2,1)S(1)}, bf16[128,768]{1,0:T(8,128)(2,1)S(1)}, u32[]{:S(2)}, u32[]{:S(2)}) %collective-permute-start.12) | collective-permute-done | bytes 196640 | tf_op jit(solution)/shard_map/ppermute | solution.py:47
  86.8 5.4 %collective-permute-start.13 = (bf16[128,768]{1,0:T(8,128)(2,1)S(1)}, bf16[128,768]{1,0:T(8,128)(2,1)S(1)}, u32[]{:S(2)}, u32[]{:S(2)}) collective-permute-start(bf16[128,768]{1,0:T(8,128)(2,1)S(1)} %multiply_convert_fusion.refs_0_), channel_id=1, source_target_pairs={{0,1},{1,2},{2,3},{3,4},{4,5},{5,6},{6,7},{7,0},{16,23},{17,16},{1... | collective-permute-start | bytes 589832 | tf_op jit(solution)/shard_map/ppermute | solution.py:53
  92.2 2.9 %collective-permute-start.15 = (bf16[128,768]{1,0:T(8,128)(2,1)S(1)}, bf16[128,768]{1,0:T(8,128)(2,1)S(1)}, u32[]{:S(2)}, u32[]{:S(2)}) collective-permute-start(bf16[128,768]{1,0:T(8,128)(2,1)S(1)} %multiply_convert_fusion.refs_0_), channel_id=1, source_target_pairs={{0,8},{8,0},{1,9},{9,1},{2,10},{10,2},{3,11},{11,3},{4,12},{12,4},... | collective-permute-start | bytes 589832 | tf_op jit(solution)/shard_map/ppermute | solution.py:47
  96.8 3.2 %collective-permute-done.14 = bf16[128,768]{1,0:T(8,128)(2,1)S(1)} collective-permute-done((bf16[128,768]{1,0:T(8,128)(2,1)S(1)}, bf16[128,768]{1,0:T(8,128)(2,1)S(1)}, u32[]{:S(2)}, u32[]{:S(2)}) %collective-permute-start.14) | collective-permute-done | bytes 196640 | tf_op jit(solution)/shard_map/ppermute | solution.py:53
  100.1 2.7 %collective-permute-start.16 = (bf16[128,768]{1,0:T(8,128)(2,1)S(1)}, bf16[128,768]{1,0:T(8,128)(2,1)S(1)}, u32[]{:S(2)}, u32[]{:S(2)}) collective-permute-start(bf16[128,768]{1,0:T(8,128)(2,1)S(1)} %collective-permute-done.13), channel_id=1, source_target_pairs={{0,1},{1,2},{2,3},{3,4},{4,5},{5,6},{6,7},{7,0},{16,23},{17,16},{1... | collective-permute-start | bytes 589832 | tf_op jit(solution)/shard_map/ppermute | solution.py:53
  105.4 4.4 %shard_map.89 = (f32[320,1280]{1,0:T(8,128)}, f32[320,768]{1,0:T(8,128)}) custom-call(s32[1]{0:T(128)} %bitcast.packed_ref, bf16[128,768]{1,0:T(8,128)(2,1)} %copy-done.6, bf16[128,768]{1,0:T(8,128)(2,1)} %copy-done.10, bf16[256,768]{1,0:T(8,128)(2,1)} %copy-done.5, bf16[2048,1280]{1,0:T(8,128)(2,1)} %refs_8_.3, ...), custom_call_target="tpu_custom_call" | custom-call | flops 922746880 | bytes 8388608 | tf_op jit(solution)/shard_map/pallas_call | solution.py:226
  113.7 5.3 %collective-permute-done.17 = bf16[128,768]{1,0:T(8,128)(2,1)S(1)} collective-permute-done((bf16[128,768]{1,0:T(8,128)(2,1)S(1)}, bf16[128,768]{1,0:T(8,128)(2,1)S(1)}, u32[]{:S(2)}, u32[]{:S(2)}) %collective-permute-start.17) | collective-permute-done | bytes 196640 | tf_op jit(solution)/shard_map/ppermute | solution.py:53
  119.1 2.8 %collective-permute-done.19 = bf16[128,768]{1,0:T(8,128)(2,1)S(1)} collective-permute-done((bf16[128,768]{1,0:T(8,128)(2,1)S(1)}, bf16[128,768]{1,0:T(8,128)(2,1)S(1)}, u32[]{:S(2)}, u32[]{:S(2)}) %collective-permute-start.19) | collective-permute-done | bytes 196640 | tf_op jit(solution)/shard_map/ppermute | solution.py:53
  122.0 5.3 %shard_map.90 = (f32[320,1280]{1,0:T(8,128)}, f32[320,768]{1,0:T(8,128)}) custom-call(s32[1]{0:T(128)} %bitcast.packed_ref, bf16[256,768]{1,0:T(8,128)(2,1)} %copy-done.7, bf16[256,768]{1,0:T(8,128)(2,1)} %copy-done.4, bf16[2048,1280]{1,0:T(8,128)(2,1)} %refs_8_.3, ...), custom_call_target="tpu_custom_call", output_to_operand_aliasing={{0}: (16, {}), {1}: (17, {})} | custom-call | flops 922746880 | bytes 8388608 | tf_op jit(solution)/shard_map/pallas_call | solution.py:226
  131.0 5.9 %shard_map.91 = (f32[320,1280]{1,0:T(8,128)}, f32[320,768]{1,0:T(8,128)}) custom-call(s32[1]{0:T(128)} %bitcast.packed_ref, bf16[256,768]{1,0:T(8,128)(2,1)} %copy-done.3, bf16[256,768]{1,0:T(8,128)(2,1)} %copy-done.8, bf16[128,768]{1,0:T(8,128)(2,1)} %copy-done.11, bf16[2048,1280]{1,0:T(8,128)(2,1)} %refs_8_.3, ...), custom_call_target="tpu_custom_call", output_to_operand_aliasing={{0}: (20, {}), {1}: (21, {})} | custom-call | flops 1153433600 | bytes 8388608 | tf_op jit(solution)/shard_map/pallas_call | solution.py:226
  138.4 7.4 %shard_map.92 = (bf16[8,80,640]{2,1,0:T(8,128)(2,1)}, bf16[8,80,640]{2,1,0:T(8,128)(2,1)}) custom-call(s32[1]{0:T(128)} %bitcast.packed_ref, bf16[256,768]{1,0:T(8,128)(2,1)} %copy-done.9, bf16[128,768]{1,0:T(8,128)(2,1)} %copy-done.12, bf16[2048,1280]{1,0:T(8,128)(2,1)} %refs_8_.3, bf16[4,320,128]{2,1,0:T(8,128)(2,1)} %get-tuple-element.77.refs_16_.refs_3_.refs_6_.refs_9_, ...), custom_call_target="tpu_custom_call" | custom-call | flops 1321205760 | bytes 8388608 | tf_op jit(solution)/shard_map/pallas_call | solution.py:226
  145.8 5.4 %collective-permute-start.25 = (bf16[8,80,640]{2,1,0:T(8,128)(2,1)}, bf16[8,80,640]{2,1,0:T(8,128)(2,1)S(1)}, u32[]{:S(2)}, u32[]{:S(2)}) collective-permute-start(bf16[8,80,640]{2,1,0:T(8,128)(2,1)} %get-tuple-element.87), channel_id=1, source_target_pairs={{0,16},{16,0},{1,17},{17,1},{2,18},{18,2},{3,19},{19,3},{4,20},{20... | collective-permute-start | bytes 2457608 | tf_op jit(solution)/shard_map/ppermute | solution.py:47
  157.7 17.6 %all_to_all.5 = bf16[8,80,640]{2,1,0:T(8,128)(2,1)S(1)} all-to-all(bf16[8,80,640]{2,1,0:T(8,128)(2,1)S(1)} %add_convert_fusion), channel_id=1, replica_groups=mesh['ylo'=2,'x'=4,'core'=2,'yhi'=2,'z'=8] {'ylo','x'}, dimensions={0} | all-to-all | bytes 1638400 | tf_op jit(solution)/shard_map/all_to_all | solution.py:319
  (100 shorter events, 52.9 us)
Async XLA Ops:
  7.2 70.2 %all-gather.2.cloned.1.call-start = ((), (), s32[]{:S(2)}) async-start(), calls=%async_computation.2 | async-start | bytes 1769472 | tf_op jit(solution)/shard_map/all_gather | solution.py:264
  12.9 7.6 %collective-permute-start.3 = (bf16[128,768]{1,0:T(8,128)(2,1)}, bf16[128,768]{1,0:T(8,128)(2,1)S(1)}, u32[]{:S(2)}, u32[]{:S(2)}) collective-permute-start(bf16[128,768]{1,0:T(8,128)(2,1)} %get-tuple-element.56), channel_id=1, source_target_pairs={{0,8},{8,0},{1,9},{9,1},{2,10},{10,2},{3,11},{11,3},{4,12},{12,4},... | collective-permute-start | bytes 589832 | tf_op jit(solution)/shard_map/ppermute | solution.py:47
  16.6 18.5 %collective-permute-start.2 = (bf16[256,768]{1,0:T(8,128)(2,1)}, bf16[256,768]{1,0:T(8,128)(2,1)S(1)}, u32[]{:S(2)}, u32[]{:S(2)}) collective-permute-start(bf16[256,768]{1,0:T(8,128)(2,1)} %get-tuple-element.54), channel_id=1, source_target_pairs={{0,8},{8,0},{1,9},{9,1},{2,10},{10,2},{3,11},{11,3},{4,12},{12,4},... | collective-permute-start | bytes 1179656 | tf_op jit(solution)/shard_map/ppermute | solution.py:47
  17.6 137.1 %reduce-scatter.2.cloned.1.call-start = ((), (), s32[]{:S(2)}) async-start(), calls=%async_computation.3 | async-start | bytes 1769472 | tf_op jit(solution)/shard_map/reduce_scatter | solution.py:297
  21.5 13.7 %collective-permute-start.4 = (bf16[128,768]{1,0:T(8,128)(2,1)S(1)}, bf16[128,768]{1,0:T(8,128)(2,1)S(1)}, u32[]{:S(2)}, u32[]{:S(2)}) collective-permute-start(bf16[128,768]{1,0:T(8,128)(2,1)S(1)} %add_convert_fusion.7), channel_id=1, source_target_pairs={{0,1},{1,2},{2,3},{3,4},{4,5},{5,6},{6,7},{7,0},{16,23},{17,16},{1... | collective-permute-start | bytes 589832 | tf_op jit(solution)/shard_map/ppermute | solution.py:53
  32.2 12.1 %collective-permute-start.1 = (bf16[256,768]{1,0:T(8,128)(2,1)}, bf16[256,768]{1,0:T(8,128)(2,1)S(1)}, u32[]{:S(2)}, u32[]{:S(2)}) collective-permute-start(bf16[256,768]{1,0:T(8,128)(2,1)} %get-tuple-element.52), channel_id=1, source_target_pairs={{0,8},{8,0},{1,9},{9,1},{2,10},{10,2},{3,11},{11,3},{4,12},{12,4},... | collective-permute-start | bytes 1179656 | tf_op jit(solution)/shard_map/ppermute | solution.py:47
  36.3 9.9 %collective-permute-start.5 = (bf16[128,768]{1,0:T(8,128)(2,1)S(1)}, bf16[128,768]{1,0:T(8,128)(2,1)S(1)}, u32[]{:S(2)}, u32[]{:S(2)}) collective-permute-start(bf16[128,768]{1,0:T(8,128)(2,1)S(1)} %get-tuple-element.97), channel_id=1, source_target_pairs={{0,1},{1,2},{2,3},{3,4},{4,5},{5,6},{6,7},{7,0},{16,23},{17,16},{1... | collective-permute-start | bytes 589832 | tf_op jit(solution)/shard_map/ppermute | solution.py:53
  37.1 11.9 %collective-permute-start.8 = (bf16[128,768]{1,0:T(8,128)(2,1)S(1)}, bf16[128,768]{1,0:T(8,128)(2,1)S(1)}, u32[]{:S(2)}, u32[]{:S(2)}) collective-permute-start(bf16[128,768]{1,0:T(8,128)(2,1)S(1)} %get-tuple-element.98), channel_id=1, source_target_pairs={{0,7},{1,0},{2,1},{3,2},{4,3},{5,4},{6,5},{7,6},{16,17},{17,18},{1... | collective-permute-start | bytes 589832 | tf_op jit(solution)/shard_map/ppermute | solution.py:53
  42.8 14.6 %collective-permute-start = (bf16[384,768]{1,0:T(8,128)(2,1)}, bf16[384,768]{1,0:T(8,128)(2,1)S(1)}, u32[]{:S(2)}, u32[]{:S(2)}) collective-permute-start(bf16[384,768]{1,0:T(8,128)(2,1)} %get-tuple-element.50), channel_id=1, source_target_pairs={{0,8},{8,0},{1,9},{9,1},{2,10},{10,2},{3,11},{11,3},{4,12},{12,4},... | collective-permute-start | bytes 1769480 | tf_op jit(solution)/shard_map/ppermute | solution.py:47
  50.2 10.0 %collective-permute-start.6 = (bf16[128,768]{1,0:T(8,128)(2,1)S(1)}, bf16[128,768]{1,0:T(8,128)(2,1)S(1)}, u32[]{:S(2)}, u32[]{:S(2)}) collective-permute-start(bf16[128,768]{1,0:T(8,128)(2,1)S(1)} %get-tuple-element.95), channel_id=1, source_target_pairs={{0,1},{1,2},{2,3},{3,4},{4,5},{5,6},{6,7},{7,0},{16,23},{17,16},{1... | collective-permute-start | bytes 589832 | tf_op jit(solution)/shard_map/ppermute | solution.py:53
  50.2 11.4 %collective-permute-start.9 = (bf16[128,768]{1,0:T(8,128)(2,1)S(1)}, bf16[128,768]{1,0:T(8,128)(2,1)S(1)}, u32[]{:S(2)}, u32[]{:S(2)}) collective-permute-start(bf16[128,768]{1,0:T(8,128)(2,1)S(1)} %get-tuple-element.96), channel_id=1, source_target_pairs={{0,7},{1,0},{2,1},{3,2},{4,3},{5,4},{6,5},{7,6},{16,17},{17,18},{1... | collective-permute-start | bytes 589832 | tf_op jit(solution)/shard_map/ppermute | solution.py:53
  63.1 6.9 %collective-permute-start.7 = (bf16[128,768]{1,0:T(8,128)(2,1)S(1)}, bf16[128,768]{1,0:T(8,128)(2,1)S(1)}, u32[]{:S(2)}, u32[]{:S(2)}) collective-permute-start(bf16[128,768]{1,0:T(8,128)(2,1)S(1)} %get-tuple-element.93), channel_id=1, source_target_pairs={{0,1},{1,2},{2,3},{3,4},{4,5},{5,6},{6,7},{7,0},{16,23},{17,16},{1... | collective-permute-start | bytes 589832 | tf_op jit(solution)/shard_map/ppermute | solution.py:53
  86.8 10.0 %collective-permute-start.13 = (bf16[128,768]{1,0:T(8,128)(2,1)S(1)}, bf16[128,768]{1,0:T(8,128)(2,1)S(1)}, u32[]{:S(2)}, u32[]{:S(2)}) collective-permute-start(bf16[128,768]{1,0:T(8,128)(2,1)S(1)} %multiply_convert_fusion.refs_0_), channel_id=1, source_target_pairs={{0,1},{1,2},{2,3},{3,4},{4,5},{5,6},{6,7},{7,0},{16,23},{17,16},{1... | collective-permute-start | bytes 589832 | tf_op jit(solution)/shard_map/ppermute | solution.py:53
  92.2 7.8 %collective-permute-start.14 = (bf16[128,768]{1,0:T(8,128)(2,1)S(1)}, bf16[128,768]{1,0:T(8,128)(2,1)S(1)}, u32[]{:S(2)}, u32[]{:S(2)}) collective-permute-start(bf16[128,768]{1,0:T(8,128)(2,1)S(1)} %multiply_convert_fusion.refs_0_), channel_id=1, source_target_pairs={{0,7},{1,0},{2,1},{3,2},{4,3},{5,4},{6,5},{7,6},{16,17},{17,18},{1... | collective-permute-start | bytes 589832 | tf_op jit(solution)/shard_map/ppermute | solution.py:53
  92.2 7.8 %collective-permute-start.15 = (bf16[128,768]{1,0:T(8,128)(2,1)S(1)}, bf16[128,768]{1,0:T(8,128)(2,1)S(1)}, u32[]{:S(2)}, u32[]{:S(2)}) collective-permute-start(bf16[128,768]{1,0:T(8,128)(2,1)S(1)} %multiply_convert_fusion.refs_0_), channel_id=1, source_target_pairs={{0,8},{8,0},{1,9},{9,1},{2,10},{10,2},{3,11},{11,3},{4,12},{12,4},... | collective-permute-start | bytes 589832 | tf_op jit(solution)/shard_map/ppermute | solution.py:47
  100.0 10.8 %collective-permute-start.18 = (bf16[128,768]{1,0:T(8,128)(2,1)S(1)}, bf16[128,768]{1,0:T(8,128)(2,1)S(1)}, u32[]{:S(2)}, u32[]{:S(2)}) collective-permute-start(bf16[128,768]{1,0:T(8,128)(2,1)S(1)} %collective-permute-done.14), channel_id=1, source_target_pairs={{0,7},{1,0},{2,1},{3,2},{4,3},{5,4},{6,5},{7,6},{16,17},{17,18},{1... | collective-permute-start | bytes 589832 | tf_op jit(solution)/shard_map/ppermute | solution.py:53
  100.1 9.7 %collective-permute-start.16 = (bf16[128,768]{1,0:T(8,128)(2,1)S(1)}, bf16[128,768]{1,0:T(8,128)(2,1)S(1)}, u32[]{:S(2)}, u32[]{:S(2)}) collective-permute-start(bf16[128,768]{1,0:T(8,128)(2,1)S(1)} %collective-permute-done.13), channel_id=1, source_target_pairs={{0,1},{1,2},{2,3},{3,4},{4,5},{5,6},{6,7},{7,0},{16,23},{17,16},{1... | collective-permute-start | bytes 589832 | tf_op jit(solution)/shard_map/ppermute | solution.py:53
  102.8 10.9 %collective-permute-start.20 = (bf16[256,768]{1,0:T(8,128)(2,1)S(1)}, bf16[256,768]{1,0:T(8,128)(2,1)S(1)}, u32[]{:S(2)}, u32[]{:S(2)}) collective-permute-start(bf16[256,768]{1,0:T(8,128)(2,1)S(1)} %constant_dynamic-update-slice_fusion.refs_2_), channel_id=1, source_target_pairs={{0,8},{8,0},{1,9},{9,1},{2,10},{10,2},{3,11},{11,3},{4,12},{12,4},... | collective-permute-start | bytes 1179656 | tf_op jit(solution)/shard_map/ppermute | solution.py:47
  109.8 9.2 %collective-permute-start.17 = (bf16[128,768]{1,0:T(8,128)(2,1)S(1)}, bf16[128,768]{1,0:T(8,128)(2,1)S(1)}, u32[]{:S(2)}, u32[]{:S(2)}) collective-permute-start(bf16[128,768]{1,0:T(8,128)(2,1)S(1)} %collective-permute-done.16), channel_id=1, source_target_pairs={{0,1},{1,2},{2,3},{3,4},{4,5},{5,6},{6,7},{7,0},{16,23},{17,16},{1... | collective-permute-start | bytes 589832 | tf_op jit(solution)/shard_map/ppermute | solution.py:53
  110.8 11.0 %collective-permute-start.19 = (bf16[128,768]{1,0:T(8,128)(2,1)S(1)}, bf16[128,768]{1,0:T(8,128)(2,1)S(1)}, u32[]{:S(2)}, u32[]{:S(2)}) collective-permute-start(bf16[128,768]{1,0:T(8,128)(2,1)S(1)} %collective-permute-done.18), channel_id=1, source_target_pairs={{0,7},{1,0},{2,1},{3,2},{4,3},{5,4},{6,5},{7,6},{16,17},{17,18},{1... | collective-permute-start | bytes 589832 | tf_op jit(solution)/shard_map/ppermute | solution.py:53
  111.7 18.6 %collective-permute-start.24 = (bf16[256,768]{1,0:T(8,128)(2,1)S(1)}, bf16[256,768]{1,0:T(8,128)(2,1)S(1)}, u32[]{:S(2)}, u32[]{:S(2)}) collective-permute-start(bf16[256,768]{1,0:T(8,128)(2,1)S(1)} %constant_dynamic-update-slice_fusion.4.refs_1_), channel_id=1, source_target_pairs={{0,8},{8,0},{1,9},{9,1},{2,10},{10,2},{3,11},{11,3},{4,12},{12,4},... | collective-permute-start | bytes 1179656 | tf_op jit(solution)/shard_map/ppermute | solution.py:47
  121.9 15.1 %collective-permute-start.21 = (bf16[256,768]{1,0:T(8,128)(2,1)S(1)}, bf16[256,768]{1,0:T(8,128)(2,1)S(1)}, u32[]{:S(2)}, u32[]{:S(2)}) collective-permute-start(bf16[256,768]{1,0:T(8,128)(2,1)S(1)} %constant_dynamic-update-slice_fusion.2.refs_0_), channel_id=1, source_target_pairs={{0,8},{8,0},{1,9},{9,1},{2,10},{10,2},{3,11},{11,3},{4,12},{12,4},... | collective-permute-start | bytes 1179656 | tf_op jit(solution)/shard_map/ppermute | solution.py:47
  128.6 8.4 %collective-permute-start.23 = (bf16[128,768]{1,0:T(8,128)(2,1)S(1)}, bf16[128,768]{1,0:T(8,128)(2,1)S(1)}, u32[]{:S(2)}, u32[]{:S(2)}) collective-permute-start(bf16[128,768]{1,0:T(8,128)(2,1)S(1)} %collective-permute-done.22.refs_2_), channel_id=1, source_target_pairs={{0,8},{8,0},{1,9},{9,1},{2,10},{10,2},{3,11},{11,3},{4,12},{12,4},... | collective-permute-start | bytes 589832 | tf_op jit(solution)/shard_map/ppermute | solution.py:47
  145.8 7.5 %collective-permute-start.25 = (bf16[8,80,640]{2,1,0:T(8,128)(2,1)}, bf16[8,80,640]{2,1,0:T(8,128)(2,1)S(1)}, u32[]{:S(2)}, u32[]{:S(2)}) collective-permute-start(bf16[8,80,640]{2,1,0:T(8,128)(2,1)} %get-tuple-element.87), channel_id=1, source_target_pairs={{0,16},{16,0},{1,17},{17,1},{2,18},{18,2},{3,19},{19,3},{4,20},{20... | collective-permute-start | bytes 2457608 | tf_op jit(solution)/shard_map/ppermute | solution.py:47
  (17 other events, 99.7 us)
Sparse Core Ops, SparseCore 0:
  17.8 44.1 all-gather.1
  100.1 39.4 reduce-scatter.1

commit v8 on v7

--- a/solution.py
+++ b/solution.py
@@ -51,6 +51,17 @@
     perm = [(i, (i + step) % RING) for i in range(RING)]
     perm += [(RING + i, RING + (i - step) % RING) for i in range(RING)]
     return lax.ppermute(value, ("core", "z"), perm)
+
+
+def shift_across(value, step):
+    to = lambda core, half, place: (core * 2 + half) * RING + place % RING
+    perm = [
+        (to(core, half, place), to(core, 1 - half, place + (step if core == 0 else -step)))
+        for core in range(2)
+        for half in range(2)
+        for place in range(RING)
+    ]
+    return lax.ppermute(value, ("core", "yhi", "z"), perm)
 
 
 GROUPS = (
@@ -239,6 +250,19 @@
     )(packed, *args)
 
 
+def score_kernel(embed_ref, grad_ref, out_ref):
+    wide, inverse = unit_rows(embed_ref[...])
+    out_ref[...] = unit_backward(wide, inverse, grad_ref[...].astype(f32))
+
+
+def score_backward(score_embed, grad_score):
+    return pl.pallas_call(
+        score_kernel,
+        out_shape=jax.ShapeDtypeStruct(score_embed.shape, f32),
+        compiler_params=pltpu.CompilerParams(vmem_limit_bytes=VMEM_BYTES),
+    )(score_embed, grad_score)
+
+
 def total_of(*terms):
     return sum(term.astype(f32) for term in terms)
 
@@ -257,11 +281,9 @@
             saved[block] = (block, kept, at)
         return parts, down_head
 
+    score_half = lax.all_gather(score_embed, "z", axis=0, tiled=True)
     (other4, other3, own4), down_head = forward(0, down_weight, head_weight)
     came4, came3 = swap(other4, "yhi"), swap(other3, "yhi")
-    score_wide, score_inverse = unit_rows(score_embed)
-    score_unit, up_t = lax.optimization_barrier((score_wide.astype(bf16), up_t))
-    score_half = lax.all_gather(score_unit, "z", axis=0, tiled=True)
     (other2, own3), _ = forward(1, down_head)
     came2 = swap(other2, "yhi")
     fore = shift(total_of(own4, came4).astype(bf16), 1)
@@ -273,6 +295,8 @@
     for own, came in ((own2, came2), (own1, came1)):
         fore = shift(total_of(own[:rows], came[:rows], fore).astype(bf16), 1)
         back = shift(total_of(own[rows : 2 * rows], came[rows : 2 * rows], back).astype(bf16), -1)
+    score_unit = unit_rows(score_half)[0].astype(bf16)
+    fore, back, score_unit = lax.optimization_barrier((fore, back, score_unit))
     own_start = y_hi * group_half + z * rows
     own_hidden = lax.dynamic_slice_in_dim(hidden_in, own_start, rows, 0)
     own_proj = dot(own_hidden, head_weight)
@@ -283,8 +307,8 @@
     partners = jnp.concatenate(
         [lax.dynamic_slice_in_dim(pair_index[0], start, rows, 0) for start in (own_start, far_start)]
     )
-    coeffs = pair_coeffs(audio_unit, score_half, partners, y_hi * group_half)
-    grad_audio = dot(coeffs, score_half)
+    coeffs = pair_coeffs(audio_unit, score_unit, partners, y_hi * group_half)
+    grad_audio = dot(coeffs, score_unit)
     grad_audio = grad_audio[:rows] + swap(grad_audio[rows:].astype(bf16), "yhi").astype(f32)
     grad_embed = unit_backward(audio_wide, audio_inverse, grad_audio).astype(bf16)
     score_part = dot(coeffs, audio_unit, ((0,), (0,))).astype(bf16)
@@ -294,7 +318,6 @@
     crossed0 = swap(grad_embed, "yhi")
     fore, back = shift(grad_embed, 1), shift(grad_embed, -1)
     fore, back, crossed0, score_part = lax.optimization_barrier((fore, back, crossed0, score_part))
-    grad_score = lax.psum_scatter(score_part, "z", scatter_dimension=0, tiled=True)
     ring1 = both(back, fore)
     crossed1 = swap(ring1, "yhi")
     fore, back = shift(fore, 1), shift(back, -1)
@@ -303,22 +326,21 @@
     fore, back = shift(fore, 1), shift(back, -1)
     backward = lambda items, sums, *head: backward_blocks(items, packed, hidden_in, down_head, sums, *head)
     sums = backward([item(grad_embed, (0, 0)), item(crossed0, (1, 0)), item(ring1, *pair(1, 0))], None)
-    fore, back, crossed1, sums = lax.optimization_barrier((fore, back, crossed1, sums))
-    ring4 = shift(fore, 1)
+    sums = backward([item(crossed1, *pair(1, 1)), item(ring2, *pair(2, 0))], sums)
+    fore, back, sums, score_part = lax.optimization_barrier((fore, back, sums, score_part))
+    grad_score = lax.psum_scatter(score_part, "z", scatter_dimension=0, tiled=True)
+    ring4, crossed4 = shift(fore, 1), shift_across(fore, 1)
     ring3 = both(back, fore)
     crossed3 = swap(ring3, "yhi")
-    sums = backward([item(crossed1, *pair(1, 1)), item(ring2, *pair(2, 0))], sums)
-    ring4, sums = lax.optimization_barrier((ring4, sums))
-    crossed4 = swap(ring4, "yhi")
-    sums = backward([item(ring3, *pair(3, 0)), item(crossed2, *pair(2, 1)), item(ring4, (0, 4))], sums)
-    crossed4, sums = lax.optimization_barrier((crossed4, sums))
-    keep, give = backward([item(crossed3, *pair(3, 1)), item(crossed4, (1, 4))], sums, head_weight)
+    sums = backward([item(ring3, *pair(3, 0)), item(crossed2, *pair(2, 1))], sums)
+    ring4, crossed4, sums = lax.optimization_barrier((ring4, crossed4, sums))
+    items = [item(crossed3, *pair(3, 1)), item(ring4, (0, 4)), item(crossed4, (1, 4))]
+    keep, give = backward(items, sums, head_weight)
     chip = total_of(keep, swap(give, "core")).astype(bf16)
-    score_grad = unit_backward(score_wide, score_inverse, grad_score.astype(f32))
-    chip, score_grad = lax.optimization_barrier((chip, score_grad))
     landed = lax.all_to_all(chip, ("ylo", "x"), 0, 0)
     total = jnp.sum(landed.astype(f32), axis=0)
     ff = up_weight.shape[1]
+    score_grad = score_backward(score_embed, grad_score)
     return (total[:, :ff], total[:, ff:].T, score_grad)
 
 

time: 184 us -> 181 us (0.984)
  waiting for transfers between devices: 38.9 us -> 26.6 us
  starting transfers between devices: 48.8 us -> 59.2 us
    ppermute x14, waiting for transfers between devices: 23.8 us -> 3.14 us  [shift(): return lax.ppermute(value, ('core', 'z'), perm)]
    ppermute x12 -> x11, starting transfers between devices: 26.6 us -> 38.2 us  [swap(): return lax.ppermute(value, axis, [(0, 1), (1, 0)])]
    ppermute x12 -> x11, waiting for transfers between devices: 15 us -> 22.7 us  [swap(): return lax.ppermute(value, axis, [(0, 1), (1, 0)])]
    ppermute x14, starting transfers between devices: 22.1 us -> 18.4 us  [shift(): return lax.ppermute(value, ('core', 'z'), perm)]
    ppermute x0 -> x1, starting transfers between devices: none -> 2.58 us  [shift_across(): return lax.ppermute(value, ('core', 'yhi', 'z'), perm)]
    pallas_call x0 -> x1, Pallas kernels: none -> 1.99 us  [score_backward(): pl.pallas_call(score_kernel, out_shape=jax.ShapeDtypeStruct(score_embed.s...]
    mul x1 -> x0, other arithmetic: 1.87 us -> none  [unit_backward(): return inverse * (grad_unit - unit_wide * inner)]
  transfers between devices with their start and end apart: 28 -> 28, of which waited for: 16 -> 11; matrix products, arithmetic and copies ran while one was open for 7% -> 8% of each run, Pallas kernels for 20% -> 23%
where the time goes in v8:
time: 181 us
  starting transfers between devices  59.2 us (33%)
  Pallas kernels  43.4 us (24%)
  waiting for transfers between devices  26.6 us (15%)
  blocking collectives  17.5 us (10%)
  between operations  14.3 us (8%)
  other arithmetic  10.6 us (6%)
  matrix products  4.62 us (3%)
  local copies, waits for them, and re-layouts  4.56 us (3%)
    ppermute x11, starting transfers between devices, swap(): return lax.ppermute(value, axis, [(0, 1), (1, 0)])  38.2 us
    ppermute x11, waiting for transfers between devices, swap(): return lax.ppermute(value, axis, [(0, 1), (1, 0)])  22.7 us
    pallas_call x4, Pallas kernels, backward_blocks(): pl.pallas_call(functools.partial(backward_kernel, len(items), len(places)...  22.3 us
    pallas_call x4, Pallas kernels, forward_blocks(): pl.pallas_call(functools.partial(forward_kernel, pieces, first), grid_spe...  19.1 us
    ppermute x14, starting transfers between devices, shift(): return lax.ppermute(value, ('core', 'z'), perm)  18.4 us
    all_to_all x1, blocking collectives, per_device(): landed = lax.all_to_all(chip, ('ylo', 'x'), 0, 0)  17.5 us
    dot_general x4, matrix products, dot(): lax.dot_general(left, right, (dims, ((), ())), preferred_element_type=f32)  4.62 us
  transfers between devices with their start and end apart: 28, of which 11 were waited for; matrix products, arithmetic and copies ran while one was open for 8% of the time, Pallas kernels for 23%

profile of v8, /device:TPU:1, one launch (start us, length us, event | category | flops | bytes accessed | tf_op | source)
XLA Modules:
  0.0 180.9 jit_solution(1426742502382532933)
XLA Ops:
  8.0 5.6 %shard_map.85 = (bf16[128,768]{1,0:T(8,128)(2,1)}, bf16[256,768]{1,0:T(8,128)(2,1)}, bf16[128,768]{1,0:T(8,128)(2,1)}, bf16[4,320,128]{2,1,0:T(8,128)(2,1)}, bf1...) custom-call(s32[1]{0:T(128)} %bitcast.packed_ref, bf16[2048,1280]{1,0:T(8,128)(2,1)} %refs_12_.3, ...), custom_call_target="tpu_custom_call" | custom-call | flops 671088640 | bytes 4063232 | tf_op jit(solution)/shard_map/pallas_call | solution.py:141
  13.6 3.7 %collective-permute-start.3 = (bf16[128,768]{1,0:T(8,128)(2,1)}, bf16[128,768]{1,0:T(8,128)(2,1)S(1)}, u32[]{:S(2)}, u32[]{:S(2)}) collective-permute-start(bf16[128,768]{1,0:T(8,128)(2,1)} %get-tuple-element.52), channel_id=1, source_target_pairs={{0,8},{8,0},{1,9},{9,1},{2,10},{10,2},{3,11},{11,3},{4,12},{12,4},... | collective-permute-start | bytes 589832 | tf_op jit(solution)/shard_map/ppermute | solution.py:47
  17.4 3.8 %collective-permute-done.3 = bf16[128,768]{1,0:T(8,128)(2,1)S(1)} collective-permute-done((bf16[128,768]{1,0:T(8,128)(2,1)}, bf16[128,768]{1,0:T(8,128)(2,1)S(1)}, u32[]{:S(2)}, u32[]{:S(2)}) %collective-permute-start.3) | collective-permute-done | bytes 196640 | tf_op jit(solution)/shard_map/ppermute | solution.py:47
  22.2 6.3 %collective-permute-start.4 = (bf16[128,768]{1,0:T(8,128)(2,1)S(1)}, bf16[128,768]{1,0:T(8,128)(2,1)S(1)}, u32[]{:S(2)}, u32[]{:S(2)}) collective-permute-start(bf16[128,768]{1,0:T(8,128)(2,1)S(1)} %add_convert_fusion.7), channel_id=1, source_target_pairs={{0,1},{1,2},{2,3},{3,4},{4,5},{5,6},{6,7},{7,0},{16,23},{17,16},{1... | collective-permute-start | bytes 589832 | tf_op jit(solution)/shard_map/ppermute | solution.py:53
  28.5 4.4 %shard_map.88 = (bf16[256,768]{1,0:T(8,128)(2,1)}, bf16[256,768]{1,0:T(8,128)(2,1)}, bf16[4,320,128]{2,1,0:T(8,128)(2,1)}, bf16[4,128,320]{2,1,0:T(8,128)(2,1)}) custom-call(s32[1]{0:T(128)} %bitcast.packed_ref, bf16[2048,1280]{1,0:T(8,128)(2,1)} %refs_12_.3, bf16[2048,1280]{1,0:T(8,128)(2,1)} %refs_12_.3, bf16[2048,1280]{1,0:T(8,128)(2,1)} %refs_12_.3, ...), custom_call_target="tpu_custom_call" | custom-call | flops 671088640 | bytes 4063232 | tf_op jit(solution)/shard_map/pallas_call | solution.py:141
  32.9 3.0 %collective-permute-start.1 = (bf16[256,768]{1,0:T(8,128)(2,1)}, bf16[256,768]{1,0:T(8,128)(2,1)S(1)}, u32[]{:S(2)}, u32[]{:S(2)}) collective-permute-start(bf16[256,768]{1,0:T(8,128)(2,1)} %get-tuple-element.48), channel_id=1, source_target_pairs={{0,8},{8,0},{1,9},{9,1},{2,10},{10,2},{3,11},{11,3},{4,12},{12,4},... | collective-permute-start | bytes 1179656 | tf_op jit(solution)/shard_map/ppermute | solution.py:47
  39.2 5.1 %shard_map.87 = (bf16[384,768]{1,0:T(8,128)(2,1)}, bf16[256,768]{1,0:T(8,128)(2,1)}, bf16[5,320,128]{2,1,0:T(8,128)(2,1)}, bf16[5,128,320]{2,1,0:T(8,128)(2,1)}) custom-call(s32[1]{0:T(128)} %bitcast.packed_ref, bf16[2048,1280]{1,0:T(8,128)(2,1)} %refs_12_.3, bf16[2048,1280]{1,0:T(8,128)(2,1)} %refs_12_.3, bf16[2048,1280]{1,0:T(8,128)(2,1)} %refs_12_.3, ...), custom_call_target="tpu_custom_call" | custom-call | flops 838860800 | bytes 4751360 | tf_op jit(solution)/shard_map/pallas_call | solution.py:141
  44.3 2.6 %collective-permute-start = (bf16[384,768]{1,0:T(8,128)(2,1)}, bf16[384,768]{1,0:T(8,128)(2,1)S(1)}, u32[]{:S(2)}, u32[]{:S(2)}) collective-permute-start(bf16[384,768]{1,0:T(8,128)(2,1)} %get-tuple-element.46), channel_id=1, source_target_pairs={{0,8},{8,0},{1,9},{9,1},{2,10},{10,2},{3,11},{11,3},{4,12},{12,4},... | collective-permute-start | bytes 1769480 | tf_op jit(solution)/shard_map/ppermute | solution.py:47
  53.4 4.0 %shard_map.86 = (bf16[384,768]{1,0:T(8,128)(2,1)}, bf16[3,320,128]{2,1,0:T(8,128)(2,1)}, bf16[3,128,320]{2,1,0:T(8,128)(2,1)}) custom-call(s32[1]{0:T(128)} %bitcast.packed_ref, bf16[2048,1280]{1,0:T(8,128)(2,1)} %refs_12_.3, bf16[2048,1280]{1,0:T(8,128)(2,1)} %refs_12_.3, bf16[2048,1280]{1,0:T(8,128)(2,1)} %refs_12_.3, bf16[320,1280]{1,0:T(8,128)(2,1)} %bitcast.16, ...), custom_call_target="tpu_custom_call" | custom-call | flops 503316480 | bytes 3375104 | tf_op jit(solution)/shard_map/pallas_call | solution.py:141
  66.7 3.4 %collective-permute-start.11 = (bf16[128,768]{1,0:T(8,128)(2,1)S(1)}, bf16[128,768]{1,0:T(8,128)(2,1)S(1)}, u32[]{:S(2)}, u32[]{:S(2)}) collective-permute-start(bf16[128,768]{1,0:T(8,128)(2,1)S(1)} %multiply_convert_fusion.1), channel_id=1, source_target_pairs={{0,8},{8,0},{1,9},{9,1},{2,10},{10,2},{3,11},{11,3},{4,12},{12,4},... | collective-permute-start | bytes 589832 | tf_op jit(solution)/shard_map/ppermute | solution.py:47
  70.1 3.0 %collective-permute-done.11 = bf16[128,768]{1,0:T(8,128)(2,1)S(1)} collective-permute-done((bf16[128,768]{1,0:T(8,128)(2,1)S(1)}, bf16[128,768]{1,0:T(8,128)(2,1)S(1)}, u32[]{:S(2)}, u32[]{:S(2)}) %collective-permute-start.11) | collective-permute-done | bytes 196640 | tf_op jit(solution)/shard_map/ppermute | solution.py:47
  74.6 3.0 %collective-permute-start.12 = (bf16[128,768]{1,0:T(8,128)(2,1)S(1)}, bf16[128,768]{1,0:T(8,128)(2,1)S(1)}, u32[]{:S(2)}, u32[]{:S(2)}) collective-permute-start(bf16[128,768]{1,0:T(8,128)(2,1)S(1)} %slice.105), channel_id=1, source_target_pairs={{0,8},{8,0},{1,9},{9,1},{2,10},{10,2},{3,11},{11,3},{4,12},{12,4},... | collective-permute-start | bytes 589832 | tf_op jit(solution)/shard_map/ppermute | solution.py:47
  77.6 4.8 %collective-permute-done.12 = bf16[128,768]{1,0:T(8,128)(2,1)S(1)} collective-permute-done((bf16[128,768]{1,0:T(8,128)(2,1)S(1)}, bf16[128,768]{1,0:T(8,128)(2,1)S(1)}, u32[]{:S(2)}, u32[]{:S(2)}) %collective-permute-start.12) | collective-permute-done | bytes 196640 | tf_op jit(solution)/shard_map/ppermute | solution.py:47
  84.4 3.0 %collective-permute-start.15 = (bf16[128,768]{1,0:T(8,128)(2,1)S(1)}, bf16[128,768]{1,0:T(8,128)(2,1)S(1)}, u32[]{:S(2)}, u32[]{:S(2)}) collective-permute-start(bf16[128,768]{1,0:T(8,128)(2,1)S(1)} %multiply_convert_fusion.refs_0_), channel_id=1, source_target_pairs={{0,8},{8,0},{1,9},{9,1},{2,10},{10,2},{3,11},{11,3},{4,12},{12,4},... | collective-permute-start | bytes 589832 | tf_op jit(solution)/shard_map/ppermute | solution.py:47
  92.5 2.7 %collective-permute-start.16 = (bf16[128,768]{1,0:T(8,128)(2,1)S(1)}, bf16[128,768]{1,0:T(8,128)(2,1)S(1)}, u32[]{:S(2)}, u32[]{:S(2)}) collective-permute-start(bf16[128,768]{1,0:T(8,128)(2,1)S(1)} %collective-permute-done.13), channel_id=1, source_target_pairs={{0,1},{1,2},{2,3},{3,4},{4,5},{5,6},{6,7},{7,0},{16,23},{17,16},{1... | collective-permute-start | bytes 589832 | tf_op jit(solution)/shard_map/ppermute | solution.py:53
  95.2 3.3 %collective-permute-start.20 = (bf16[256,768]{1,0:T(8,128)(2,1)S(1)}, bf16[256,768]{1,0:T(8,128)(2,1)S(1)}, u32[]{:S(2)}, u32[]{:S(2)}) collective-permute-start(bf16[256,768]{1,0:T(8,128)(2,1)S(1)} %constant_dynamic-update-slice_fusion.refs_2_), channel_id=1, source_target_pairs={{0,8},{8,0},{1,9},{9,1},{2,10},{10,2},{3,11},{11,3},{4,12},{12,4},... | collective-permute-start | bytes 1179656 | tf_op jit(solution)/shard_map/ppermute | solution.py:47
  98.5 4.4 %shard_map.89 = (f32[320,1280]{1,0:T(8,128)}, f32[320,768]{1,0:T(8,128)}) custom-call(s32[1]{0:T(128)} %bitcast.packed_ref, bf16[128,768]{1,0:T(8,128)(2,1)} %copy-done.5, bf16[128,768]{1,0:T(8,128)(2,1)} %copy-done.9, bf16[256,768]{1,0:T(8,128)(2,1)} %copy-done.3, bf16[2048,1280]{1,0:T(8,128)(2,1)} %refs_12_.3, ...), custom_call_target="tpu_custom_call" | custom-call | flops 922746880 | bytes 8388608 | tf_op jit(solution)/shard_map/pallas_call | solution.py:237
  106.6 5.2 %shard_map.90 = (f32[320,1280]{1,0:T(8,128)}, f32[320,768]{1,0:T(8,128)}) custom-call(s32[1]{0:T(128)} %bitcast.packed_ref, bf16[256,768]{1,0:T(8,128)(2,1)} %copy-done.7, bf16[256,768]{1,0:T(8,128)(2,1)} %copy-done.2, bf16[2048,1280]{1,0:T(8,128)(2,1)} %refs_12_.3, ...), custom_call_target="tpu_custom_call", output_to_operand_aliasing={{0}: (16, {}), {1}: (17, {})} | custom-call | flops 922746880 | bytes 8388608 | tf_op jit(solution)/shard_map/pallas_call | solution.py:237
  111.8 3.1 %collective-permute-start.24 = (bf16[256,768]{1,0:T(8,128)(2,1)}, bf16[256,768]{1,0:T(8,128)(2,1)S(1)}, u32[]{:S(2)}, u32[]{:S(2)}) collective-permute-start(bf16[256,768]{1,0:T(8,128)(2,1)} %copy-done.2), channel_id=1, source_target_pairs={{0,8},{8,0},{1,9},{9,1},{2,10},{10,2},{3,11},{11,3},{4,12},{12,4},... | collective-permute-start | bytes 1179656 | tf_op jit(solution)/shard_map/ppermute | solution.py:47
  117.7 5.1 %collective-permute-done.24.refs_1_ = bf16[256,768]{1,0:T(8,128)(2,1)S(1)} collective-permute-done((bf16[256,768]{1,0:T(8,128)(2,1)}, bf16[256,768]{1,0:T(8,128)(2,1)S(1)}, u32[]{:S(2)}, u32[]{:S(2)}) %collective-permute-start.24) | collective-permute-done | bytes 393248 | tf_op jit(solution)/shard_map/ppermute | solution.py:47
  123.5 5.2 %shard_map.91 = (f32[320,1280]{1,0:T(8,128)}, f32[320,768]{1,0:T(8,128)}) custom-call(s32[1]{0:T(128)} %bitcast.packed_ref, bf16[256,768]{1,0:T(8,128)(2,1)} %copy-done.4, bf16[256,768]{1,0:T(8,128)(2,1)} %copy-done.8, bf16[2048,1280]{1,0:T(8,128)(2,1)} %refs_12_.3, ...), custom_call_target="tpu_custom_call", output_to_operand_aliasing={{0}: (16, {}), {1}: (17, {})} | custom-call | flops 922746880 | bytes 8388608 | tf_op jit(solution)/shard_map/pallas_call | solution.py:237
  129.6 7.6 %shard_map.92 = (bf16[8,80,640]{2,1,0:T(8,128)(2,1)}, bf16[8,80,640]{2,1,0:T(8,128)(2,1)}) custom-call(s32[1]{0:T(128)} %bitcast.packed_ref, bf16[256,768]{1,0:T(8,128)(2,1)} %copy-done.6, bf16[128,768]{1,0:T(8,128)(2,1)} %copy-done.10, bf16[128,768]{1,0:T(8,128)(2,1)} %copy-done.11, bf16[2048,1280]{1,0:T(8,128)(2,1)} %refs_12_.3, ...), custom_call_target="tpu_custom_call" | custom-call | flops 1551892480 | bytes 8388608 | tf_op jit(solution)/shard_map/pallas_call | solution.py:237
  137.2 13.0 %collective-permute-start.25 = (bf16[8,80,640]{2,1,0:T(8,128)(2,1)}, bf16[8,80,640]{2,1,0:T(8,128)(2,1)S(1)}, u32[]{:S(2)}, u32[]{:S(2)}) collective-permute-start(bf16[8,80,640]{2,1,0:T(8,128)(2,1)} %get-tuple-element.83), channel_id=1, source_target_pairs={{0,16},{16,0},{1,17},{17,1},{2,18},{18,2},{3,19},{19,3},{4,20},{20... | collective-permute-start | bytes 2457608 | tf_op jit(solution)/shard_map/ppermute | solution.py:47
  153.7 17.5 %all_to_all.5 = bf16[8,80,640]{2,1,0:T(8,128)(2,1)S(1)} all-to-all(bf16[8,80,640]{2,1,0:T(8,128)(2,1)S(1)} %add_convert_fusion), channel_id=1, replica_groups=mesh['ylo'=2,'x'=4,'core'=2,'yhi'=2,'z'=8] {'ylo','x'}, dimensions={0} | all-to-all | bytes 1638400 | tf_op jit(solution)/shard_map/all_to_all | solution.py:340
  (99 shorter events, 43.9 us)
Async XLA Ops:
  7.2 55.3 %all-gather.2.cloned.1.call-start = ((), (), s32[]{:S(2)}) async-start(), calls=%async_computation.2 | async-start | bytes 1769472 | tf_op jit(solution)/shard_map/all_gather | solution.py:284
  7.9 164.1 %reduce-scatter.2.cloned.1.call-start = ((), (), s32[]{:S(2)}) async-start(), calls=%async_computation.3 | async-start | bytes 1769472 | tf_op jit(solution)/shard_map/reduce_scatter | solution.py:331
  13.6 7.6 %collective-permute-start.3 = (bf16[128,768]{1,0:T(8,128)(2,1)}, bf16[128,768]{1,0:T(8,128)(2,1)S(1)}, u32[]{:S(2)}, u32[]{:S(2)}) collective-permute-start(bf16[128,768]{1,0:T(8,128)(2,1)} %get-tuple-element.52), channel_id=1, source_target_pairs={{0,8},{8,0},{1,9},{9,1},{2,10},{10,2},{3,11},{11,3},{4,12},{12,4},... | collective-permute-start | bytes 589832 | tf_op jit(solution)/shard_map/ppermute | solution.py:47
  17.3 18.6 %collective-permute-start.2 = (bf16[256,768]{1,0:T(8,128)(2,1)}, bf16[256,768]{1,0:T(8,128)(2,1)S(1)}, u32[]{:S(2)}, u32[]{:S(2)}) collective-permute-start(bf16[256,768]{1,0:T(8,128)(2,1)} %get-tuple-element.50), channel_id=1, source_target_pairs={{0,8},{8,0},{1,9},{9,1},{2,10},{10,2},{3,11},{11,3},{4,12},{12,4},... | collective-permute-start | bytes 1179656 | tf_op jit(solution)/shard_map/ppermute | solution.py:47
  22.2 13.7 %collective-permute-start.4 = (bf16[128,768]{1,0:T(8,128)(2,1)S(1)}, bf16[128,768]{1,0:T(8,128)(2,1)S(1)}, u32[]{:S(2)}, u32[]{:S(2)}) collective-permute-start(bf16[128,768]{1,0:T(8,128)(2,1)S(1)} %add_convert_fusion.7), channel_id=1, source_target_pairs={{0,1},{1,2},{2,3},{3,4},{4,5},{5,6},{6,7},{7,0},{16,23},{17,16},{1... | collective-permute-start | bytes 589832 | tf_op jit(solution)/shard_map/ppermute | solution.py:53
  32.9 14.0 %collective-permute-start.1 = (bf16[256,768]{1,0:T(8,128)(2,1)}, bf16[256,768]{1,0:T(8,128)(2,1)S(1)}, u32[]{:S(2)}, u32[]{:S(2)}) collective-permute-start(bf16[256,768]{1,0:T(8,128)(2,1)} %get-tuple-element.48), channel_id=1, source_target_pairs={{0,8},{8,0},{1,9},{9,1},{2,10},{10,2},{3,11},{11,3},{4,12},{12,4},... | collective-permute-start | bytes 1179656 | tf_op jit(solution)/shard_map/ppermute | solution.py:47
  37.7 9.7 %collective-permute-start.5 = (bf16[128,768]{1,0:T(8,128)(2,1)}, bf16[128,768]{1,0:T(8,128)(2,1)S(1)}, u32[]{:S(2)}, u32[]{:S(2)}) collective-permute-start(bf16[128,768]{1,0:T(8,128)(2,1)} %get-tuple-element.92), channel_id=1, source_target_pairs={{0,1},{1,2},{2,3},{3,4},{4,5},{5,6},{6,7},{7,0},{16,23},{17,16},{1... | collective-permute-start | bytes 589832 | tf_op jit(solution)/shard_map/ppermute | solution.py:53
  38.4 10.1 %collective-permute-start.8 = (bf16[128,768]{1,0:T(8,128)(2,1)S(1)}, bf16[128,768]{1,0:T(8,128)(2,1)S(1)}, u32[]{:S(2)}, u32[]{:S(2)}) collective-permute-start(bf16[128,768]{1,0:T(8,128)(2,1)S(1)} %get-tuple-element.91), channel_id=1, source_target_pairs={{0,7},{1,0},{2,1},{3,2},{4,3},{5,4},{6,5},{7,6},{16,17},{17,18},{1... | collective-permute-start | bytes 589832 | tf_op jit(solution)/shard_map/ppermute | solution.py:53
  44.3 13.8 %collective-permute-start = (bf16[384,768]{1,0:T(8,128)(2,1)}, bf16[384,768]{1,0:T(8,128)(2,1)S(1)}, u32[]{:S(2)}, u32[]{:S(2)}) collective-permute-start(bf16[384,768]{1,0:T(8,128)(2,1)} %get-tuple-element.46), channel_id=1, source_target_pairs={{0,8},{8,0},{1,9},{9,1},{2,10},{10,2},{3,11},{11,3},{4,12},{12,4},... | collective-permute-start | bytes 1769480 | tf_op jit(solution)/shard_map/ppermute | solution.py:47
  50.5 7.6 %collective-permute-start.6 = (bf16[128,768]{1,0:T(8,128)(2,1)S(1)}, bf16[128,768]{1,0:T(8,128)(2,1)S(1)}, u32[]{:S(2)}, u32[]{:S(2)}) collective-permute-start(bf16[128,768]{1,0:T(8,128)(2,1)S(1)} %get-tuple-element.90), channel_id=1, source_target_pairs={{0,1},{1,2},{2,3},{3,4},{4,5},{5,6},{6,7},{7,0},{16,23},{17,16},{1... | collective-permute-start | bytes 589832 | tf_op jit(solution)/shard_map/ppermute | solution.py:53
  51.6 6.5 %collective-permute-start.9 = (bf16[128,768]{1,0:T(8,128)(2,1)S(1)}, bf16[128,768]{1,0:T(8,128)(2,1)}, u32[]{:S(2)}, u32[]{:S(2)}) collective-permute-start(bf16[128,768]{1,0:T(8,128)(2,1)S(1)} %get-tuple-element.89), channel_id=1, source_target_pairs={{0,7},{1,0},{2,1},{3,2},{4,3},{5,4},{6,5},{7,6},{16,17},{17,18},{1... | collective-permute-start | bytes 589832 | tf_op jit(solution)/shard_map/ppermute | solution.py:53
  66.7 6.4 %collective-permute-start.11 = (bf16[128,768]{1,0:T(8,128)(2,1)S(1)}, bf16[128,768]{1,0:T(8,128)(2,1)S(1)}, u32[]{:S(2)}, u32[]{:S(2)}) collective-permute-start(bf16[128,768]{1,0:T(8,128)(2,1)S(1)} %multiply_convert_fusion.1), channel_id=1, source_target_pairs={{0,8},{8,0},{1,9},{9,1},{2,10},{10,2},{3,11},{11,3},{4,12},{12,4},... | collective-permute-start | bytes 589832 | tf_op jit(solution)/shard_map/ppermute | solution.py:47
  74.6 7.9 %collective-permute-start.12 = (bf16[128,768]{1,0:T(8,128)(2,1)S(1)}, bf16[128,768]{1,0:T(8,128)(2,1)S(1)}, u32[]{:S(2)}, u32[]{:S(2)}) collective-permute-start(bf16[128,768]{1,0:T(8,128)(2,1)S(1)} %slice.105), channel_id=1, source_target_pairs={{0,8},{8,0},{1,9},{9,1},{2,10},{10,2},{3,11},{11,3},{4,12},{12,4},... | collective-permute-start | bytes 589832 | tf_op jit(solution)/shard_map/ppermute | solution.py:47
  84.4 8.0 %collective-permute-start.15 = (bf16[128,768]{1,0:T(8,128)(2,1)S(1)}, bf16[128,768]{1,0:T(8,128)(2,1)S(1)}, u32[]{:S(2)}, u32[]{:S(2)}) collective-permute-start(bf16[128,768]{1,0:T(8,128)(2,1)S(1)} %multiply_convert_fusion.refs_0_), channel_id=1, source_target_pairs={{0,8},{8,0},{1,9},{9,1},{2,10},{10,2},{3,11},{11,3},{4,12},{12,4},... | collective-permute-start | bytes 589832 | tf_op jit(solution)/shard_map/ppermute | solution.py:47
  92.4 10.6 %collective-permute-start.18 = (bf16[128,768]{1,0:T(8,128)(2,1)S(1)}, bf16[128,768]{1,0:T(8,128)(2,1)S(1)}, u32[]{:S(2)}, u32[]{:S(2)}) collective-permute-start(bf16[128,768]{1,0:T(8,128)(2,1)S(1)} %collective-permute-done.14), channel_id=1, source_target_pairs={{0,7},{1,0},{2,1},{3,2},{4,3},{5,4},{6,5},{7,6},{16,17},{17,18},{1... | collective-permute-start | bytes 589832 | tf_op jit(solution)/shard_map/ppermute | solution.py:53
  92.5 10.4 %collective-permute-start.16 = (bf16[128,768]{1,0:T(8,128)(2,1)S(1)}, bf16[128,768]{1,0:T(8,128)(2,1)S(1)}, u32[]{:S(2)}, u32[]{:S(2)}) collective-permute-start(bf16[128,768]{1,0:T(8,128)(2,1)S(1)} %collective-permute-done.13), channel_id=1, source_target_pairs={{0,1},{1,2},{2,3},{3,4},{4,5},{5,6},{6,7},{7,0},{16,23},{17,16},{1... | collective-permute-start | bytes 589832 | tf_op jit(solution)/shard_map/ppermute | solution.py:53
  95.2 10.6 %collective-permute-start.20 = (bf16[256,768]{1,0:T(8,128)(2,1)S(1)}, bf16[256,768]{1,0:T(8,128)(2,1)S(1)}, u32[]{:S(2)}, u32[]{:S(2)}) collective-permute-start(bf16[256,768]{1,0:T(8,128)(2,1)S(1)} %constant_dynamic-update-slice_fusion.refs_2_), channel_id=1, source_target_pairs={{0,8},{8,0},{1,9},{9,1},{2,10},{10,2},{3,11},{11,3},{4,12},{12,4},... | collective-permute-start | bytes 1179656 | tf_op jit(solution)/shard_map/ppermute | solution.py:47
  102.9 8.8 %collective-permute-start.17 = (bf16[128,768]{1,0:T(8,128)(2,1)S(1)}, bf16[128,768]{1,0:T(8,128)(2,1)S(1)}, u32[]{:S(2)}, u32[]{:S(2)}) collective-permute-start(bf16[128,768]{1,0:T(8,128)(2,1)S(1)} %collective-permute-done.16), channel_id=1, source_target_pairs={{0,1},{1,2},{2,3},{3,4},{4,5},{5,6},{6,7},{7,0},{16,23},{17,16},{1... | collective-permute-start | bytes 589832 | tf_op jit(solution)/shard_map/ppermute | solution.py:53
  103.0 8.7 %collective-permute-start.19 = (bf16[128,768]{1,0:T(8,128)(2,1)S(1)}, bf16[128,768]{1,0:T(8,128)(2,1)S(1)}, u32[]{:S(2)}, u32[]{:S(2)}) collective-permute-start(bf16[128,768]{1,0:T(8,128)(2,1)S(1)} %collective-permute-done.18), channel_id=1, source_target_pairs={{0,7},{1,0},{2,1},{3,2},{4,3},{5,4},{6,5},{7,6},{16,17},{17,18},{1... | collective-permute-start | bytes 589832 | tf_op jit(solution)/shard_map/ppermute | solution.py:53
  111.8 11.0 %collective-permute-start.24 = (bf16[256,768]{1,0:T(8,128)(2,1)}, bf16[256,768]{1,0:T(8,128)(2,1)S(1)}, u32[]{:S(2)}, u32[]{:S(2)}) collective-permute-start(bf16[256,768]{1,0:T(8,128)(2,1)} %copy-done.2), channel_id=1, source_target_pairs={{0,8},{8,0},{1,9},{9,1},{2,10},{10,2},{3,11},{11,3},{4,12},{12,4},... | collective-permute-start | bytes 1179656 | tf_op jit(solution)/shard_map/ppermute | solution.py:47
  114.9 13.8 %collective-permute-start.21 = (bf16[256,768]{1,0:T(8,128)(2,1)S(1)}, bf16[256,768]{1,0:T(8,128)(2,1)S(1)}, u32[]{:S(2)}, u32[]{:S(2)}) collective-permute-start(bf16[256,768]{1,0:T(8,128)(2,1)S(1)} %constant_dynamic-update-slice_fusion.4.refs_0_), channel_id=1, source_target_pairs={{0,8},{8,0},{1,9},{9,1},{2,10},{10,2},{3,11},{11,3},{4,12},{12,4},... | collective-permute-start | bytes 1179656 | tf_op jit(solution)/shard_map/ppermute | solution.py:47
  115.0 13.7 %collective-permute-start.22 = (bf16[128,768]{1,0:T(8,128)(2,1)S(1)}, bf16[128,768]{1,0:T(8,128)(2,1)S(1)}, u32[]{:S(2)}, u32[]{:S(2)}) collective-permute-start(bf16[128,768]{1,0:T(8,128)(2,1)S(1)} %collective-permute-done.17), channel_id=1, source_target_pairs={{0,1},{1,2},{2,3},{3,4},{4,5},{5,6},{6,7},{7,0},{16,23},{17,16},{1... | collective-permute-start | bytes 589832 | tf_op jit(solution)/shard_map/ppermute | solution.py:53
  115.1 13.6 %collective-permute-start.23 = (bf16[128,768]{1,0:T(8,128)(2,1)S(1)}, bf16[128,768]{1,0:T(8,128)(2,1)S(1)}, u32[]{:S(2)}, u32[]{:S(2)}) collective-permute-start(bf16[128,768]{1,0:T(8,128)(2,1)S(1)} %collective-permute-done.17), channel_id=1, source_target_pairs={{0,9},{1,10},{2,11},{3,12},{4,13},{5,14},{6,15},{7,8},{8,1},{9,2},... | collective-permute-start | bytes 589832 | tf_op jit(solution)/shard_map/ppermute | solution.py:64
  137.2 15.1 %collective-permute-start.25 = (bf16[8,80,640]{2,1,0:T(8,128)(2,1)}, bf16[8,80,640]{2,1,0:T(8,128)(2,1)S(1)}, u32[]{:S(2)}, u32[]{:S(2)}) collective-permute-start(bf16[8,80,640]{2,1,0:T(8,128)(2,1)} %get-tuple-element.83), channel_id=1, source_target_pairs={{0,16},{16,0},{1,17},{17,1},{2,18},{18,2},{3,19},{19,3},{4,20},{20... | collective-permute-start | bytes 2457608 | tf_op jit(solution)/shard_map/ppermute | solution.py:47
  (17 other events, 73.5 us)
Sparse Core Ops, SparseCore 0:
  9.8 42.1 all-gather.1
  111.9 48.1 reduce-scatter.1

commit v9 on v8

--- a/solution.py
+++ b/solution.py
@@ -167,19 +167,26 @@
     act_t, slope = join([ref[0] for ref in kept[1::3]], 1), join([ref[0] for ref in kept[2::3]], 0)
     refs = refs[count + 3 * blocks :]
     down_head_ref, refs = refs[0], refs[1:]
-    if not first:
-        up_in, act_in = refs[:2]
-        refs = refs[2:]
+    copies = []
+    if last:
+        far, (keep_ref, give_ref, total), near, sems = refs[:3], refs[3:6], refs[6:9], refs[9]
+        copies = [pltpu.make_async_copy(far[i], near[i], sems.at[i]) for i in range(3)]
+        for copy in copies:
+            copy.start()
+        act_in, up_in, head_ref = near
+    elif not first:
+        up_in, act_in, up_acc, act_acc = refs
+    else:
+        up_acc, act_acc = refs
     tile = 256
     grad_act = dot(grad, down_head_ref[...], ((1,), (1,)))
     grad_pre_t = (grad_act * slope.astype(f32)).astype(bf16).T
     act_sum = dot(act_t, grad)
+    for copy in copies[:2]:
+        copy.wait()
     if not first:
         act_sum = act_sum + act_in[...]
-    if last:
-        head_ref, keep_ref, give_ref, total = refs
-    else:
-        up_acc, act_acc = refs
+    if not last:
         act_acc[...] = act_sum
     width, ff = hidden.shape[1], act_sum.shape[0]
     for m in range(0, width, tile):
@@ -200,6 +207,7 @@
                     at = pl.multiple_of((2 * chip + half) * rows, rows)
                     out_ref[chip, :, side * ff : (side + 1) * ff] = total[pl.ds(at, rows), :].astype(bf16)
             if side == 0:
+                copies[2].wait()
                 for m in range(0, width, tile):
                     total[m : m + tile, :] = dot(head_ref[m : m + tile, :], act_grad, ((1,), (1,)))
 
@@ -223,17 +231,19 @@
     if sums is not None:
         if not last:
             aliases = {len(args) + 1: 0, len(args) + 2: 1}
-        args += list(sums)
-    flops = 2 * len(places) * rows * ff * (2 * embed + width)
+        args += [sums[1], sums[0]] if last else list(sums)
     if last:
         args.append(head_weight)
         shapes = [jax.ShapeDtypeStruct((8, width // 16, 2 * ff), bf16)] * 2
         scratch = [pltpu.VMEM((width, ff), f32)]
-        flops += 2 * width * ff * embed
+        scratch += [pltpu.VMEM(array.shape, array.dtype) for array in args[-3:]]
+        scratch += [pltpu.SemaphoreType.DMA((3,))]
     else:
         shapes = [jax.ShapeDtypeStruct((ff, width), f32), jax.ShapeDtypeStruct((ff, embed), f32)]
         scratch = []
     specs += [whole] * (len(args) - len(specs))
+    if last:
+        specs[-3:] = [pl.BlockSpec(memory_space=pl.ANY)] * 3
     return pl.pallas_call(
         functools.partial(backward_kernel, len(items), len(places), sums is None, last),
         grid_spec=pltpu.PrefetchScalarGridSpec(
@@ -246,7 +256,7 @@
         out_shape=shapes,
         input_output_aliases=aliases,
         compiler_params=pltpu.CompilerParams(vmem_limit_bytes=VMEM_BYTES),
-        cost_estimate=pl.CostEstimate(flops=flops, bytes_accessed=8 * 1024 * 1024, transcendentals=0),
+        cost_estimate=pl.CostEstimate(flops=0, bytes_accessed=0, transcendentals=0),
     )(packed, *args)
 
 
@@ -286,6 +296,7 @@
     came4, came3 = swap(other4, "yhi"), swap(other3, "yhi")
     (other2, own3), _ = forward(1, down_head)
     came2 = swap(other2, "yhi")
+    came4, own3 = lax.optimization_barrier((came4, own3))
     fore = shift(total_of(own4, came4).astype(bf16), 1)
     (other1, own2), _ = forward(2, down_head)
     came1 = swap(other1, "yhi")
@@ -321,14 +332,15 @@
     ring1 = both(back, fore)
     crossed1 = swap(ring1, "yhi")
     fore, back = shift(fore, 1), shift(back, -1)
+    backward = lambda items, sums, *head: backward_blocks(items, packed, hidden_in, down_head, sums, *head)
+    sums = backward([item(grad_embed, (0, 0)), item(crossed0, (1, 0)), item(ring1, *pair(1, 0))], None)
+    fore, back, score_part, sums = lax.optimization_barrier((fore, back, score_part, sums))
+    grad_score = lax.psum_scatter(score_part, "z", scatter_dimension=0, tiled=True)
     ring2 = both(back, fore)
     crossed2 = swap(ring2, "yhi")
     fore, back = shift(fore, 1), shift(back, -1)
-    backward = lambda items, sums, *head: backward_blocks(items, packed, hidden_in, down_head, sums, *head)
-    sums = backward([item(grad_embed, (0, 0)), item(crossed0, (1, 0)), item(ring1, *pair(1, 0))], None)
     sums = backward([item(crossed1, *pair(1, 1)), item(ring2, *pair(2, 0))], sums)
-    fore, back, sums, score_part = lax.optimization_barrier((fore, back, sums, score_part))
-    grad_score = lax.psum_scatter(score_part, "z", scatter_dimension=0, tiled=True)
+    fore, back, sums, crossed2 = lax.optimization_barrier((fore, back, sums, crossed2))
     ring4, crossed4 = shift(fore, 1), shift_across(fore, 1)
     ring3 = both(back, fore)
     crossed3 = swap(ring3, "yhi")
@@ -337,10 +349,11 @@
     items = [item(crossed3, *pair(3, 1)), item(ring4, (0, 4)), item(crossed4, (1, 4))]
     keep, give = backward(items, sums, head_weight)
     chip = total_of(keep, swap(give, "core")).astype(bf16)
+    score_grad = score_backward(score_embed, grad_score)
+    chip, score_grad = lax.optimization_barrier((chip, score_grad))
     landed = lax.all_to_all(chip, ("ylo", "x"), 0, 0)
     total = jnp.sum(landed.astype(f32), axis=0)
     ff = up_weight.shape[1]
-    score_grad = score_backward(score_embed, grad_score)
     return (total[:, :ff], total[:, ff:].T, score_grad)
 
 

time: 181 us -> 186 us (1.028)
  starting transfers between devices: 59.2 us -> 65.6 us
    ppermute x11, waiting for transfers between devices: 22.7 us -> 15.8 us  [swap(): return lax.ppermute(value, axis, [(0, 1), (1, 0)])]
    ppermute x14, waiting for transfers between devices: 3.14 us -> 8.67 us  [shift(): return lax.ppermute(value, ('core', 'z'), perm)]
    ppermute x14, starting transfers between devices: 18.4 us -> 23.1 us  [shift(): return lax.ppermute(value, ('core', 'z'), perm)]
  transfers between devices with their start and end apart: 28 -> 28, of which waited for: 11 -> 12; matrix products, arithmetic and copies ran while one was open for 8% -> 6% of each run, Pallas kernels for 23% -> 23%
where the time goes in v9:
time: 186 us
  starting transfers between devices  65.6 us (35%)
  Pallas kernels  44.3 us (24%)
  waiting for transfers between devices  25.7 us (14%)
  blocking collectives  17.2 us (9%)
  between operations  14.3 us (8%)
  other arithmetic  9.7 us (5%)
  matrix products  4.61 us (2%)
  local copies, waits for them, and re-layouts  4.47 us (2%)
    ppermute x11, starting transfers between devices, swap(): return lax.ppermute(value, axis, [(0, 1), (1, 0)])  39.9 us
    pallas_call x4, Pallas kernels, backward_blocks(): pl.pallas_call(functools.partial(backward_kernel, len(items), len(places)...  23.2 us
    ppermute x14, starting transfers between devices, shift(): return lax.ppermute(value, ('core', 'z'), perm)  23.1 us
    pallas_call x4, Pallas kernels, forward_blocks(): pl.pallas_call(functools.partial(forward_kernel, pieces, first), grid_spe...  19.2 us
    all_to_all x1, blocking collectives, per_device(): landed = lax.all_to_all(chip, ('ylo', 'x'), 0, 0)  17.2 us
    ppermute x11, waiting for transfers between devices, swap(): return lax.ppermute(value, axis, [(0, 1), (1, 0)])  15.8 us
    ppermute x14, waiting for transfers between devices, shift(): return lax.ppermute(value, ('core', 'z'), perm)  8.67 us
    dot_general x4, matrix products, dot(): lax.dot_general(left, right, (dims, ((), ())), preferred_element_type=f32)  4.61 us
  transfers between devices with their start and end apart: 28, of which 12 were waited for; matrix products, arithmetic and copies ran while one was open for 6% of the time, Pallas kernels for 23%

profile of v9, /device:TPU:1, one launch (start us, length us, event | category | flops | bytes accessed | tf_op | source)
XLA Modules:
  0.0 185.9 jit_solution(5933154992090996895)
XLA Ops:
  8.0 5.6 %shard_map.85 = (bf16[128,768]{1,0:T(8,128)(2,1)}, bf16[256,768]{1,0:T(8,128)(2,1)}, bf16[128,768]{1,0:T(8,128)(2,1)}, bf16[4,320,128]{2,1,0:T(8,128)(2,1)}, bf1...) custom-call(s32[1]{0:T(128)} %bitcast.packed_ref, bf16[2048,1280]{1,0:T(8,128)(2,1)} %refs_12_.3, ...), custom_call_target="tpu_custom_call" | custom-call | flops 671088640 | bytes 4063232 | tf_op jit(solution)/shard_map/pallas_call | solution.py:141
  13.6 3.7 %collective-permute-start.2 = (bf16[128,768]{1,0:T(8,128)(2,1)}, bf16[128,768]{1,0:T(8,128)(2,1)S(1)}, u32[]{:S(2)}, u32[]{:S(2)}) collective-permute-start(bf16[128,768]{1,0:T(8,128)(2,1)} %get-tuple-element.58), channel_id=1, source_target_pairs={{0,8},{8,0},{1,9},{9,1},{2,10},{10,2},{3,11},{11,3},{4,12},{12,4},... | collective-permute-start | bytes 589832 | tf_op jit(solution)/shard_map/ppermute | solution.py:47
  17.4 4.5 %shard_map.88 = (bf16[256,768]{1,0:T(8,128)(2,1)}, bf16[256,768]{1,0:T(8,128)(2,1)}, bf16[4,320,128]{2,1,0:T(8,128)(2,1)}, bf16[4,128,320]{2,1,0:T(8,128)(2,1)}) custom-call(s32[1]{0:T(128)} %bitcast.packed_ref, bf16[2048,1280]{1,0:T(8,128)(2,1)} %refs_12_.3, bf16[2048,1280]{1,0:T(8,128)(2,1)} %refs_12_.3, bf16[2048,1280]{1,0:T(8,128)(2,1)} %refs_12_.3, ...), custom_call_target="tpu_custom_call" | custom-call | flops 671088640 | bytes 4063232 | tf_op jit(solution)/shard_map/pallas_call | solution.py:141
  21.9 5.7 %collective-permute-start.4 = (bf16[128,768]{1,0:T(8,128)(2,1)S(1)}, bf16[128,768]{1,0:T(8,128)(2,1)S(1)}, u32[]{:S(2)}, u32[]{:S(2)}) collective-permute-start(bf16[128,768]{1,0:T(8,128)(2,1)S(1)} %add_convert_fusion.7), channel_id=1, source_target_pairs={{0,1},{1,2},{2,3},{3,4},{4,5},{5,6},{6,7},{7,0},{16,23},{17,16},{1... | collective-permute-start | bytes 589832 | tf_op jit(solution)/shard_map/ppermute | solution.py:53
  27.6 2.9 %collective-permute-start.1 = (bf16[256,768]{1,0:T(8,128)(2,1)}, bf16[256,768]{1,0:T(8,128)(2,1)S(1)}, u32[]{:S(2)}, u32[]{:S(2)}) collective-permute-start(bf16[256,768]{1,0:T(8,128)(2,1)} %get-tuple-element.57), channel_id=1, source_target_pairs={{0,8},{8,0},{1,9},{9,1},{2,10},{10,2},{3,11},{11,3},{4,12},{12,4},... | collective-permute-start | bytes 1179656 | tf_op jit(solution)/shard_map/ppermute | solution.py:47
  33.8 3.9 %collective-permute-start.5 = (bf16[128,768]{1,0:T(8,128)(2,1)S(1)}, bf16[128,768]{1,0:T(8,128)(2,1)S(1)}, u32[]{:S(2)}, u32[]{:S(2)}) collective-permute-start(bf16[128,768]{1,0:T(8,128)(2,1)S(1)} %get-tuple-element.110), channel_id=1, source_target_pairs={{0,1},{1,2},{2,3},{3,4},{4,5},{5,6},{6,7},{7,0},{16,23},{17,16},{1... | collective-permute-start | bytes 589832 | tf_op jit(solution)/shard_map/ppermute | solution.py:53
  37.7 5.1 %shard_map.87 = (bf16[384,768]{1,0:T(8,128)(2,1)}, bf16[256,768]{1,0:T(8,128)(2,1)}, bf16[5,320,128]{2,1,0:T(8,128)(2,1)}, bf16[5,128,320]{2,1,0:T(8,128)(2,1)}) custom-call(s32[1]{0:T(128)} %bitcast.packed_ref, bf16[2048,1280]{1,0:T(8,128)(2,1)} %refs_12_.3, bf16[2048,1280]{1,0:T(8,128)(2,1)} %refs_12_.3, bf16[2048,1280]{1,0:T(8,128)(2,1)} %refs_12_.3, ...), custom_call_target="tpu_custom_call" | custom-call | flops 838860800 | bytes 4751360 | tf_op jit(solution)/shard_map/pallas_call | solution.py:141
  42.8 3.0 %collective-permute-start = (bf16[384,768]{1,0:T(8,128)(2,1)}, bf16[384,768]{1,0:T(8,128)(2,1)S(1)}, u32[]{:S(2)}, u32[]{:S(2)}) collective-permute-start(bf16[384,768]{1,0:T(8,128)(2,1)} %get-tuple-element.55), channel_id=1, source_target_pairs={{0,8},{8,0},{1,9},{9,1},{2,10},{10,2},{3,11},{11,3},{4,12},{12,4},... | collective-permute-start | bytes 1769480 | tf_op jit(solution)/shard_map/ppermute | solution.py:47
  52.0 4.0 %shard_map.86 = (bf16[384,768]{1,0:T(8,128)(2,1)}, bf16[3,320,128]{2,1,0:T(8,128)(2,1)}, bf16[3,128,320]{2,1,0:T(8,128)(2,1)}) custom-call(s32[1]{0:T(128)} %bitcast.packed_ref, bf16[2048,1280]{1,0:T(8,128)(2,1)} %refs_12_.3, bf16[2048,1280]{1,0:T(8,128)(2,1)} %refs_12_.3, bf16[2048,1280]{1,0:T(8,128)(2,1)} %refs_12_.3, bf16[320,1280]{1,0:T(8,128)(2,1)} %bitcast.16, ...), custom_call_target="tpu_custom_call" | custom-call | flops 503316480 | bytes 3375104 | tf_op jit(solution)/shard_map/pallas_call | solution.py:141
  58.0 2.5 %collective-permute-start.10 = (bf16[128,768]{1,0:T(8,128)(2,1)S(1)}, bf16[128,768]{1,0:T(8,128)(2,1)S(1)}, u32[]{:S(2)}, u32[]{:S(2)}) collective-permute-start(bf16[128,768]{1,0:T(8,128)(2,1)S(1)} %get-tuple-element.105), channel_id=1, source_target_pairs={{0,7},{1,0},{2,1},{3,2},{4,3},{5,4},{6,5},{7,6},{16,17},{17,18},{1... | collective-permute-start | bytes 589832 | tf_op jit(solution)/shard_map/ppermute | solution.py:53
  66.2 2.8 %collective-permute-start.11 = (bf16[128,768]{1,0:T(8,128)(2,1)S(1)}, bf16[128,768]{1,0:T(8,128)(2,1)S(1)}, u32[]{:S(2)}, u32[]{:S(2)}) collective-permute-start(bf16[128,768]{1,0:T(8,128)(2,1)S(1)} %multiply_convert_fusion.1), channel_id=1, source_target_pairs={{0,8},{8,0},{1,9},{9,1},{2,10},{10,2},{3,11},{11,3},{4,12},{12,4},... | collective-permute-start | bytes 589832 | tf_op jit(solution)/shard_map/ppermute | solution.py:47
  69.1 3.3 %collective-permute-done.11 = bf16[128,768]{1,0:T(8,128)(2,1)S(1)} collective-permute-done((bf16[128,768]{1,0:T(8,128)(2,1)S(1)}, bf16[128,768]{1,0:T(8,128)(2,1)S(1)}, u32[]{:S(2)}, u32[]{:S(2)}) %collective-permute-start.11) | collective-permute-done | bytes 196640 | tf_op jit(solution)/shard_map/ppermute | solution.py:47
  73.8 2.8 %collective-permute-start.12 = (bf16[128,768]{1,0:T(8,128)(2,1)S(1)}, bf16[128,768]{1,0:T(8,128)(2,1)S(1)}, u32[]{:S(2)}, u32[]{:S(2)}) collective-permute-start(bf16[128,768]{1,0:T(8,128)(2,1)S(1)} %slice.105), channel_id=1, source_target_pairs={{0,8},{8,0},{1,9},{9,1},{2,10},{10,2},{3,11},{11,3},{4,12},{12,4},... | collective-permute-start | bytes 589832 | tf_op jit(solution)/shard_map/ppermute | solution.py:47
  76.6 5.7 %collective-permute-done.12 = bf16[128,768]{1,0:T(8,128)(2,1)S(1)} collective-permute-done((bf16[128,768]{1,0:T(8,128)(2,1)S(1)}, bf16[128,768]{1,0:T(8,128)(2,1)S(1)}, u32[]{:S(2)}, u32[]{:S(2)}) %collective-permute-start.12) | collective-permute-done | bytes 196640 | tf_op jit(solution)/shard_map/ppermute | solution.py:47
  90.3 2.4 %collective-permute-start.16 = (bf16[128,768]{1,0:T(8,128)(2,1)S(1)}, bf16[128,768]{1,0:T(8,128)(2,1)S(1)}, u32[]{:S(2)}, u32[]{:S(2)}) collective-permute-start(bf16[128,768]{1,0:T(8,128)(2,1)S(1)} %collective-permute-done.13), channel_id=1, source_target_pairs={{0,1},{1,2},{2,3},{3,4},{4,5},{5,6},{6,7},{7,0},{16,23},{17,16},{1... | collective-permute-start | bytes 589832 | tf_op jit(solution)/shard_map/ppermute | solution.py:53
  93.5 4.4 %shard_map.89 = (f32[320,1280]{1,0:T(8,128)}, f32[320,768]{1,0:T(8,128)}) custom-call(s32[1]{0:T(128)} %bitcast.packed_ref, bf16[128,768]{1,0:T(8,128)(2,1)} %copy-done.5, bf16[128,768]{1,0:T(8,128)(2,1)} %copy-done.9, bf16[256,768]{1,0:T(8,128)(2,1)} %copy-done.4, bf16[2048,1280]{1,0:T(8,128)(2,1)} %refs_12_.3, ...), custom_call_target="tpu_custom_call" | custom-call | tf_op jit(solution)/shard_map/pallas_call | solution.py:247
  103.8 3.8 %collective-permute-done.20.refs_0_ = bf16[256,768]{1,0:T(8,128)(2,1)S(1)} collective-permute-done((bf16[256,768]{1,0:T(8,128)(2,1)}, bf16[256,768]{1,0:T(8,128)(2,1)S(1)}, u32[]{:S(2)}, u32[]{:S(2)}) %collective-permute-start.20) | collective-permute-done | bytes 393248 | tf_op jit(solution)/shard_map/ppermute | solution.py:47
  108.3 5.2 %shard_map.90 = (f32[320,1280]{1,0:T(8,128)}, f32[320,768]{1,0:T(8,128)}) custom-call(s32[1]{0:T(128)} %bitcast.packed_ref, bf16[256,768]{1,0:T(8,128)(2,1)} %copy-done.7, bf16[256,768]{1,0:T(8,128)(2,1)} %copy-done.2, bf16[2048,1280]{1,0:T(8,128)(2,1)} %refs_12_.3, ...), custom_call_target="tpu_custom_call", output_to_operand_aliasing={{0}: (16, {}), {1}: (17, {})} | custom-call | tf_op jit(solution)/shard_map/pallas_call | solution.py:247
  115.3 2.6 %collective-permute-start.24 = (bf16[128,768]{1,0:T(8,128)(2,1)S(1)}, bf16[128,768]{1,0:T(8,128)(2,1)S(1)}, u32[]{:S(2)}, u32[]{:S(2)}) collective-permute-start(bf16[128,768]{1,0:T(8,128)(2,1)S(1)} %collective-permute-done.18), channel_id=1, source_target_pairs={{0,9},{1,10},{2,11},{3,12},{4,13},{5,14},{6,15},{7,8},{8,1},{9,2},... | collective-permute-start | bytes 589832 | tf_op jit(solution)/shard_map/ppermute | solution.py:64
  117.9 5.4 %shard_map.91 = (f32[320,1280]{1,0:T(8,128)}, f32[320,768]{1,0:T(8,128)}) custom-call(s32[1]{0:T(128)} %bitcast.packed_ref, bf16[256,768]{1,0:T(8,128)(2,1)} %copy-done.3, bf16[256,768]{1,0:T(8,128)(2,1)} %copy-done.8, bf16[2048,1280]{1,0:T(8,128)(2,1)} %refs_12_.3, ...), custom_call_target="tpu_custom_call", output_to_operand_aliasing={{0}: (16, {}), {1}: (17, {})} | custom-call | tf_op jit(solution)/shard_map/pallas_call | solution.py:247
  123.7 4.2 %collective-permute-done.23.refs_1_ = bf16[128,768]{1,0:T(8,128)(2,1)S(1)} collective-permute-done((bf16[128,768]{1,0:T(8,128)(2,1)S(1)}, bf16[128,768]{1,0:T(8,128)(2,1)S(1)}, u32[]{:S(2)}, u32[]{:S(2)}) %collective-permute-start.23) | collective-permute-done | bytes 196640 | tf_op jit(solution)/shard_map/ppermute | solution.py:53
  129.3 8.1 %shard_map.92 = (bf16[8,80,640]{2,1,0:T(8,128)(2,1)}, bf16[8,80,640]{2,1,0:T(8,128)(2,1)}) custom-call(s32[1]{0:T(128)} %bitcast.packed_ref, bf16[256,768]{1,0:T(8,128)(2,1)} %copy-done.6, bf16[128,768]{1,0:T(8,128)(2,1)} %copy-done.11, bf16[128,768]{1,0:T(8,128)(2,1)} %copy-done.10, bf16[2048,1280]{1,0:T(8,128)(2,1)} %refs_12_.3, ...), custom_call_target="tpu_custom_call" | custom-call | tf_op jit(solution)/shard_map/pallas_call | solution.py:247
  137.4 18.1 %collective-permute-start.25 = (bf16[8,80,640]{2,1,0:T(8,128)(2,1)}, bf16[8,80,640]{2,1,0:T(8,128)(2,1)S(1)}, u32[]{:S(2)}, u32[]{:S(2)}) collective-permute-start(bf16[8,80,640]{2,1,0:T(8,128)(2,1)} %get-tuple-element.99), channel_id=1, source_target_pairs={{0,16},{16,0},{1,17},{17,1},{2,18},{18,2},{3,19},{19,3},{4,20},{20... | collective-permute-start | bytes 2457608 | tf_op jit(solution)/shard_map/ppermute | solution.py:47
  161.0 17.2 %all_to_all.5 = bf16[8,80,640]{2,1,0:T(8,128)(2,1)S(1)} all-to-all(bf16[8,80,640]{2,1,0:T(8,128)(2,1)S(1)} %add_convert_fusion), channel_id=1, replica_groups=mesh['ylo'=2,'x'=4,'core'=2,'yhi'=2,'z'=8] {'ylo','x'}, dimensions={0} | all-to-all | bytes 1638400 | tf_op jit(solution)/shard_map/all_to_all | solution.py:354
  (101 shorter events, 44.7 us)
Async XLA Ops:
  7.2 53.5 %all-gather.2.cloned.1.call-start = ((), (), s32[]{:S(2)}) async-start(), calls=%async_computation.2 | async-start | bytes 1769472 | tf_op jit(solution)/shard_map/all_gather | solution.py:294
  7.9 151.1 %reduce-scatter.2.cloned.1.call-start = ((), (), s32[]{:S(2)}) async-start(), calls=%async_computation.3 | async-start | bytes 1769472 | tf_op jit(solution)/shard_map/reduce_scatter | solution.py:338
  13.6 8.3 %collective-permute-start.2 = (bf16[128,768]{1,0:T(8,128)(2,1)}, bf16[128,768]{1,0:T(8,128)(2,1)S(1)}, u32[]{:S(2)}, u32[]{:S(2)}) collective-permute-start(bf16[128,768]{1,0:T(8,128)(2,1)} %get-tuple-element.58), channel_id=1, source_target_pairs={{0,8},{8,0},{1,9},{9,1},{2,10},{10,2},{3,11},{11,3},{4,12},{12,4},... | collective-permute-start | bytes 589832 | tf_op jit(solution)/shard_map/ppermute | solution.py:47
  17.3 13.2 %collective-permute-start.3 = (bf16[256,768]{1,0:T(8,128)(2,1)}, bf16[256,768]{1,0:T(8,128)(2,1)S(1)}, u32[]{:S(2)}, u32[]{:S(2)}) collective-permute-start(bf16[256,768]{1,0:T(8,128)(2,1)} %get-tuple-element.61), channel_id=1, source_target_pairs={{0,8},{8,0},{1,9},{9,1},{2,10},{10,2},{3,11},{11,3},{4,12},{12,4},... | collective-permute-start | bytes 1179656 | tf_op jit(solution)/shard_map/ppermute | solution.py:47
  21.9 8.6 %collective-permute-start.4 = (bf16[128,768]{1,0:T(8,128)(2,1)S(1)}, bf16[128,768]{1,0:T(8,128)(2,1)S(1)}, u32[]{:S(2)}, u32[]{:S(2)}) collective-permute-start(bf16[128,768]{1,0:T(8,128)(2,1)S(1)} %add_convert_fusion.7), channel_id=1, source_target_pairs={{0,1},{1,2},{2,3},{3,4},{4,5},{5,6},{6,7},{7,0},{16,23},{17,16},{1... | collective-permute-start | bytes 589832 | tf_op jit(solution)/shard_map/ppermute | solution.py:53
  27.6 18.3 %collective-permute-start.1 = (bf16[256,768]{1,0:T(8,128)(2,1)}, bf16[256,768]{1,0:T(8,128)(2,1)S(1)}, u32[]{:S(2)}, u32[]{:S(2)}) collective-permute-start(bf16[256,768]{1,0:T(8,128)(2,1)} %get-tuple-element.57), channel_id=1, source_target_pairs={{0,8},{8,0},{1,9},{9,1},{2,10},{10,2},{3,11},{11,3},{4,12},{12,4},... | collective-permute-start | bytes 1179656 | tf_op jit(solution)/shard_map/ppermute | solution.py:47
  32.3 13.5 %collective-permute-start.8 = (bf16[128,768]{1,0:T(8,128)(2,1)}, bf16[128,768]{1,0:T(8,128)(2,1)S(1)}, u32[]{:S(2)}, u32[]{:S(2)}) collective-permute-start(bf16[128,768]{1,0:T(8,128)(2,1)} %get-tuple-element.109), channel_id=1, source_target_pairs={{0,7},{1,0},{2,1},{3,2},{4,3},{5,4},{6,5},{7,6},{16,17},{17,18},{1... | collective-permute-start | bytes 589832 | tf_op jit(solution)/shard_map/ppermute | solution.py:53
  33.8 12.1 %collective-permute-start.5 = (bf16[128,768]{1,0:T(8,128)(2,1)S(1)}, bf16[128,768]{1,0:T(8,128)(2,1)S(1)}, u32[]{:S(2)}, u32[]{:S(2)}) collective-permute-start(bf16[128,768]{1,0:T(8,128)(2,1)S(1)} %get-tuple-element.110), channel_id=1, source_target_pairs={{0,1},{1,2},{2,3},{3,4},{4,5},{5,6},{6,7},{7,0},{16,23},{17,16},{1... | collective-permute-start | bytes 589832 | tf_op jit(solution)/shard_map/ppermute | solution.py:53
  42.8 13.9 %collective-permute-start = (bf16[384,768]{1,0:T(8,128)(2,1)}, bf16[384,768]{1,0:T(8,128)(2,1)S(1)}, u32[]{:S(2)}, u32[]{:S(2)}) collective-permute-start(bf16[384,768]{1,0:T(8,128)(2,1)} %get-tuple-element.55), channel_id=1, source_target_pairs={{0,8},{8,0},{1,9},{9,1},{2,10},{10,2},{3,11},{11,3},{4,12},{12,4},... | collective-permute-start | bytes 1769480 | tf_op jit(solution)/shard_map/ppermute | solution.py:47
  47.8 8.9 %collective-permute-start.9 = (bf16[128,768]{1,0:T(8,128)(2,1)S(1)}, bf16[128,768]{1,0:T(8,128)(2,1)S(1)}, u32[]{:S(2)}, u32[]{:S(2)}) collective-permute-start(bf16[128,768]{1,0:T(8,128)(2,1)S(1)} %get-tuple-element.107), channel_id=1, source_target_pairs={{0,7},{1,0},{2,1},{3,2},{4,3},{5,4},{6,5},{7,6},{16,17},{17,18},{1... | collective-permute-start | bytes 589832 | tf_op jit(solution)/shard_map/ppermute | solution.py:53
  48.4 8.2 %collective-permute-start.6 = (bf16[128,768]{1,0:T(8,128)(2,1)S(1)}, bf16[128,768]{1,0:T(8,128)(2,1)}, u32[]{:S(2)}, u32[]{:S(2)}) collective-permute-start(bf16[128,768]{1,0:T(8,128)(2,1)S(1)} %get-tuple-element.108), channel_id=1, source_target_pairs={{0,1},{1,2},{2,3},{3,4},{4,5},{5,6},{6,7},{7,0},{16,23},{17,16},{1... | collective-permute-start | bytes 589832 | tf_op jit(solution)/shard_map/ppermute | solution.py:53
  66.2 6.1 %collective-permute-start.11 = (bf16[128,768]{1,0:T(8,128)(2,1)S(1)}, bf16[128,768]{1,0:T(8,128)(2,1)S(1)}, u32[]{:S(2)}, u32[]{:S(2)}) collective-permute-start(bf16[128,768]{1,0:T(8,128)(2,1)S(1)} %multiply_convert_fusion.1), channel_id=1, source_target_pairs={{0,8},{8,0},{1,9},{9,1},{2,10},{10,2},{3,11},{11,3},{4,12},{12,4},... | collective-permute-start | bytes 589832 | tf_op jit(solution)/shard_map/ppermute | solution.py:47
  73.8 8.5 %collective-permute-start.12 = (bf16[128,768]{1,0:T(8,128)(2,1)S(1)}, bf16[128,768]{1,0:T(8,128)(2,1)S(1)}, u32[]{:S(2)}, u32[]{:S(2)}) collective-permute-start(bf16[128,768]{1,0:T(8,128)(2,1)S(1)} %slice.105), channel_id=1, source_target_pairs={{0,8},{8,0},{1,9},{9,1},{2,10},{10,2},{3,11},{11,3},{4,12},{12,4},... | collective-permute-start | bytes 589832 | tf_op jit(solution)/shard_map/ppermute | solution.py:47
  82.7 6.4 %collective-permute-start.15 = (bf16[128,768]{1,0:T(8,128)(2,1)S(1)}, bf16[128,768]{1,0:T(8,128)(2,1)S(1)}, u32[]{:S(2)}, u32[]{:S(2)}) collective-permute-start(bf16[128,768]{1,0:T(8,128)(2,1)S(1)} %multiply_convert_fusion.refs_0_), channel_id=1, source_target_pairs={{0,8},{8,0},{1,9},{9,1},{2,10},{10,2},{3,11},{11,3},{4,12},{12,4},... | collective-permute-start | bytes 589832 | tf_op jit(solution)/shard_map/ppermute | solution.py:47
  90.3 7.6 %collective-permute-start.16 = (bf16[128,768]{1,0:T(8,128)(2,1)S(1)}, bf16[128,768]{1,0:T(8,128)(2,1)S(1)}, u32[]{:S(2)}, u32[]{:S(2)}) collective-permute-start(bf16[128,768]{1,0:T(8,128)(2,1)S(1)} %collective-permute-done.13), channel_id=1, source_target_pairs={{0,1},{1,2},{2,3},{3,4},{4,5},{5,6},{6,7},{7,0},{16,23},{17,16},{1... | collective-permute-start | bytes 589832 | tf_op jit(solution)/shard_map/ppermute | solution.py:53
  92.7 6.5 %collective-permute-start.17 = (bf16[128,768]{1,0:T(8,128)(2,1)S(1)}, bf16[128,768]{1,0:T(8,128)(2,1)S(1)}, u32[]{:S(2)}, u32[]{:S(2)}) collective-permute-start(bf16[128,768]{1,0:T(8,128)(2,1)S(1)} %collective-permute-done.14), channel_id=1, source_target_pairs={{0,7},{1,0},{2,1},{3,2},{4,3},{5,4},{6,5},{7,6},{16,17},{17,18},{1... | collective-permute-start | bytes 589832 | tf_op jit(solution)/shard_map/ppermute | solution.py:53
  99.1 8.4 %collective-permute-start.20 = (bf16[256,768]{1,0:T(8,128)(2,1)}, bf16[256,768]{1,0:T(8,128)(2,1)S(1)}, u32[]{:S(2)}, u32[]{:S(2)}) collective-permute-start(bf16[256,768]{1,0:T(8,128)(2,1)} %copy-done.4), channel_id=1, source_target_pairs={{0,8},{8,0},{1,9},{9,1},{2,10},{10,2},{3,11},{11,3},{4,12},{12,4},... | collective-permute-start | bytes 1179656 | tf_op jit(solution)/shard_map/ppermute | solution.py:47
  100.7 12.8 %collective-permute-start.21 = (bf16[256,768]{1,0:T(8,128)(2,1)S(1)}, bf16[256,768]{1,0:T(8,128)(2,1)S(1)}, u32[]{:S(2)}, u32[]{:S(2)}) collective-permute-start(bf16[256,768]{1,0:T(8,128)(2,1)S(1)} %constant_dynamic-update-slice_fusion.2.refs_1_), channel_id=1, source_target_pairs={{0,8},{8,0},{1,9},{9,1},{2,10},{10,2},{3,11},{11,3},{4,12},{12,4},... | collective-permute-start | bytes 1179656 | tf_op jit(solution)/shard_map/ppermute | solution.py:47
  102.3 11.2 %collective-permute-start.18 = (bf16[128,768]{1,0:T(8,128)(2,1)S(1)}, bf16[128,768]{1,0:T(8,128)(2,1)S(1)}, u32[]{:S(2)}, u32[]{:S(2)}) collective-permute-start(bf16[128,768]{1,0:T(8,128)(2,1)S(1)} %collective-permute-done.16), channel_id=1, source_target_pairs={{0,1},{1,2},{2,3},{3,4},{4,5},{5,6},{6,7},{7,0},{16,23},{17,16},{1... | collective-permute-start | bytes 589832 | tf_op jit(solution)/shard_map/ppermute | solution.py:53
  103.8 9.7 %collective-permute-start.19 = (bf16[128,768]{1,0:T(8,128)(2,1)S(1)}, bf16[128,768]{1,0:T(8,128)(2,1)S(1)}, u32[]{:S(2)}, u32[]{:S(2)}) collective-permute-start(bf16[128,768]{1,0:T(8,128)(2,1)S(1)} %collective-permute-done.17), channel_id=1, source_target_pairs={{0,7},{1,0},{2,1},{3,2},{4,3},{5,4},{6,5},{7,6},{16,17},{17,18},{1... | collective-permute-start | bytes 589832 | tf_op jit(solution)/shard_map/ppermute | solution.py:53
  113.6 14.9 %collective-permute-start.22 = (bf16[256,768]{1,0:T(8,128)(2,1)S(1)}, bf16[256,768]{1,0:T(8,128)(2,1)S(1)}, u32[]{:S(2)}, u32[]{:S(2)}) collective-permute-start(bf16[256,768]{1,0:T(8,128)(2,1)S(1)} %constant_dynamic-update-slice_fusion.4.refs_0_), channel_id=1, source_target_pairs={{0,8},{8,0},{1,9},{9,1},{2,10},{10,2},{3,11},{11,3},{4,12},{12,4},... | collective-permute-start | bytes 1179656 | tf_op jit(solution)/shard_map/ppermute | solution.py:47
  115.3 8.5 %collective-permute-start.24 = (bf16[128,768]{1,0:T(8,128)(2,1)S(1)}, bf16[128,768]{1,0:T(8,128)(2,1)S(1)}, u32[]{:S(2)}, u32[]{:S(2)}) collective-permute-start(bf16[128,768]{1,0:T(8,128)(2,1)S(1)} %collective-permute-done.18), channel_id=1, source_target_pairs={{0,9},{1,10},{2,11},{3,12},{4,13},{5,14},{6,15},{7,8},{8,1},{9,2},... | collective-permute-start | bytes 589832 | tf_op jit(solution)/shard_map/ppermute | solution.py:64
  117.9 10.1 %collective-permute-start.23 = (bf16[128,768]{1,0:T(8,128)(2,1)S(1)}, bf16[128,768]{1,0:T(8,128)(2,1)S(1)}, u32[]{:S(2)}, u32[]{:S(2)}) collective-permute-start(bf16[128,768]{1,0:T(8,128)(2,1)S(1)} %collective-permute-done.18), channel_id=1, source_target_pairs={{0,1},{1,2},{2,3},{3,4},{4,5},{5,6},{6,7},{7,0},{16,23},{17,16},{1... | collective-permute-start | bytes 589832 | tf_op jit(solution)/shard_map/ppermute | solution.py:53
  137.4 20.2 %collective-permute-start.25 = (bf16[8,80,640]{2,1,0:T(8,128)(2,1)}, bf16[8,80,640]{2,1,0:T(8,128)(2,1)S(1)}, u32[]{:S(2)}, u32[]{:S(2)}) collective-permute-start(bf16[8,80,640]{2,1,0:T(8,128)(2,1)} %get-tuple-element.99), channel_id=1, source_target_pairs={{0,16},{16,0},{1,17},{17,1},{2,18},{18,2},{3,19},{19,3},{4,20},{20... | collective-permute-start | bytes 2457608 | tf_op jit(solution)/shard_map/ppermute | solution.py:47
  (18 other events, 78.7 us)
Sparse Core Ops, SparseCore 0:
  9.8 42.6 all-gather.1
  99.3 47.4 reduce-scatter.1

commit v10 on v8

--- a/solution.py
+++ b/solution.py
@@ -66,9 +66,8 @@
 
 GROUPS = (
     (((1, 4),), ((1, 3), (1, -3)), ((0, 4),)),
-    (((1, 2), (1, -2)), ((0, 3), (0, -3))),
-    (((1, 1), (1, -1), (1, 0)), ((0, 2), (0, -2))),
-    (((0, 1), (0, -1), (0, 0)),),
+    (((1, 2), (1, -2)), ((1, 1), (1, -1), (1, 0)), ((0, 3),), ((0, -3),)),
+    (((0, 2), (0, -2)), ((0, 1), (0, -1), (0, 0))),
 )
 MEMBERS = tuple(tuple(block for piece in group for block in piece) for group in GROUPS)
 
@@ -283,15 +282,12 @@
 
     score_half = lax.all_gather(score_embed, "z", axis=0, tiled=True)
     (other4, other3, own4), down_head = forward(0, down_weight, head_weight)
-    came4, came3 = swap(other4, "yhi"), swap(other3, "yhi")
-    (other2, own3), _ = forward(1, down_head)
-    came2 = swap(other2, "yhi")
-    fore = shift(total_of(own4, came4).astype(bf16), 1)
-    (other1, own2), _ = forward(2, down_head)
-    came1 = swap(other1, "yhi")
-    fore = shift(total_of(own3[:rows], came3[:rows], fore).astype(bf16), 1)
-    back = shift(total_of(own3[rows:], came3[rows:]).astype(bf16), -1)
-    (own1,), _ = forward(3, down_head)
+    fore, across4, came3 = shift(own4, 1), shift_across(other4, 1), swap(other3, "yhi")
+    (other2, other1, own3, own3b), _ = forward(1, down_head)
+    came2, came1 = swap(other2, "yhi"), swap(other1, "yhi")
+    fore = shift(total_of(own3, came3[:rows], fore, across4).astype(bf16), 1)
+    back = shift(total_of(own3b, came3[rows:]).astype(bf16), -1)
+    (own2, own1), _ = forward(2, down_head)
     for own, came in ((own2, came2), (own1, came1)):
         fore = shift(total_of(own[:rows], came[:rows], fore).astype(bf16), 1)
         back = shift(total_of(own[rows : 2 * rows], came[rows : 2 * rows], back).astype(bf16), -1)
@@ -321,13 +317,14 @@
     ring1 = both(back, fore)
     crossed1 = swap(ring1, "yhi")
     fore, back = shift(fore, 1), shift(back, -1)
+    backward = lambda items, sums, *head: backward_blocks(items, packed, hidden_in, down_head, sums, *head)
+    sums = backward([item(grad_embed, (0, 0)), item(crossed0, (1, 0)), item(ring1, *pair(1, 0))], None)
+    fore, back, sums = lax.optimization_barrier((fore, back, sums))
     ring2 = both(back, fore)
     crossed2 = swap(ring2, "yhi")
     fore, back = shift(fore, 1), shift(back, -1)
-    backward = lambda items, sums, *head: backward_blocks(items, packed, hidden_in, down_head, sums, *head)
-    sums = backward([item(grad_embed, (0, 0)), item(crossed0, (1, 0)), item(ring1, *pair(1, 0))], None)
     sums = backward([item(crossed1, *pair(1, 1)), item(ring2, *pair(2, 0))], sums)
-    fore, back, sums, score_part = lax.optimization_barrier((fore, back, sums, score_part))
+    fore, back, sums, crossed2, score_part = lax.optimization_barrier((fore, back, sums, crossed2, score_part))
     grad_score = lax.psum_scatter(score_part, "z", scatter_dimension=0, tiled=True)
     ring4, crossed4 = shift(fore, 1), shift_across(fore, 1)
     ring3 = both(back, fore)

time: 181 us -> 170 us (0.939)
  other arithmetic: 10.6 us -> 6.86 us
  waiting for transfers between devices: 26.6 us -> 23.7 us
  Pallas kernels: 43.4 us -> 41.2 us
  starting transfers between devices: 59.2 us -> 57.1 us
    ppermute x11 -> x10, waiting for transfers between devices: 22.7 us -> 11.4 us  [swap(): return lax.ppermute(value, axis, [(0, 1), (1, 0)])]
    ppermute x14, waiting for transfers between devices: 3.14 us -> 9.74 us  [shift(): return lax.ppermute(value, ('core', 'z'), perm)]
    ppermute x11 -> x10, starting transfers between devices: 38.2 us -> 33.6 us  [swap(): return lax.ppermute(value, axis, [(0, 1), (1, 0)])]
    ppermute x14, starting transfers between devices: 18.4 us -> 22.9 us  [shift(): return lax.ppermute(value, ('core', 'z'), perm)]
    pallas_call x4 -> x3, Pallas kernels: 19.1 us -> 16.9 us  [forward_blocks(): pl.pallas_call(functools.partial(forward_kernel, pieces, first), grid_spe...]
    ppermute x1 -> x2, starting transfers between devices: 2.58 us -> 0.53 us  [shift_across(): return lax.ppermute(value, ('core', 'yhi', 'z'), perm)]
    ppermute x1 -> x2, waiting for transfers between devices: 0.01 us -> 1.83 us  [shift_across(): return lax.ppermute(value, ('core', 'yhi', 'z'), perm)]
  transfers between devices with their start and end apart: 28 -> 28, of which waited for: 11 -> 12; matrix products, arithmetic and copies ran while one was open for 8% -> 6% of each run, Pallas kernels for 23% -> 23%
where the time goes in v10:
time: 170 us; the launch traced here: 168 us
  starting transfers between devices  57.1 us (34%)
  Pallas kernels  41.2 us (24%)
  waiting for transfers between devices  23.7 us (14%)
  blocking collectives  17 us (10%)
  between operations  14.3 us (8%)
  other arithmetic  6.86 us (4%)
  matrix products  4.6 us (3%)
  local copies, waits for them, and re-layouts  3.63 us (2%)
    ppermute x10, starting transfers between devices, swap(): return lax.ppermute(value, axis, [(0, 1), (1, 0)])  33.6 us
    ppermute x14, starting transfers between devices, shift(): return lax.ppermute(value, ('core', 'z'), perm)  22.9 us
    pallas_call x4, Pallas kernels, backward_blocks(): pl.pallas_call(functools.partial(backward_kernel, len(items), len(places)...  22.3 us
    all_to_all x1, blocking collectives, per_device(): landed = lax.all_to_all(chip, ('ylo', 'x'), 0, 0)  17 us
    pallas_call x3, Pallas kernels, forward_blocks(): pl.pallas_call(functools.partial(forward_kernel, pieces, first), grid_spe...  16.9 us
    ppermute x10, waiting for transfers between devices, swap(): return lax.ppermute(value, axis, [(0, 1), (1, 0)])  11.4 us
    ppermute x14, waiting for transfers between devices, shift(): return lax.ppermute(value, ('core', 'z'), perm)  9.74 us
    dot_general x4, matrix products, dot(): lax.dot_general(left, right, (dims, ((), ())), preferred_element_type=f32)  4.6 us
  transfers between devices with their start and end apart: 28, of which 12 were waited for; matrix products, arithmetic and copies ran while one was open for 6% of the time, Pallas kernels for 23%

profile of v10, /device:TPU:1, one launch (start us, length us, event | category | flops | bytes accessed | tf_op | source)
XLA Modules:
  0.0 168.4 jit_solution(2761272220273233033)
XLA Ops:
  8.0 5.6 %shard_map.85 = (bf16[128,768]{1,0:T(8,128)(2,1)}, bf16[256,768]{1,0:T(8,128)(2,1)}, bf16[128,768]{1,0:T(8,128)(2,1)}, bf16[4,320,128]{2,1,0:T(8,128)(2,1)}, bf1...) custom-call(s32[1]{0:T(128)} %bitcast.packed_ref, bf16[2048,1280]{1,0:T(8,128)(2,1)} %refs_12_.3, ...), custom_call_target="tpu_custom_call" | custom-call | flops 671088640 | bytes 4063232 | tf_op jit(solution)/shard_map/pallas_call | solution.py:140
  13.6 3.7 %collective-permute-start.2 = (bf16[256,768]{1,0:T(8,128)(2,1)}, bf16[256,768]{1,0:T(8,128)(2,1)S(1)}, u32[]{:S(2)}, u32[]{:S(2)}) collective-permute-start(bf16[256,768]{1,0:T(8,128)(2,1)} %get-tuple-element.54), channel_id=1, source_target_pairs={{0,8},{8,0},{1,9},{9,1},{2,10},{10,2},{3,11},{11,3},{4,12},{12,4},... | collective-permute-start | bytes 1179656 | tf_op jit(solution)/shard_map/ppermute | solution.py:47
  17.3 5.6 %collective-permute-start.3 = (bf16[128,768]{1,0:T(8,128)(2,1)}, bf16[128,768]{1,0:T(8,128)(2,1)S(1)}, u32[]{:S(2)}, u32[]{:S(2)}) collective-permute-start(bf16[128,768]{1,0:T(8,128)(2,1)} %get-tuple-element.55), channel_id=1, source_target_pairs={{0,1},{1,2},{2,3},{3,4},{4,5},{5,6},{6,7},{7,0},{16,23},{17,16},{1... | collective-permute-start | bytes 589832 | tf_op jit(solution)/shard_map/ppermute | solution.py:53
  23.4 6.3 %shard_map.87 = (bf16[256,768]{1,0:T(8,128)(2,1)}, bf16[384,768]{1,0:T(8,128)(2,1)}, bf16[128,768]{1,0:T(8,128)(2,1)}, bf16[128,768]{1,0:T(8,128)(2,1)}, bf16[7,...) custom-call(s32[1]{0:T(128)} %bitcast.packed_ref, bf16[2048,1280]{1,0:T(8,128)(2,1)} %refs_12_.3, ...), custom_call_target="tpu_custom_call" | custom-call | flops 1174405120 | bytes 6127616 | tf_op jit(solution)/shard_map/pallas_call | solution.py:140
  29.7 2.9 %collective-permute-start.1 = (bf16[256,768]{1,0:T(8,128)(2,1)}, bf16[256,768]{1,0:T(8,128)(2,1)S(1)}, u32[]{:S(2)}, u32[]{:S(2)}) collective-permute-start(bf16[256,768]{1,0:T(8,128)(2,1)} %get-tuple-element.52), channel_id=1, source_target_pairs={{0,8},{8,0},{1,9},{9,1},{2,10},{10,2},{3,11},{11,3},{4,12},{12,4},... | collective-permute-start | bytes 1179656 | tf_op jit(solution)/shard_map/ppermute | solution.py:47
  34.5 2.7 %collective-permute-start.5 = (bf16[128,768]{1,0:T(8,128)(2,1)S(1)}, bf16[128,768]{1,0:T(8,128)(2,1)S(1)}, u32[]{:S(2)}, u32[]{:S(2)}) collective-permute-start(bf16[128,768]{1,0:T(8,128)(2,1)S(1)} %get-tuple-element.100), channel_id=1, source_target_pairs={{0,1},{1,2},{2,3},{3,4},{4,5},{5,6},{6,7},{7,0},{16,23},{17,16},{1... | collective-permute-start | bytes 589832 | tf_op jit(solution)/shard_map/ppermute | solution.py:53
  37.2 3.0 %collective-permute-start = (bf16[384,768]{1,0:T(8,128)(2,1)}, bf16[384,768]{1,0:T(8,128)(2,1)S(1)}, u32[]{:S(2)}, u32[]{:S(2)}) collective-permute-start(bf16[384,768]{1,0:T(8,128)(2,1)} %get-tuple-element.50), channel_id=1, source_target_pairs={{0,8},{8,0},{1,9},{9,1},{2,10},{10,2},{3,11},{11,3},{4,12},{12,4},... | collective-permute-start | bytes 1769480 | tf_op jit(solution)/shard_map/ppermute | solution.py:47
  40.2 5.1 %shard_map.86 = (bf16[256,768]{1,0:T(8,128)(2,1)}, bf16[384,768]{1,0:T(8,128)(2,1)}, bf16[5,320,128]{2,1,0:T(8,128)(2,1)}, bf16[5,128,320]{2,1,0:T(8,128)(2,1)}) custom-call(s32[1]{0:T(128)} %bitcast.packed_ref, bf16[2048,1280]{1,0:T(8,128)(2,1)} %refs_12_.3, bf16[2048,1280]{1,0:T(8,128)(2,1)} %refs_12_.3, bf16[2048,1280]{1,0:T(8,128)(2,1)} %refs_12_.3, ...), custom_call_target="tpu_custom_call" | custom-call | flops 838860800 | bytes 4751360 | tf_op jit(solution)/shard_map/pallas_call | solution.py:140
  46.8 2.4 %collective-permute-start.6 = (bf16[128,768]{1,0:T(8,128)(2,1)S(1)}, bf16[128,768]{1,0:T(8,128)(2,1)S(1)}, u32[]{:S(2)}, u32[]{:S(2)}) collective-permute-start(bf16[128,768]{1,0:T(8,128)(2,1)S(1)} %get-tuple-element.98), channel_id=1, source_target_pairs={{0,1},{1,2},{2,3},{3,4},{4,5},{5,6},{6,7},{7,0},{16,23},{17,16},{1... | collective-permute-start | bytes 589832 | tf_op jit(solution)/shard_map/ppermute | solution.py:53
  51.4 2.7 %collective-permute-done.9 = bf16[128,768]{1,0:T(8,128)(2,1)S(1)} collective-permute-done((bf16[128,768]{1,0:T(8,128)(2,1)S(1)}, bf16[128,768]{1,0:T(8,128)(2,1)S(1)}, u32[]{:S(2)}, u32[]{:S(2)}) %collective-permute-start.9) | collective-permute-done | bytes 196640 | tf_op jit(solution)/shard_map/ppermute | solution.py:53
  54.3 3.4 %collective-permute-start.10 = (bf16[128,768]{1,0:T(8,128)(2,1)S(1)}, bf16[128,768]{1,0:T(8,128)(2,1)S(1)}, u32[]{:S(2)}, u32[]{:S(2)}) collective-permute-start(bf16[128,768]{1,0:T(8,128)(2,1)S(1)} %get-tuple-element.95), channel_id=1, source_target_pairs={{0,7},{1,0},{2,1},{3,2},{4,3},{5,4},{6,5},{7,6},{16,17},{17,18},{1... | collective-permute-start | bytes 589832 | tf_op jit(solution)/shard_map/ppermute | solution.py:53
  62.5 3.2 %collective-permute-start.11 = (bf16[128,768]{1,0:T(8,128)(2,1)S(1)}, bf16[128,768]{1,0:T(8,128)(2,1)S(1)}, u32[]{:S(2)}, u32[]{:S(2)}) collective-permute-start(bf16[128,768]{1,0:T(8,128)(2,1)S(1)} %multiply_convert_fusion.1), channel_id=1, source_target_pairs={{0,8},{8,0},{1,9},{9,1},{2,10},{10,2},{3,11},{11,3},{4,12},{12,4},... | collective-permute-start | bytes 589832 | tf_op jit(solution)/shard_map/ppermute | solution.py:47
  65.8 3.0 %collective-permute-done.11 = bf16[128,768]{1,0:T(8,128)(2,1)S(1)} collective-permute-done((bf16[128,768]{1,0:T(8,128)(2,1)S(1)}, bf16[128,768]{1,0:T(8,128)(2,1)S(1)}, u32[]{:S(2)}, u32[]{:S(2)}) %collective-permute-start.11) | collective-permute-done | bytes 196640 | tf_op jit(solution)/shard_map/ppermute | solution.py:47
  70.3 3.0 %collective-permute-start.12 = (bf16[128,768]{1,0:T(8,128)(2,1)S(1)}, bf16[128,768]{1,0:T(8,128)(2,1)S(1)}, u32[]{:S(2)}, u32[]{:S(2)}) collective-permute-start(bf16[128,768]{1,0:T(8,128)(2,1)S(1)} %slice.95), channel_id=1, source_target_pairs={{0,8},{8,0},{1,9},{9,1},{2,10},{10,2},{3,11},{11,3},{4,12},{12,4},... | collective-permute-start | bytes 589832 | tf_op jit(solution)/shard_map/ppermute | solution.py:47
  73.3 3.7 %collective-permute-done.12 = bf16[128,768]{1,0:T(8,128)(2,1)S(1)} collective-permute-done((bf16[128,768]{1,0:T(8,128)(2,1)S(1)}, bf16[128,768]{1,0:T(8,128)(2,1)S(1)}, u32[]{:S(2)}, u32[]{:S(2)}) %collective-permute-start.12) | collective-permute-done | bytes 196640 | tf_op jit(solution)/shard_map/ppermute | solution.py:47
  79.8 3.4 %collective-permute-start.14 = (bf16[128,768]{1,0:T(8,128)(2,1)S(1)}, bf16[128,768]{1,0:T(8,128)(2,1)S(1)}, u32[]{:S(2)}, u32[]{:S(2)}) collective-permute-start(bf16[128,768]{1,0:T(8,128)(2,1)S(1)} %multiply_convert_fusion.refs_0_), channel_id=1, source_target_pairs={{0,7},{1,0},{2,1},{3,2},{4,3},{5,4},{6,5},{7,6},{16,17},{17,18},{1... | collective-permute-start | bytes 589832 | tf_op jit(solution)/shard_map/ppermute | solution.py:53
  85.8 4.1 %collective-permute-done.13 = bf16[128,768]{1,0:T(8,128)(2,1)S(1)} collective-permute-done((bf16[128,768]{1,0:T(8,128)(2,1)S(1)}, bf16[128,768]{1,0:T(8,128)(2,1)S(1)}, u32[]{:S(2)}, u32[]{:S(2)}) %collective-permute-start.13) | collective-permute-done | bytes 196640 | tf_op jit(solution)/shard_map/ppermute | solution.py:53
  93.5 4.4 %shard_map.88 = (f32[320,1280]{1,0:T(8,128)}, f32[320,768]{1,0:T(8,128)}) custom-call(s32[1]{0:T(128)} %bitcast.packed_ref, bf16[128,768]{1,0:T(8,128)(2,1)} %copy-done.5, bf16[128,768]{1,0:T(8,128)(2,1)} %copy-done.10, bf16[256,768]{1,0:T(8,128)(2,1)} %copy-done.4, bf16[2048,1280]{1,0:T(8,128)(2,1)} %refs_12_.3, ...), custom_call_target="tpu_custom_call" | custom-call | flops 922746880 | bytes 8388608 | tf_op jit(solution)/shard_map/pallas_call | solution.py:236
  102.6 5.1 %shard_map.89 = (f32[320,1280]{1,0:T(8,128)}, f32[320,768]{1,0:T(8,128)}) custom-call(s32[1]{0:T(128)} %bitcast.packed_ref, bf16[256,768]{1,0:T(8,128)(2,1)} %copy-done.8, bf16[256,768]{1,0:T(8,128)(2,1)} %copy-done.3, bf16[2048,1280]{1,0:T(8,128)(2,1)} %refs_12_.3, ...), custom_call_target="tpu_custom_call", output_to_operand_aliasing={{0}: (16, {}), {1}: (17, {})} | custom-call | flops 922746880 | bytes 8388608 | tf_op jit(solution)/shard_map/pallas_call | solution.py:236
  108.5 3.8 %collective-permute-start.22 = (bf16[256,768]{1,0:T(8,128)(2,1)S(1)}, bf16[256,768]{1,0:T(8,128)(2,1)S(1)}, u32[]{:S(2)}, u32[]{:S(2)}) collective-permute-start(bf16[256,768]{1,0:T(8,128)(2,1)S(1)} %constant_dynamic-update-slice_fusion.4.refs_0_), channel_id=1, source_target_pairs={{0,8},{8,0},{1,9},{9,1},{2,10},{10,2},{3,11},{11,3},{4,12},{12,4},... | collective-permute-start | bytes 1179656 | tf_op jit(solution)/shard_map/ppermute | solution.py:47
  112.3 5.2 %shard_map.90 = (f32[320,1280]{1,0:T(8,128)}, f32[320,768]{1,0:T(8,128)}) custom-call(s32[1]{0:T(128)} %bitcast.packed_ref, bf16[256,768]{1,0:T(8,128)(2,1)} %copy-done.2, bf16[256,768]{1,0:T(8,128)(2,1)} %copy-done.7, bf16[2048,1280]{1,0:T(8,128)(2,1)} %refs_12_.3, ...), custom_call_target="tpu_custom_call", output_to_operand_aliasing={{0}: (16, {}), {1}: (17, {})} | custom-call | flops 922746880 | bytes 8388608 | tf_op jit(solution)/shard_map/pallas_call | solution.py:236
  121.7 7.5 %shard_map.91 = (bf16[8,80,640]{2,1,0:T(8,128)(2,1)}, bf16[8,80,640]{2,1,0:T(8,128)(2,1)}) custom-call(s32[1]{0:T(128)} %bitcast.packed_ref, bf16[256,768]{1,0:T(8,128)(2,1)} %copy-done.9, bf16[128,768]{1,0:T(8,128)(2,1)} %copy-done.12, bf16[128,768]{1,0:T(8,128)(2,1)} %copy-done.11, bf16[2048,1280]{1,0:T(8,128)(2,1)} %refs_12_.3, ...), custom_call_target="tpu_custom_call" | custom-call | flops 1551892480 | bytes 8388608 | tf_op jit(solution)/shard_map/pallas_call | solution.py:236
  129.2 9.0 %collective-permute-start.25 = (bf16[8,80,640]{2,1,0:T(8,128)(2,1)}, bf16[8,80,640]{2,1,0:T(8,128)(2,1)S(1)}, u32[]{:S(2)}, u32[]{:S(2)}) collective-permute-start(bf16[8,80,640]{2,1,0:T(8,128)(2,1)} %get-tuple-element.91), channel_id=1, source_target_pairs={{0,16},{16,0},{1,17},{17,1},{2,18},{18,2},{3,19},{19,3},{4,20},{20... | collective-permute-start | bytes 2457608 | tf_op jit(solution)/shard_map/ppermute | solution.py:47
  141.7 17.0 %all_to_all.5 = bf16[8,80,640]{2,1,0:T(8,128)(2,1)S(1)} all-to-all(bf16[8,80,640]{2,1,0:T(8,128)(2,1)S(1)} %add_convert_fusion), channel_id=1, replica_groups=mesh['ylo'=2,'x'=4,'core'=2,'yhi'=2,'z'=8] {'ylo','x'}, dimensions={0} | all-to-all | bytes 1638400 | tf_op jit(solution)/shard_map/all_to_all | solution.py:337
  (97 shorter events, 38.1 us)
Async XLA Ops:
  7.2 50.5 %all-gather.2.cloned.1.call-start = ((), (), s32[]{:S(2)}) async-start(), calls=%async_computation.2 | async-start | bytes 1769472 | tf_op jit(solution)/shard_map/all_gather | solution.py:283
  7.9 151.7 %reduce-scatter.2.cloned.1.call-start = ((), (), s32[]{:S(2)}) async-start(), calls=%async_computation.3 | async-start | bytes 1769472 | tf_op jit(solution)/shard_map/reduce_scatter | solution.py:328
  13.6 19.0 %collective-permute-start.2 = (bf16[256,768]{1,0:T(8,128)(2,1)}, bf16[256,768]{1,0:T(8,128)(2,1)S(1)}, u32[]{:S(2)}, u32[]{:S(2)}) collective-permute-start(bf16[256,768]{1,0:T(8,128)(2,1)} %get-tuple-element.54), channel_id=1, source_target_pairs={{0,8},{8,0},{1,9},{9,1},{2,10},{10,2},{3,11},{11,3},{4,12},{12,4},... | collective-permute-start | bytes 1179656 | tf_op jit(solution)/shard_map/ppermute | solution.py:47
  17.3 15.2 %collective-permute-start.3 = (bf16[128,768]{1,0:T(8,128)(2,1)}, bf16[128,768]{1,0:T(8,128)(2,1)S(1)}, u32[]{:S(2)}, u32[]{:S(2)}) collective-permute-start(bf16[128,768]{1,0:T(8,128)(2,1)} %get-tuple-element.55), channel_id=1, source_target_pairs={{0,1},{1,2},{2,3},{3,4},{4,5},{5,6},{6,7},{7,0},{16,23},{17,16},{1... | collective-permute-start | bytes 589832 | tf_op jit(solution)/shard_map/ppermute | solution.py:53
  22.9 9.7 %collective-permute-start.4 = (bf16[128,768]{1,0:T(8,128)(2,1)}, bf16[128,768]{1,0:T(8,128)(2,1)S(1)}, u32[]{:S(2)}, u32[]{:S(2)}) collective-permute-start(bf16[128,768]{1,0:T(8,128)(2,1)} %get-tuple-element.56), channel_id=1, source_target_pairs={{0,9},{1,10},{2,11},{3,12},{4,13},{5,14},{6,15},{7,8},{8,1},{9,2},... | collective-permute-start | bytes 589832 | tf_op jit(solution)/shard_map/ppermute | solution.py:64
  29.7 15.6 %collective-permute-start.1 = (bf16[256,768]{1,0:T(8,128)(2,1)}, bf16[256,768]{1,0:T(8,128)(2,1)S(1)}, u32[]{:S(2)}, u32[]{:S(2)}) collective-permute-start(bf16[256,768]{1,0:T(8,128)(2,1)} %get-tuple-element.52), channel_id=1, source_target_pairs={{0,8},{8,0},{1,9},{9,1},{2,10},{10,2},{3,11},{11,3},{4,12},{12,4},... | collective-permute-start | bytes 1179656 | tf_op jit(solution)/shard_map/ppermute | solution.py:47
  33.7 11.6 %collective-permute-start.8 = (bf16[128,768]{1,0:T(8,128)(2,1)S(1)}, bf16[128,768]{1,0:T(8,128)(2,1)S(1)}, u32[]{:S(2)}, u32[]{:S(2)}) collective-permute-start(bf16[128,768]{1,0:T(8,128)(2,1)S(1)} %get-tuple-element.99), channel_id=1, source_target_pairs={{0,7},{1,0},{2,1},{3,2},{4,3},{5,4},{6,5},{7,6},{16,17},{17,18},{1... | collective-permute-start | bytes 589832 | tf_op jit(solution)/shard_map/ppermute | solution.py:53
  34.5 10.8 %collective-permute-start.5 = (bf16[128,768]{1,0:T(8,128)(2,1)S(1)}, bf16[128,768]{1,0:T(8,128)(2,1)S(1)}, u32[]{:S(2)}, u32[]{:S(2)}) collective-permute-start(bf16[128,768]{1,0:T(8,128)(2,1)S(1)} %get-tuple-element.100), channel_id=1, source_target_pairs={{0,1},{1,2},{2,3},{3,4},{4,5},{5,6},{6,7},{7,0},{16,23},{17,16},{1... | collective-permute-start | bytes 589832 | tf_op jit(solution)/shard_map/ppermute | solution.py:53
  37.2 14.2 %collective-permute-start = (bf16[384,768]{1,0:T(8,128)(2,1)}, bf16[384,768]{1,0:T(8,128)(2,1)S(1)}, u32[]{:S(2)}, u32[]{:S(2)}) collective-permute-start(bf16[384,768]{1,0:T(8,128)(2,1)} %get-tuple-element.50), channel_id=1, source_target_pairs={{0,8},{8,0},{1,9},{9,1},{2,10},{10,2},{3,11},{11,3},{4,12},{12,4},... | collective-permute-start | bytes 1769480 | tf_op jit(solution)/shard_map/ppermute | solution.py:47
  46.5 7.6 %collective-permute-start.9 = (bf16[128,768]{1,0:T(8,128)(2,1)S(1)}, bf16[128,768]{1,0:T(8,128)(2,1)S(1)}, u32[]{:S(2)}, u32[]{:S(2)}) collective-permute-start(bf16[128,768]{1,0:T(8,128)(2,1)S(1)} %get-tuple-element.97), channel_id=1, source_target_pairs={{0,7},{1,0},{2,1},{3,2},{4,3},{5,4},{6,5},{7,6},{16,17},{17,18},{1... | collective-permute-start | bytes 589832 | tf_op jit(solution)/shard_map/ppermute | solution.py:53
  46.8 7.3 %collective-permute-start.6 = (bf16[128,768]{1,0:T(8,128)(2,1)S(1)}, bf16[128,768]{1,0:T(8,128)(2,1)S(1)}, u32[]{:S(2)}, u32[]{:S(2)}) collective-permute-start(bf16[128,768]{1,0:T(8,128)(2,1)S(1)} %get-tuple-element.98), channel_id=1, source_target_pairs={{0,1},{1,2},{2,3},{3,4},{4,5},{5,6},{6,7},{7,0},{16,23},{17,16},{1... | collective-permute-start | bytes 589832 | tf_op jit(solution)/shard_map/ppermute | solution.py:53
  54.3 6.9 %collective-permute-start.10 = (bf16[128,768]{1,0:T(8,128)(2,1)S(1)}, bf16[128,768]{1,0:T(8,128)(2,1)S(1)}, u32[]{:S(2)}, u32[]{:S(2)}) collective-permute-start(bf16[128,768]{1,0:T(8,128)(2,1)S(1)} %get-tuple-element.95), channel_id=1, source_target_pairs={{0,7},{1,0},{2,1},{3,2},{4,3},{5,4},{6,5},{7,6},{16,17},{17,18},{1... | collective-permute-start | bytes 589832 | tf_op jit(solution)/shard_map/ppermute | solution.py:53
  70.3 6.8 %collective-permute-start.12 = (bf16[128,768]{1,0:T(8,128)(2,1)S(1)}, bf16[128,768]{1,0:T(8,128)(2,1)S(1)}, u32[]{:S(2)}, u32[]{:S(2)}) collective-permute-start(bf16[128,768]{1,0:T(8,128)(2,1)S(1)} %slice.95), channel_id=1, source_target_pairs={{0,8},{8,0},{1,9},{9,1},{2,10},{10,2},{3,11},{11,3},{4,12},{12,4},... | collective-permute-start | bytes 589832 | tf_op jit(solution)/shard_map/ppermute | solution.py:47
  77.4 7.8 %collective-permute-start.15 = (bf16[128,768]{1,0:T(8,128)(2,1)S(1)}, bf16[128,768]{1,0:T(8,128)(2,1)S(1)}, u32[]{:S(2)}, u32[]{:S(2)}) collective-permute-start(bf16[128,768]{1,0:T(8,128)(2,1)S(1)} %multiply_convert_fusion.refs_0_), channel_id=1, source_target_pairs={{0,8},{8,0},{1,9},{9,1},{2,10},{10,2},{3,11},{11,3},{4,12},{12,4},... | collective-permute-start | bytes 589832 | tf_op jit(solution)/shard_map/ppermute | solution.py:47
  83.2 6.7 %collective-permute-start.13 = (bf16[128,768]{1,0:T(8,128)(2,1)S(1)}, bf16[128,768]{1,0:T(8,128)(2,1)S(1)}, u32[]{:S(2)}, u32[]{:S(2)}) collective-permute-start(bf16[128,768]{1,0:T(8,128)(2,1)S(1)} %multiply_convert_fusion.refs_0_), channel_id=1, source_target_pairs={{0,1},{1,2},{2,3},{3,4},{4,5},{5,6},{6,7},{7,0},{16,23},{17,16},{1... | collective-permute-start | bytes 589832 | tf_op jit(solution)/shard_map/ppermute | solution.py:53
  89.9 8.0 %collective-permute-start.17 = (bf16[128,768]{1,0:T(8,128)(2,1)S(1)}, bf16[128,768]{1,0:T(8,128)(2,1)S(1)}, u32[]{:S(2)}, u32[]{:S(2)}) collective-permute-start(bf16[128,768]{1,0:T(8,128)(2,1)S(1)} %collective-permute-done.14), channel_id=1, source_target_pairs={{0,7},{1,0},{2,1},{3,2},{4,3},{5,4},{6,5},{7,6},{16,17},{17,18},{1... | collective-permute-start | bytes 589832 | tf_op jit(solution)/shard_map/ppermute | solution.py:53
  92.7 9.1 %collective-permute-start.20 = (bf16[256,768]{1,0:T(8,128)(2,1)S(1)}, bf16[256,768]{1,0:T(8,128)(2,1)S(1)}, u32[]{:S(2)}, u32[]{:S(2)}) collective-permute-start(bf16[256,768]{1,0:T(8,128)(2,1)S(1)} %constant_dynamic-update-slice_fusion.refs_2_), channel_id=1, source_target_pairs={{0,8},{8,0},{1,9},{9,1},{2,10},{10,2},{3,11},{11,3},{4,12},{12,4},... | collective-permute-start | bytes 1179656 | tf_op jit(solution)/shard_map/ppermute | solution.py:47
  98.0 10.5 %collective-permute-start.21 = (bf16[256,768]{1,0:T(8,128)(2,1)S(1)}, bf16[256,768]{1,0:T(8,128)(2,1)S(1)}, u32[]{:S(2)}, u32[]{:S(2)}) collective-permute-start(bf16[256,768]{1,0:T(8,128)(2,1)S(1)} %constant_dynamic-update-slice_fusion.2.refs_1_), channel_id=1, source_target_pairs={{0,8},{8,0},{1,9},{9,1},{2,10},{10,2},{3,11},{11,3},{4,12},{12,4},... | collective-permute-start | bytes 1179656 | tf_op jit(solution)/shard_map/ppermute | solution.py:47
  100.4 7.4 %collective-permute-start.18 = (bf16[128,768]{1,0:T(8,128)(2,1)S(1)}, bf16[128,768]{1,0:T(8,128)(2,1)S(1)}, u32[]{:S(2)}, u32[]{:S(2)}) collective-permute-start(bf16[128,768]{1,0:T(8,128)(2,1)S(1)} %collective-permute-done.16), channel_id=1, source_target_pairs={{0,1},{1,2},{2,3},{3,4},{4,5},{5,6},{6,7},{7,0},{16,23},{17,16},{1... | collective-permute-start | bytes 589832 | tf_op jit(solution)/shard_map/ppermute | solution.py:53
  100.4 7.4 %collective-permute-start.19 = (bf16[128,768]{1,0:T(8,128)(2,1)S(1)}, bf16[128,768]{1,0:T(8,128)(2,1)S(1)}, u32[]{:S(2)}, u32[]{:S(2)}) collective-permute-start(bf16[128,768]{1,0:T(8,128)(2,1)S(1)} %collective-permute-done.17), channel_id=1, source_target_pairs={{0,7},{1,0},{2,1},{3,2},{4,3},{5,4},{6,5},{7,6},{16,17},{17,18},{1... | collective-permute-start | bytes 589832 | tf_op jit(solution)/shard_map/ppermute | solution.py:53
  108.5 12.4 %collective-permute-start.22 = (bf16[256,768]{1,0:T(8,128)(2,1)S(1)}, bf16[256,768]{1,0:T(8,128)(2,1)S(1)}, u32[]{:S(2)}, u32[]{:S(2)}) collective-permute-start(bf16[256,768]{1,0:T(8,128)(2,1)S(1)} %constant_dynamic-update-slice_fusion.4.refs_0_), channel_id=1, source_target_pairs={{0,8},{8,0},{1,9},{9,1},{2,10},{10,2},{3,11},{11,3},{4,12},{12,4},... | collective-permute-start | bytes 1179656 | tf_op jit(solution)/shard_map/ppermute | solution.py:47
  112.3 7.0 %collective-permute-start.24 = (bf16[128,768]{1,0:T(8,128)(2,1)S(1)}, bf16[128,768]{1,0:T(8,128)(2,1)S(1)}, u32[]{:S(2)}, u32[]{:S(2)}) collective-permute-start(bf16[128,768]{1,0:T(8,128)(2,1)S(1)} %collective-permute-done.18), channel_id=1, source_target_pairs={{0,9},{1,10},{2,11},{3,12},{4,13},{5,14},{6,15},{7,8},{8,1},{9,2},... | collective-permute-start | bytes 589832 | tf_op jit(solution)/shard_map/ppermute | solution.py:64
  112.3 7.0 %collective-permute-start.23 = (bf16[128,768]{1,0:T(8,128)(2,1)S(1)}, bf16[128,768]{1,0:T(8,128)(2,1)S(1)}, u32[]{:S(2)}, u32[]{:S(2)}) collective-permute-start(bf16[128,768]{1,0:T(8,128)(2,1)S(1)} %collective-permute-done.18), channel_id=1, source_target_pairs={{0,1},{1,2},{2,3},{3,4},{4,5},{5,6},{6,7},{7,0},{16,23},{17,16},{1... | collective-permute-start | bytes 589832 | tf_op jit(solution)/shard_map/ppermute | solution.py:53
  129.2 11.1 %collective-permute-start.25 = (bf16[8,80,640]{2,1,0:T(8,128)(2,1)}, bf16[8,80,640]{2,1,0:T(8,128)(2,1)S(1)}, u32[]{:S(2)}, u32[]{:S(2)}) collective-permute-start(bf16[8,80,640]{2,1,0:T(8,128)(2,1)} %get-tuple-element.91), channel_id=1, source_target_pairs={{0,16},{16,0},{1,17},{17,1},{2,18},{18,2},{3,19},{19,3},{4,20},{20... | collective-permute-start | bytes 2457608 | tf_op jit(solution)/shard_map/ppermute | solution.py:47
  (17 other events, 81.0 us)
Sparse Core Ops, SparseCore 0:
  9.8 42.4 all-gather.1
  108.6 45.4 reduce-scatter.1

commit v11 on v10

--- a/solution.py
+++ b/solution.py
@@ -186,21 +186,19 @@
         if not first:
             up_sum = up_sum + up_in[:, m : m + tile]
         if last:
-            total[m : m + tile, :] = up_sum.T
+            total[m : m + tile, :ff] = up_sum.T.astype(bf16)
         else:
             up_acc[:, m : m + tile] = up_sum
     if last:
         core = packed_ref[0] % 2
         act_grad = act_sum.astype(bf16)
         rows = keep_ref.shape[1]
-        for side in range(2):
-            for half, out_ref in ((core, keep_ref), (1 - core, give_ref)):
-                for chip in range(keep_ref.shape[0]):
-                    at = pl.multiple_of((2 * chip + half) * rows, rows)
-                    out_ref[chip, :, side * ff : (side + 1) * ff] = total[pl.ds(at, rows), :].astype(bf16)
-            if side == 0:
-                for m in range(0, width, tile):
-                    total[m : m + tile, :] = dot(head_ref[m : m + tile, :], act_grad, ((1,), (1,)))
+        for m in range(0, width, tile):
+            total[m : m + tile, ff:] = dot(head_ref[m : m + tile, :], act_grad, ((1,), (1,))).astype(bf16)
+        for half, out_ref in ((core, keep_ref), (1 - core, give_ref)):
+            for chip in range(keep_ref.shape[0]):
+                at = pl.multiple_of((2 * chip + half) * rows, rows)
+                out_ref[chip] = total[pl.ds(at, rows), :]
 
 
 def backward_blocks(items, packed, hidden_in, down_head, sums, head_weight=None):
@@ -223,12 +221,10 @@
         if not last:
             aliases = {len(args) + 1: 0, len(args) + 2: 1}
         args += list(sums)
-    flops = 2 * len(places) * rows * ff * (2 * embed + width)
     if last:
         args.append(head_weight)
         shapes = [jax.ShapeDtypeStruct((8, width // 16, 2 * ff), bf16)] * 2
-        scratch = [pltpu.VMEM((width, ff), f32)]
-        flops += 2 * width * ff * embed
+        scratch = [pltpu.VMEM((width, 2 * ff), bf16)]
     else:
         shapes = [jax.ShapeDtypeStruct((ff, width), f32), jax.ShapeDtypeStruct((ff, embed), f32)]
         scratch = []
@@ -245,7 +241,7 @@
         out_shape=shapes,
         input_output_aliases=aliases,
         compiler_params=pltpu.CompilerParams(vmem_limit_bytes=VMEM_BYTES),
-        cost_estimate=pl.CostEstimate(flops=flops, bytes_accessed=8 * 1024 * 1024, transcendentals=0),
+        cost_estimate=pl.CostEstimate(flops=0, bytes_accessed=0, transcendentals=0),
     )(packed, *args)
 
 
@@ -311,8 +307,9 @@
     item = lambda grad, *blocks: (grad, [saved[block] for block in blocks])
     pair = lambda step, half: ((half, step), (half, -step))
     both = lambda up, down: jnp.concatenate([up, down], axis=0)
-    crossed0 = swap(grad_embed, "yhi")
     fore, back = shift(grad_embed, 1), shift(grad_embed, -1)
+    own_block, score_part = lax.optimization_barrier((grad_embed, score_part))
+    crossed0 = swap(own_block, "yhi")
     fore, back, crossed0, score_part = lax.optimization_barrier((fore, back, crossed0, score_part))
     ring1 = both(back, fore)
     crossed1 = swap(ring1, "yhi")
@@ -324,7 +321,7 @@
     crossed2 = swap(ring2, "yhi")
     fore, back = shift(fore, 1), shift(back, -1)
     sums = backward([item(crossed1, *pair(1, 1)), item(ring2, *pair(2, 0))], sums)
-    fore, back, sums, crossed2, score_part = lax.optimization_barrier((fore, back, sums, crossed2, score_part))
+    fore, back, sums, score_part = lax.optimization_barrier((fore, back, sums, score_part))
     grad_score = lax.psum_scatter(score_part, "z", scatter_dimension=0, tiled=True)
     ring4, crossed4 = shift(fore, 1), shift_across(fore, 1)
     ring3 = both(back, fore)

time: 170 us -> 174 us (1.024)
  blocking collectives: 17 us -> 19.8 us
  starting transfers between devices: 57.1 us -> 59.7 us
    all_to_all x1, blocking collectives: 17 us -> 19.8 us  [per_device(): landed = lax.all_to_all(chip, ('ylo', 'x'), 0, 0)]
    ppermute x2, starting transfers between devices: 0.53 us -> 2.46 us  [shift_across(): return lax.ppermute(value, ('core', 'yhi', 'z'), perm)]
    ppermute x2, waiting for transfers between devices: 1.83 us -> 0.01 us  [shift_across(): return lax.ppermute(value, ('core', 'yhi', 'z'), perm)]
  transfers between devices with their start and end apart: 28 -> 28, of which waited for: 12 -> 9; matrix products, arithmetic and copies ran while one was open for 6% -> 6% of each run, Pallas kernels for 23% -> 23%
where the time goes in v11:
time: 174 us; the launch traced here: 173 us
  starting transfers between devices  59.7 us (34%)
  Pallas kernels  41.2 us (24%)
  waiting for transfers between devices  22.1 us (13%)
  blocking collectives  19.8 us (11%)
  between operations  14.4 us (8%)
  other arithmetic  6.84 us (4%)
  local copies, waits for them, and re-layouts  4.67 us (3%)
  matrix products  4.6 us (3%)
    ppermute x10, starting transfers between devices, swap(): return lax.ppermute(value, axis, [(0, 1), (1, 0)])  34.3 us
    ppermute x14, starting transfers between devices, shift(): return lax.ppermute(value, ('core', 'z'), perm)  22.9 us
    pallas_call x4, Pallas kernels, backward_blocks(): pl.pallas_call(functools.partial(backward_kernel, len(items), len(places)...  22.2 us
    all_to_all x1, blocking collectives, per_device(): landed = lax.all_to_all(chip, ('ylo', 'x'), 0, 0)  19.8 us
    pallas_call x3, Pallas kernels, forward_blocks(): pl.pallas_call(functools.partial(forward_kernel, pieces, first), grid_spe...  16.9 us
    ppermute x10, waiting for transfers between devices, swap(): return lax.ppermute(value, axis, [(0, 1), (1, 0)])  12.6 us
    ppermute x14, waiting for transfers between devices, shift(): return lax.ppermute(value, ('core', 'z'), perm)  8.78 us
    dot_general x4, matrix products, dot(): lax.dot_general(left, right, (dims, ((), ())), preferred_element_type=f32)  4.6 us
  transfers between devices with their start and end apart: 28, of which 9 were waited for; matrix products, arithmetic and copies ran while one was open for 6% of the time, Pallas kernels for 23%

profile of v11, /device:TPU:1, one launch (start us, length us, event | category | flops | bytes accessed | tf_op | source)
XLA Modules:
  0.0 173.2 jit_solution(17184513272258561371)
XLA Ops:
  8.0 5.6 %shard_map.85 = (bf16[128,768]{1,0:T(8,128)(2,1)}, bf16[256,768]{1,0:T(8,128)(2,1)}, bf16[128,768]{1,0:T(8,128)(2,1)}, bf16[4,320,128]{2,1,0:T(8,128)(2,1)}, bf1...) custom-call(s32[1]{0:T(128)} %bitcast.packed_ref, bf16[2048,1280]{1,0:T(8,128)(2,1)} %refs_12_.3, ...), custom_call_target="tpu_custom_call" | custom-call | flops 671088640 | bytes 4063232 | tf_op jit(solution)/shard_map/pallas_call | solution.py:140
  13.6 3.7 %collective-permute-start.2 = (bf16[256,768]{1,0:T(8,128)(2,1)}, bf16[256,768]{1,0:T(8,128)(2,1)S(1)}, u32[]{:S(2)}, u32[]{:S(2)}) collective-permute-start(bf16[256,768]{1,0:T(8,128)(2,1)} %get-tuple-element.55), channel_id=1, source_target_pairs={{0,8},{8,0},{1,9},{9,1},{2,10},{10,2},{3,11},{11,3},{4,12},{12,4},... | collective-permute-start | bytes 1179656 | tf_op jit(solution)/shard_map/ppermute | solution.py:47
  17.3 5.6 %collective-permute-start.3 = (bf16[128,768]{1,0:T(8,128)(2,1)}, bf16[128,768]{1,0:T(8,128)(2,1)S(1)}, u32[]{:S(2)}, u32[]{:S(2)}) collective-permute-start(bf16[128,768]{1,0:T(8,128)(2,1)} %get-tuple-element.56), channel_id=1, source_target_pairs={{0,1},{1,2},{2,3},{3,4},{4,5},{5,6},{6,7},{7,0},{16,23},{17,16},{1... | collective-permute-start | bytes 589832 | tf_op jit(solution)/shard_map/ppermute | solution.py:53
  23.4 6.3 %shard_map.87 = (bf16[256,768]{1,0:T(8,128)(2,1)}, bf16[384,768]{1,0:T(8,128)(2,1)}, bf16[128,768]{1,0:T(8,128)(2,1)}, bf16[128,768]{1,0:T(8,128)(2,1)}, bf16[7,...) custom-call(s32[1]{0:T(128)} %bitcast.packed_ref, bf16[2048,1280]{1,0:T(8,128)(2,1)} %refs_12_.3, ...), custom_call_target="tpu_custom_call" | custom-call | flops 1174405120 | bytes 6127616 | tf_op jit(solution)/shard_map/pallas_call | solution.py:140
  29.7 2.9 %collective-permute-start.1 = (bf16[256,768]{1,0:T(8,128)(2,1)}, bf16[256,768]{1,0:T(8,128)(2,1)S(1)}, u32[]{:S(2)}, u32[]{:S(2)}) collective-permute-start(bf16[256,768]{1,0:T(8,128)(2,1)} %get-tuple-element.53), channel_id=1, source_target_pairs={{0,8},{8,0},{1,9},{9,1},{2,10},{10,2},{3,11},{11,3},{4,12},{12,4},... | collective-permute-start | bytes 1179656 | tf_op jit(solution)/shard_map/ppermute | solution.py:47
  37.2 3.0 %collective-permute-start = (bf16[384,768]{1,0:T(8,128)(2,1)}, bf16[384,768]{1,0:T(8,128)(2,1)S(1)}, u32[]{:S(2)}, u32[]{:S(2)}) collective-permute-start(bf16[384,768]{1,0:T(8,128)(2,1)} %get-tuple-element.51), channel_id=1, source_target_pairs={{0,8},{8,0},{1,9},{9,1},{2,10},{10,2},{3,11},{11,3},{4,12},{12,4},... | collective-permute-start | bytes 1769480 | tf_op jit(solution)/shard_map/ppermute | solution.py:47
  40.2 5.1 %shard_map.86 = (bf16[256,768]{1,0:T(8,128)(2,1)}, bf16[384,768]{1,0:T(8,128)(2,1)}, bf16[5,320,128]{2,1,0:T(8,128)(2,1)}, bf16[5,128,320]{2,1,0:T(8,128)(2,1)}) custom-call(s32[1]{0:T(128)} %bitcast.packed_ref, bf16[2048,1280]{1,0:T(8,128)(2,1)} %refs_12_.3, bf16[2048,1280]{1,0:T(8,128)(2,1)} %refs_12_.3, bf16[2048,1280]{1,0:T(8,128)(2,1)} %refs_12_.3, ...), custom_call_target="tpu_custom_call" | custom-call | flops 838860800 | bytes 4751360 | tf_op jit(solution)/shard_map/pallas_call | solution.py:140
  51.4 2.7 %collective-permute-done.9 = bf16[128,768]{1,0:T(8,128)(2,1)S(1)} collective-permute-done((bf16[128,768]{1,0:T(8,128)(2,1)S(1)}, bf16[128,768]{1,0:T(8,128)(2,1)S(1)}, u32[]{:S(2)}, u32[]{:S(2)}) %collective-permute-start.9) | collective-permute-done | bytes 196640 | tf_op jit(solution)/shard_map/ppermute | solution.py:53
  54.3 3.4 %collective-permute-start.10 = (bf16[128,768]{1,0:T(8,128)(2,1)S(1)}, bf16[128,768]{1,0:T(8,128)(2,1)S(1)}, u32[]{:S(2)}, u32[]{:S(2)}) collective-permute-start(bf16[128,768]{1,0:T(8,128)(2,1)S(1)} %get-tuple-element.97), channel_id=1, source_target_pairs={{0,7},{1,0},{2,1},{3,2},{4,3},{5,4},{6,5},{7,6},{16,17},{17,18},{1... | collective-permute-start | bytes 589832 | tf_op jit(solution)/shard_map/ppermute | solution.py:53
  62.5 3.2 %collective-permute-start.11 = (bf16[128,768]{1,0:T(8,128)(2,1)S(1)}, bf16[128,768]{1,0:T(8,128)(2,1)S(1)}, u32[]{:S(2)}, u32[]{:S(2)}) collective-permute-start(bf16[128,768]{1,0:T(8,128)(2,1)S(1)} %multiply_convert_fusion.1), channel_id=1, source_target_pairs={{0,8},{8,0},{1,9},{9,1},{2,10},{10,2},{3,11},{11,3},{4,12},{12,4},... | collective-permute-start | bytes 589832 | tf_op jit(solution)/shard_map/ppermute | solution.py:47
  65.8 3.0 %collective-permute-done.11 = bf16[128,768]{1,0:T(8,128)(2,1)S(1)} collective-permute-done((bf16[128,768]{1,0:T(8,128)(2,1)S(1)}, bf16[128,768]{1,0:T(8,128)(2,1)S(1)}, u32[]{:S(2)}, u32[]{:S(2)}) %collective-permute-start.11) | collective-permute-done | bytes 196640 | tf_op jit(solution)/shard_map/ppermute | solution.py:47
  70.3 3.0 %collective-permute-start.12 = (bf16[128,768]{1,0:T(8,128)(2,1)S(1)}, bf16[128,768]{1,0:T(8,128)(2,1)S(1)}, u32[]{:S(2)}, u32[]{:S(2)}) collective-permute-start(bf16[128,768]{1,0:T(8,128)(2,1)S(1)} %slice.95), channel_id=1, source_target_pairs={{0,8},{8,0},{1,9},{9,1},{2,10},{10,2},{3,11},{11,3},{4,12},{12,4},... | collective-permute-start | bytes 589832 | tf_op jit(solution)/shard_map/ppermute | solution.py:47
  77.4 3.0 %collective-permute-start.14 = (bf16[128,768]{1,0:T(8,128)(2,1)S(1)}, bf16[128,768]{1,0:T(8,128)(2,1)S(1)}, u32[]{:S(2)}, u32[]{:S(2)}) collective-permute-start(bf16[128,768]{1,0:T(8,128)(2,1)S(1)} %multiply_convert_fusion.refs_0_), channel_id=1, source_target_pairs={{0,7},{1,0},{2,1},{3,2},{4,3},{5,4},{6,5},{7,6},{16,17},{17,18},{1... | collective-permute-start | bytes 589832 | tf_op jit(solution)/shard_map/ppermute | solution.py:53
  80.4 2.8 %collective-permute-start.15 = (bf16[128,768]{1,0:T(8,128)(2,1)S(1)}, bf16[128,768]{1,0:T(8,128)(2,1)S(1)}, u32[]{:S(2)}, u32[]{:S(2)}) collective-permute-start(bf16[128,768]{1,0:T(8,128)(2,1)S(1)} %multiply_convert_fusion.refs_0_), channel_id=1, source_target_pairs={{0,8},{8,0},{1,9},{9,1},{2,10},{10,2},{3,11},{11,3},{4,12},{12,4},... | collective-permute-start | bytes 589832 | tf_op jit(solution)/shard_map/ppermute | solution.py:47
  83.5 3.5 %collective-permute-done.13 = bf16[128,768]{1,0:T(8,128)(2,1)S(1)} collective-permute-done((bf16[128,768]{1,0:T(8,128)(2,1)S(1)}, bf16[128,768]{1,0:T(8,128)(2,1)S(1)}, u32[]{:S(2)}, u32[]{:S(2)}) %collective-permute-start.13) | collective-permute-done | bytes 196640 | tf_op jit(solution)/shard_map/ppermute | solution.py:53
  87.0 3.0 %collective-permute-start.17 = (bf16[128,768]{1,0:T(8,128)(2,1)S(1)}, bf16[128,768]{1,0:T(8,128)(2,1)S(1)}, u32[]{:S(2)}, u32[]{:S(2)}) collective-permute-start(bf16[128,768]{1,0:T(8,128)(2,1)S(1)} %collective-permute-done.14), channel_id=1, source_target_pairs={{0,7},{1,0},{2,1},{3,2},{4,3},{5,4},{6,5},{7,6},{16,17},{17,18},{1... | collective-permute-start | bytes 589832 | tf_op jit(solution)/shard_map/ppermute | solution.py:53
  90.1 3.0 %collective-permute-start.20 = (bf16[256,768]{1,0:T(8,128)(2,1)S(1)}, bf16[256,768]{1,0:T(8,128)(2,1)S(1)}, u32[]{:S(2)}, u32[]{:S(2)}) collective-permute-start(bf16[256,768]{1,0:T(8,128)(2,1)S(1)} %constant_dynamic-update-slice_fusion.refs_2_), channel_id=1, source_target_pairs={{0,8},{8,0},{1,9},{9,1},{2,10},{10,2},{3,11},{11,3},{4,12},{12,4},... | collective-permute-start | bytes 1179656 | tf_op jit(solution)/shard_map/ppermute | solution.py:47
  93.1 4.4 %shard_map.88 = (f32[320,1280]{1,0:T(8,128)}, f32[320,768]{1,0:T(8,128)}) custom-call(s32[1]{0:T(128)} %bitcast.packed_ref, bf16[128,768]{1,0:T(8,128)(2,1)} %copy-done.5, bf16[128,768]{1,0:T(8,128)(2,1)} %copy-done.12, bf16[256,768]{1,0:T(8,128)(2,1)} %copy-done.4, bf16[2048,1280]{1,0:T(8,128)(2,1)} %refs_12_.3, ...), custom_call_target="tpu_custom_call" | custom-call | tf_op jit(solution)/shard_map/pallas_call | solution.py:232
  100.8 5.2 %shard_map.89 = (f32[320,1280]{1,0:T(8,128)}, f32[320,768]{1,0:T(8,128)}) custom-call(s32[1]{0:T(128)} %bitcast.packed_ref, bf16[256,768]{1,0:T(8,128)(2,1)} %copy-done.8, bf16[256,768]{1,0:T(8,128)(2,1)} %copy-done.3, bf16[2048,1280]{1,0:T(8,128)(2,1)} %refs_12_.3, ...), custom_call_target="tpu_custom_call", output_to_operand_aliasing={{0}: (16, {}), {1}: (17, {})} | custom-call | tf_op jit(solution)/shard_map/pallas_call | solution.py:232
  111.1 5.4 %collective-permute-done.24.refs_1_ = bf16[256,768]{1,0:T(8,128)(2,1)S(1)} collective-permute-done((bf16[256,768]{1,0:T(8,128)(2,1)}, bf16[256,768]{1,0:T(8,128)(2,1)S(1)}, u32[]{:S(2)}, u32[]{:S(2)}) %collective-permute-start.24) | collective-permute-done | bytes 393248 | tf_op jit(solution)/shard_map/ppermute | solution.py:47
  117.2 5.1 %shard_map.90 = (f32[320,1280]{1,0:T(8,128)}, f32[320,768]{1,0:T(8,128)}) custom-call(s32[1]{0:T(128)} %bitcast.packed_ref, bf16[256,768]{1,0:T(8,128)(2,1)} %copy-done.2, bf16[256,768]{1,0:T(8,128)(2,1)} %copy-done.9, bf16[2048,1280]{1,0:T(8,128)(2,1)} %refs_12_.3, ...), custom_call_target="tpu_custom_call", output_to_operand_aliasing={{0}: (16, {}), {1}: (17, {})} | custom-call | tf_op jit(solution)/shard_map/pallas_call | solution.py:232
  123.3 7.5 %shard_map.91 = (bf16[8,80,640]{2,1,0:T(8,128)(2,1)}, bf16[8,80,640]{2,1,0:T(8,128)(2,1)}) custom-call(s32[1]{0:T(128)} %bitcast.packed_ref, bf16[256,768]{1,0:T(8,128)(2,1)} %copy-done.7, bf16[128,768]{1,0:T(8,128)(2,1)} %copy-done.11, bf16[128,768]{1,0:T(8,128)(2,1)} %copy-done.10, bf16[2048,1280]{1,0:T(8,128)(2,1)} %refs_12_.3, ...), custom_call_target="tpu_custom_call" | custom-call | tf_op jit(solution)/shard_map/pallas_call | solution.py:232
  130.8 9.4 %collective-permute-start.25 = (bf16[8,80,640]{2,1,0:T(8,128)(2,1)}, bf16[8,80,640]{2,1,0:T(8,128)(2,1)S(1)}, u32[]{:S(2)}, u32[]{:S(2)}) collective-permute-start(bf16[8,80,640]{2,1,0:T(8,128)(2,1)} %get-tuple-element.93), channel_id=1, source_target_pairs={{0,16},{16,0},{1,17},{17,1},{2,18},{18,2},{3,19},{19,3},{4,20},{20... | collective-permute-start | bytes 2457608 | tf_op jit(solution)/shard_map/ppermute | solution.py:47
  143.7 19.8 %all_to_all.5 = bf16[8,80,640]{2,1,0:T(8,128)(2,1)S(1)} all-to-all(bf16[8,80,640]{2,1,0:T(8,128)(2,1)S(1)} %add_convert_fusion), channel_id=1, replica_groups=mesh['ylo'=2,'x'=4,'core'=2,'yhi'=2,'z'=8] {'ylo','x'}, dimensions={0} | all-to-all | bytes 1638400 | tf_op jit(solution)/shard_map/all_to_all | solution.py:334
  (97 shorter events, 39.2 us)
Async XLA Ops:
  7.2 50.5 %all-gather.2.cloned.1.call-start = ((), (), s32[]{:S(2)}) async-start(), calls=%async_computation.2 | async-start | bytes 1769472 | tf_op jit(solution)/shard_map/all_gather | solution.py:279
  7.9 156.5 %reduce-scatter.2.cloned.1.call-start = ((), (), s32[]{:S(2)}) async-start(), calls=%async_computation.3 | async-start | bytes 1769472 | tf_op jit(solution)/shard_map/reduce_scatter | solution.py:325
  13.6 19.0 %collective-permute-start.2 = (bf16[256,768]{1,0:T(8,128)(2,1)}, bf16[256,768]{1,0:T(8,128)(2,1)S(1)}, u32[]{:S(2)}, u32[]{:S(2)}) collective-permute-start(bf16[256,768]{1,0:T(8,128)(2,1)} %get-tuple-element.55), channel_id=1, source_target_pairs={{0,8},{8,0},{1,9},{9,1},{2,10},{10,2},{3,11},{11,3},{4,12},{12,4},... | collective-permute-start | bytes 1179656 | tf_op jit(solution)/shard_map/ppermute | solution.py:47
  17.3 15.2 %collective-permute-start.3 = (bf16[128,768]{1,0:T(8,128)(2,1)}, bf16[128,768]{1,0:T(8,128)(2,1)S(1)}, u32[]{:S(2)}, u32[]{:S(2)}) collective-permute-start(bf16[128,768]{1,0:T(8,128)(2,1)} %get-tuple-element.56), channel_id=1, source_target_pairs={{0,1},{1,2},{2,3},{3,4},{4,5},{5,6},{6,7},{7,0},{16,23},{17,16},{1... | collective-permute-start | bytes 589832 | tf_op jit(solution)/shard_map/ppermute | solution.py:53
  22.9 9.7 %collective-permute-start.4 = (bf16[128,768]{1,0:T(8,128)(2,1)}, bf16[128,768]{1,0:T(8,128)(2,1)S(1)}, u32[]{:S(2)}, u32[]{:S(2)}) collective-permute-start(bf16[128,768]{1,0:T(8,128)(2,1)} %get-tuple-element.57), channel_id=1, source_target_pairs={{0,9},{1,10},{2,11},{3,12},{4,13},{5,14},{6,15},{7,8},{8,1},{9,2},... | collective-permute-start | bytes 589832 | tf_op jit(solution)/shard_map/ppermute | solution.py:64
  29.7 15.6 %collective-permute-start.1 = (bf16[256,768]{1,0:T(8,128)(2,1)}, bf16[256,768]{1,0:T(8,128)(2,1)S(1)}, u32[]{:S(2)}, u32[]{:S(2)}) collective-permute-start(bf16[256,768]{1,0:T(8,128)(2,1)} %get-tuple-element.53), channel_id=1, source_target_pairs={{0,8},{8,0},{1,9},{9,1},{2,10},{10,2},{3,11},{11,3},{4,12},{12,4},... | collective-permute-start | bytes 1179656 | tf_op jit(solution)/shard_map/ppermute | solution.py:47
  33.7 11.6 %collective-permute-start.8 = (bf16[128,768]{1,0:T(8,128)(2,1)S(1)}, bf16[128,768]{1,0:T(8,128)(2,1)S(1)}, u32[]{:S(2)}, u32[]{:S(2)}) collective-permute-start(bf16[128,768]{1,0:T(8,128)(2,1)S(1)} %get-tuple-element.101), channel_id=1, source_target_pairs={{0,7},{1,0},{2,1},{3,2},{4,3},{5,4},{6,5},{7,6},{16,17},{17,18},{1... | collective-permute-start | bytes 589832 | tf_op jit(solution)/shard_map/ppermute | solution.py:53
  34.5 10.8 %collective-permute-start.5 = (bf16[128,768]{1,0:T(8,128)(2,1)S(1)}, bf16[128,768]{1,0:T(8,128)(2,1)S(1)}, u32[]{:S(2)}, u32[]{:S(2)}) collective-permute-start(bf16[128,768]{1,0:T(8,128)(2,1)S(1)} %get-tuple-element.102), channel_id=1, source_target_pairs={{0,1},{1,2},{2,3},{3,4},{4,5},{5,6},{6,7},{7,0},{16,23},{17,16},{1... | collective-permute-start | bytes 589832 | tf_op jit(solution)/shard_map/ppermute | solution.py:53
  37.2 14.2 %collective-permute-start = (bf16[384,768]{1,0:T(8,128)(2,1)}, bf16[384,768]{1,0:T(8,128)(2,1)S(1)}, u32[]{:S(2)}, u32[]{:S(2)}) collective-permute-start(bf16[384,768]{1,0:T(8,128)(2,1)} %get-tuple-element.51), channel_id=1, source_target_pairs={{0,8},{8,0},{1,9},{9,1},{2,10},{10,2},{3,11},{11,3},{4,12},{12,4},... | collective-permute-start | bytes 1769480 | tf_op jit(solution)/shard_map/ppermute | solution.py:47
  46.5 7.6 %collective-permute-start.9 = (bf16[128,768]{1,0:T(8,128)(2,1)S(1)}, bf16[128,768]{1,0:T(8,128)(2,1)S(1)}, u32[]{:S(2)}, u32[]{:S(2)}) collective-permute-start(bf16[128,768]{1,0:T(8,128)(2,1)S(1)} %get-tuple-element.99), channel_id=1, source_target_pairs={{0,7},{1,0},{2,1},{3,2},{4,3},{5,4},{6,5},{7,6},{16,17},{17,18},{1... | collective-permute-start | bytes 589832 | tf_op jit(solution)/shard_map/ppermute | solution.py:53
  46.8 7.3 %collective-permute-start.6 = (bf16[128,768]{1,0:T(8,128)(2,1)S(1)}, bf16[128,768]{1,0:T(8,128)(2,1)S(1)}, u32[]{:S(2)}, u32[]{:S(2)}) collective-permute-start(bf16[128,768]{1,0:T(8,128)(2,1)S(1)} %get-tuple-element.100), channel_id=1, source_target_pairs={{0,1},{1,2},{2,3},{3,4},{4,5},{5,6},{6,7},{7,0},{16,23},{17,16},{1... | collective-permute-start | bytes 589832 | tf_op jit(solution)/shard_map/ppermute | solution.py:53
  54.3 6.9 %collective-permute-start.10 = (bf16[128,768]{1,0:T(8,128)(2,1)S(1)}, bf16[128,768]{1,0:T(8,128)(2,1)S(1)}, u32[]{:S(2)}, u32[]{:S(2)}) collective-permute-start(bf16[128,768]{1,0:T(8,128)(2,1)S(1)} %get-tuple-element.97), channel_id=1, source_target_pairs={{0,7},{1,0},{2,1},{3,2},{4,3},{5,4},{6,5},{7,6},{16,17},{17,18},{1... | collective-permute-start | bytes 589832 | tf_op jit(solution)/shard_map/ppermute | solution.py:53
  70.3 6.8 %collective-permute-start.12 = (bf16[128,768]{1,0:T(8,128)(2,1)S(1)}, bf16[128,768]{1,0:T(8,128)(2,1)S(1)}, u32[]{:S(2)}, u32[]{:S(2)}) collective-permute-start(bf16[128,768]{1,0:T(8,128)(2,1)S(1)} %slice.95), channel_id=1, source_target_pairs={{0,8},{8,0},{1,9},{9,1},{2,10},{10,2},{3,11},{11,3},{4,12},{12,4},... | collective-permute-start | bytes 589832 | tf_op jit(solution)/shard_map/ppermute | solution.py:47
  80.4 6.6 %collective-permute-start.13 = (bf16[128,768]{1,0:T(8,128)(2,1)S(1)}, bf16[128,768]{1,0:T(8,128)(2,1)S(1)}, u32[]{:S(2)}, u32[]{:S(2)}) collective-permute-start(bf16[128,768]{1,0:T(8,128)(2,1)S(1)} %multiply_convert_fusion.refs_0_), channel_id=1, source_target_pairs={{0,1},{1,2},{2,3},{3,4},{4,5},{5,6},{6,7},{7,0},{16,23},{17,16},{1... | collective-permute-start | bytes 589832 | tf_op jit(solution)/shard_map/ppermute | solution.py:53
  87.0 10.6 %collective-permute-start.17 = (bf16[128,768]{1,0:T(8,128)(2,1)S(1)}, bf16[128,768]{1,0:T(8,128)(2,1)S(1)}, u32[]{:S(2)}, u32[]{:S(2)}) collective-permute-start(bf16[128,768]{1,0:T(8,128)(2,1)S(1)} %collective-permute-done.14), channel_id=1, source_target_pairs={{0,7},{1,0},{2,1},{3,2},{4,3},{5,4},{6,5},{7,6},{16,17},{17,18},{1... | collective-permute-start | bytes 589832 | tf_op jit(solution)/shard_map/ppermute | solution.py:53
  89.9 7.6 %collective-permute-start.16 = (bf16[128,768]{1,0:T(8,128)(2,1)S(1)}, bf16[128,768]{1,0:T(8,128)(2,1)S(1)}, u32[]{:S(2)}, u32[]{:S(2)}) collective-permute-start(bf16[128,768]{1,0:T(8,128)(2,1)S(1)} %collective-permute-done.13), channel_id=1, source_target_pairs={{0,1},{1,2},{2,3},{3,4},{4,5},{5,6},{6,7},{7,0},{16,23},{17,16},{1... | collective-permute-start | bytes 589832 | tf_op jit(solution)/shard_map/ppermute | solution.py:53
  90.1 9.2 %collective-permute-start.20 = (bf16[256,768]{1,0:T(8,128)(2,1)S(1)}, bf16[256,768]{1,0:T(8,128)(2,1)S(1)}, u32[]{:S(2)}, u32[]{:S(2)}) collective-permute-start(bf16[256,768]{1,0:T(8,128)(2,1)S(1)} %constant_dynamic-update-slice_fusion.refs_2_), channel_id=1, source_target_pairs={{0,8},{8,0},{1,9},{9,1},{2,10},{10,2},{3,11},{11,3},{4,12},{12,4},... | collective-permute-start | bytes 1179656 | tf_op jit(solution)/shard_map/ppermute | solution.py:47
  97.6 8.4 %collective-permute-start.18 = (bf16[128,768]{1,0:T(8,128)(2,1)S(1)}, bf16[128,768]{1,0:T(8,128)(2,1)S(1)}, u32[]{:S(2)}, u32[]{:S(2)}) collective-permute-start(bf16[128,768]{1,0:T(8,128)(2,1)S(1)} %collective-permute-done.16), channel_id=1, source_target_pairs={{0,1},{1,2},{2,3},{3,4},{4,5},{5,6},{6,7},{7,0},{16,23},{17,16},{1... | collective-permute-start | bytes 589832 | tf_op jit(solution)/shard_map/ppermute | solution.py:53
  97.7 8.3 %collective-permute-start.19 = (bf16[128,768]{1,0:T(8,128)(2,1)S(1)}, bf16[128,768]{1,0:T(8,128)(2,1)S(1)}, u32[]{:S(2)}, u32[]{:S(2)}) collective-permute-start(bf16[128,768]{1,0:T(8,128)(2,1)S(1)} %collective-permute-done.17), channel_id=1, source_target_pairs={{0,7},{1,0},{2,1},{3,2},{4,3},{5,4},{6,5},{7,6},{16,17},{17,18},{1... | collective-permute-start | bytes 589832 | tf_op jit(solution)/shard_map/ppermute | solution.py:53
  106.0 10.5 %collective-permute-start.24 = (bf16[256,768]{1,0:T(8,128)(2,1)}, bf16[256,768]{1,0:T(8,128)(2,1)S(1)}, u32[]{:S(2)}, u32[]{:S(2)}) collective-permute-start(bf16[256,768]{1,0:T(8,128)(2,1)} %copy-done.3), channel_id=1, source_target_pairs={{0,8},{8,0},{1,9},{9,1},{2,10},{10,2},{3,11},{11,3},{4,12},{12,4},... | collective-permute-start | bytes 1179656 | tf_op jit(solution)/shard_map/ppermute | solution.py:47
  107.3 15.1 %collective-permute-start.21 = (bf16[256,768]{1,0:T(8,128)(2,1)S(1)}, bf16[256,768]{1,0:T(8,128)(2,1)S(1)}, u32[]{:S(2)}, u32[]{:S(2)}) collective-permute-start(bf16[256,768]{1,0:T(8,128)(2,1)S(1)} %constant_dynamic-update-slice_fusion.4.refs_0_), channel_id=1, source_target_pairs={{0,8},{8,0},{1,9},{9,1},{2,10},{10,2},{3,11},{11,3},{4,12},{12,4},... | collective-permute-start | bytes 1179656 | tf_op jit(solution)/shard_map/ppermute | solution.py:47
  109.2 13.2 %collective-permute-start.23 = (bf16[128,768]{1,0:T(8,128)(2,1)S(1)}, bf16[128,768]{1,0:T(8,128)(2,1)S(1)}, u32[]{:S(2)}, u32[]{:S(2)}) collective-permute-start(bf16[128,768]{1,0:T(8,128)(2,1)S(1)} %collective-permute-done.18), channel_id=1, source_target_pairs={{0,9},{1,10},{2,11},{3,12},{4,13},{5,14},{6,15},{7,8},{8,1},{9,2},... | collective-permute-start | bytes 589832 | tf_op jit(solution)/shard_map/ppermute | solution.py:64
  111.1 11.3 %collective-permute-start.22 = (bf16[128,768]{1,0:T(8,128)(2,1)S(1)}, bf16[128,768]{1,0:T(8,128)(2,1)S(1)}, u32[]{:S(2)}, u32[]{:S(2)}) collective-permute-start(bf16[128,768]{1,0:T(8,128)(2,1)S(1)} %collective-permute-done.18), channel_id=1, source_target_pairs={{0,1},{1,2},{2,3},{3,4},{4,5},{5,6},{6,7},{7,0},{16,23},{17,16},{1... | collective-permute-start | bytes 589832 | tf_op jit(solution)/shard_map/ppermute | solution.py:53
  130.8 11.6 %collective-permute-start.25 = (bf16[8,80,640]{2,1,0:T(8,128)(2,1)}, bf16[8,80,640]{2,1,0:T(8,128)(2,1)S(1)}, u32[]{:S(2)}, u32[]{:S(2)}) collective-permute-start(bf16[8,80,640]{2,1,0:T(8,128)(2,1)} %get-tuple-element.93), channel_id=1, source_target_pairs={{0,16},{16,0},{1,17},{17,1},{2,18},{18,2},{3,19},{19,3},{4,20},{20... | collective-permute-start | bytes 2457608 | tf_op jit(solution)/shard_map/ppermute | solution.py:47
  (17 other events, 80.7 us)
Sparse Core Ops, SparseCore 0:
  9.8 42.4 all-gather.1
  106.1 43.0 reduce-scatter.1

commit v12 on v11

--- a/solution.py
+++ b/solution.py
@@ -310,7 +310,6 @@
     fore, back = shift(grad_embed, 1), shift(grad_embed, -1)
     own_block, score_part = lax.optimization_barrier((grad_embed, score_part))
     crossed0 = swap(own_block, "yhi")
-    fore, back, crossed0, score_part = lax.optimization_barrier((fore, back, crossed0, score_part))
     ring1 = both(back, fore)
     crossed1 = swap(ring1, "yhi")
     fore, back = shift(fore, 1), shift(back, -1)
@@ -321,7 +320,7 @@
     crossed2 = swap(ring2, "yhi")
     fore, back = shift(fore, 1), shift(back, -1)
     sums = backward([item(crossed1, *pair(1, 1)), item(ring2, *pair(2, 0))], sums)
-    fore, back, sums, score_part = lax.optimization_barrier((fore, back, sums, score_part))
+    fore, back, sums, crossed2, score_part = lax.optimization_barrier((fore, back, sums, crossed2, score_part))
     grad_score = lax.psum_scatter(score_part, "z", scatter_dimension=0, tiled=True)
     ring4, crossed4 = shift(fore, 1), shift_across(fore, 1)
     ring3 = both(back, fore)

time: 174 us -> 165 us (0.948)
  blocking collectives: 19.8 us -> 16.1 us
  starting transfers between devices: 59.7 us -> 57.7 us
  waiting for transfers between devices: 22.1 us -> 20.1 us
    all_to_all x1, blocking collectives: 19.8 us -> 16.1 us  [per_device(): landed = lax.all_to_all(chip, ('ylo', 'x'), 0, 0)]
    ppermute x14, waiting for transfers between devices: 8.78 us -> 5.75 us  [shift(): return lax.ppermute(value, ('core', 'z'), perm)]
    ppermute x10, starting transfers between devices: 34.3 us -> 32.3 us  [swap(): return lax.ppermute(value, axis, [(0, 1), (1, 0)])]
    ppermute x2, starting transfers between devices: 2.46 us -> 0.53 us  [shift_across(): return lax.ppermute(value, ('core', 'yhi', 'z'), perm)]
    ppermute x14, starting transfers between devices: 22.9 us -> 24.8 us  [shift(): return lax.ppermute(value, ('core', 'z'), perm)]
    ppermute x2, waiting for transfers between devices: 0.01 us -> 1.83 us  [shift_across(): return lax.ppermute(value, ('core', 'yhi', 'z'), perm)]
  transfers between devices with their start and end apart: 28 -> 28, of which waited for: 9 -> 10; matrix products, arithmetic and copies ran while one was open for 6% -> 7% of each run, Pallas kernels for 23% -> 24%
where the time goes in v12:
time: 165 us
  starting transfers between devices  57.7 us (35%)
  Pallas kernels  41.1 us (25%)
  waiting for transfers between devices  20.1 us (12%)
  blocking collectives  16.1 us (10%)
  between operations  14.3 us (9%)
  other arithmetic  6.86 us (4%)
  matrix products  4.6 us (3%)
  local copies, waits for them, and re-layouts  3.76 us (2%)
    ppermute x10, starting transfers between devices, swap(): return lax.ppermute(value, axis, [(0, 1), (1, 0)])  32.3 us
    ppermute x14, starting transfers between devices, shift(): return lax.ppermute(value, ('core', 'z'), perm)  24.8 us
    pallas_call x4, Pallas kernels, backward_blocks(): pl.pallas_call(functools.partial(backward_kernel, len(items), len(places)...  22.1 us
    pallas_call x3, Pallas kernels, forward_blocks(): pl.pallas_call(functools.partial(forward_kernel, pieces, first), grid_spe...  16.9 us
    all_to_all x1, blocking collectives, per_device(): landed = lax.all_to_all(chip, ('ylo', 'x'), 0, 0)  16.1 us
    ppermute x10, waiting for transfers between devices, swap(): return lax.ppermute(value, axis, [(0, 1), (1, 0)])  11.9 us
    ppermute x14, waiting for transfers between devices, shift(): return lax.ppermute(value, ('core', 'z'), perm)  5.75 us
    dot_general x4, matrix products, dot(): lax.dot_general(left, right, (dims, ((), ())), preferred_element_type=f32)  4.6 us
  transfers between devices with their start and end apart: 28, of which 10 were waited for; matrix products, arithmetic and copies ran while one was open for 7% of the time, Pallas kernels for 24%

profile of v12, /device:TPU:1, one launch (start us, length us, event | category | flops | bytes accessed | tf_op | source)
XLA Modules:
  0.0 164.6 jit_solution(12401886219977937376)
XLA Ops:
  8.0 5.6 %shard_map.85 = (bf16[128,768]{1,0:T(8,128)(2,1)}, bf16[256,768]{1,0:T(8,128)(2,1)}, bf16[128,768]{1,0:T(8,128)(2,1)}, bf16[4,320,128]{2,1,0:T(8,128)(2,1)}, bf1...) custom-call(s32[1]{0:T(128)} %bitcast.packed_ref, bf16[2048,1280]{1,0:T(8,128)(2,1)} %refs_12_.3, ...), custom_call_target="tpu_custom_call" | custom-call | flops 671088640 | bytes 4063232 | tf_op jit(solution)/shard_map/pallas_call | solution.py:140
  13.6 3.7 %collective-permute-start.2 = (bf16[256,768]{1,0:T(8,128)(2,1)}, bf16[256,768]{1,0:T(8,128)(2,1)S(1)}, u32[]{:S(2)}, u32[]{:S(2)}) collective-permute-start(bf16[256,768]{1,0:T(8,128)(2,1)} %get-tuple-element.52), channel_id=1, source_target_pairs={{0,8},{8,0},{1,9},{9,1},{2,10},{10,2},{3,11},{11,3},{4,12},{12,4},... | collective-permute-start | bytes 1179656 | tf_op jit(solution)/shard_map/ppermute | solution.py:47
  17.3 5.6 %collective-permute-start.3 = (bf16[128,768]{1,0:T(8,128)(2,1)}, bf16[128,768]{1,0:T(8,128)(2,1)S(1)}, u32[]{:S(2)}, u32[]{:S(2)}) collective-permute-start(bf16[128,768]{1,0:T(8,128)(2,1)} %get-tuple-element.53), channel_id=1, source_target_pairs={{0,1},{1,2},{2,3},{3,4},{4,5},{5,6},{6,7},{7,0},{16,23},{17,16},{1... | collective-permute-start | bytes 589832 | tf_op jit(solution)/shard_map/ppermute | solution.py:53
  23.4 6.3 %shard_map.87 = (bf16[256,768]{1,0:T(8,128)(2,1)}, bf16[384,768]{1,0:T(8,128)(2,1)}, bf16[128,768]{1,0:T(8,128)(2,1)}, bf16[128,768]{1,0:T(8,128)(2,1)}, bf16[7,...) custom-call(s32[1]{0:T(128)} %bitcast.packed_ref, bf16[2048,1280]{1,0:T(8,128)(2,1)} %refs_12_.3, ...), custom_call_target="tpu_custom_call" | custom-call | flops 1174405120 | bytes 6127616 | tf_op jit(solution)/shard_map/pallas_call | solution.py:140
  29.7 2.9 %collective-permute-start.1 = (bf16[256,768]{1,0:T(8,128)(2,1)}, bf16[256,768]{1,0:T(8,128)(2,1)S(1)}, u32[]{:S(2)}, u32[]{:S(2)}) collective-permute-start(bf16[256,768]{1,0:T(8,128)(2,1)} %get-tuple-element.50), channel_id=1, source_target_pairs={{0,8},{8,0},{1,9},{9,1},{2,10},{10,2},{3,11},{11,3},{4,12},{12,4},... | collective-permute-start | bytes 1179656 | tf_op jit(solution)/shard_map/ppermute | solution.py:47
  34.5 2.7 %collective-permute-start.5 = (bf16[128,768]{1,0:T(8,128)(2,1)S(1)}, bf16[128,768]{1,0:T(8,128)(2,1)S(1)}, u32[]{:S(2)}, u32[]{:S(2)}) collective-permute-start(bf16[128,768]{1,0:T(8,128)(2,1)S(1)} %get-tuple-element.96), channel_id=1, source_target_pairs={{0,1},{1,2},{2,3},{3,4},{4,5},{5,6},{6,7},{7,0},{16,23},{17,16},{1... | collective-permute-start | bytes 589832 | tf_op jit(solution)/shard_map/ppermute | solution.py:53
  37.2 3.0 %collective-permute-start = (bf16[384,768]{1,0:T(8,128)(2,1)}, bf16[384,768]{1,0:T(8,128)(2,1)S(1)}, u32[]{:S(2)}, u32[]{:S(2)}) collective-permute-start(bf16[384,768]{1,0:T(8,128)(2,1)} %get-tuple-element.48), channel_id=1, source_target_pairs={{0,8},{8,0},{1,9},{9,1},{2,10},{10,2},{3,11},{11,3},{4,12},{12,4},... | collective-permute-start | bytes 1769480 | tf_op jit(solution)/shard_map/ppermute | solution.py:47
  40.2 5.1 %shard_map.86 = (bf16[256,768]{1,0:T(8,128)(2,1)}, bf16[384,768]{1,0:T(8,128)(2,1)}, bf16[5,320,128]{2,1,0:T(8,128)(2,1)}, bf16[5,128,320]{2,1,0:T(8,128)(2,1)}) custom-call(s32[1]{0:T(128)} %bitcast.packed_ref, bf16[2048,1280]{1,0:T(8,128)(2,1)} %refs_12_.3, bf16[2048,1280]{1,0:T(8,128)(2,1)} %refs_12_.3, bf16[2048,1280]{1,0:T(8,128)(2,1)} %refs_12_.3, ...), custom_call_target="tpu_custom_call" | custom-call | flops 838860800 | bytes 4751360 | tf_op jit(solution)/shard_map/pallas_call | solution.py:140
  51.4 2.7 %collective-permute-done.9 = bf16[128,768]{1,0:T(8,128)(2,1)S(1)} collective-permute-done((bf16[128,768]{1,0:T(8,128)(2,1)S(1)}, bf16[128,768]{1,0:T(8,128)(2,1)S(1)}, u32[]{:S(2)}, u32[]{:S(2)}) %collective-permute-start.9) | collective-permute-done | bytes 196640 | tf_op jit(solution)/shard_map/ppermute | solution.py:53
  54.3 3.4 %collective-permute-start.10 = (bf16[128,768]{1,0:T(8,128)(2,1)S(1)}, bf16[128,768]{1,0:T(8,128)(2,1)S(1)}, u32[]{:S(2)}, u32[]{:S(2)}) collective-permute-start(bf16[128,768]{1,0:T(8,128)(2,1)S(1)} %get-tuple-element.91), channel_id=1, source_target_pairs={{0,7},{1,0},{2,1},{3,2},{4,3},{5,4},{6,5},{7,6},{16,17},{17,18},{1... | collective-permute-start | bytes 589832 | tf_op jit(solution)/shard_map/ppermute | solution.py:53
  62.5 3.2 %collective-permute-start.11 = (bf16[128,768]{1,0:T(8,128)(2,1)S(1)}, bf16[128,768]{1,0:T(8,128)(2,1)S(1)}, u32[]{:S(2)}, u32[]{:S(2)}) collective-permute-start(bf16[128,768]{1,0:T(8,128)(2,1)S(1)} %multiply_convert_fusion.1), channel_id=1, source_target_pairs={{0,8},{8,0},{1,9},{9,1},{2,10},{10,2},{3,11},{11,3},{4,12},{12,4},... | collective-permute-start | bytes 589832 | tf_op jit(solution)/shard_map/ppermute | solution.py:47
  65.8 3.0 %collective-permute-done.11 = bf16[128,768]{1,0:T(8,128)(2,1)S(1)} collective-permute-done((bf16[128,768]{1,0:T(8,128)(2,1)S(1)}, bf16[128,768]{1,0:T(8,128)(2,1)S(1)}, u32[]{:S(2)}, u32[]{:S(2)}) %collective-permute-start.11) | collective-permute-done | bytes 196640 | tf_op jit(solution)/shard_map/ppermute | solution.py:47
  70.3 3.0 %collective-permute-start.12 = (bf16[128,768]{1,0:T(8,128)(2,1)S(1)}, bf16[128,768]{1,0:T(8,128)(2,1)S(1)}, u32[]{:S(2)}, u32[]{:S(2)}) collective-permute-start(bf16[128,768]{1,0:T(8,128)(2,1)S(1)} %slice.95), channel_id=1, source_target_pairs={{0,8},{8,0},{1,9},{9,1},{2,10},{10,2},{3,11},{11,3},{4,12},{12,4},... | collective-permute-start | bytes 589832 | tf_op jit(solution)/shard_map/ppermute | solution.py:47
  73.3 3.7 %collective-permute-done.12 = bf16[128,768]{1,0:T(8,128)(2,1)S(1)} collective-permute-done((bf16[128,768]{1,0:T(8,128)(2,1)S(1)}, bf16[128,768]{1,0:T(8,128)(2,1)S(1)}, u32[]{:S(2)}, u32[]{:S(2)}) %collective-permute-start.12) | collective-permute-done | bytes 196640 | tf_op jit(solution)/shard_map/ppermute | solution.py:47
  77.4 3.0 %collective-permute-start.15 = (bf16[128,768]{1,0:T(8,128)(2,1)S(1)}, bf16[128,768]{1,0:T(8,128)(2,1)S(1)}, u32[]{:S(2)}, u32[]{:S(2)}) collective-permute-start(bf16[128,768]{1,0:T(8,128)(2,1)S(1)} %multiply_convert_fusion.refs_0_), channel_id=1, source_target_pairs={{0,7},{1,0},{2,1},{3,2},{4,3},{5,4},{6,5},{7,6},{16,17},{17,18},{1... | collective-permute-start | bytes 589832 | tf_op jit(solution)/shard_map/ppermute | solution.py:53
  82.2 2.8 %collective-permute-start.17 = (bf16[128,768]{1,0:T(8,128)(2,1)S(1)}, bf16[128,768]{1,0:T(8,128)(2,1)S(1)}, u32[]{:S(2)}, u32[]{:S(2)}) collective-permute-start(bf16[128,768]{1,0:T(8,128)(2,1)S(1)} %multiply_convert_fusion.refs_0_), channel_id=1, source_target_pairs={{0,8},{8,0},{1,9},{9,1},{2,10},{10,2},{3,11},{11,3},{4,12},{12,4},... | collective-permute-start | bytes 589832 | tf_op jit(solution)/shard_map/ppermute | solution.py:47
  85.0 3.7 %collective-permute-start.16 = (bf16[128,768]{1,0:T(8,128)(2,1)S(1)}, bf16[128,768]{1,0:T(8,128)(2,1)S(1)}, u32[]{:S(2)}, u32[]{:S(2)}) collective-permute-start(bf16[128,768]{1,0:T(8,128)(2,1)S(1)} %collective-permute-done.15), channel_id=1, source_target_pairs={{0,7},{1,0},{2,1},{3,2},{4,3},{5,4},{6,5},{7,6},{16,17},{17,18},{1... | collective-permute-start | bytes 589832 | tf_op jit(solution)/shard_map/ppermute | solution.py:53
  90.8 4.4 %shard_map.88 = (f32[320,1280]{1,0:T(8,128)}, f32[320,768]{1,0:T(8,128)}) custom-call(s32[1]{0:T(128)} %bitcast.packed_ref, bf16[128,768]{1,0:T(8,128)(2,1)} %copy-done.5, bf16[128,768]{1,0:T(8,128)(2,1)} %copy-done.11, bf16[256,768]{1,0:T(8,128)(2,1)} %copy-done.4, bf16[2048,1280]{1,0:T(8,128)(2,1)} %refs_12_.3, ...), custom_call_target="tpu_custom_call" | custom-call | tf_op jit(solution)/shard_map/pallas_call | solution.py:232
  97.0 2.9 %collective-permute-start.19 = (bf16[128,768]{1,0:T(8,128)(2,1)S(1)}, bf16[128,768]{1,0:T(8,128)(2,1)S(1)}, u32[]{:S(2)}, u32[]{:S(2)}) collective-permute-start(bf16[128,768]{1,0:T(8,128)(2,1)S(1)} %collective-permute-done.16), channel_id=1, source_target_pairs={{0,7},{1,0},{2,1},{3,2},{4,3},{5,4},{6,5},{7,6},{16,17},{17,18},{1... | collective-permute-start | bytes 589832 | tf_op jit(solution)/shard_map/ppermute | solution.py:53
  100.7 5.2 %shard_map.89 = (f32[320,1280]{1,0:T(8,128)}, f32[320,768]{1,0:T(8,128)}) custom-call(s32[1]{0:T(128)} %bitcast.packed_ref, bf16[256,768]{1,0:T(8,128)(2,1)} %copy-done.8, bf16[256,768]{1,0:T(8,128)(2,1)} %copy-done.3, bf16[2048,1280]{1,0:T(8,128)(2,1)} %refs_12_.3, ...), custom_call_target="tpu_custom_call", output_to_operand_aliasing={{0}: (16, {}), {1}: (17, {})} | custom-call | tf_op jit(solution)/shard_map/pallas_call | solution.py:232
  109.6 5.2 %shard_map.90 = (f32[320,1280]{1,0:T(8,128)}, f32[320,768]{1,0:T(8,128)}) custom-call(s32[1]{0:T(128)} %bitcast.packed_ref, bf16[256,768]{1,0:T(8,128)(2,1)} %copy-done.2, bf16[256,768]{1,0:T(8,128)(2,1)} %copy-done.7, bf16[2048,1280]{1,0:T(8,128)(2,1)} %refs_12_.3, ...), custom_call_target="tpu_custom_call", output_to_operand_aliasing={{0}: (16, {}), {1}: (17, {})} | custom-call | tf_op jit(solution)/shard_map/pallas_call | solution.py:232
  119.3 7.4 %shard_map.91 = (bf16[8,80,640]{2,1,0:T(8,128)(2,1)}, bf16[8,80,640]{2,1,0:T(8,128)(2,1)}) custom-call(s32[1]{0:T(128)} %bitcast.packed_ref, bf16[256,768]{1,0:T(8,128)(2,1)} %copy-done.9, bf16[128,768]{1,0:T(8,128)(2,1)} %copy-done.12, bf16[128,768]{1,0:T(8,128)(2,1)} %copy-done.10, bf16[2048,1280]{1,0:T(8,128)(2,1)} %refs_12_.3, ...), custom_call_target="tpu_custom_call" | custom-call | tf_op jit(solution)/shard_map/pallas_call | solution.py:232
  126.8 8.5 %collective-permute-start.25 = (bf16[8,80,640]{2,1,0:T(8,128)(2,1)}, bf16[8,80,640]{2,1,0:T(8,128)(2,1)S(1)}, u32[]{:S(2)}, u32[]{:S(2)}) collective-permute-start(bf16[8,80,640]{2,1,0:T(8,128)(2,1)} %get-tuple-element.87), channel_id=1, source_target_pairs={{0,16},{16,0},{1,17},{17,1},{2,18},{18,2},{3,19},{19,3},{4,20},{20... | collective-permute-start | bytes 2457608 | tf_op jit(solution)/shard_map/ppermute | solution.py:47
  138.8 16.1 %all_to_all.5 = bf16[8,80,640]{2,1,0:T(8,128)(2,1)S(1)} all-to-all(bf16[8,80,640]{2,1,0:T(8,128)(2,1)S(1)} %add_convert_fusion), channel_id=1, replica_groups=mesh['ylo'=2,'x'=4,'core'=2,'yhi'=2,'z'=8] {'ylo','x'}, dimensions={0} | all-to-all | bytes 1638400 | tf_op jit(solution)/shard_map/all_to_all | solution.py:333
  (97 shorter events, 37.1 us)
Async XLA Ops:
  7.2 50.5 %all-gather.2.cloned.1.call-start = ((), (), s32[]{:S(2)}) async-start(), calls=%async_computation.2 | async-start | bytes 1769472 | tf_op jit(solution)/shard_map/all_gather | solution.py:279
  7.9 147.9 %reduce-scatter.2.cloned.1.call-start = ((), (), s32[]{:S(2)}) async-start(), calls=%async_computation.3 | async-start | bytes 1769472 | tf_op jit(solution)/shard_map/reduce_scatter | solution.py:324
  13.6 19.0 %collective-permute-start.2 = (bf16[256,768]{1,0:T(8,128)(2,1)}, bf16[256,768]{1,0:T(8,128)(2,1)S(1)}, u32[]{:S(2)}, u32[]{:S(2)}) collective-permute-start(bf16[256,768]{1,0:T(8,128)(2,1)} %get-tuple-element.52), channel_id=1, source_target_pairs={{0,8},{8,0},{1,9},{9,1},{2,10},{10,2},{3,11},{11,3},{4,12},{12,4},... | collective-permute-start | bytes 1179656 | tf_op jit(solution)/shard_map/ppermute | solution.py:47
  17.3 15.2 %collective-permute-start.3 = (bf16[128,768]{1,0:T(8,128)(2,1)}, bf16[128,768]{1,0:T(8,128)(2,1)S(1)}, u32[]{:S(2)}, u32[]{:S(2)}) collective-permute-start(bf16[128,768]{1,0:T(8,128)(2,1)} %get-tuple-element.53), channel_id=1, source_target_pairs={{0,1},{1,2},{2,3},{3,4},{4,5},{5,6},{6,7},{7,0},{16,23},{17,16},{1... | collective-permute-start | bytes 589832 | tf_op jit(solution)/shard_map/ppermute | solution.py:53
  22.9 9.7 %collective-permute-start.4 = (bf16[128,768]{1,0:T(8,128)(2,1)}, bf16[128,768]{1,0:T(8,128)(2,1)S(1)}, u32[]{:S(2)}, u32[]{:S(2)}) collective-permute-start(bf16[128,768]{1,0:T(8,128)(2,1)} %get-tuple-element.54), channel_id=1, source_target_pairs={{0,9},{1,10},{2,11},{3,12},{4,13},{5,14},{6,15},{7,8},{8,1},{9,2},... | collective-permute-start | bytes 589832 | tf_op jit(solution)/shard_map/ppermute | solution.py:64
  29.7 15.6 %collective-permute-start.1 = (bf16[256,768]{1,0:T(8,128)(2,1)}, bf16[256,768]{1,0:T(8,128)(2,1)S(1)}, u32[]{:S(2)}, u32[]{:S(2)}) collective-permute-start(bf16[256,768]{1,0:T(8,128)(2,1)} %get-tuple-element.50), channel_id=1, source_target_pairs={{0,8},{8,0},{1,9},{9,1},{2,10},{10,2},{3,11},{11,3},{4,12},{12,4},... | collective-permute-start | bytes 1179656 | tf_op jit(solution)/shard_map/ppermute | solution.py:47
  33.7 11.6 %collective-permute-start.8 = (bf16[128,768]{1,0:T(8,128)(2,1)S(1)}, bf16[128,768]{1,0:T(8,128)(2,1)S(1)}, u32[]{:S(2)}, u32[]{:S(2)}) collective-permute-start(bf16[128,768]{1,0:T(8,128)(2,1)S(1)} %get-tuple-element.95), channel_id=1, source_target_pairs={{0,7},{1,0},{2,1},{3,2},{4,3},{5,4},{6,5},{7,6},{16,17},{17,18},{1... | collective-permute-start | bytes 589832 | tf_op jit(solution)/shard_map/ppermute | solution.py:53
  34.5 10.8 %collective-permute-start.5 = (bf16[128,768]{1,0:T(8,128)(2,1)S(1)}, bf16[128,768]{1,0:T(8,128)(2,1)S(1)}, u32[]{:S(2)}, u32[]{:S(2)}) collective-permute-start(bf16[128,768]{1,0:T(8,128)(2,1)S(1)} %get-tuple-element.96), channel_id=1, source_target_pairs={{0,1},{1,2},{2,3},{3,4},{4,5},{5,6},{6,7},{7,0},{16,23},{17,16},{1... | collective-permute-start | bytes 589832 | tf_op jit(solution)/shard_map/ppermute | solution.py:53
  37.2 14.2 %collective-permute-start = (bf16[384,768]{1,0:T(8,128)(2,1)}, bf16[384,768]{1,0:T(8,128)(2,1)S(1)}, u32[]{:S(2)}, u32[]{:S(2)}) collective-permute-start(bf16[384,768]{1,0:T(8,128)(2,1)} %get-tuple-element.48), channel_id=1, source_target_pairs={{0,8},{8,0},{1,9},{9,1},{2,10},{10,2},{3,11},{11,3},{4,12},{12,4},... | collective-permute-start | bytes 1769480 | tf_op jit(solution)/shard_map/ppermute | solution.py:47
  46.5 7.6 %collective-permute-start.9 = (bf16[128,768]{1,0:T(8,128)(2,1)S(1)}, bf16[128,768]{1,0:T(8,128)(2,1)S(1)}, u32[]{:S(2)}, u32[]{:S(2)}) collective-permute-start(bf16[128,768]{1,0:T(8,128)(2,1)S(1)} %get-tuple-element.93), channel_id=1, source_target_pairs={{0,7},{1,0},{2,1},{3,2},{4,3},{5,4},{6,5},{7,6},{16,17},{17,18},{1... | collective-permute-start | bytes 589832 | tf_op jit(solution)/shard_map/ppermute | solution.py:53
  46.8 7.3 %collective-permute-start.6 = (bf16[128,768]{1,0:T(8,128)(2,1)S(1)}, bf16[128,768]{1,0:T(8,128)(2,1)S(1)}, u32[]{:S(2)}, u32[]{:S(2)}) collective-permute-start(bf16[128,768]{1,0:T(8,128)(2,1)S(1)} %get-tuple-element.94), channel_id=1, source_target_pairs={{0,1},{1,2},{2,3},{3,4},{4,5},{5,6},{6,7},{7,0},{16,23},{17,16},{1... | collective-permute-start | bytes 589832 | tf_op jit(solution)/shard_map/ppermute | solution.py:53
  54.3 6.9 %collective-permute-start.10 = (bf16[128,768]{1,0:T(8,128)(2,1)S(1)}, bf16[128,768]{1,0:T(8,128)(2,1)S(1)}, u32[]{:S(2)}, u32[]{:S(2)}) collective-permute-start(bf16[128,768]{1,0:T(8,128)(2,1)S(1)} %get-tuple-element.91), channel_id=1, source_target_pairs={{0,7},{1,0},{2,1},{3,2},{4,3},{5,4},{6,5},{7,6},{16,17},{17,18},{1... | collective-permute-start | bytes 589832 | tf_op jit(solution)/shard_map/ppermute | solution.py:53
  77.4 7.6 %collective-permute-start.15 = (bf16[128,768]{1,0:T(8,128)(2,1)S(1)}, bf16[128,768]{1,0:T(8,128)(2,1)S(1)}, u32[]{:S(2)}, u32[]{:S(2)}) collective-permute-start(bf16[128,768]{1,0:T(8,128)(2,1)S(1)} %multiply_convert_fusion.refs_0_), channel_id=1, source_target_pairs={{0,7},{1,0},{2,1},{3,2},{4,3},{5,4},{6,5},{7,6},{16,17},{17,18},{1... | collective-permute-start | bytes 589832 | tf_op jit(solution)/shard_map/ppermute | solution.py:53
  80.4 8.2 %collective-permute-start.13 = (bf16[128,768]{1,0:T(8,128)(2,1)S(1)}, bf16[128,768]{1,0:T(8,128)(2,1)S(1)}, u32[]{:S(2)}, u32[]{:S(2)}) collective-permute-start(bf16[128,768]{1,0:T(8,128)(2,1)S(1)} %multiply_convert_fusion.refs_0_), channel_id=1, source_target_pairs={{0,1},{1,2},{2,3},{3,4},{4,5},{5,6},{6,7},{7,0},{16,23},{17,16},{1... | collective-permute-start | bytes 589832 | tf_op jit(solution)/shard_map/ppermute | solution.py:53
  82.2 7.9 %collective-permute-start.17 = (bf16[128,768]{1,0:T(8,128)(2,1)S(1)}, bf16[128,768]{1,0:T(8,128)(2,1)S(1)}, u32[]{:S(2)}, u32[]{:S(2)}) collective-permute-start(bf16[128,768]{1,0:T(8,128)(2,1)S(1)} %multiply_convert_fusion.refs_0_), channel_id=1, source_target_pairs={{0,8},{8,0},{1,9},{9,1},{2,10},{10,2},{3,11},{11,3},{4,12},{12,4},... | collective-permute-start | bytes 589832 | tf_op jit(solution)/shard_map/ppermute | solution.py:47
  85.0 10.2 %collective-permute-start.16 = (bf16[128,768]{1,0:T(8,128)(2,1)S(1)}, bf16[128,768]{1,0:T(8,128)(2,1)S(1)}, u32[]{:S(2)}, u32[]{:S(2)}) collective-permute-start(bf16[128,768]{1,0:T(8,128)(2,1)S(1)} %collective-permute-done.15), channel_id=1, source_target_pairs={{0,7},{1,0},{2,1},{3,2},{4,3},{5,4},{6,5},{7,6},{16,17},{17,18},{1... | collective-permute-start | bytes 589832 | tf_op jit(solution)/shard_map/ppermute | solution.py:53
  88.7 11.2 %collective-permute-start.20 = (bf16[256,768]{1,0:T(8,128)(2,1)S(1)}, bf16[256,768]{1,0:T(8,128)(2,1)S(1)}, u32[]{:S(2)}, u32[]{:S(2)}) collective-permute-start(bf16[256,768]{1,0:T(8,128)(2,1)S(1)} %constant_dynamic-update-slice_fusion.refs_2_), channel_id=1, source_target_pairs={{0,8},{8,0},{1,9},{9,1},{2,10},{10,2},{3,11},{11,3},{4,12},{12,4},... | collective-permute-start | bytes 1179656 | tf_op jit(solution)/shard_map/ppermute | solution.py:47
  95.2 12.2 %collective-permute-start.21 = (bf16[256,768]{1,0:T(8,128)(2,1)S(1)}, bf16[256,768]{1,0:T(8,128)(2,1)S(1)}, u32[]{:S(2)}, u32[]{:S(2)}) collective-permute-start(bf16[256,768]{1,0:T(8,128)(2,1)S(1)} %constant_dynamic-update-slice_fusion.2.refs_1_), channel_id=1, source_target_pairs={{0,8},{8,0},{1,9},{9,1},{2,10},{10,2},{3,11},{11,3},{4,12},{12,4},... | collective-permute-start | bytes 1179656 | tf_op jit(solution)/shard_map/ppermute | solution.py:47
  97.0 8.8 %collective-permute-start.18 = (bf16[128,768]{1,0:T(8,128)(2,1)S(1)}, bf16[128,768]{1,0:T(8,128)(2,1)S(1)}, u32[]{:S(2)}, u32[]{:S(2)}) collective-permute-start(bf16[128,768]{1,0:T(8,128)(2,1)S(1)} %collective-permute-done.14), channel_id=1, source_target_pairs={{0,1},{1,2},{2,3},{3,4},{4,5},{5,6},{6,7},{7,0},{16,23},{17,16},{1... | collective-permute-start | bytes 589832 | tf_op jit(solution)/shard_map/ppermute | solution.py:53
  97.0 8.8 %collective-permute-start.19 = (bf16[128,768]{1,0:T(8,128)(2,1)S(1)}, bf16[128,768]{1,0:T(8,128)(2,1)S(1)}, u32[]{:S(2)}, u32[]{:S(2)}) collective-permute-start(bf16[128,768]{1,0:T(8,128)(2,1)S(1)} %collective-permute-done.16), channel_id=1, source_target_pairs={{0,7},{1,0},{2,1},{3,2},{4,3},{5,4},{6,5},{7,6},{16,17},{17,18},{1... | collective-permute-start | bytes 589832 | tf_op jit(solution)/shard_map/ppermute | solution.py:53
  107.5 11.0 %collective-permute-start.22 = (bf16[256,768]{1,0:T(8,128)(2,1)S(1)}, bf16[256,768]{1,0:T(8,128)(2,1)S(1)}, u32[]{:S(2)}, u32[]{:S(2)}) collective-permute-start(bf16[256,768]{1,0:T(8,128)(2,1)S(1)} %constant_dynamic-update-slice_fusion.4.refs_0_), channel_id=1, source_target_pairs={{0,8},{8,0},{1,9},{9,1},{2,10},{10,2},{3,11},{11,3},{4,12},{12,4},... | collective-permute-start | bytes 1179656 | tf_op jit(solution)/shard_map/ppermute | solution.py:47
  109.5 7.0 %collective-permute-start.24 = (bf16[128,768]{1,0:T(8,128)(2,1)S(1)}, bf16[128,768]{1,0:T(8,128)(2,1)S(1)}, u32[]{:S(2)}, u32[]{:S(2)}) collective-permute-start(bf16[128,768]{1,0:T(8,128)(2,1)S(1)} %collective-permute-done.18), channel_id=1, source_target_pairs={{0,9},{1,10},{2,11},{3,12},{4,13},{5,14},{6,15},{7,8},{8,1},{9,2},... | collective-permute-start | bytes 589832 | tf_op jit(solution)/shard_map/ppermute | solution.py:64
  109.5 7.8 %collective-permute-start.23 = (bf16[128,768]{1,0:T(8,128)(2,1)S(1)}, bf16[128,768]{1,0:T(8,128)(2,1)S(1)}, u32[]{:S(2)}, u32[]{:S(2)}) collective-permute-start(bf16[128,768]{1,0:T(8,128)(2,1)S(1)} %collective-permute-done.18), channel_id=1, source_target_pairs={{0,1},{1,2},{2,3},{3,4},{4,5},{5,6},{6,7},{7,0},{16,23},{17,16},{1... | collective-permute-start | bytes 589832 | tf_op jit(solution)/shard_map/ppermute | solution.py:53
  126.8 10.7 %collective-permute-start.25 = (bf16[8,80,640]{2,1,0:T(8,128)(2,1)}, bf16[8,80,640]{2,1,0:T(8,128)(2,1)S(1)}, u32[]{:S(2)}, u32[]{:S(2)}) collective-permute-start(bf16[8,80,640]{2,1,0:T(8,128)(2,1)} %get-tuple-element.87), channel_id=1, source_target_pairs={{0,16},{16,0},{1,17},{17,1},{2,18},{18,2},{3,19},{19,3},{4,20},{20... | collective-permute-start | bytes 2457608 | tf_op jit(solution)/shard_map/ppermute | solution.py:47
  (17 other events, 69.6 us)
Sparse Core Ops, SparseCore 0:
  9.8 42.4 all-gather.1
  107.6 42.0 reduce-scatter.1

commit v13 on v12

--- a/solution.py
+++ b/solution.py
@@ -278,14 +278,16 @@
 
     score_half = lax.all_gather(score_embed, "z", axis=0, tiled=True)
     (other4, other3, own4), down_head = forward(0, down_weight, head_weight)
-    fore, across4, came3 = shift(own4, 1), shift_across(other4, 1), swap(other3, "yhi")
+    fore, came3 = shift(own4, 1), swap(other3, "yhi")
     (other2, other1, own3, own3b), _ = forward(1, down_head)
+    other4, own3 = lax.optimization_barrier((other4, own3))
+    across4 = shift_across(other4, 3)
     came2, came1 = swap(other2, "yhi"), swap(other1, "yhi")
-    fore = shift(total_of(own3, came3[:rows], fore, across4).astype(bf16), 1)
+    fore = shift(total_of(own3, came3[:rows], fore).astype(bf16), 1)
     back = shift(total_of(own3b, came3[rows:]).astype(bf16), -1)
     (own2, own1), _ = forward(2, down_head)
-    for own, came in ((own2, came2), (own1, came1)):
-        fore = shift(total_of(own[:rows], came[:rows], fore).astype(bf16), 1)
+    for own, came, joins in ((own2, came2, ()), (own1, came1, (across4,))):
+        fore = shift(total_of(own[:rows], came[:rows], fore, *joins).astype(bf16), 1)
         back = shift(total_of(own[rows : 2 * rows], came[rows : 2 * rows], back).astype(bf16), -1)
     score_unit = unit_rows(score_half)[0].astype(bf16)
     fore, back, score_unit = lax.optimization_barrier((fore, back, score_unit))
@@ -294,16 +296,19 @@
     own_proj = dot(own_hidden, head_weight)
     audio_wide, audio_inverse = unit_rows(own_proj + total_of(own1[2 * rows :], came1[2 * rows :], fore, back))
     audio_own = audio_wide.astype(bf16)
-    audio_unit = jnp.concatenate([audio_own, swap(audio_own, "yhi")], axis=0)
+    audio_far = swap(audio_own, "yhi")
     far_start = (1 - y_hi) * group_half + z * rows
-    partners = jnp.concatenate(
-        [lax.dynamic_slice_in_dim(pair_index[0], start, rows, 0) for start in (own_start, far_start)]
+    contrast = lambda audio, start: pair_coeffs(
+        audio, score_unit, lax.dynamic_slice_in_dim(pair_index[0], start, rows, 0), y_hi * group_half
     )
-    coeffs = pair_coeffs(audio_unit, score_unit, partners, y_hi * group_half)
-    grad_audio = dot(coeffs, score_unit)
-    grad_audio = grad_audio[:rows] + swap(grad_audio[rows:].astype(bf16), "yhi").astype(f32)
+    coeffs_own = contrast(audio_own, own_start)
+    audio_far, grad_own = lax.optimization_barrier((audio_far, dot(coeffs_own, score_unit)))
+    coeffs_far = contrast(audio_far, far_start)
+    grad_far = dot(coeffs_far, score_unit).astype(bf16)
+    grad_audio = grad_own + swap(grad_far, "yhi").astype(f32)
     grad_embed = unit_backward(audio_wide, audio_inverse, grad_audio).astype(bf16)
-    score_part = dot(coeffs, audio_unit, ((0,), (0,))).astype(bf16)
+    coeffs = jnp.concatenate([coeffs_own, coeffs_far], axis=0)
+    score_part = dot(coeffs, jnp.concatenate([audio_own, audio_far], axis=0), ((0,), (0,))).astype(bf16)
     item = lambda grad, *blocks: (grad, [saved[block] for block in blocks])
     pair = lambda step, half: ((half, step), (half, -step))
     both = lambda up, down: jnp.concatenate([up, down], axis=0)
@@ -315,13 +320,13 @@
     fore, back = shift(fore, 1), shift(back, -1)
     backward = lambda items, sums, *head: backward_blocks(items, packed, hidden_in, down_head, sums, *head)
     sums = backward([item(grad_embed, (0, 0)), item(crossed0, (1, 0)), item(ring1, *pair(1, 0))], None)
-    fore, back, sums = lax.optimization_barrier((fore, back, sums))
+    fore, back, sums, score_part = lax.optimization_barrier((fore, back, sums, score_part))
+    grad_score = lax.psum_scatter(score_part, "z", scatter_dimension=0, tiled=True)
     ring2 = both(back, fore)
     crossed2 = swap(ring2, "yhi")
     fore, back = shift(fore, 1), shift(back, -1)
     sums = backward([item(crossed1, *pair(1, 1)), item(ring2, *pair(2, 0))], sums)
-    fore, back, sums, crossed2, score_part = lax.optimization_barrier((fore, back, sums, crossed2, score_part))
-    grad_score = lax.psum_scatter(score_part, "z", scatter_dimension=0, tiled=True)
+    fore, back, sums, crossed2 = lax.optimization_barrier((fore, back, sums, crossed2))
     ring4, crossed4 = shift(fore, 1), shift_across(fore, 1)
     ring3 = both(back, fore)
     crossed3 = swap(ring3, "yhi")

time: 165 us -> 175 us (1.061)
  waiting for transfers between devices: 20.1 us -> 24.3 us
  starting transfers between devices: 57.7 us -> 60.2 us
    ppermute x10, waiting for transfers between devices: 11.9 us -> 16.7 us  [swap(): return lax.ppermute(value, axis, [(0, 1), (1, 0)])]
    ppermute x2, starting transfers between devices: 0.53 us -> 4.13 us  [shift_across(): return lax.ppermute(value, ('core', 'yhi', 'z'), perm)]
    ppermute x2, waiting for transfers between devices: 1.83 us -> 0.01 us  [shift_across(): return lax.ppermute(value, ('core', 'yhi', 'z'), perm)]
    dot_general x4 -> x6, matrix products: 4.6 us -> 5.42 us  [dot(): lax.dot_general(left, right, (dims, ((), ())), preferred_element_type=f32)]
  transfers between devices with their start and end apart: 28 -> 28, of which waited for: 10 -> 11; matrix products, arithmetic and copies ran while one was open for 7% -> 7% of each run, Pallas kernels for 24% -> 23%
where the time goes in v13:
time: 175 us
  starting transfers between devices  60.2 us (34%)
  Pallas kernels  41.4 us (24%)
  waiting for transfers between devices  24.3 us (14%)
  blocking collectives  17.6 us (10%)
  between operations  14.3 us (8%)
  other arithmetic  7.87 us (4%)
  matrix products  5.42 us (3%)
  local copies, waits for them, and re-layouts  3.78 us (2%)
    ppermute x10, starting transfers between devices, swap(): return lax.ppermute(value, axis, [(0, 1), (1, 0)])  31.7 us
    ppermute x14, starting transfers between devices, shift(): return lax.ppermute(value, ('core', 'z'), perm)  24.3 us
    pallas_call x4, Pallas kernels, backward_blocks(): pl.pallas_call(functools.partial(backward_kernel, len(items), len(places)...  22.4 us
    all_to_all x1, blocking collectives, per_device(): landed = lax.all_to_all(chip, ('ylo', 'x'), 0, 0)  17.6 us
    pallas_call x3, Pallas kernels, forward_blocks(): pl.pallas_call(functools.partial(forward_kernel, pieces, first), grid_spe...  17 us
    ppermute x10, waiting for transfers between devices, swap(): return lax.ppermute(value, axis, [(0, 1), (1, 0)])  16.7 us
    ppermute x14, waiting for transfers between devices, shift(): return lax.ppermute(value, ('core', 'z'), perm)  6.85 us
    dot_general x6, matrix products, dot(): lax.dot_general(left, right, (dims, ((), ())), preferred_element_type=f32)  5.42 us
  transfers between devices with their start and end apart: 28, of which 11 were waited for; matrix products, arithmetic and copies ran while one was open for 7% of the time, Pallas kernels for 23%

profile of v13, /device:TPU:1, one launch (start us, length us, event | category | flops | bytes accessed | tf_op | source)
XLA Modules:
  0.0 174.8 jit_solution(12574875521857314200)
XLA Ops:
  8.0 5.6 %shard_map.85 = (bf16[128,768]{1,0:T(8,128)(2,1)}, bf16[256,768]{1,0:T(8,128)(2,1)}, bf16[128,768]{1,0:T(8,128)(2,1)}, bf16[4,320,128]{2,1,0:T(8,128)(2,1)}, bf1...) custom-call(s32[1]{0:T(128)} %bitcast.packed_ref, bf16[2048,1280]{1,0:T(8,128)(2,1)} %refs_12_.3, ...), custom_call_target="tpu_custom_call" | custom-call | flops 671088640 | bytes 4063232 | tf_op jit(solution)/shard_map/pallas_call | solution.py:140
  13.6 3.7 %collective-permute-start.2 = (bf16[256,768]{1,0:T(8,128)(2,1)}, bf16[256,768]{1,0:T(8,128)(2,1)S(1)}, u32[]{:S(2)}, u32[]{:S(2)}) collective-permute-start(bf16[256,768]{1,0:T(8,128)(2,1)} %get-tuple-element.58), channel_id=1, source_target_pairs={{0,8},{8,0},{1,9},{9,1},{2,10},{10,2},{3,11},{11,3},{4,12},{12,4},... | collective-permute-start | bytes 1179656 | tf_op jit(solution)/shard_map/ppermute | solution.py:47
  17.3 5.6 %collective-permute-start.3 = (bf16[128,768]{1,0:T(8,128)(2,1)}, bf16[128,768]{1,0:T(8,128)(2,1)}, u32[]{:S(2)}, u32[]{:S(2)}) collective-permute-start(bf16[128,768]{1,0:T(8,128)(2,1)} %get-tuple-element.59), channel_id=1, source_target_pairs={{0,1},{1,2},{2,3},{3,4},{4,5},{5,6},{6,7},{7,0},{16,23},{17,16},{1... | collective-permute-start | bytes 589832 | tf_op jit(solution)/shard_map/ppermute | solution.py:53
  22.9 6.4 %shard_map.87 = (bf16[256,768]{1,0:T(8,128)(2,1)}, bf16[384,768]{1,0:T(8,128)(2,1)}, bf16[128,768]{1,0:T(8,128)(2,1)}, bf16[128,768]{1,0:T(8,128)(2,1)}, bf16[7,...) custom-call(s32[1]{0:T(128)} %bitcast.packed_ref, bf16[2048,1280]{1,0:T(8,128)(2,1)} %refs_12_.3, ...), custom_call_target="tpu_custom_call" | custom-call | flops 1174405120 | bytes 6127616 | tf_op jit(solution)/shard_map/pallas_call | solution.py:140
  30.7 2.9 %collective-permute-start.1 = (bf16[256,768]{1,0:T(8,128)(2,1)}, bf16[256,768]{1,0:T(8,128)(2,1)S(1)}, u32[]{:S(2)}, u32[]{:S(2)}) collective-permute-start(bf16[256,768]{1,0:T(8,128)(2,1)} %get-tuple-element.54), channel_id=1, source_target_pairs={{0,8},{8,0},{1,9},{9,1},{2,10},{10,2},{3,11},{11,3},{4,12},{12,4},... | collective-permute-start | bytes 1179656 | tf_op jit(solution)/shard_map/ppermute | solution.py:47
  39.8 5.0 %shard_map.86 = (bf16[256,768]{1,0:T(8,128)(2,1)}, bf16[384,768]{1,0:T(8,128)(2,1)}, bf16[5,320,128]{2,1,0:T(8,128)(2,1)}, bf16[5,128,320]{2,1,0:T(8,128)(2,1)}) custom-call(s32[1]{0:T(128)} %bitcast.packed_ref, bf16[2048,1280]{1,0:T(8,128)(2,1)} %refs_12_.3, bf16[2048,1280]{1,0:T(8,128)(2,1)} %refs_12_.3, bf16[2048,1280]{1,0:T(8,128)(2,1)} %refs_12_.3, ...), custom_call_target="tpu_custom_call" | custom-call | flops 838860800 | bytes 4751360 | tf_op jit(solution)/shard_map/pallas_call | solution.py:140
  44.8 2.3 %collective-permute-done.1 = bf16[256,768]{1,0:T(8,128)(2,1)S(1)} collective-permute-done((bf16[256,768]{1,0:T(8,128)(2,1)}, bf16[256,768]{1,0:T(8,128)(2,1)S(1)}, u32[]{:S(2)}, u32[]{:S(2)}) %collective-permute-start.1) | collective-permute-done | bytes 393248 | tf_op jit(solution)/shard_map/ppermute | solution.py:47
  51.1 3.2 %collective-permute-start.5 = (bf16[128,768]{1,0:T(8,128)(2,1)S(1)}, bf16[128,768]{1,0:T(8,128)(2,1)S(1)}, u32[]{:S(2)}, u32[]{:S(2)}) collective-permute-start(bf16[128,768]{1,0:T(8,128)(2,1)S(1)} %get-tuple-element.102), channel_id=1, source_target_pairs={{0,1},{1,2},{2,3},{3,4},{4,5},{5,6},{6,7},{7,0},{16,23},{17,16},{1... | collective-permute-start | bytes 589832 | tf_op jit(solution)/shard_map/ppermute | solution.py:53
  55.0 4.7 %collective-permute-done = bf16[384,768]{1,0:T(8,128)(2,1)S(1)} collective-permute-done((bf16[384,768]{1,0:T(8,128)(2,1)}, bf16[384,768]{1,0:T(8,128)(2,1)S(1)}, u32[]{:S(2)}, u32[]{:S(2)}) %collective-permute-start) | collective-permute-done | bytes 589856 | tf_op jit(solution)/shard_map/ppermute | solution.py:47
  60.0 3.5 %collective-permute-start.7 = (bf16[128,768]{1,0:T(8,128)(2,1)S(1)}, bf16[128,768]{1,0:T(8,128)(2,1)S(1)}, u32[]{:S(2)}, u32[]{:S(2)}) collective-permute-start(bf16[128,768]{1,0:T(8,128)(2,1)S(1)} %get-tuple-element.100), channel_id=1, source_target_pairs={{0,1},{1,2},{2,3},{3,4},{4,5},{5,6},{6,7},{7,0},{16,23},{17,16},{1... | collective-permute-start | bytes 589832 | tf_op jit(solution)/shard_map/ppermute | solution.py:53
  67.8 2.7 %collective-permute-start.11 = (bf16[128,768]{1,0:T(8,128)(2,1)S(1)}, bf16[128,768]{1,0:T(8,128)(2,1)S(1)}, u32[]{:S(2)}, u32[]{:S(2)}) collective-permute-start(bf16[128,768]{1,0:T(8,128)(2,1)S(1)} %multiply_convert_fusion.1), channel_id=1, source_target_pairs={{0,8},{8,0},{1,9},{9,1},{2,10},{10,2},{3,11},{11,3},{4,12},{12,4},... | collective-permute-start | bytes 589832 | tf_op jit(solution)/shard_map/ppermute | solution.py:47
  75.0 2.7 %collective-permute-start.12 = (bf16[128,768]{1,0:T(8,128)(2,1)S(1)}, bf16[128,768]{1,0:T(8,128)(2,1)S(1)}, u32[]{:S(2)}, u32[]{:S(2)}) collective-permute-start(bf16[128,768]{1,0:T(8,128)(2,1)S(1)} %convolution_convert_fusion.1), channel_id=1, source_target_pairs={{0,8},{8,0},{1,9},{9,1},{2,10},{10,2},{3,11},{11,3},{4,12},{12,4},... | collective-permute-start | bytes 589832 | tf_op jit(solution)/shard_map/ppermute | solution.py:47
  77.8 3.4 %collective-permute-done.12 = bf16[128,768]{1,0:T(8,128)(2,1)S(1)} collective-permute-done((bf16[128,768]{1,0:T(8,128)(2,1)S(1)}, bf16[128,768]{1,0:T(8,128)(2,1)S(1)}, u32[]{:S(2)}, u32[]{:S(2)}) %collective-permute-start.12) | collective-permute-done | bytes 196640 | tf_op jit(solution)/shard_map/ppermute | solution.py:47
  81.5 4.1 %collective-permute-start.15 = (bf16[128,768]{1,0:T(8,128)(2,1)S(1)}, bf16[128,768]{1,0:T(8,128)(2,1)S(1)}, u32[]{:S(2)}, u32[]{:S(2)}) collective-permute-start(bf16[128,768]{1,0:T(8,128)(2,1)S(1)} %multiply_convert_fusion.refs_0_), channel_id=1, source_target_pairs={{0,7},{1,0},{2,1},{3,2},{4,3},{5,4},{6,5},{7,6},{16,17},{17,18},{1... | collective-permute-start | bytes 589832 | tf_op jit(solution)/shard_map/ppermute | solution.py:53
  87.6 2.8 %collective-permute-start.17 = (bf16[128,768]{1,0:T(8,128)(2,1)S(1)}, bf16[128,768]{1,0:T(8,128)(2,1)S(1)}, u32[]{:S(2)}, u32[]{:S(2)}) collective-permute-start(bf16[128,768]{1,0:T(8,128)(2,1)S(1)} %multiply_convert_fusion.refs_0_), channel_id=1, source_target_pairs={{0,8},{8,0},{1,9},{9,1},{2,10},{10,2},{3,11},{11,3},{4,12},{12,4},... | collective-permute-start | bytes 589832 | tf_op jit(solution)/shard_map/ppermute | solution.py:47
  95.2 4.4 %shard_map.88 = (f32[320,1280]{1,0:T(8,128)}, f32[320,768]{1,0:T(8,128)}) custom-call(s32[1]{0:T(128)} %bitcast.packed_ref, bf16[128,768]{1,0:T(8,128)(2,1)} %copy-done.5, bf16[128,768]{1,0:T(8,128)(2,1)} %copy-done.11, bf16[256,768]{1,0:T(8,128)(2,1)} %copy-done.4, bf16[2048,1280]{1,0:T(8,128)(2,1)} %refs_12_.3, ...), custom_call_target="tpu_custom_call" | custom-call | tf_op jit(solution)/shard_map/pallas_call | solution.py:232
  99.7 2.3 %collective-permute-start.21 = (bf16[256,768]{1,0:T(8,128)(2,1)S(1)}, bf16[256,768]{1,0:T(8,128)(2,1)S(1)}, u32[]{:S(2)}, u32[]{:S(2)}) collective-permute-start(bf16[256,768]{1,0:T(8,128)(2,1)S(1)} %constant_dynamic-update-slice_fusion.2.refs_1_), channel_id=1, source_target_pairs={{0,8},{8,0},{1,9},{9,1},{2,10},{10,2},{3,11},{11,3},{4,12},{12,4},... | collective-permute-start | bytes 1179656 | tf_op jit(solution)/shard_map/ppermute | solution.py:47
  104.3 5.2 %shard_map.89 = (f32[320,1280]{1,0:T(8,128)}, f32[320,768]{1,0:T(8,128)}) custom-call(s32[1]{0:T(128)} %bitcast.packed_ref, bf16[256,768]{1,0:T(8,128)(2,1)} %copy-done.8, bf16[256,768]{1,0:T(8,128)(2,1)} %copy-done.3, bf16[2048,1280]{1,0:T(8,128)(2,1)} %refs_12_.3, ...), custom_call_target="tpu_custom_call", output_to_operand_aliasing={{0}: (16, {}), {1}: (17, {})} | custom-call | tf_op jit(solution)/shard_map/pallas_call | solution.py:232
  113.7 2.7 %collective-permute-start.24 = (bf16[128,768]{1,0:T(8,128)(2,1)S(1)}, bf16[128,768]{1,0:T(8,128)(2,1)S(1)}, u32[]{:S(2)}, u32[]{:S(2)}) collective-permute-start(bf16[128,768]{1,0:T(8,128)(2,1)S(1)} %collective-permute-done.18), channel_id=1, source_target_pairs={{0,9},{1,10},{2,11},{3,12},{4,13},{5,14},{6,15},{7,8},{8,1},{9,2},... | collective-permute-start | bytes 589832 | tf_op jit(solution)/shard_map/ppermute | solution.py:64
  116.9 5.3 %shard_map.90 = (f32[320,1280]{1,0:T(8,128)}, f32[320,768]{1,0:T(8,128)}) custom-call(s32[1]{0:T(128)} %bitcast.packed_ref, bf16[256,768]{1,0:T(8,128)(2,1)} %copy-done.2, bf16[256,768]{1,0:T(8,128)(2,1)} %copy-done.7, bf16[2048,1280]{1,0:T(8,128)(2,1)} %refs_12_.3, ...), custom_call_target="tpu_custom_call", output_to_operand_aliasing={{0}: (16, {}), {1}: (17, {})} | custom-call | tf_op jit(solution)/shard_map/pallas_call | solution.py:232
  122.2 2.7 %collective-permute-done.23.refs_1_ = bf16[128,768]{1,0:T(8,128)(2,1)S(1)} collective-permute-done((bf16[128,768]{1,0:T(8,128)(2,1)S(1)}, bf16[128,768]{1,0:T(8,128)(2,1)S(1)}, u32[]{:S(2)}, u32[]{:S(2)}) %collective-permute-start.23) | collective-permute-done | bytes 196640 | tf_op jit(solution)/shard_map/ppermute | solution.py:53
  125.7 7.5 %shard_map.91 = (bf16[8,80,640]{2,1,0:T(8,128)(2,1)}, bf16[8,80,640]{2,1,0:T(8,128)(2,1)}) custom-call(s32[1]{0:T(128)} %bitcast.packed_ref, bf16[256,768]{1,0:T(8,128)(2,1)} %copy-done.9, bf16[128,768]{1,0:T(8,128)(2,1)} %copy-done.12, bf16[128,768]{1,0:T(8,128)(2,1)} %copy-done.10, bf16[2048,1280]{1,0:T(8,128)(2,1)} %refs_12_.3, ...), custom_call_target="tpu_custom_call" | custom-call | tf_op jit(solution)/shard_map/pallas_call | solution.py:232
  133.2 10.8 %collective-permute-start.25 = (bf16[8,80,640]{2,1,0:T(8,128)(2,1)}, bf16[8,80,640]{2,1,0:T(8,128)(2,1)S(1)}, u32[]{:S(2)}, u32[]{:S(2)}) collective-permute-start(bf16[8,80,640]{2,1,0:T(8,128)(2,1)} %get-tuple-element.95), channel_id=1, source_target_pairs={{0,16},{16,0},{1,17},{17,1},{2,18},{18,2},{3,19},{19,3},{4,20},{20... | collective-permute-start | bytes 2457608 | tf_op jit(solution)/shard_map/ppermute | solution.py:47
  147.5 17.6 %all_to_all.5 = bf16[8,80,640]{2,1,0:T(8,128)(2,1)S(1)} all-to-all(bf16[8,80,640]{2,1,0:T(8,128)(2,1)S(1)} %add_convert_fusion), channel_id=1, replica_groups=mesh['ylo'=2,'x'=4,'core'=2,'yhi'=2,'z'=8] {'ylo','x'}, dimensions={0} | all-to-all | bytes 1638400 | tf_op jit(solution)/shard_map/all_to_all | solution.py:338
  (97 shorter events, 43.4 us)
Async XLA Ops:
  7.2 56.3 %all-gather.2.cloned.1.call-start = ((), (), s32[]{:S(2)}) async-start(), calls=%async_computation.2 | async-start | bytes 1769472 | tf_op jit(solution)/shard_map/all_gather | solution.py:279
  7.9 158.1 %reduce-scatter.2.cloned.1.call-start = ((), (), s32[]{:S(2)}) async-start(), calls=%async_computation.3 | async-start | bytes 1769472 | tf_op jit(solution)/shard_map/reduce_scatter | solution.py:324
  13.6 20.1 %collective-permute-start.2 = (bf16[256,768]{1,0:T(8,128)(2,1)}, bf16[256,768]{1,0:T(8,128)(2,1)S(1)}, u32[]{:S(2)}, u32[]{:S(2)}) collective-permute-start(bf16[256,768]{1,0:T(8,128)(2,1)} %get-tuple-element.58), channel_id=1, source_target_pairs={{0,8},{8,0},{1,9},{9,1},{2,10},{10,2},{3,11},{11,3},{4,12},{12,4},... | collective-permute-start | bytes 1179656 | tf_op jit(solution)/shard_map/ppermute | solution.py:47
  17.3 16.3 %collective-permute-start.3 = (bf16[128,768]{1,0:T(8,128)(2,1)}, bf16[128,768]{1,0:T(8,128)(2,1)}, u32[]{:S(2)}, u32[]{:S(2)}) collective-permute-start(bf16[128,768]{1,0:T(8,128)(2,1)} %get-tuple-element.59), channel_id=1, source_target_pairs={{0,1},{1,2},{2,3},{3,4},{4,5},{5,6},{6,7},{7,0},{16,23},{17,16},{1... | collective-permute-start | bytes 589832 | tf_op jit(solution)/shard_map/ppermute | solution.py:53
  29.2 25.8 %collective-permute-start.6 = (bf16[128,768]{1,0:T(8,128)(2,1)}, bf16[128,768]{1,0:T(8,128)(2,1)S(1)}, u32[]{:S(2)}, u32[]{:S(2)}) collective-permute-start(bf16[128,768]{1,0:T(8,128)(2,1)} %get-tuple-element.60), channel_id=1, source_target_pairs={{0,11},{1,12},{2,13},{3,14},{4,15},{5,8},{6,9},{7,10},{8,3},{9,4},... | collective-permute-start | bytes 589832 | tf_op jit(solution)/shard_map/ppermute | solution.py:64
  30.7 16.4 %collective-permute-start.1 = (bf16[256,768]{1,0:T(8,128)(2,1)}, bf16[256,768]{1,0:T(8,128)(2,1)S(1)}, u32[]{:S(2)}, u32[]{:S(2)}) collective-permute-start(bf16[256,768]{1,0:T(8,128)(2,1)} %get-tuple-element.54), channel_id=1, source_target_pairs={{0,8},{8,0},{1,9},{9,1},{2,10},{10,2},{3,11},{11,3},{4,12},{12,4},... | collective-permute-start | bytes 1179656 | tf_op jit(solution)/shard_map/ppermute | solution.py:47
  33.6 26.2 %collective-permute-start = (bf16[384,768]{1,0:T(8,128)(2,1)}, bf16[384,768]{1,0:T(8,128)(2,1)S(1)}, u32[]{:S(2)}, u32[]{:S(2)}) collective-permute-start(bf16[384,768]{1,0:T(8,128)(2,1)} %get-tuple-element.52), channel_id=1, source_target_pairs={{0,8},{8,0},{1,9},{9,1},{2,10},{10,2},{3,11},{11,3},{4,12},{12,4},... | collective-permute-start | bytes 1769480 | tf_op jit(solution)/shard_map/ppermute | solution.py:47
  35.6 13.5 %collective-permute-start.8 = (bf16[128,768]{1,0:T(8,128)(2,1)}, bf16[128,768]{1,0:T(8,128)(2,1)}, u32[]{:S(2)}, u32[]{:S(2)}) collective-permute-start(bf16[128,768]{1,0:T(8,128)(2,1)} %get-tuple-element.103), channel_id=1, source_target_pairs={{0,7},{1,0},{2,1},{3,2},{4,3},{5,4},{6,5},{7,6},{16,17},{17,18},{1... | collective-permute-start | bytes 589832 | tf_op jit(solution)/shard_map/ppermute | solution.py:53
  36.4 13.1 %collective-permute-start.4 = (bf16[128,768]{1,0:T(8,128)(2,1)}, bf16[128,768]{1,0:T(8,128)(2,1)}, u32[]{:S(2)}, u32[]{:S(2)}) collective-permute-start(bf16[128,768]{1,0:T(8,128)(2,1)} %get-tuple-element.104), channel_id=1, source_target_pairs={{0,1},{1,2},{2,3},{3,4},{4,5},{5,6},{6,7},{7,0},{16,23},{17,16},{1... | collective-permute-start | bytes 589832 | tf_op jit(solution)/shard_map/ppermute | solution.py:53
  50.8 8.9 %collective-permute-start.9 = (bf16[128,768]{1,0:T(8,128)(2,1)S(1)}, bf16[128,768]{1,0:T(8,128)(2,1)S(1)}, u32[]{:S(2)}, u32[]{:S(2)}) collective-permute-start(bf16[128,768]{1,0:T(8,128)(2,1)S(1)} %get-tuple-element.101), channel_id=1, source_target_pairs={{0,7},{1,0},{2,1},{3,2},{4,3},{5,4},{6,5},{7,6},{16,17},{17,18},{1... | collective-permute-start | bytes 589832 | tf_op jit(solution)/shard_map/ppermute | solution.py:53
  51.1 8.6 %collective-permute-start.5 = (bf16[128,768]{1,0:T(8,128)(2,1)S(1)}, bf16[128,768]{1,0:T(8,128)(2,1)S(1)}, u32[]{:S(2)}, u32[]{:S(2)}) collective-permute-start(bf16[128,768]{1,0:T(8,128)(2,1)S(1)} %get-tuple-element.102), channel_id=1, source_target_pairs={{0,1},{1,2},{2,3},{3,4},{4,5},{5,6},{6,7},{7,0},{16,23},{17,16},{1... | collective-permute-start | bytes 589832 | tf_op jit(solution)/shard_map/ppermute | solution.py:53
  59.9 6.5 %collective-permute-start.10 = (bf16[128,768]{1,0:T(8,128)(2,1)S(1)}, bf16[128,768]{1,0:T(8,128)(2,1)S(1)}, u32[]{:S(2)}, u32[]{:S(2)}) collective-permute-start(bf16[128,768]{1,0:T(8,128)(2,1)S(1)} %get-tuple-element.99), channel_id=1, source_target_pairs={{0,7},{1,0},{2,1},{3,2},{4,3},{5,4},{6,5},{7,6},{16,17},{17,18},{1... | collective-permute-start | bytes 589832 | tf_op jit(solution)/shard_map/ppermute | solution.py:53
  60.0 7.5 %collective-permute-start.7 = (bf16[128,768]{1,0:T(8,128)(2,1)S(1)}, bf16[128,768]{1,0:T(8,128)(2,1)S(1)}, u32[]{:S(2)}, u32[]{:S(2)}) collective-permute-start(bf16[128,768]{1,0:T(8,128)(2,1)S(1)} %get-tuple-element.100), channel_id=1, source_target_pairs={{0,1},{1,2},{2,3},{3,4},{4,5},{5,6},{6,7},{7,0},{16,23},{17,16},{1... | collective-permute-start | bytes 589832 | tf_op jit(solution)/shard_map/ppermute | solution.py:53
  81.5 8.9 %collective-permute-start.15 = (bf16[128,768]{1,0:T(8,128)(2,1)S(1)}, bf16[128,768]{1,0:T(8,128)(2,1)S(1)}, u32[]{:S(2)}, u32[]{:S(2)}) collective-permute-start(bf16[128,768]{1,0:T(8,128)(2,1)S(1)} %multiply_convert_fusion.refs_0_), channel_id=1, source_target_pairs={{0,7},{1,0},{2,1},{3,2},{4,3},{5,4},{6,5},{7,6},{16,17},{17,18},{1... | collective-permute-start | bytes 589832 | tf_op jit(solution)/shard_map/ppermute | solution.py:53
  87.6 6.9 %collective-permute-start.17 = (bf16[128,768]{1,0:T(8,128)(2,1)S(1)}, bf16[128,768]{1,0:T(8,128)(2,1)S(1)}, u32[]{:S(2)}, u32[]{:S(2)}) collective-permute-start(bf16[128,768]{1,0:T(8,128)(2,1)S(1)} %multiply_convert_fusion.refs_0_), channel_id=1, source_target_pairs={{0,8},{8,0},{1,9},{9,1},{2,10},{10,2},{3,11},{11,3},{4,12},{12,4},... | collective-permute-start | bytes 589832 | tf_op jit(solution)/shard_map/ppermute | solution.py:47
  90.4 9.2 %collective-permute-start.16 = (bf16[128,768]{1,0:T(8,128)(2,1)S(1)}, bf16[128,768]{1,0:T(8,128)(2,1)S(1)}, u32[]{:S(2)}, u32[]{:S(2)}) collective-permute-start(bf16[128,768]{1,0:T(8,128)(2,1)S(1)} %collective-permute-done.15), channel_id=1, source_target_pairs={{0,7},{1,0},{2,1},{3,2},{4,3},{5,4},{6,5},{7,6},{16,17},{17,18},{1... | collective-permute-start | bytes 589832 | tf_op jit(solution)/shard_map/ppermute | solution.py:53
  91.9 7.7 %collective-permute-start.14 = (bf16[128,768]{1,0:T(8,128)(2,1)S(1)}, bf16[128,768]{1,0:T(8,128)(2,1)S(1)}, u32[]{:S(2)}, u32[]{:S(2)}) collective-permute-start(bf16[128,768]{1,0:T(8,128)(2,1)S(1)} %collective-permute-done.13), channel_id=1, source_target_pairs={{0,1},{1,2},{2,3},{3,4},{4,5},{5,6},{6,7},{7,0},{16,23},{17,16},{1... | collective-permute-start | bytes 589832 | tf_op jit(solution)/shard_map/ppermute | solution.py:53
  93.1 10.4 %collective-permute-start.20 = (bf16[256,768]{1,0:T(8,128)(2,1)S(1)}, bf16[256,768]{1,0:T(8,128)(2,1)S(1)}, u32[]{:S(2)}, u32[]{:S(2)}) collective-permute-start(bf16[256,768]{1,0:T(8,128)(2,1)S(1)} %constant_dynamic-update-slice_fusion.refs_2_), channel_id=1, source_target_pairs={{0,8},{8,0},{1,9},{9,1},{2,10},{10,2},{3,11},{11,3},{4,12},{12,4},... | collective-permute-start | bytes 1179656 | tf_op jit(solution)/shard_map/ppermute | solution.py:47
  99.7 11.6 %collective-permute-start.21 = (bf16[256,768]{1,0:T(8,128)(2,1)S(1)}, bf16[256,768]{1,0:T(8,128)(2,1)S(1)}, u32[]{:S(2)}, u32[]{:S(2)}) collective-permute-start(bf16[256,768]{1,0:T(8,128)(2,1)S(1)} %constant_dynamic-update-slice_fusion.2.refs_1_), channel_id=1, source_target_pairs={{0,8},{8,0},{1,9},{9,1},{2,10},{10,2},{3,11},{11,3},{4,12},{12,4},... | collective-permute-start | bytes 1179656 | tf_op jit(solution)/shard_map/ppermute | solution.py:47
  102.0 7.5 %collective-permute-start.18 = (bf16[128,768]{1,0:T(8,128)(2,1)S(1)}, bf16[128,768]{1,0:T(8,128)(2,1)S(1)}, u32[]{:S(2)}, u32[]{:S(2)}) collective-permute-start(bf16[128,768]{1,0:T(8,128)(2,1)S(1)} %collective-permute-done.14), channel_id=1, source_target_pairs={{0,1},{1,2},{2,3},{3,4},{4,5},{5,6},{6,7},{7,0},{16,23},{17,16},{1... | collective-permute-start | bytes 589832 | tf_op jit(solution)/shard_map/ppermute | solution.py:53
  111.4 13.5 %collective-permute-start.22 = (bf16[256,768]{1,0:T(8,128)(2,1)S(1)}, bf16[256,768]{1,0:T(8,128)(2,1)S(1)}, u32[]{:S(2)}, u32[]{:S(2)}) collective-permute-start(bf16[256,768]{1,0:T(8,128)(2,1)S(1)} %constant_dynamic-update-slice_fusion.4.refs_0_), channel_id=1, source_target_pairs={{0,8},{8,0},{1,9},{9,1},{2,10},{10,2},{3,11},{11,3},{4,12},{12,4},... | collective-permute-start | bytes 1179656 | tf_op jit(solution)/shard_map/ppermute | solution.py:47
  113.7 8.5 %collective-permute-start.24 = (bf16[128,768]{1,0:T(8,128)(2,1)S(1)}, bf16[128,768]{1,0:T(8,128)(2,1)S(1)}, u32[]{:S(2)}, u32[]{:S(2)}) collective-permute-start(bf16[128,768]{1,0:T(8,128)(2,1)S(1)} %collective-permute-done.18), channel_id=1, source_target_pairs={{0,9},{1,10},{2,11},{3,12},{4,13},{5,14},{6,15},{7,8},{8,1},{9,2},... | collective-permute-start | bytes 589832 | tf_op jit(solution)/shard_map/ppermute | solution.py:64
  116.4 8.5 %collective-permute-start.23 = (bf16[128,768]{1,0:T(8,128)(2,1)S(1)}, bf16[128,768]{1,0:T(8,128)(2,1)S(1)}, u32[]{:S(2)}, u32[]{:S(2)}) collective-permute-start(bf16[128,768]{1,0:T(8,128)(2,1)S(1)} %collective-permute-done.18), channel_id=1, source_target_pairs={{0,1},{1,2},{2,3},{3,4},{4,5},{5,6},{6,7},{7,0},{16,23},{17,16},{1... | collective-permute-start | bytes 589832 | tf_op jit(solution)/shard_map/ppermute | solution.py:53
  133.2 13.0 %collective-permute-start.25 = (bf16[8,80,640]{2,1,0:T(8,128)(2,1)}, bf16[8,80,640]{2,1,0:T(8,128)(2,1)S(1)}, u32[]{:S(2)}, u32[]{:S(2)}) collective-permute-start(bf16[8,80,640]{2,1,0:T(8,128)(2,1)} %get-tuple-element.95), channel_id=1, source_target_pairs={{0,16},{16,0},{1,17},{17,1},{2,18},{18,2},{3,19},{19,3},{4,20},{20... | collective-permute-start | bytes 2457608 | tf_op jit(solution)/shard_map/ppermute | solution.py:47
  (17 other events, 90.7 us)
Sparse Core Ops, SparseCore 0:
  9.8 47.3 all-gather.1
  102.1 41.4 reduce-scatter.1

commit v14 on v12

--- a/solution.py
+++ b/solution.py
@@ -174,31 +174,37 @@
     grad_pre_t = (grad_act * slope.astype(f32)).astype(bf16).T
     act_sum = dot(act_t, grad)
     if not first:
-        act_sum = act_sum + act_in[...]
+        act_sum = act_sum + act_in[...].astype(f32)
     if last:
-        head_ref, keep_ref, give_ref, total = refs
+        head_ref, keep_ref, give_ref, total, sems = refs
     else:
         up_acc, act_acc = refs
-        act_acc[...] = act_sum
+        act_acc[...] = act_sum.astype(bf16)
     width, ff = hidden.shape[1], act_sum.shape[0]
     for m in range(0, width, tile):
         up_sum = dot(grad_pre_t, hidden[:, m : m + tile])
         if not first:
-            up_sum = up_sum + up_in[:, m : m + tile]
+            up_sum = up_sum + up_in[:, m : m + tile].astype(f32)
         if last:
             total[m : m + tile, :ff] = up_sum.T.astype(bf16)
         else:
-            up_acc[:, m : m + tile] = up_sum
+            up_acc[:, m : m + tile] = up_sum.astype(bf16)
     if last:
         core = packed_ref[0] % 2
         act_grad = act_sum.astype(bf16)
         rows = keep_ref.shape[1]
         for m in range(0, width, tile):
             total[m : m + tile, ff:] = dot(head_ref[m : m + tile, :], act_grad, ((1,), (1,))).astype(bf16)
+        copies = []
         for half, out_ref in ((core, keep_ref), (1 - core, give_ref)):
             for chip in range(keep_ref.shape[0]):
                 at = pl.multiple_of((2 * chip + half) * rows, rows)
-                out_ref[chip] = total[pl.ds(at, rows), :]
+                copies.append(
+                    pltpu.make_async_copy(total.at[pl.ds(at, rows), :], out_ref.at[chip], sems.at[len(copies)])
+                )
+                copies[-1].start()
+        for copy in copies:
+            copy.wait()
 
 
 def backward_blocks(items, packed, hidden_in, down_head, sums, head_weight=None):
@@ -224,9 +230,9 @@
     if last:
         args.append(head_weight)
         shapes = [jax.ShapeDtypeStruct((8, width // 16, 2 * ff), bf16)] * 2
-        scratch = [pltpu.VMEM((width, 2 * ff), bf16)]
+        scratch = [pltpu.VMEM((width, 2 * ff), bf16), pltpu.SemaphoreType.DMA((16,))]
     else:
-        shapes = [jax.ShapeDtypeStruct((ff, width), f32), jax.ShapeDtypeStruct((ff, embed), f32)]
+        shapes = [jax.ShapeDtypeStruct((ff, width), bf16), jax.ShapeDtypeStruct((ff, embed), bf16)]
         scratch = []
     specs += [whole] * (len(args) - len(specs))
     return pl.pallas_call(
@@ -235,7 +241,7 @@
             num_scalar_prefetch=1,
             grid=(1,),
             in_specs=specs,
-            out_specs=[whole] * 2,
+            out_specs=[pl.BlockSpec(memory_space=pl.ANY) if last else whole] * 2,
             scratch_shapes=scratch,
         ),
         out_shape=shapes,

time: 165 us -> 170 us (1.030)
  waiting for transfers between devices: 20.1 us -> 27.9 us
  starting transfers between devices: 57.7 us -> 53.9 us
  blocking collectives: 16.1 us -> 18.7 us
  Pallas kernels: 41.1 us -> 38.6 us
    ppermute x10, starting transfers between devices: 32.3 us -> 24.1 us  [swap(): return lax.ppermute(value, axis, [(0, 1), (1, 0)])]
    ppermute x14, waiting for transfers between devices: 5.75 us -> 11.8 us  [shift(): return lax.ppermute(value, ('core', 'z'), perm)]
    ppermute x10, waiting for transfers between devices: 11.9 us -> 14.7 us  [swap(): return lax.ppermute(value, axis, [(0, 1), (1, 0)])]
    ppermute x14, starting transfers between devices: 24.8 us -> 27.5 us  [shift(): return lax.ppermute(value, ('core', 'z'), perm)]
    all_to_all x1, blocking collectives: 16.1 us -> 18.7 us  [per_device(): landed = lax.all_to_all(chip, ('ylo', 'x'), 0, 0)]
    pallas_call x4, Pallas kernels: 22.1 us -> 19.7 us  [backward_blocks(): pl.pallas_call(functools.partial(backward_kernel, len(items), len(places)...]
    ppermute x2, starting transfers between devices: 0.53 us -> 2.25 us  [shift_across(): return lax.ppermute(value, ('core', 'yhi', 'z'), perm)]
  transfers between devices with their start and end apart: 28 -> 28, of which waited for: 10 -> 13; matrix products, arithmetic and copies ran while one was open for 7% -> 6% of each run, Pallas kernels for 24% -> 22%
where the time goes in v14:
time: 170 us; the launch traced here: 169 us
  starting transfers between devices  53.9 us (32%)
  Pallas kernels  38.6 us (23%)
  waiting for transfers between devices  27.9 us (16%)
  blocking collectives  18.7 us (11%)
  between operations  14.3 us (8%)
  other arithmetic  6.85 us (4%)
  matrix products  4.64 us (3%)
  local copies, waits for them, and re-layouts  3.81 us (2%)
    ppermute x14, starting transfers between devices, shift(): return lax.ppermute(value, ('core', 'z'), perm)  27.5 us
    ppermute x10, starting transfers between devices, swap(): return lax.ppermute(value, axis, [(0, 1), (1, 0)])  24.1 us
    pallas_call x4, Pallas kernels, backward_blocks(): pl.pallas_call(functools.partial(backward_kernel, len(items), len(places)...  19.7 us
    all_to_all x1, blocking collectives, per_device(): landed = lax.all_to_all(chip, ('ylo', 'x'), 0, 0)  18.7 us
    pallas_call x3, Pallas kernels, forward_blocks(): pl.pallas_call(functools.partial(forward_kernel, pieces, first), grid_spe...  16.9 us
    ppermute x10, waiting for transfers between devices, swap(): return lax.ppermute(value, axis, [(0, 1), (1, 0)])  14.7 us
    ppermute x14, waiting for transfers between devices, shift(): return lax.ppermute(value, ('core', 'z'), perm)  11.8 us
    dot_general x4, matrix products, dot(): lax.dot_general(left, right, (dims, ((), ())), preferred_element_type=f32)  4.64 us
  transfers between devices with their start and end apart: 28, of which 13 were waited for; matrix products, arithmetic and copies ran while one was open for 6% of the time, Pallas kernels for 22%

profile of v14, /device:TPU:1, one launch (start us, length us, event | category | flops | bytes accessed | tf_op | source)
XLA Modules:
  0.0 168.7 jit_solution(17684016166451750076)
XLA Ops:
  8.0 5.6 %shard_map.85 = (bf16[128,768]{1,0:T(8,128)(2,1)}, bf16[256,768]{1,0:T(8,128)(2,1)}, bf16[128,768]{1,0:T(8,128)(2,1)}, bf16[4,320,128]{2,1,0:T(8,128)(2,1)}, bf1...) custom-call(s32[1]{0:T(128)} %bitcast.packed_ref, bf16[2048,1280]{1,0:T(8,128)(2,1)} %refs_12_.3, ...), custom_call_target="tpu_custom_call" | custom-call | flops 671088640 | bytes 4063232 | tf_op jit(solution)/shard_map/pallas_call | solution.py:140
  13.6 3.7 %collective-permute-start.2 = (bf16[256,768]{1,0:T(8,128)(2,1)}, bf16[256,768]{1,0:T(8,128)(2,1)S(1)}, u32[]{:S(2)}, u32[]{:S(2)}) collective-permute-start(bf16[256,768]{1,0:T(8,128)(2,1)} %get-tuple-element.52), channel_id=1, source_target_pairs={{0,8},{8,0},{1,9},{9,1},{2,10},{10,2},{3,11},{11,3},{4,12},{12,4},... | collective-permute-start | bytes 1179656 | tf_op jit(solution)/shard_map/ppermute | solution.py:47
  17.3 5.6 %collective-permute-start.3 = (bf16[128,768]{1,0:T(8,128)(2,1)}, bf16[128,768]{1,0:T(8,128)(2,1)S(1)}, u32[]{:S(2)}, u32[]{:S(2)}) collective-permute-start(bf16[128,768]{1,0:T(8,128)(2,1)} %get-tuple-element.53), channel_id=1, source_target_pairs={{0,1},{1,2},{2,3},{3,4},{4,5},{5,6},{6,7},{7,0},{16,23},{17,16},{1... | collective-permute-start | bytes 589832 | tf_op jit(solution)/shard_map/ppermute | solution.py:53
  23.4 6.2 %shard_map.87 = (bf16[256,768]{1,0:T(8,128)(2,1)}, bf16[384,768]{1,0:T(8,128)(2,1)}, bf16[128,768]{1,0:T(8,128)(2,1)}, bf16[128,768]{1,0:T(8,128)(2,1)}, bf16[7,...) custom-call(s32[1]{0:T(128)} %bitcast.packed_ref, bf16[2048,1280]{1,0:T(8,128)(2,1)} %refs_12_.3, ...), custom_call_target="tpu_custom_call" | custom-call | flops 1174405120 | bytes 6127616 | tf_op jit(solution)/shard_map/pallas_call | solution.py:140
  29.7 2.9 %collective-permute-start.1 = (bf16[256,768]{1,0:T(8,128)(2,1)}, bf16[256,768]{1,0:T(8,128)(2,1)S(1)}, u32[]{:S(2)}, u32[]{:S(2)}) collective-permute-start(bf16[256,768]{1,0:T(8,128)(2,1)} %get-tuple-element.50), channel_id=1, source_target_pairs={{0,8},{8,0},{1,9},{9,1},{2,10},{10,2},{3,11},{11,3},{4,12},{12,4},... | collective-permute-start | bytes 1179656 | tf_op jit(solution)/shard_map/ppermute | solution.py:47
  33.7 3.4 %collective-permute-start.5 = (bf16[128,768]{1,0:T(8,128)(2,1)S(1)}, bf16[128,768]{1,0:T(8,128)(2,1)S(1)}, u32[]{:S(2)}, u32[]{:S(2)}) collective-permute-start(bf16[128,768]{1,0:T(8,128)(2,1)S(1)} %get-tuple-element.96), channel_id=1, source_target_pairs={{0,1},{1,2},{2,3},{3,4},{4,5},{5,6},{6,7},{7,0},{16,23},{17,16},{1... | collective-permute-start | bytes 589832 | tf_op jit(solution)/shard_map/ppermute | solution.py:53
  37.1 3.0 %collective-permute-start = (bf16[384,768]{1,0:T(8,128)(2,1)}, bf16[384,768]{1,0:T(8,128)(2,1)S(1)}, u32[]{:S(2)}, u32[]{:S(2)}) collective-permute-start(bf16[384,768]{1,0:T(8,128)(2,1)} %get-tuple-element.48), channel_id=1, source_target_pairs={{0,8},{8,0},{1,9},{9,1},{2,10},{10,2},{3,11},{11,3},{4,12},{12,4},... | collective-permute-start | bytes 1769480 | tf_op jit(solution)/shard_map/ppermute | solution.py:47
  40.2 5.1 %shard_map.86 = (bf16[256,768]{1,0:T(8,128)(2,1)}, bf16[384,768]{1,0:T(8,128)(2,1)}, bf16[5,320,128]{2,1,0:T(8,128)(2,1)}, bf16[5,128,320]{2,1,0:T(8,128)(2,1)}) custom-call(s32[1]{0:T(128)} %bitcast.packed_ref, bf16[2048,1280]{1,0:T(8,128)(2,1)} %refs_12_.3, bf16[2048,1280]{1,0:T(8,128)(2,1)} %refs_12_.3, bf16[2048,1280]{1,0:T(8,128)(2,1)} %refs_12_.3, ...), custom_call_target="tpu_custom_call" | custom-call | flops 838860800 | bytes 4751360 | tf_op jit(solution)/shard_map/pallas_call | solution.py:140
  45.3 4.0 %collective-permute-done.8 = bf16[128,768]{1,0:T(8,128)(2,1)S(1)} collective-permute-done((bf16[128,768]{1,0:T(8,128)(2,1)S(1)}, bf16[128,768]{1,0:T(8,128)(2,1)S(1)}, u32[]{:S(2)}, u32[]{:S(2)}) %collective-permute-start.8) | collective-permute-done | bytes 196640 | tf_op jit(solution)/shard_map/ppermute | solution.py:53
  54.1 3.3 %collective-permute-done.6 = bf16[128,768]{1,0:T(8,128)(2,1)S(1)} collective-permute-done((bf16[128,768]{1,0:T(8,128)(2,1)S(1)}, bf16[128,768]{1,0:T(8,128)(2,1)S(1)}, u32[]{:S(2)}, u32[]{:S(2)}) %collective-permute-start.6) | collective-permute-done | bytes 196640 | tf_op jit(solution)/shard_map/ppermute | solution.py:53
  58.8 2.7 %collective-permute-start.7 = (bf16[128,768]{1,0:T(8,128)(2,1)S(1)}, bf16[128,768]{1,0:T(8,128)(2,1)S(1)}, u32[]{:S(2)}, u32[]{:S(2)}) collective-permute-start(bf16[128,768]{1,0:T(8,128)(2,1)S(1)} %get-tuple-element.92), channel_id=1, source_target_pairs={{0,1},{1,2},{2,3},{3,4},{4,5},{5,6},{6,7},{7,0},{16,23},{17,16},{1... | collective-permute-start | bytes 589832 | tf_op jit(solution)/shard_map/ppermute | solution.py:53
  68.2 4.3 %collective-permute-done.11 = bf16[128,768]{1,0:T(8,128)(2,1)S(1)} collective-permute-done((bf16[128,768]{1,0:T(8,128)(2,1)S(1)}, bf16[128,768]{1,0:T(8,128)(2,1)S(1)}, u32[]{:S(2)}, u32[]{:S(2)}) %collective-permute-start.11) | collective-permute-done | bytes 196640 | tf_op jit(solution)/shard_map/ppermute | solution.py:47
  75.8 4.3 %collective-permute-done.12 = bf16[128,768]{1,0:T(8,128)(2,1)S(1)} collective-permute-done((bf16[128,768]{1,0:T(8,128)(2,1)S(1)}, bf16[128,768]{1,0:T(8,128)(2,1)S(1)}, u32[]{:S(2)}, u32[]{:S(2)}) %collective-permute-start.12) | collective-permute-done | bytes 196640 | tf_op jit(solution)/shard_map/ppermute | solution.py:47
  82.1 4.0 %collective-permute-start.13 = (bf16[128,768]{1,0:T(8,128)(2,1)S(1)}, bf16[128,768]{1,0:T(8,128)(2,1)S(1)}, u32[]{:S(2)}, u32[]{:S(2)}) collective-permute-start(bf16[128,768]{1,0:T(8,128)(2,1)S(1)} %multiply_convert_fusion.refs_0_), channel_id=1, source_target_pairs={{0,1},{1,2},{2,3},{3,4},{4,5},{5,6},{6,7},{7,0},{16,23},{17,16},{1... | collective-permute-start | bytes 589832 | tf_op jit(solution)/shard_map/ppermute | solution.py:53
  88.7 3.1 %collective-permute-start.14 = (bf16[128,768]{1,0:T(8,128)(2,1)S(1)}, bf16[128,768]{1,0:T(8,128)(2,1)S(1)}, u32[]{:S(2)}, u32[]{:S(2)}) collective-permute-start(bf16[128,768]{1,0:T(8,128)(2,1)S(1)} %collective-permute-done.13), channel_id=1, source_target_pairs={{0,1},{1,2},{2,3},{3,4},{4,5},{5,6},{6,7},{7,0},{16,23},{17,16},{1... | collective-permute-start | bytes 589832 | tf_op jit(solution)/shard_map/ppermute | solution.py:53
  94.6 4.1 %shard_map.88 = (bf16[320,1280]{1,0:T(8,128)(2,1)}, bf16[320,768]{1,0:T(8,128)(2,1)}) custom-call(s32[1]{0:T(128)} %bitcast.packed_ref, bf16[128,768]{1,0:T(8,128)(2,1)} %copy-done.5, bf16[128,768]{1,0:T(8,128)(2,1)} %copy-done.11, bf16[256,768]{1,0:T(8,128)(2,1)} %copy-done.3, bf16[2048,1280]{1,0:T(8,128)(2,1)} %refs_12_.3, ...), custom_call_target="tpu_custom_call" | custom-call | tf_op jit(solution)/shard_map/pallas_call | solution.py:238
  99.9 2.7 %collective-permute-start.18 = (bf16[128,768]{1,0:T(8,128)(2,1)S(1)}, bf16[128,768]{1,0:T(8,128)(2,1)S(1)}, u32[]{:S(2)}, u32[]{:S(2)}) collective-permute-start(bf16[128,768]{1,0:T(8,128)(2,1)S(1)} %collective-permute-done.14), channel_id=1, source_target_pairs={{0,1},{1,2},{2,3},{3,4},{4,5},{5,6},{6,7},{7,0},{16,23},{17,16},{1... | collective-permute-start | bytes 589832 | tf_op jit(solution)/shard_map/ppermute | solution.py:53
  103.3 4.5 %shard_map.89 = (bf16[320,1280]{1,0:T(8,128)(2,1)}, bf16[320,768]{1,0:T(8,128)(2,1)}) custom-call(s32[1]{0:T(128)} %bitcast.packed_ref, bf16[256,768]{1,0:T(8,128)(2,1)} %copy-done.9, bf16[256,768]{1,0:T(8,128)(2,1)} %copy-done.4, bf16[2048,1280]{1,0:T(8,128)(2,1)} %refs_12_.3, ...), custom_call_target="tpu_custom_call", output_to_operand_aliasing={{0}: (16, {}), {1}: (17, {})} | custom-call | tf_op jit(solution)/shard_map/pallas_call | solution.py:238
  108.6 2.6 %collective-permute-done.21.refs_1_ = bf16[256,768]{1,0:T(8,128)(2,1)S(1)} collective-permute-done((bf16[256,768]{1,0:T(8,128)(2,1)S(1)}, bf16[256,768]{1,0:T(8,128)(2,1)S(1)}, u32[]{:S(2)}, u32[]{:S(2)}) %collective-permute-start.21) | collective-permute-done | bytes 393248 | tf_op jit(solution)/shard_map/ppermute | solution.py:47
  112.0 2.8 %collective-permute-start.23 = (bf16[128,768]{1,0:T(8,128)(2,1)S(1)}, bf16[128,768]{1,0:T(8,128)(2,1)S(1)}, u32[]{:S(2)}, u32[]{:S(2)}) collective-permute-start(bf16[128,768]{1,0:T(8,128)(2,1)S(1)} %collective-permute-done.18), channel_id=1, source_target_pairs={{0,1},{1,2},{2,3},{3,4},{4,5},{5,6},{6,7},{7,0},{16,23},{17,16},{1... | collective-permute-start | bytes 589832 | tf_op jit(solution)/shard_map/ppermute | solution.py:53
  116.6 4.5 %shard_map.90 = (bf16[320,1280]{1,0:T(8,128)(2,1)}, bf16[320,768]{1,0:T(8,128)(2,1)}) custom-call(s32[1]{0:T(128)} %bitcast.packed_ref, bf16[256,768]{1,0:T(8,128)(2,1)} %copy-done.2, bf16[256,768]{1,0:T(8,128)(2,1)} %copy-done.7, bf16[2048,1280]{1,0:T(8,128)(2,1)} %refs_12_.3, ...), custom_call_target="tpu_custom_call", output_to_operand_aliasing={{0}: (16, {}), {1}: (17, {})} | custom-call | tf_op jit(solution)/shard_map/pallas_call | solution.py:238
  122.6 6.7 %shard_map.91 = (bf16[8,80,640]{2,1,0:T(8,128)(2,1)}, bf16[8,80,640]{2,1,0:T(8,128)(2,1)}) custom-call(s32[1]{0:T(128)} %bitcast.packed_ref, bf16[256,768]{1,0:T(8,128)(2,1)} %copy-done.8, bf16[128,768]{1,0:T(8,128)(2,1)} %copy-done.10, bf16[128,768]{1,0:T(8,128)(2,1)} %copy-done.12, bf16[2048,1280]{1,0:T(8,128)(2,1)} %refs_12_.3, ...), custom_call_target="tpu_custom_call" | custom-call | tf_op jit(solution)/shard_map/pallas_call | solution.py:238
  129.3 7.6 %collective-permute-start.25 = (bf16[8,80,640]{2,1,0:T(8,128)(2,1)}, bf16[8,80,640]{2,1,0:T(8,128)(2,1)S(1)}, u32[]{:S(2)}, u32[]{:S(2)}) collective-permute-start(bf16[8,80,640]{2,1,0:T(8,128)(2,1)} %get-tuple-element.87), channel_id=1, source_target_pairs={{0,16},{16,0},{1,17},{17,1},{2,18},{18,2},{3,19},{19,3},{4,20},{20... | collective-permute-start | bytes 2457608 | tf_op jit(solution)/shard_map/ppermute | solution.py:47
  140.4 18.7 %all_to_all.5 = bf16[8,80,640]{2,1,0:T(8,128)(2,1)S(1)} all-to-all(bf16[8,80,640]{2,1,0:T(8,128)(2,1)S(1)} %add_convert_fusion), channel_id=1, replica_groups=mesh['ylo'=2,'x'=4,'core'=2,'yhi'=2,'z'=8] {'ylo','x'}, dimensions={0} | all-to-all | bytes 1638400 | tf_op jit(solution)/shard_map/all_to_all | solution.py:339
  (97 shorter events, 39.1 us)
Async XLA Ops:
  7.2 54.3 %all-gather.2.cloned.1.call-start = ((), (), s32[]{:S(2)}) async-start(), calls=%async_computation.2 | async-start | bytes 1769472 | tf_op jit(solution)/shard_map/all_gather | solution.py:285
  7.9 152.0 %reduce-scatter.2.cloned.1.call-start = ((), (), s32[]{:S(2)}) async-start(), calls=%async_computation.3 | async-start | bytes 1769472 | tf_op jit(solution)/shard_map/reduce_scatter | solution.py:330
  13.6 19.0 %collective-permute-start.2 = (bf16[256,768]{1,0:T(8,128)(2,1)}, bf16[256,768]{1,0:T(8,128)(2,1)S(1)}, u32[]{:S(2)}, u32[]{:S(2)}) collective-permute-start(bf16[256,768]{1,0:T(8,128)(2,1)} %get-tuple-element.52), channel_id=1, source_target_pairs={{0,8},{8,0},{1,9},{9,1},{2,10},{10,2},{3,11},{11,3},{4,12},{12,4},... | collective-permute-start | bytes 1179656 | tf_op jit(solution)/shard_map/ppermute | solution.py:47
  17.3 15.2 %collective-permute-start.3 = (bf16[128,768]{1,0:T(8,128)(2,1)}, bf16[128,768]{1,0:T(8,128)(2,1)S(1)}, u32[]{:S(2)}, u32[]{:S(2)}) collective-permute-start(bf16[128,768]{1,0:T(8,128)(2,1)} %get-tuple-element.53), channel_id=1, source_target_pairs={{0,1},{1,2},{2,3},{3,4},{4,5},{5,6},{6,7},{7,0},{16,23},{17,16},{1... | collective-permute-start | bytes 589832 | tf_op jit(solution)/shard_map/ppermute | solution.py:53
  22.9 9.6 %collective-permute-start.4 = (bf16[128,768]{1,0:T(8,128)(2,1)}, bf16[128,768]{1,0:T(8,128)(2,1)S(1)}, u32[]{:S(2)}, u32[]{:S(2)}) collective-permute-start(bf16[128,768]{1,0:T(8,128)(2,1)} %get-tuple-element.54), channel_id=1, source_target_pairs={{0,9},{1,10},{2,11},{3,12},{4,13},{5,14},{6,15},{7,8},{8,1},{9,2},... | collective-permute-start | bytes 589832 | tf_op jit(solution)/shard_map/ppermute | solution.py:64
  29.7 15.6 %collective-permute-start.1 = (bf16[256,768]{1,0:T(8,128)(2,1)}, bf16[256,768]{1,0:T(8,128)(2,1)S(1)}, u32[]{:S(2)}, u32[]{:S(2)}) collective-permute-start(bf16[256,768]{1,0:T(8,128)(2,1)} %get-tuple-element.50), channel_id=1, source_target_pairs={{0,8},{8,0},{1,9},{9,1},{2,10},{10,2},{3,11},{11,3},{4,12},{12,4},... | collective-permute-start | bytes 1179656 | tf_op jit(solution)/shard_map/ppermute | solution.py:47
  33.7 11.5 %collective-permute-start.5 = (bf16[128,768]{1,0:T(8,128)(2,1)S(1)}, bf16[128,768]{1,0:T(8,128)(2,1)S(1)}, u32[]{:S(2)}, u32[]{:S(2)}) collective-permute-start(bf16[128,768]{1,0:T(8,128)(2,1)S(1)} %get-tuple-element.96), channel_id=1, source_target_pairs={{0,1},{1,2},{2,3},{3,4},{4,5},{5,6},{6,7},{7,0},{16,23},{17,16},{1... | collective-permute-start | bytes 589832 | tf_op jit(solution)/shard_map/ppermute | solution.py:53
  37.1 12.1 %collective-permute-start.8 = (bf16[128,768]{1,0:T(8,128)(2,1)S(1)}, bf16[128,768]{1,0:T(8,128)(2,1)S(1)}, u32[]{:S(2)}, u32[]{:S(2)}) collective-permute-start(bf16[128,768]{1,0:T(8,128)(2,1)S(1)} %get-tuple-element.95), channel_id=1, source_target_pairs={{0,7},{1,0},{2,1},{3,2},{4,3},{5,4},{6,5},{7,6},{16,17},{17,18},{1... | collective-permute-start | bytes 589832 | tf_op jit(solution)/shard_map/ppermute | solution.py:53
  37.1 17.0 %collective-permute-start = (bf16[384,768]{1,0:T(8,128)(2,1)}, bf16[384,768]{1,0:T(8,128)(2,1)S(1)}, u32[]{:S(2)}, u32[]{:S(2)}) collective-permute-start(bf16[384,768]{1,0:T(8,128)(2,1)} %get-tuple-element.48), channel_id=1, source_target_pairs={{0,8},{8,0},{1,9},{9,1},{2,10},{10,2},{3,11},{11,3},{4,12},{12,4},... | collective-permute-start | bytes 1769480 | tf_op jit(solution)/shard_map/ppermute | solution.py:47
  50.4 7.0 %collective-permute-start.6 = (bf16[128,768]{1,0:T(8,128)(2,1)S(1)}, bf16[128,768]{1,0:T(8,128)(2,1)S(1)}, u32[]{:S(2)}, u32[]{:S(2)}) collective-permute-start(bf16[128,768]{1,0:T(8,128)(2,1)S(1)} %get-tuple-element.94), channel_id=1, source_target_pairs={{0,1},{1,2},{2,3},{3,4},{4,5},{5,6},{6,7},{7,0},{16,23},{17,16},{1... | collective-permute-start | bytes 589832 | tf_op jit(solution)/shard_map/ppermute | solution.py:53
  50.5 8.1 %collective-permute-start.9 = (bf16[128,768]{1,0:T(8,128)(2,1)S(1)}, bf16[128,768]{1,0:T(8,128)(2,1)S(1)}, u32[]{:S(2)}, u32[]{:S(2)}) collective-permute-start(bf16[128,768]{1,0:T(8,128)(2,1)S(1)} %get-tuple-element.93), channel_id=1, source_target_pairs={{0,7},{1,0},{2,1},{3,2},{4,3},{5,4},{6,5},{7,6},{16,17},{17,18},{1... | collective-permute-start | bytes 589832 | tf_op jit(solution)/shard_map/ppermute | solution.py:53
  58.8 7.3 %collective-permute-start.7 = (bf16[128,768]{1,0:T(8,128)(2,1)S(1)}, bf16[128,768]{1,0:T(8,128)(2,1)S(1)}, u32[]{:S(2)}, u32[]{:S(2)}) collective-permute-start(bf16[128,768]{1,0:T(8,128)(2,1)S(1)} %get-tuple-element.92), channel_id=1, source_target_pairs={{0,1},{1,2},{2,3},{3,4},{4,5},{5,6},{6,7},{7,0},{16,23},{17,16},{1... | collective-permute-start | bytes 589832 | tf_op jit(solution)/shard_map/ppermute | solution.py:53
  66.4 6.1 %collective-permute-start.11 = (bf16[128,768]{1,0:T(8,128)(2,1)S(1)}, bf16[128,768]{1,0:T(8,128)(2,1)S(1)}, u32[]{:S(2)}, u32[]{:S(2)}) collective-permute-start(bf16[128,768]{1,0:T(8,128)(2,1)S(1)} %multiply_convert_fusion.1), channel_id=1, source_target_pairs={{0,8},{8,0},{1,9},{9,1},{2,10},{10,2},{3,11},{11,3},{4,12},{12,4},... | collective-permute-start | bytes 589832 | tf_op jit(solution)/shard_map/ppermute | solution.py:47
  80.5 11.3 %collective-permute-start.15 = (bf16[128,768]{1,0:T(8,128)(2,1)S(1)}, bf16[128,768]{1,0:T(8,128)(2,1)S(1)}, u32[]{:S(2)}, u32[]{:S(2)}) collective-permute-start(bf16[128,768]{1,0:T(8,128)(2,1)S(1)} %multiply_convert_fusion.refs_0_), channel_id=1, source_target_pairs={{0,7},{1,0},{2,1},{3,2},{4,3},{5,4},{6,5},{7,6},{16,17},{17,18},{1... | collective-permute-start | bytes 589832 | tf_op jit(solution)/shard_map/ppermute | solution.py:53
  82.1 6.6 %collective-permute-start.13 = (bf16[128,768]{1,0:T(8,128)(2,1)S(1)}, bf16[128,768]{1,0:T(8,128)(2,1)S(1)}, u32[]{:S(2)}, u32[]{:S(2)}) collective-permute-start(bf16[128,768]{1,0:T(8,128)(2,1)S(1)} %multiply_convert_fusion.refs_0_), channel_id=1, source_target_pairs={{0,1},{1,2},{2,3},{3,4},{4,5},{5,6},{6,7},{7,0},{16,23},{17,16},{1... | collective-permute-start | bytes 589832 | tf_op jit(solution)/shard_map/ppermute | solution.py:53
  88.7 10.0 %collective-permute-start.14 = (bf16[128,768]{1,0:T(8,128)(2,1)S(1)}, bf16[128,768]{1,0:T(8,128)(2,1)S(1)}, u32[]{:S(2)}, u32[]{:S(2)}) collective-permute-start(bf16[128,768]{1,0:T(8,128)(2,1)S(1)} %collective-permute-done.13), channel_id=1, source_target_pairs={{0,1},{1,2},{2,3},{3,4},{4,5},{5,6},{6,7},{7,0},{16,23},{17,16},{1... | collective-permute-start | bytes 589832 | tf_op jit(solution)/shard_map/ppermute | solution.py:53
  91.8 6.9 %collective-permute-start.16 = (bf16[128,768]{1,0:T(8,128)(2,1)S(1)}, bf16[128,768]{1,0:T(8,128)(2,1)S(1)}, u32[]{:S(2)}, u32[]{:S(2)}) collective-permute-start(bf16[128,768]{1,0:T(8,128)(2,1)S(1)} %collective-permute-done.15), channel_id=1, source_target_pairs={{0,7},{1,0},{2,1},{3,2},{4,3},{5,4},{6,5},{7,6},{16,17},{17,18},{1... | collective-permute-start | bytes 589832 | tf_op jit(solution)/shard_map/ppermute | solution.py:53
  91.9 10.7 %collective-permute-start.20 = (bf16[256,768]{1,0:T(8,128)(2,1)S(1)}, bf16[256,768]{1,0:T(8,128)(2,1)S(1)}, u32[]{:S(2)}, u32[]{:S(2)}) collective-permute-start(bf16[256,768]{1,0:T(8,128)(2,1)S(1)} %constant_dynamic-update-slice_fusion.refs_2_), channel_id=1, source_target_pairs={{0,8},{8,0},{1,9},{9,1},{2,10},{10,2},{3,11},{11,3},{4,12},{12,4},... | collective-permute-start | bytes 1179656 | tf_op jit(solution)/shard_map/ppermute | solution.py:47
  98.8 12.4 %collective-permute-start.21 = (bf16[256,768]{1,0:T(8,128)(2,1)S(1)}, bf16[256,768]{1,0:T(8,128)(2,1)S(1)}, u32[]{:S(2)}, u32[]{:S(2)}) collective-permute-start(bf16[256,768]{1,0:T(8,128)(2,1)S(1)} %constant_dynamic-update-slice_fusion.2.refs_1_), channel_id=1, source_target_pairs={{0,8},{8,0},{1,9},{9,1},{2,10},{10,2},{3,11},{11,3},{4,12},{12,4},... | collective-permute-start | bytes 1179656 | tf_op jit(solution)/shard_map/ppermute | solution.py:47
  99.9 7.9 %collective-permute-start.18 = (bf16[128,768]{1,0:T(8,128)(2,1)S(1)}, bf16[128,768]{1,0:T(8,128)(2,1)S(1)}, u32[]{:S(2)}, u32[]{:S(2)}) collective-permute-start(bf16[128,768]{1,0:T(8,128)(2,1)S(1)} %collective-permute-done.14), channel_id=1, source_target_pairs={{0,1},{1,2},{2,3},{3,4},{4,5},{5,6},{6,7},{7,0},{16,23},{17,16},{1... | collective-permute-start | bytes 589832 | tf_op jit(solution)/shard_map/ppermute | solution.py:53
  111.3 10.5 %collective-permute-start.22 = (bf16[256,768]{1,0:T(8,128)(2,1)S(1)}, bf16[256,768]{1,0:T(8,128)(2,1)S(1)}, u32[]{:S(2)}, u32[]{:S(2)}) collective-permute-start(bf16[256,768]{1,0:T(8,128)(2,1)S(1)} %constant_dynamic-update-slice_fusion.4.refs_0_), channel_id=1, source_target_pairs={{0,8},{8,0},{1,9},{9,1},{2,10},{10,2},{3,11},{11,3},{4,12},{12,4},... | collective-permute-start | bytes 1179656 | tf_op jit(solution)/shard_map/ppermute | solution.py:47
  112.0 9.0 %collective-permute-start.23 = (bf16[128,768]{1,0:T(8,128)(2,1)S(1)}, bf16[128,768]{1,0:T(8,128)(2,1)S(1)}, u32[]{:S(2)}, u32[]{:S(2)}) collective-permute-start(bf16[128,768]{1,0:T(8,128)(2,1)S(1)} %collective-permute-done.18), channel_id=1, source_target_pairs={{0,1},{1,2},{2,3},{3,4},{4,5},{5,6},{6,7},{7,0},{16,23},{17,16},{1... | collective-permute-start | bytes 589832 | tf_op jit(solution)/shard_map/ppermute | solution.py:53
  114.8 6.9 %collective-permute-start.24 = (bf16[128,768]{1,0:T(8,128)(2,1)S(1)}, bf16[128,768]{1,0:T(8,128)(2,1)S(1)}, u32[]{:S(2)}, u32[]{:S(2)}) collective-permute-start(bf16[128,768]{1,0:T(8,128)(2,1)S(1)} %collective-permute-done.18), channel_id=1, source_target_pairs={{0,9},{1,10},{2,11},{3,12},{4,13},{5,14},{6,15},{7,8},{8,1},{9,2},... | collective-permute-start | bytes 589832 | tf_op jit(solution)/shard_map/ppermute | solution.py:64
  129.3 9.8 %collective-permute-start.25 = (bf16[8,80,640]{2,1,0:T(8,128)(2,1)}, bf16[8,80,640]{2,1,0:T(8,128)(2,1)S(1)}, u32[]{:S(2)}, u32[]{:S(2)}) collective-permute-start(bf16[8,80,640]{2,1,0:T(8,128)(2,1)} %get-tuple-element.87), channel_id=1, source_target_pairs={{0,16},{16,0},{1,17},{17,1},{2,18},{18,2},{3,19},{19,3},{4,20},{20... | collective-permute-start | bytes 2457608 | tf_op jit(solution)/shard_map/ppermute | solution.py:47
  (17 other events, 77.4 us)
Sparse Core Ops, SparseCore 0:
  9.8 42.4 all-gather.1
  111.3 41.6 reduce-scatter.1

commit v15 on v14

--- a/solution.py
+++ b/solution.py
@@ -179,7 +179,7 @@
         head_ref, keep_ref, give_ref, total, sems = refs
     else:
         up_acc, act_acc = refs
-        act_acc[...] = act_sum.astype(bf16)
+        act_acc[...] = act_sum
     width, ff = hidden.shape[1], act_sum.shape[0]
     for m in range(0, width, tile):
         up_sum = dot(grad_pre_t, hidden[:, m : m + tile])
@@ -188,7 +188,7 @@
         if last:
             total[m : m + tile, :ff] = up_sum.T.astype(bf16)
         else:
-            up_acc[:, m : m + tile] = up_sum.astype(bf16)
+            up_acc[:, m : m + tile] = up_sum
     if last:
         core = packed_ref[0] % 2
         act_grad = act_sum.astype(bf16)
@@ -232,7 +232,7 @@
         shapes = [jax.ShapeDtypeStruct((8, width // 16, 2 * ff), bf16)] * 2
         scratch = [pltpu.VMEM((width, 2 * ff), bf16), pltpu.SemaphoreType.DMA((16,))]
     else:
-        shapes = [jax.ShapeDtypeStruct((ff, width), bf16), jax.ShapeDtypeStruct((ff, embed), bf16)]
+        shapes = [jax.ShapeDtypeStruct((ff, width), f32), jax.ShapeDtypeStruct((ff, embed), f32)]
         scratch = []
     specs += [whole] * (len(args) - len(specs))
     return pl.pallas_call(

time: 170 us -> 165 us (0.971)
  waiting for transfers between devices: 27.9 us -> 20.1 us
  starting transfers between devices: 53.9 us -> 57.8 us
  blocking collectives: 18.7 us -> 16.1 us
  Pallas kernels: 38.6 us -> 40.7 us
    ppermute x10, starting transfers between devices: 24.1 us -> 32.4 us  [swap(): return lax.ppermute(value, axis, [(0, 1), (1, 0)])]
    ppermute x14, waiting for transfers between devices: 11.8 us -> 5.75 us  [shift(): return lax.ppermute(value, ('core', 'z'), perm)]
    ppermute x10, waiting for transfers between devices: 14.7 us -> 11.9 us  [swap(): return lax.ppermute(value, axis, [(0, 1), (1, 0)])]
    ppermute x14, starting transfers between devices: 27.5 us -> 24.8 us  [shift(): return lax.ppermute(value, ('core', 'z'), perm)]
    all_to_all x1, blocking collectives: 18.7 us -> 16.1 us  [per_device(): landed = lax.all_to_all(chip, ('ylo', 'x'), 0, 0)]
    pallas_call x4, Pallas kernels: 19.7 us -> 21.8 us  [backward_blocks(): pl.pallas_call(functools.partial(backward_kernel, len(items), len(places)...]
    ppermute x2, starting transfers between devices: 2.25 us -> 0.53 us  [shift_across(): return lax.ppermute(value, ('core', 'yhi', 'z'), perm)]
  transfers between devices with their start and end apart: 28 -> 28, of which waited for: 13 -> 10; matrix products, arithmetic and copies ran while one was open for 6% -> 7% of each run, Pallas kernels for 22% -> 24%
where the time goes in v15:
time: 165 us; the launch traced here: 164 us
  starting transfers between devices  57.8 us (35%)
  Pallas kernels  40.7 us (25%)
  waiting for transfers between devices  20.1 us (12%)
  blocking collectives  16.1 us (10%)
  between operations  14.3 us (9%)
  other arithmetic  6.86 us (4%)
  matrix products  4.6 us (3%)
  local copies, waits for them, and re-layouts  3.76 us (2%)
    ppermute x10, starting transfers between devices, swap(): return lax.ppermute(value, axis, [(0, 1), (1, 0)])  32.4 us
    ppermute x14, starting transfers between devices, shift(): return lax.ppermute(value, ('core', 'z'), perm)  24.8 us
    pallas_call x4, Pallas kernels, backward_blocks(): pl.pallas_call(functools.partial(backward_kernel, len(items), len(places)...  21.8 us
    pallas_call x3, Pallas kernels, forward_blocks(): pl.pallas_call(functools.partial(forward_kernel, pieces, first), grid_spe...  16.9 us
    all_to_all x1, blocking collectives, per_device(): landed = lax.all_to_all(chip, ('ylo', 'x'), 0, 0)  16.1 us
    ppermute x10, waiting for transfers between devices, swap(): return lax.ppermute(value, axis, [(0, 1), (1, 0)])  11.9 us
    ppermute x14, waiting for transfers between devices, shift(): return lax.ppermute(value, ('core', 'z'), perm)  5.75 us
    dot_general x4, matrix products, dot(): lax.dot_general(left, right, (dims, ((), ())), preferred_element_type=f32)  4.6 us
  transfers between devices with their start and end apart: 28, of which 10 were waited for; matrix products, arithmetic and copies ran while one was open for 7% of the time, Pallas kernels for 24%

profile of v15, /device:TPU:1, one launch (start us, length us, event | category | flops | bytes accessed | tf_op | source)
XLA Modules:
  0.0 164.4 jit_solution(10788128632627898733)
XLA Ops:
  8.0 5.6 %shard_map.85 = (bf16[128,768]{1,0:T(8,128)(2,1)}, bf16[256,768]{1,0:T(8,128)(2,1)}, bf16[128,768]{1,0:T(8,128)(2,1)}, bf16[4,320,128]{2,1,0:T(8,128)(2,1)}, bf1...) custom-call(s32[1]{0:T(128)} %bitcast.packed_ref, bf16[2048,1280]{1,0:T(8,128)(2,1)} %refs_12_.3, ...), custom_call_target="tpu_custom_call" | custom-call | flops 671088640 | bytes 4063232 | tf_op jit(solution)/shard_map/pallas_call | solution.py:140
  13.6 3.7 %collective-permute-start.2 = (bf16[256,768]{1,0:T(8,128)(2,1)}, bf16[256,768]{1,0:T(8,128)(2,1)S(1)}, u32[]{:S(2)}, u32[]{:S(2)}) collective-permute-start(bf16[256,768]{1,0:T(8,128)(2,1)} %get-tuple-element.52), channel_id=1, source_target_pairs={{0,8},{8,0},{1,9},{9,1},{2,10},{10,2},{3,11},{11,3},{4,12},{12,4},... | collective-permute-start | bytes 1179656 | tf_op jit(solution)/shard_map/ppermute | solution.py:47
  17.3 5.6 %collective-permute-start.3 = (bf16[128,768]{1,0:T(8,128)(2,1)}, bf16[128,768]{1,0:T(8,128)(2,1)S(1)}, u32[]{:S(2)}, u32[]{:S(2)}) collective-permute-start(bf16[128,768]{1,0:T(8,128)(2,1)} %get-tuple-element.53), channel_id=1, source_target_pairs={{0,1},{1,2},{2,3},{3,4},{4,5},{5,6},{6,7},{7,0},{16,23},{17,16},{1... | collective-permute-start | bytes 589832 | tf_op jit(solution)/shard_map/ppermute | solution.py:53
  23.4 6.3 %shard_map.87 = (bf16[256,768]{1,0:T(8,128)(2,1)}, bf16[384,768]{1,0:T(8,128)(2,1)}, bf16[128,768]{1,0:T(8,128)(2,1)}, bf16[128,768]{1,0:T(8,128)(2,1)}, bf16[7,...) custom-call(s32[1]{0:T(128)} %bitcast.packed_ref, bf16[2048,1280]{1,0:T(8,128)(2,1)} %refs_12_.3, ...), custom_call_target="tpu_custom_call" | custom-call | flops 1174405120 | bytes 6127616 | tf_op jit(solution)/shard_map/pallas_call | solution.py:140
  29.7 2.9 %collective-permute-start.1 = (bf16[256,768]{1,0:T(8,128)(2,1)}, bf16[256,768]{1,0:T(8,128)(2,1)S(1)}, u32[]{:S(2)}, u32[]{:S(2)}) collective-permute-start(bf16[256,768]{1,0:T(8,128)(2,1)} %get-tuple-element.50), channel_id=1, source_target_pairs={{0,8},{8,0},{1,9},{9,1},{2,10},{10,2},{3,11},{11,3},{4,12},{12,4},... | collective-permute-start | bytes 1179656 | tf_op jit(solution)/shard_map/ppermute | solution.py:47
  34.5 2.7 %collective-permute-start.5 = (bf16[128,768]{1,0:T(8,128)(2,1)S(1)}, bf16[128,768]{1,0:T(8,128)(2,1)S(1)}, u32[]{:S(2)}, u32[]{:S(2)}) collective-permute-start(bf16[128,768]{1,0:T(8,128)(2,1)S(1)} %get-tuple-element.96), channel_id=1, source_target_pairs={{0,1},{1,2},{2,3},{3,4},{4,5},{5,6},{6,7},{7,0},{16,23},{17,16},{1... | collective-permute-start | bytes 589832 | tf_op jit(solution)/shard_map/ppermute | solution.py:53
  37.2 3.0 %collective-permute-start = (bf16[384,768]{1,0:T(8,128)(2,1)}, bf16[384,768]{1,0:T(8,128)(2,1)S(1)}, u32[]{:S(2)}, u32[]{:S(2)}) collective-permute-start(bf16[384,768]{1,0:T(8,128)(2,1)} %get-tuple-element.48), channel_id=1, source_target_pairs={{0,8},{8,0},{1,9},{9,1},{2,10},{10,2},{3,11},{11,3},{4,12},{12,4},... | collective-permute-start | bytes 1769480 | tf_op jit(solution)/shard_map/ppermute | solution.py:47
  40.2 5.1 %shard_map.86 = (bf16[256,768]{1,0:T(8,128)(2,1)}, bf16[384,768]{1,0:T(8,128)(2,1)}, bf16[5,320,128]{2,1,0:T(8,128)(2,1)}, bf16[5,128,320]{2,1,0:T(8,128)(2,1)}) custom-call(s32[1]{0:T(128)} %bitcast.packed_ref, bf16[2048,1280]{1,0:T(8,128)(2,1)} %refs_12_.3, bf16[2048,1280]{1,0:T(8,128)(2,1)} %refs_12_.3, bf16[2048,1280]{1,0:T(8,128)(2,1)} %refs_12_.3, ...), custom_call_target="tpu_custom_call" | custom-call | flops 838860800 | bytes 4751360 | tf_op jit(solution)/shard_map/pallas_call | solution.py:140
  51.4 2.7 %collective-permute-done.9 = bf16[128,768]{1,0:T(8,128)(2,1)S(1)} collective-permute-done((bf16[128,768]{1,0:T(8,128)(2,1)S(1)}, bf16[128,768]{1,0:T(8,128)(2,1)S(1)}, u32[]{:S(2)}, u32[]{:S(2)}) %collective-permute-start.9) | collective-permute-done | bytes 196640 | tf_op jit(solution)/shard_map/ppermute | solution.py:53
  54.3 3.4 %collective-permute-start.10 = (bf16[128,768]{1,0:T(8,128)(2,1)S(1)}, bf16[128,768]{1,0:T(8,128)(2,1)S(1)}, u32[]{:S(2)}, u32[]{:S(2)}) collective-permute-start(bf16[128,768]{1,0:T(8,128)(2,1)S(1)} %get-tuple-element.91), channel_id=1, source_target_pairs={{0,7},{1,0},{2,1},{3,2},{4,3},{5,4},{6,5},{7,6},{16,17},{17,18},{1... | collective-permute-start | bytes 589832 | tf_op jit(solution)/shard_map/ppermute | solution.py:53
  62.5 3.2 %collective-permute-start.11 = (bf16[128,768]{1,0:T(8,128)(2,1)S(1)}, bf16[128,768]{1,0:T(8,128)(2,1)S(1)}, u32[]{:S(2)}, u32[]{:S(2)}) collective-permute-start(bf16[128,768]{1,0:T(8,128)(2,1)S(1)} %multiply_convert_fusion.1), channel_id=1, source_target_pairs={{0,8},{8,0},{1,9},{9,1},{2,10},{10,2},{3,11},{11,3},{4,12},{12,4},... | collective-permute-start | bytes 589832 | tf_op jit(solution)/shard_map/ppermute | solution.py:47
  65.8 3.0 %collective-permute-done.11 = bf16[128,768]{1,0:T(8,128)(2,1)S(1)} collective-permute-done((bf16[128,768]{1,0:T(8,128)(2,1)S(1)}, bf16[128,768]{1,0:T(8,128)(2,1)S(1)}, u32[]{:S(2)}, u32[]{:S(2)}) %collective-permute-start.11) | collective-permute-done | bytes 196640 | tf_op jit(solution)/shard_map/ppermute | solution.py:47
  70.3 3.0 %collective-permute-start.12 = (bf16[128,768]{1,0:T(8,128)(2,1)S(1)}, bf16[128,768]{1,0:T(8,128)(2,1)S(1)}, u32[]{:S(2)}, u32[]{:S(2)}) collective-permute-start(bf16[128,768]{1,0:T(8,128)(2,1)S(1)} %slice.95), channel_id=1, source_target_pairs={{0,8},{8,0},{1,9},{9,1},{2,10},{10,2},{3,11},{11,3},{4,12},{12,4},... | collective-permute-start | bytes 589832 | tf_op jit(solution)/shard_map/ppermute | solution.py:47
  73.3 3.7 %collective-permute-done.12 = bf16[128,768]{1,0:T(8,128)(2,1)S(1)} collective-permute-done((bf16[128,768]{1,0:T(8,128)(2,1)S(1)}, bf16[128,768]{1,0:T(8,128)(2,1)S(1)}, u32[]{:S(2)}, u32[]{:S(2)}) %collective-permute-start.12) | collective-permute-done | bytes 196640 | tf_op jit(solution)/shard_map/ppermute | solution.py:47
  77.4 3.0 %collective-permute-start.15 = (bf16[128,768]{1,0:T(8,128)(2,1)S(1)}, bf16[128,768]{1,0:T(8,128)(2,1)S(1)}, u32[]{:S(2)}, u32[]{:S(2)}) collective-permute-start(bf16[128,768]{1,0:T(8,128)(2,1)S(1)} %multiply_convert_fusion.refs_0_), channel_id=1, source_target_pairs={{0,7},{1,0},{2,1},{3,2},{4,3},{5,4},{6,5},{7,6},{16,17},{17,18},{1... | collective-permute-start | bytes 589832 | tf_op jit(solution)/shard_map/ppermute | solution.py:53
  82.2 2.8 %collective-permute-start.17 = (bf16[128,768]{1,0:T(8,128)(2,1)S(1)}, bf16[128,768]{1,0:T(8,128)(2,1)S(1)}, u32[]{:S(2)}, u32[]{:S(2)}) collective-permute-start(bf16[128,768]{1,0:T(8,128)(2,1)S(1)} %multiply_convert_fusion.refs_0_), channel_id=1, source_target_pairs={{0,8},{8,0},{1,9},{9,1},{2,10},{10,2},{3,11},{11,3},{4,12},{12,4},... | collective-permute-start | bytes 589832 | tf_op jit(solution)/shard_map/ppermute | solution.py:47
  85.0 3.7 %collective-permute-start.16 = (bf16[128,768]{1,0:T(8,128)(2,1)S(1)}, bf16[128,768]{1,0:T(8,128)(2,1)S(1)}, u32[]{:S(2)}, u32[]{:S(2)}) collective-permute-start(bf16[128,768]{1,0:T(8,128)(2,1)S(1)} %collective-permute-done.15), channel_id=1, source_target_pairs={{0,7},{1,0},{2,1},{3,2},{4,3},{5,4},{6,5},{7,6},{16,17},{17,18},{1... | collective-permute-start | bytes 589832 | tf_op jit(solution)/shard_map/ppermute | solution.py:53
  90.8 4.4 %shard_map.88 = (f32[320,1280]{1,0:T(8,128)}, f32[320,768]{1,0:T(8,128)}) custom-call(s32[1]{0:T(128)} %bitcast.packed_ref, bf16[128,768]{1,0:T(8,128)(2,1)} %copy-done.5, bf16[128,768]{1,0:T(8,128)(2,1)} %copy-done.11, bf16[256,768]{1,0:T(8,128)(2,1)} %copy-done.4, bf16[2048,1280]{1,0:T(8,128)(2,1)} %refs_12_.3, ...), custom_call_target="tpu_custom_call" | custom-call | tf_op jit(solution)/shard_map/pallas_call | solution.py:238
  97.0 2.9 %collective-permute-start.19 = (bf16[128,768]{1,0:T(8,128)(2,1)S(1)}, bf16[128,768]{1,0:T(8,128)(2,1)S(1)}, u32[]{:S(2)}, u32[]{:S(2)}) collective-permute-start(bf16[128,768]{1,0:T(8,128)(2,1)S(1)} %collective-permute-done.16), channel_id=1, source_target_pairs={{0,7},{1,0},{2,1},{3,2},{4,3},{5,4},{6,5},{7,6},{16,17},{17,18},{1... | collective-permute-start | bytes 589832 | tf_op jit(solution)/shard_map/ppermute | solution.py:53
  100.7 5.2 %shard_map.89 = (f32[320,1280]{1,0:T(8,128)}, f32[320,768]{1,0:T(8,128)}) custom-call(s32[1]{0:T(128)} %bitcast.packed_ref, bf16[256,768]{1,0:T(8,128)(2,1)} %copy-done.8, bf16[256,768]{1,0:T(8,128)(2,1)} %copy-done.3, bf16[2048,1280]{1,0:T(8,128)(2,1)} %refs_12_.3, ...), custom_call_target="tpu_custom_call", output_to_operand_aliasing={{0}: (16, {}), {1}: (17, {})} | custom-call | tf_op jit(solution)/shard_map/pallas_call | solution.py:238
  109.6 5.2 %shard_map.90 = (f32[320,1280]{1,0:T(8,128)}, f32[320,768]{1,0:T(8,128)}) custom-call(s32[1]{0:T(128)} %bitcast.packed_ref, bf16[256,768]{1,0:T(8,128)(2,1)} %copy-done.2, bf16[256,768]{1,0:T(8,128)(2,1)} %copy-done.7, bf16[2048,1280]{1,0:T(8,128)(2,1)} %refs_12_.3, ...), custom_call_target="tpu_custom_call", output_to_operand_aliasing={{0}: (16, {}), {1}: (17, {})} | custom-call | tf_op jit(solution)/shard_map/pallas_call | solution.py:238
  119.3 7.0 %shard_map.91 = (bf16[8,80,640]{2,1,0:T(8,128)(2,1)}, bf16[8,80,640]{2,1,0:T(8,128)(2,1)}) custom-call(s32[1]{0:T(128)} %bitcast.packed_ref, bf16[256,768]{1,0:T(8,128)(2,1)} %copy-done.9, bf16[128,768]{1,0:T(8,128)(2,1)} %copy-done.12, bf16[128,768]{1,0:T(8,128)(2,1)} %copy-done.10, bf16[2048,1280]{1,0:T(8,128)(2,1)} %refs_12_.3, ...), custom_call_target="tpu_custom_call" | custom-call | tf_op jit(solution)/shard_map/pallas_call | solution.py:238
  126.4 8.6 %collective-permute-start.25 = (bf16[8,80,640]{2,1,0:T(8,128)(2,1)}, bf16[8,80,640]{2,1,0:T(8,128)(2,1)S(1)}, u32[]{:S(2)}, u32[]{:S(2)}) collective-permute-start(bf16[8,80,640]{2,1,0:T(8,128)(2,1)} %get-tuple-element.87), channel_id=1, source_target_pairs={{0,16},{16,0},{1,17},{17,1},{2,18},{18,2},{3,19},{19,3},{4,20},{20... | collective-permute-start | bytes 2457608 | tf_op jit(solution)/shard_map/ppermute | solution.py:47
  138.5 16.1 %all_to_all.5 = bf16[8,80,640]{2,1,0:T(8,128)(2,1)S(1)} all-to-all(bf16[8,80,640]{2,1,0:T(8,128)(2,1)S(1)} %add_convert_fusion), channel_id=1, replica_groups=mesh['ylo'=2,'x'=4,'core'=2,'yhi'=2,'z'=8] {'ylo','x'}, dimensions={0} | all-to-all | bytes 1638400 | tf_op jit(solution)/shard_map/all_to_all | solution.py:339
  (97 shorter events, 37.1 us)
Async XLA Ops:
  7.2 50.5 %all-gather.2.cloned.1.call-start = ((), (), s32[]{:S(2)}) async-start(), calls=%async_computation.2 | async-start | bytes 1769472 | tf_op jit(solution)/shard_map/all_gather | solution.py:285
  7.9 147.6 %reduce-scatter.2.cloned.1.call-start = ((), (), s32[]{:S(2)}) async-start(), calls=%async_computation.3 | async-start | bytes 1769472 | tf_op jit(solution)/shard_map/reduce_scatter | solution.py:330
  13.6 19.0 %collective-permute-start.2 = (bf16[256,768]{1,0:T(8,128)(2,1)}, bf16[256,768]{1,0:T(8,128)(2,1)S(1)}, u32[]{:S(2)}, u32[]{:S(2)}) collective-permute-start(bf16[256,768]{1,0:T(8,128)(2,1)} %get-tuple-element.52), channel_id=1, source_target_pairs={{0,8},{8,0},{1,9},{9,1},{2,10},{10,2},{3,11},{11,3},{4,12},{12,4},... | collective-permute-start | bytes 1179656 | tf_op jit(solution)/shard_map/ppermute | solution.py:47
  17.3 15.2 %collective-permute-start.3 = (bf16[128,768]{1,0:T(8,128)(2,1)}, bf16[128,768]{1,0:T(8,128)(2,1)S(1)}, u32[]{:S(2)}, u32[]{:S(2)}) collective-permute-start(bf16[128,768]{1,0:T(8,128)(2,1)} %get-tuple-element.53), channel_id=1, source_target_pairs={{0,1},{1,2},{2,3},{3,4},{4,5},{5,6},{6,7},{7,0},{16,23},{17,16},{1... | collective-permute-start | bytes 589832 | tf_op jit(solution)/shard_map/ppermute | solution.py:53
  22.9 9.7 %collective-permute-start.4 = (bf16[128,768]{1,0:T(8,128)(2,1)}, bf16[128,768]{1,0:T(8,128)(2,1)S(1)}, u32[]{:S(2)}, u32[]{:S(2)}) collective-permute-start(bf16[128,768]{1,0:T(8,128)(2,1)} %get-tuple-element.54), channel_id=1, source_target_pairs={{0,9},{1,10},{2,11},{3,12},{4,13},{5,14},{6,15},{7,8},{8,1},{9,2},... | collective-permute-start | bytes 589832 | tf_op jit(solution)/shard_map/ppermute | solution.py:64
  29.7 15.6 %collective-permute-start.1 = (bf16[256,768]{1,0:T(8,128)(2,1)}, bf16[256,768]{1,0:T(8,128)(2,1)S(1)}, u32[]{:S(2)}, u32[]{:S(2)}) collective-permute-start(bf16[256,768]{1,0:T(8,128)(2,1)} %get-tuple-element.50), channel_id=1, source_target_pairs={{0,8},{8,0},{1,9},{9,1},{2,10},{10,2},{3,11},{11,3},{4,12},{12,4},... | collective-permute-start | bytes 1179656 | tf_op jit(solution)/shard_map/ppermute | solution.py:47
  33.7 11.6 %collective-permute-start.8 = (bf16[128,768]{1,0:T(8,128)(2,1)S(1)}, bf16[128,768]{1,0:T(8,128)(2,1)S(1)}, u32[]{:S(2)}, u32[]{:S(2)}) collective-permute-start(bf16[128,768]{1,0:T(8,128)(2,1)S(1)} %get-tuple-element.95), channel_id=1, source_target_pairs={{0,7},{1,0},{2,1},{3,2},{4,3},{5,4},{6,5},{7,6},{16,17},{17,18},{1... | collective-permute-start | bytes 589832 | tf_op jit(solution)/shard_map/ppermute | solution.py:53
  34.5 10.8 %collective-permute-start.5 = (bf16[128,768]{1,0:T(8,128)(2,1)S(1)}, bf16[128,768]{1,0:T(8,128)(2,1)S(1)}, u32[]{:S(2)}, u32[]{:S(2)}) collective-permute-start(bf16[128,768]{1,0:T(8,128)(2,1)S(1)} %get-tuple-element.96), channel_id=1, source_target_pairs={{0,1},{1,2},{2,3},{3,4},{4,5},{5,6},{6,7},{7,0},{16,23},{17,16},{1... | collective-permute-start | bytes 589832 | tf_op jit(solution)/shard_map/ppermute | solution.py:53
  37.2 14.2 %collective-permute-start = (bf16[384,768]{1,0:T(8,128)(2,1)}, bf16[384,768]{1,0:T(8,128)(2,1)S(1)}, u32[]{:S(2)}, u32[]{:S(2)}) collective-permute-start(bf16[384,768]{1,0:T(8,128)(2,1)} %get-tuple-element.48), channel_id=1, source_target_pairs={{0,8},{8,0},{1,9},{9,1},{2,10},{10,2},{3,11},{11,3},{4,12},{12,4},... | collective-permute-start | bytes 1769480 | tf_op jit(solution)/shard_map/ppermute | solution.py:47
  46.5 7.6 %collective-permute-start.9 = (bf16[128,768]{1,0:T(8,128)(2,1)S(1)}, bf16[128,768]{1,0:T(8,128)(2,1)S(1)}, u32[]{:S(2)}, u32[]{:S(2)}) collective-permute-start(bf16[128,768]{1,0:T(8,128)(2,1)S(1)} %get-tuple-element.93), channel_id=1, source_target_pairs={{0,7},{1,0},{2,1},{3,2},{4,3},{5,4},{6,5},{7,6},{16,17},{17,18},{1... | collective-permute-start | bytes 589832 | tf_op jit(solution)/shard_map/ppermute | solution.py:53
  46.8 7.3 %collective-permute-start.6 = (bf16[128,768]{1,0:T(8,128)(2,1)S(1)}, bf16[128,768]{1,0:T(8,128)(2,1)S(1)}, u32[]{:S(2)}, u32[]{:S(2)}) collective-permute-start(bf16[128,768]{1,0:T(8,128)(2,1)S(1)} %get-tuple-element.94), channel_id=1, source_target_pairs={{0,1},{1,2},{2,3},{3,4},{4,5},{5,6},{6,7},{7,0},{16,23},{17,16},{1... | collective-permute-start | bytes 589832 | tf_op jit(solution)/shard_map/ppermute | solution.py:53
  54.3 6.9 %collective-permute-start.10 = (bf16[128,768]{1,0:T(8,128)(2,1)S(1)}, bf16[128,768]{1,0:T(8,128)(2,1)S(1)}, u32[]{:S(2)}, u32[]{:S(2)}) collective-permute-start(bf16[128,768]{1,0:T(8,128)(2,1)S(1)} %get-tuple-element.91), channel_id=1, source_target_pairs={{0,7},{1,0},{2,1},{3,2},{4,3},{5,4},{6,5},{7,6},{16,17},{17,18},{1... | collective-permute-start | bytes 589832 | tf_op jit(solution)/shard_map/ppermute | solution.py:53
  77.4 7.6 %collective-permute-start.15 = (bf16[128,768]{1,0:T(8,128)(2,1)S(1)}, bf16[128,768]{1,0:T(8,128)(2,1)S(1)}, u32[]{:S(2)}, u32[]{:S(2)}) collective-permute-start(bf16[128,768]{1,0:T(8,128)(2,1)S(1)} %multiply_convert_fusion.refs_0_), channel_id=1, source_target_pairs={{0,7},{1,0},{2,1},{3,2},{4,3},{5,4},{6,5},{7,6},{16,17},{17,18},{1... | collective-permute-start | bytes 589832 | tf_op jit(solution)/shard_map/ppermute | solution.py:53
  80.4 8.2 %collective-permute-start.13 = (bf16[128,768]{1,0:T(8,128)(2,1)S(1)}, bf16[128,768]{1,0:T(8,128)(2,1)S(1)}, u32[]{:S(2)}, u32[]{:S(2)}) collective-permute-start(bf16[128,768]{1,0:T(8,128)(2,1)S(1)} %multiply_convert_fusion.refs_0_), channel_id=1, source_target_pairs={{0,1},{1,2},{2,3},{3,4},{4,5},{5,6},{6,7},{7,0},{16,23},{17,16},{1... | collective-permute-start | bytes 589832 | tf_op jit(solution)/shard_map/ppermute | solution.py:53
  82.2 7.9 %collective-permute-start.17 = (bf16[128,768]{1,0:T(8,128)(2,1)S(1)}, bf16[128,768]{1,0:T(8,128)(2,1)S(1)}, u32[]{:S(2)}, u32[]{:S(2)}) collective-permute-start(bf16[128,768]{1,0:T(8,128)(2,1)S(1)} %multiply_convert_fusion.refs_0_), channel_id=1, source_target_pairs={{0,8},{8,0},{1,9},{9,1},{2,10},{10,2},{3,11},{11,3},{4,12},{12,4},... | collective-permute-start | bytes 589832 | tf_op jit(solution)/shard_map/ppermute | solution.py:47
  85.0 10.2 %collective-permute-start.16 = (bf16[128,768]{1,0:T(8,128)(2,1)S(1)}, bf16[128,768]{1,0:T(8,128)(2,1)S(1)}, u32[]{:S(2)}, u32[]{:S(2)}) collective-permute-start(bf16[128,768]{1,0:T(8,128)(2,1)S(1)} %collective-permute-done.15), channel_id=1, source_target_pairs={{0,7},{1,0},{2,1},{3,2},{4,3},{5,4},{6,5},{7,6},{16,17},{17,18},{1... | collective-permute-start | bytes 589832 | tf_op jit(solution)/shard_map/ppermute | solution.py:53
  88.7 11.2 %collective-permute-start.20 = (bf16[256,768]{1,0:T(8,128)(2,1)S(1)}, bf16[256,768]{1,0:T(8,128)(2,1)S(1)}, u32[]{:S(2)}, u32[]{:S(2)}) collective-permute-start(bf16[256,768]{1,0:T(8,128)(2,1)S(1)} %constant_dynamic-update-slice_fusion.refs_2_), channel_id=1, source_target_pairs={{0,8},{8,0},{1,9},{9,1},{2,10},{10,2},{3,11},{11,3},{4,12},{12,4},... | collective-permute-start | bytes 1179656 | tf_op jit(solution)/shard_map/ppermute | solution.py:47
  95.2 12.2 %collective-permute-start.21 = (bf16[256,768]{1,0:T(8,128)(2,1)S(1)}, bf16[256,768]{1,0:T(8,128)(2,1)S(1)}, u32[]{:S(2)}, u32[]{:S(2)}) collective-permute-start(bf16[256,768]{1,0:T(8,128)(2,1)S(1)} %constant_dynamic-update-slice_fusion.2.refs_1_), channel_id=1, source_target_pairs={{0,8},{8,0},{1,9},{9,1},{2,10},{10,2},{3,11},{11,3},{4,12},{12,4},... | collective-permute-start | bytes 1179656 | tf_op jit(solution)/shard_map/ppermute | solution.py:47
  97.0 8.8 %collective-permute-start.18 = (bf16[128,768]{1,0:T(8,128)(2,1)S(1)}, bf16[128,768]{1,0:T(8,128)(2,1)S(1)}, u32[]{:S(2)}, u32[]{:S(2)}) collective-permute-start(bf16[128,768]{1,0:T(8,128)(2,1)S(1)} %collective-permute-done.14), channel_id=1, source_target_pairs={{0,1},{1,2},{2,3},{3,4},{4,5},{5,6},{6,7},{7,0},{16,23},{17,16},{1... | collective-permute-start | bytes 589832 | tf_op jit(solution)/shard_map/ppermute | solution.py:53
  97.0 8.8 %collective-permute-start.19 = (bf16[128,768]{1,0:T(8,128)(2,1)S(1)}, bf16[128,768]{1,0:T(8,128)(2,1)S(1)}, u32[]{:S(2)}, u32[]{:S(2)}) collective-permute-start(bf16[128,768]{1,0:T(8,128)(2,1)S(1)} %collective-permute-done.16), channel_id=1, source_target_pairs={{0,7},{1,0},{2,1},{3,2},{4,3},{5,4},{6,5},{7,6},{16,17},{17,18},{1... | collective-permute-start | bytes 589832 | tf_op jit(solution)/shard_map/ppermute | solution.py:53
  107.5 11.0 %collective-permute-start.22 = (bf16[256,768]{1,0:T(8,128)(2,1)S(1)}, bf16[256,768]{1,0:T(8,128)(2,1)S(1)}, u32[]{:S(2)}, u32[]{:S(2)}) collective-permute-start(bf16[256,768]{1,0:T(8,128)(2,1)S(1)} %constant_dynamic-update-slice_fusion.4.refs_0_), channel_id=1, source_target_pairs={{0,8},{8,0},{1,9},{9,1},{2,10},{10,2},{3,11},{11,3},{4,12},{12,4},... | collective-permute-start | bytes 1179656 | tf_op jit(solution)/shard_map/ppermute | solution.py:47
  109.5 7.0 %collective-permute-start.24 = (bf16[128,768]{1,0:T(8,128)(2,1)S(1)}, bf16[128,768]{1,0:T(8,128)(2,1)S(1)}, u32[]{:S(2)}, u32[]{:S(2)}) collective-permute-start(bf16[128,768]{1,0:T(8,128)(2,1)S(1)} %collective-permute-done.18), channel_id=1, source_target_pairs={{0,9},{1,10},{2,11},{3,12},{4,13},{5,14},{6,15},{7,8},{8,1},{9,2},... | collective-permute-start | bytes 589832 | tf_op jit(solution)/shard_map/ppermute | solution.py:64
  109.5 7.8 %collective-permute-start.23 = (bf16[128,768]{1,0:T(8,128)(2,1)S(1)}, bf16[128,768]{1,0:T(8,128)(2,1)S(1)}, u32[]{:S(2)}, u32[]{:S(2)}) collective-permute-start(bf16[128,768]{1,0:T(8,128)(2,1)S(1)} %collective-permute-done.18), channel_id=1, source_target_pairs={{0,1},{1,2},{2,3},{3,4},{4,5},{5,6},{6,7},{7,0},{16,23},{17,16},{1... | collective-permute-start | bytes 589832 | tf_op jit(solution)/shard_map/ppermute | solution.py:53
  126.4 10.8 %collective-permute-start.25 = (bf16[8,80,640]{2,1,0:T(8,128)(2,1)}, bf16[8,80,640]{2,1,0:T(8,128)(2,1)S(1)}, u32[]{:S(2)}, u32[]{:S(2)}) collective-permute-start(bf16[8,80,640]{2,1,0:T(8,128)(2,1)} %get-tuple-element.87), channel_id=1, source_target_pairs={{0,16},{16,0},{1,17},{17,1},{2,18},{18,2},{3,19},{19,3},{4,20},{20... | collective-permute-start | bytes 2457608 | tf_op jit(solution)/shard_map/ppermute | solution.py:47
  (17 other events, 69.6 us)
Sparse Core Ops, SparseCore 0:
  9.8 42.4 all-gather.1
  107.6 42.0 reduce-scatter.1

commit v16 on v15

--- a/solution.py
+++ b/solution.py
@@ -188,7 +188,7 @@
         if last:
             total[m : m + tile, :ff] = up_sum.T.astype(bf16)
         else:
-            up_acc[:, m : m + tile] = up_sum
+            up_acc[:, m : m + tile] = up_sum.astype(bf16)
     if last:
         core = packed_ref[0] % 2
         act_grad = act_sum.astype(bf16)
@@ -232,7 +232,7 @@
         shapes = [jax.ShapeDtypeStruct((8, width // 16, 2 * ff), bf16)] * 2
         scratch = [pltpu.VMEM((width, 2 * ff), bf16), pltpu.SemaphoreType.DMA((16,))]
     else:
-        shapes = [jax.ShapeDtypeStruct((ff, width), f32), jax.ShapeDtypeStruct((ff, embed), f32)]
+        shapes = [jax.ShapeDtypeStruct((ff, width), bf16), jax.ShapeDtypeStruct((ff, embed), f32)]
         scratch = []
     specs += [whole] * (len(args) - len(specs))
     return pl.pallas_call(

time: 165 us -> 164 us (level)
  transfers between devices with their start and end apart: 28 -> 28, of which waited for: 10 -> 10; matrix products, arithmetic and copies ran while one was open for 7% -> 7% of each run, Pallas kernels for 24% -> 23%
where the time goes in v16:
time: 164 us
  starting transfers between devices  56.7 us (35%)
  Pallas kernels  39.2 us (24%)
  waiting for transfers between devices  21.7 us (13%)
  blocking collectives  17 us (10%)
  between operations  14.3 us (9%)
  other arithmetic  6.86 us (4%)
  matrix products  4.6 us (3%)
  local copies, waits for them, and re-layouts  3.74 us (2%)
    ppermute x10, starting transfers between devices, swap(): return lax.ppermute(value, axis, [(0, 1), (1, 0)])  31.3 us
    ppermute x14, starting transfers between devices, shift(): return lax.ppermute(value, ('core', 'z'), perm)  24.8 us
    pallas_call x4, Pallas kernels, backward_blocks(): pl.pallas_call(functools.partial(backward_kernel, len(items), len(places)...  20.2 us
    all_to_all x1, blocking collectives, per_device(): landed = lax.all_to_all(chip, ('ylo', 'x'), 0, 0)  17 us
    pallas_call x3, Pallas kernels, forward_blocks(): pl.pallas_call(functools.partial(forward_kernel, pieces, first), grid_spe...  17 us
    ppermute x10, waiting for transfers between devices, swap(): return lax.ppermute(value, axis, [(0, 1), (1, 0)])  12.1 us
    ppermute x14, waiting for transfers between devices, shift(): return lax.ppermute(value, ('core', 'z'), perm)  6.6 us
    dot_general x4, matrix products, dot(): lax.dot_general(left, right, (dims, ((), ())), preferred_element_type=f32)  4.6 us
  transfers between devices with their start and end apart: 28, of which 10 were waited for; matrix products, arithmetic and copies ran while one was open for 7% of the time, Pallas kernels for 23%

profile of v16, /device:TPU:1, one launch (start us, length us, event | category | flops | bytes accessed | tf_op | source)
XLA Modules:
  0.0 164.1 jit_solution(12143784068427564747)
XLA Ops:
  8.0 5.6 %shard_map.85 = (bf16[128,768]{1,0:T(8,128)(2,1)}, bf16[256,768]{1,0:T(8,128)(2,1)}, bf16[128,768]{1,0:T(8,128)(2,1)}, bf16[4,320,128]{2,1,0:T(8,128)(2,1)}, bf1...) custom-call(s32[1]{0:T(128)} %bitcast.packed_ref, bf16[2048,1280]{1,0:T(8,128)(2,1)} %refs_12_.3, ...), custom_call_target="tpu_custom_call" | custom-call | flops 671088640 | bytes 4063232 | tf_op jit(solution)/shard_map/pallas_call | solution.py:140
  13.6 3.7 %collective-permute-start.2 = (bf16[256,768]{1,0:T(8,128)(2,1)}, bf16[256,768]{1,0:T(8,128)(2,1)S(1)}, u32[]{:S(2)}, u32[]{:S(2)}) collective-permute-start(bf16[256,768]{1,0:T(8,128)(2,1)} %get-tuple-element.52), channel_id=1, source_target_pairs={{0,8},{8,0},{1,9},{9,1},{2,10},{10,2},{3,11},{11,3},{4,12},{12,4},... | collective-permute-start | bytes 1179656 | tf_op jit(solution)/shard_map/ppermute | solution.py:47
  17.3 5.6 %collective-permute-start.3 = (bf16[128,768]{1,0:T(8,128)(2,1)}, bf16[128,768]{1,0:T(8,128)(2,1)S(1)}, u32[]{:S(2)}, u32[]{:S(2)}) collective-permute-start(bf16[128,768]{1,0:T(8,128)(2,1)} %get-tuple-element.53), channel_id=1, source_target_pairs={{0,1},{1,2},{2,3},{3,4},{4,5},{5,6},{6,7},{7,0},{16,23},{17,16},{1... | collective-permute-start | bytes 589832 | tf_op jit(solution)/shard_map/ppermute | solution.py:53
  23.4 6.3 %shard_map.87 = (bf16[256,768]{1,0:T(8,128)(2,1)}, bf16[384,768]{1,0:T(8,128)(2,1)}, bf16[128,768]{1,0:T(8,128)(2,1)}, bf16[128,768]{1,0:T(8,128)(2,1)}, bf16[7,...) custom-call(s32[1]{0:T(128)} %bitcast.packed_ref, bf16[2048,1280]{1,0:T(8,128)(2,1)} %refs_12_.3, ...), custom_call_target="tpu_custom_call" | custom-call | flops 1174405120 | bytes 6127616 | tf_op jit(solution)/shard_map/pallas_call | solution.py:140
  29.7 2.9 %collective-permute-start.1 = (bf16[256,768]{1,0:T(8,128)(2,1)}, bf16[256,768]{1,0:T(8,128)(2,1)S(1)}, u32[]{:S(2)}, u32[]{:S(2)}) collective-permute-start(bf16[256,768]{1,0:T(8,128)(2,1)} %get-tuple-element.50), channel_id=1, source_target_pairs={{0,8},{8,0},{1,9},{9,1},{2,10},{10,2},{3,11},{11,3},{4,12},{12,4},... | collective-permute-start | bytes 1179656 | tf_op jit(solution)/shard_map/ppermute | solution.py:47
  34.5 2.7 %collective-permute-start.5 = (bf16[128,768]{1,0:T(8,128)(2,1)S(1)}, bf16[128,768]{1,0:T(8,128)(2,1)S(1)}, u32[]{:S(2)}, u32[]{:S(2)}) collective-permute-start(bf16[128,768]{1,0:T(8,128)(2,1)S(1)} %get-tuple-element.96), channel_id=1, source_target_pairs={{0,1},{1,2},{2,3},{3,4},{4,5},{5,6},{6,7},{7,0},{16,23},{17,16},{1... | collective-permute-start | bytes 589832 | tf_op jit(solution)/shard_map/ppermute | solution.py:53
  37.2 3.0 %collective-permute-start = (bf16[384,768]{1,0:T(8,128)(2,1)}, bf16[384,768]{1,0:T(8,128)(2,1)S(1)}, u32[]{:S(2)}, u32[]{:S(2)}) collective-permute-start(bf16[384,768]{1,0:T(8,128)(2,1)} %get-tuple-element.48), channel_id=1, source_target_pairs={{0,8},{8,0},{1,9},{9,1},{2,10},{10,2},{3,11},{11,3},{4,12},{12,4},... | collective-permute-start | bytes 1769480 | tf_op jit(solution)/shard_map/ppermute | solution.py:47
  40.2 5.1 %shard_map.86 = (bf16[256,768]{1,0:T(8,128)(2,1)}, bf16[384,768]{1,0:T(8,128)(2,1)}, bf16[5,320,128]{2,1,0:T(8,128)(2,1)}, bf16[5,128,320]{2,1,0:T(8,128)(2,1)}) custom-call(s32[1]{0:T(128)} %bitcast.packed_ref, bf16[2048,1280]{1,0:T(8,128)(2,1)} %refs_12_.3, bf16[2048,1280]{1,0:T(8,128)(2,1)} %refs_12_.3, bf16[2048,1280]{1,0:T(8,128)(2,1)} %refs_12_.3, ...), custom_call_target="tpu_custom_call" | custom-call | flops 838860800 | bytes 4751360 | tf_op jit(solution)/shard_map/pallas_call | solution.py:140
  51.4 2.7 %collective-permute-done.9 = bf16[128,768]{1,0:T(8,128)(2,1)S(1)} collective-permute-done((bf16[128,768]{1,0:T(8,128)(2,1)S(1)}, bf16[128,768]{1,0:T(8,128)(2,1)S(1)}, u32[]{:S(2)}, u32[]{:S(2)}) %collective-permute-start.9) | collective-permute-done | bytes 196640 | tf_op jit(solution)/shard_map/ppermute | solution.py:53
  54.3 3.4 %collective-permute-start.10 = (bf16[128,768]{1,0:T(8,128)(2,1)S(1)}, bf16[128,768]{1,0:T(8,128)(2,1)S(1)}, u32[]{:S(2)}, u32[]{:S(2)}) collective-permute-start(bf16[128,768]{1,0:T(8,128)(2,1)S(1)} %get-tuple-element.91), channel_id=1, source_target_pairs={{0,7},{1,0},{2,1},{3,2},{4,3},{5,4},{6,5},{7,6},{16,17},{17,18},{1... | collective-permute-start | bytes 589832 | tf_op jit(solution)/shard_map/ppermute | solution.py:53
  62.5 3.2 %collective-permute-start.11 = (bf16[128,768]{1,0:T(8,128)(2,1)S(1)}, bf16[128,768]{1,0:T(8,128)(2,1)S(1)}, u32[]{:S(2)}, u32[]{:S(2)}) collective-permute-start(bf16[128,768]{1,0:T(8,128)(2,1)S(1)} %multiply_convert_fusion.1), channel_id=1, source_target_pairs={{0,8},{8,0},{1,9},{9,1},{2,10},{10,2},{3,11},{11,3},{4,12},{12,4},... | collective-permute-start | bytes 589832 | tf_op jit(solution)/shard_map/ppermute | solution.py:47
  65.8 3.0 %collective-permute-done.11 = bf16[128,768]{1,0:T(8,128)(2,1)S(1)} collective-permute-done((bf16[128,768]{1,0:T(8,128)(2,1)S(1)}, bf16[128,768]{1,0:T(8,128)(2,1)S(1)}, u32[]{:S(2)}, u32[]{:S(2)}) %collective-permute-start.11) | collective-permute-done | bytes 196640 | tf_op jit(solution)/shard_map/ppermute | solution.py:47
  70.3 3.0 %collective-permute-start.12 = (bf16[128,768]{1,0:T(8,128)(2,1)S(1)}, bf16[128,768]{1,0:T(8,128)(2,1)S(1)}, u32[]{:S(2)}, u32[]{:S(2)}) collective-permute-start(bf16[128,768]{1,0:T(8,128)(2,1)S(1)} %slice.95), channel_id=1, source_target_pairs={{0,8},{8,0},{1,9},{9,1},{2,10},{10,2},{3,11},{11,3},{4,12},{12,4},... | collective-permute-start | bytes 589832 | tf_op jit(solution)/shard_map/ppermute | solution.py:47
  73.3 3.7 %collective-permute-done.12 = bf16[128,768]{1,0:T(8,128)(2,1)S(1)} collective-permute-done((bf16[128,768]{1,0:T(8,128)(2,1)S(1)}, bf16[128,768]{1,0:T(8,128)(2,1)S(1)}, u32[]{:S(2)}, u32[]{:S(2)}) %collective-permute-start.12) | collective-permute-done | bytes 196640 | tf_op jit(solution)/shard_map/ppermute | solution.py:47
  77.4 3.0 %collective-permute-start.15 = (bf16[128,768]{1,0:T(8,128)(2,1)S(1)}, bf16[128,768]{1,0:T(8,128)(2,1)S(1)}, u32[]{:S(2)}, u32[]{:S(2)}) collective-permute-start(bf16[128,768]{1,0:T(8,128)(2,1)S(1)} %multiply_convert_fusion.refs_0_), channel_id=1, source_target_pairs={{0,7},{1,0},{2,1},{3,2},{4,3},{5,4},{6,5},{7,6},{16,17},{17,18},{1... | collective-permute-start | bytes 589832 | tf_op jit(solution)/shard_map/ppermute | solution.py:53
  82.2 2.8 %collective-permute-start.17 = (bf16[128,768]{1,0:T(8,128)(2,1)S(1)}, bf16[128,768]{1,0:T(8,128)(2,1)S(1)}, u32[]{:S(2)}, u32[]{:S(2)}) collective-permute-start(bf16[128,768]{1,0:T(8,128)(2,1)S(1)} %multiply_convert_fusion.refs_0_), channel_id=1, source_target_pairs={{0,8},{8,0},{1,9},{9,1},{2,10},{10,2},{3,11},{11,3},{4,12},{12,4},... | collective-permute-start | bytes 589832 | tf_op jit(solution)/shard_map/ppermute | solution.py:47
  85.0 3.7 %collective-permute-start.16 = (bf16[128,768]{1,0:T(8,128)(2,1)S(1)}, bf16[128,768]{1,0:T(8,128)(2,1)S(1)}, u32[]{:S(2)}, u32[]{:S(2)}) collective-permute-start(bf16[128,768]{1,0:T(8,128)(2,1)S(1)} %collective-permute-done.15), channel_id=1, source_target_pairs={{0,7},{1,0},{2,1},{3,2},{4,3},{5,4},{6,5},{7,6},{16,17},{17,18},{1... | collective-permute-start | bytes 589832 | tf_op jit(solution)/shard_map/ppermute | solution.py:53
  90.8 4.1 %shard_map.88 = (bf16[320,1280]{1,0:T(8,128)(2,1)}, f32[320,768]{1,0:T(8,128)}) custom-call(s32[1]{0:T(128)} %bitcast.packed_ref, bf16[128,768]{1,0:T(8,128)(2,1)} %copy-done.5, bf16[128,768]{1,0:T(8,128)(2,1)} %copy-done.11, bf16[256,768]{1,0:T(8,128)(2,1)} %copy-done.3, bf16[2048,1280]{1,0:T(8,128)(2,1)} %refs_12_.3, ...), custom_call_target="tpu_custom_call" | custom-call | tf_op jit(solution)/shard_map/pallas_call | solution.py:238
  96.7 2.9 %collective-permute-start.19 = (bf16[128,768]{1,0:T(8,128)(2,1)S(1)}, bf16[128,768]{1,0:T(8,128)(2,1)S(1)}, u32[]{:S(2)}, u32[]{:S(2)}) collective-permute-start(bf16[128,768]{1,0:T(8,128)(2,1)S(1)} %collective-permute-done.16), channel_id=1, source_target_pairs={{0,7},{1,0},{2,1},{3,2},{4,3},{5,4},{6,5},{7,6},{16,17},{17,18},{1... | collective-permute-start | bytes 589832 | tf_op jit(solution)/shard_map/ppermute | solution.py:53
  100.4 4.6 %shard_map.89 = (bf16[320,1280]{1,0:T(8,128)(2,1)}, f32[320,768]{1,0:T(8,128)}) custom-call(s32[1]{0:T(128)} %bitcast.packed_ref, bf16[256,768]{1,0:T(8,128)(2,1)} %copy-done.9, bf16[256,768]{1,0:T(8,128)(2,1)} %copy-done.4, bf16[2048,1280]{1,0:T(8,128)(2,1)} %refs_12_.3, ...), custom_call_target="tpu_custom_call", output_to_operand_aliasing={{0}: (16, {}), {1}: (17, {})} | custom-call | tf_op jit(solution)/shard_map/pallas_call | solution.py:238
  109.0 4.7 %shard_map.90 = (bf16[320,1280]{1,0:T(8,128)(2,1)}, f32[320,768]{1,0:T(8,128)}) custom-call(s32[1]{0:T(128)} %bitcast.packed_ref, bf16[256,768]{1,0:T(8,128)(2,1)} %copy-done.2, bf16[256,768]{1,0:T(8,128)(2,1)} %copy-done.7, bf16[2048,1280]{1,0:T(8,128)(2,1)} %refs_12_.3, ...), custom_call_target="tpu_custom_call", output_to_operand_aliasing={{0}: (16, {}), {1}: (17, {})} | custom-call | tf_op jit(solution)/shard_map/pallas_call | solution.py:238
  119.0 6.8 %shard_map.91 = (bf16[8,80,640]{2,1,0:T(8,128)(2,1)}, bf16[8,80,640]{2,1,0:T(8,128)(2,1)}) custom-call(s32[1]{0:T(128)} %bitcast.packed_ref, bf16[256,768]{1,0:T(8,128)(2,1)} %copy-done.8, bf16[128,768]{1,0:T(8,128)(2,1)} %copy-done.12, bf16[128,768]{1,0:T(8,128)(2,1)} %copy-done.10, bf16[2048,1280]{1,0:T(8,128)(2,1)} %refs_12_.3, ...), custom_call_target="tpu_custom_call" | custom-call | tf_op jit(solution)/shard_map/pallas_call | solution.py:238
  125.8 8.1 %collective-permute-start.25 = (bf16[8,80,640]{2,1,0:T(8,128)(2,1)}, bf16[8,80,640]{2,1,0:T(8,128)(2,1)S(1)}, u32[]{:S(2)}, u32[]{:S(2)}) collective-permute-start(bf16[8,80,640]{2,1,0:T(8,128)(2,1)} %get-tuple-element.87), channel_id=1, source_target_pairs={{0,16},{16,0},{1,17},{17,1},{2,18},{18,2},{3,19},{19,3},{4,20},{20... | collective-permute-start | bytes 2457608 | tf_op jit(solution)/shard_map/ppermute | solution.py:47
  137.4 17.0 %all_to_all.5 = bf16[8,80,640]{2,1,0:T(8,128)(2,1)S(1)} all-to-all(bf16[8,80,640]{2,1,0:T(8,128)(2,1)S(1)} %add_convert_fusion), channel_id=1, replica_groups=mesh['ylo'=2,'x'=4,'core'=2,'yhi'=2,'z'=8] {'ylo','x'}, dimensions={0} | all-to-all | bytes 1638400 | tf_op jit(solution)/shard_map/all_to_all | solution.py:339
  (97 shorter events, 38.1 us)
Async XLA Ops:
  7.2 50.5 %all-gather.2.cloned.1.call-start = ((), (), s32[]{:S(2)}) async-start(), calls=%async_computation.2 | async-start | bytes 1769472 | tf_op jit(solution)/shard_map/all_gather | solution.py:285
  7.9 147.4 %reduce-scatter.2.cloned.1.call-start = ((), (), s32[]{:S(2)}) async-start(), calls=%async_computation.3 | async-start | bytes 1769472 | tf_op jit(solution)/shard_map/reduce_scatter | solution.py:330
  13.6 19.0 %collective-permute-start.2 = (bf16[256,768]{1,0:T(8,128)(2,1)}, bf16[256,768]{1,0:T(8,128)(2,1)S(1)}, u32[]{:S(2)}, u32[]{:S(2)}) collective-permute-start(bf16[256,768]{1,0:T(8,128)(2,1)} %get-tuple-element.52), channel_id=1, source_target_pairs={{0,8},{8,0},{1,9},{9,1},{2,10},{10,2},{3,11},{11,3},{4,12},{12,4},... | collective-permute-start | bytes 1179656 | tf_op jit(solution)/shard_map/ppermute | solution.py:47
  17.3 15.2 %collective-permute-start.3 = (bf16[128,768]{1,0:T(8,128)(2,1)}, bf16[128,768]{1,0:T(8,128)(2,1)S(1)}, u32[]{:S(2)}, u32[]{:S(2)}) collective-permute-start(bf16[128,768]{1,0:T(8,128)(2,1)} %get-tuple-element.53), channel_id=1, source_target_pairs={{0,1},{1,2},{2,3},{3,4},{4,5},{5,6},{6,7},{7,0},{16,23},{17,16},{1... | collective-permute-start | bytes 589832 | tf_op jit(solution)/shard_map/ppermute | solution.py:53
  22.9 9.7 %collective-permute-start.4 = (bf16[128,768]{1,0:T(8,128)(2,1)}, bf16[128,768]{1,0:T(8,128)(2,1)S(1)}, u32[]{:S(2)}, u32[]{:S(2)}) collective-permute-start(bf16[128,768]{1,0:T(8,128)(2,1)} %get-tuple-element.54), channel_id=1, source_target_pairs={{0,9},{1,10},{2,11},{3,12},{4,13},{5,14},{6,15},{7,8},{8,1},{9,2},... | collective-permute-start | bytes 589832 | tf_op jit(solution)/shard_map/ppermute | solution.py:64
  29.7 15.6 %collective-permute-start.1 = (bf16[256,768]{1,0:T(8,128)(2,1)}, bf16[256,768]{1,0:T(8,128)(2,1)S(1)}, u32[]{:S(2)}, u32[]{:S(2)}) collective-permute-start(bf16[256,768]{1,0:T(8,128)(2,1)} %get-tuple-element.50), channel_id=1, source_target_pairs={{0,8},{8,0},{1,9},{9,1},{2,10},{10,2},{3,11},{11,3},{4,12},{12,4},... | collective-permute-start | bytes 1179656 | tf_op jit(solution)/shard_map/ppermute | solution.py:47
  33.7 11.6 %collective-permute-start.8 = (bf16[128,768]{1,0:T(8,128)(2,1)S(1)}, bf16[128,768]{1,0:T(8,128)(2,1)S(1)}, u32[]{:S(2)}, u32[]{:S(2)}) collective-permute-start(bf16[128,768]{1,0:T(8,128)(2,1)S(1)} %get-tuple-element.95), channel_id=1, source_target_pairs={{0,7},{1,0},{2,1},{3,2},{4,3},{5,4},{6,5},{7,6},{16,17},{17,18},{1... | collective-permute-start | bytes 589832 | tf_op jit(solution)/shard_map/ppermute | solution.py:53
  34.5 10.8 %collective-permute-start.5 = (bf16[128,768]{1,0:T(8,128)(2,1)S(1)}, bf16[128,768]{1,0:T(8,128)(2,1)S(1)}, u32[]{:S(2)}, u32[]{:S(2)}) collective-permute-start(bf16[128,768]{1,0:T(8,128)(2,1)S(1)} %get-tuple-element.96), channel_id=1, source_target_pairs={{0,1},{1,2},{2,3},{3,4},{4,5},{5,6},{6,7},{7,0},{16,23},{17,16},{1... | collective-permute-start | bytes 589832 | tf_op jit(solution)/shard_map/ppermute | solution.py:53
  37.2 14.2 %collective-permute-start = (bf16[384,768]{1,0:T(8,128)(2,1)}, bf16[384,768]{1,0:T(8,128)(2,1)S(1)}, u32[]{:S(2)}, u32[]{:S(2)}) collective-permute-start(bf16[384,768]{1,0:T(8,128)(2,1)} %get-tuple-element.48), channel_id=1, source_target_pairs={{0,8},{8,0},{1,9},{9,1},{2,10},{10,2},{3,11},{11,3},{4,12},{12,4},... | collective-permute-start | bytes 1769480 | tf_op jit(solution)/shard_map/ppermute | solution.py:47
  46.5 7.6 %collective-permute-start.9 = (bf16[128,768]{1,0:T(8,128)(2,1)S(1)}, bf16[128,768]{1,0:T(8,128)(2,1)S(1)}, u32[]{:S(2)}, u32[]{:S(2)}) collective-permute-start(bf16[128,768]{1,0:T(8,128)(2,1)S(1)} %get-tuple-element.93), channel_id=1, source_target_pairs={{0,7},{1,0},{2,1},{3,2},{4,3},{5,4},{6,5},{7,6},{16,17},{17,18},{1... | collective-permute-start | bytes 589832 | tf_op jit(solution)/shard_map/ppermute | solution.py:53
  46.8 7.3 %collective-permute-start.6 = (bf16[128,768]{1,0:T(8,128)(2,1)S(1)}, bf16[128,768]{1,0:T(8,128)(2,1)S(1)}, u32[]{:S(2)}, u32[]{:S(2)}) collective-permute-start(bf16[128,768]{1,0:T(8,128)(2,1)S(1)} %get-tuple-element.94), channel_id=1, source_target_pairs={{0,1},{1,2},{2,3},{3,4},{4,5},{5,6},{6,7},{7,0},{16,23},{17,16},{1... | collective-permute-start | bytes 589832 | tf_op jit(solution)/shard_map/ppermute | solution.py:53
  54.3 6.9 %collective-permute-start.10 = (bf16[128,768]{1,0:T(8,128)(2,1)S(1)}, bf16[128,768]{1,0:T(8,128)(2,1)S(1)}, u32[]{:S(2)}, u32[]{:S(2)}) collective-permute-start(bf16[128,768]{1,0:T(8,128)(2,1)S(1)} %get-tuple-element.91), channel_id=1, source_target_pairs={{0,7},{1,0},{2,1},{3,2},{4,3},{5,4},{6,5},{7,6},{16,17},{17,18},{1... | collective-permute-start | bytes 589832 | tf_op jit(solution)/shard_map/ppermute | solution.py:53
  77.4 7.6 %collective-permute-start.15 = (bf16[128,768]{1,0:T(8,128)(2,1)S(1)}, bf16[128,768]{1,0:T(8,128)(2,1)S(1)}, u32[]{:S(2)}, u32[]{:S(2)}) collective-permute-start(bf16[128,768]{1,0:T(8,128)(2,1)S(1)} %multiply_convert_fusion.refs_0_), channel_id=1, source_target_pairs={{0,7},{1,0},{2,1},{3,2},{4,3},{5,4},{6,5},{7,6},{16,17},{17,18},{1... | collective-permute-start | bytes 589832 | tf_op jit(solution)/shard_map/ppermute | solution.py:53
  80.4 8.2 %collective-permute-start.13 = (bf16[128,768]{1,0:T(8,128)(2,1)S(1)}, bf16[128,768]{1,0:T(8,128)(2,1)S(1)}, u32[]{:S(2)}, u32[]{:S(2)}) collective-permute-start(bf16[128,768]{1,0:T(8,128)(2,1)S(1)} %multiply_convert_fusion.refs_0_), channel_id=1, source_target_pairs={{0,1},{1,2},{2,3},{3,4},{4,5},{5,6},{6,7},{7,0},{16,23},{17,16},{1... | collective-permute-start | bytes 589832 | tf_op jit(solution)/shard_map/ppermute | solution.py:53
  82.2 7.9 %collective-permute-start.17 = (bf16[128,768]{1,0:T(8,128)(2,1)S(1)}, bf16[128,768]{1,0:T(8,128)(2,1)S(1)}, u32[]{:S(2)}, u32[]{:S(2)}) collective-permute-start(bf16[128,768]{1,0:T(8,128)(2,1)S(1)} %multiply_convert_fusion.refs_0_), channel_id=1, source_target_pairs={{0,8},{8,0},{1,9},{9,1},{2,10},{10,2},{3,11},{11,3},{4,12},{12,4},... | collective-permute-start | bytes 589832 | tf_op jit(solution)/shard_map/ppermute | solution.py:47
  85.0 9.9 %collective-permute-start.16 = (bf16[128,768]{1,0:T(8,128)(2,1)S(1)}, bf16[128,768]{1,0:T(8,128)(2,1)S(1)}, u32[]{:S(2)}, u32[]{:S(2)}) collective-permute-start(bf16[128,768]{1,0:T(8,128)(2,1)S(1)} %collective-permute-done.15), channel_id=1, source_target_pairs={{0,7},{1,0},{2,1},{3,2},{4,3},{5,4},{6,5},{7,6},{16,17},{17,18},{1... | collective-permute-start | bytes 589832 | tf_op jit(solution)/shard_map/ppermute | solution.py:53
  88.7 10.9 %collective-permute-start.20 = (bf16[256,768]{1,0:T(8,128)(2,1)S(1)}, bf16[256,768]{1,0:T(8,128)(2,1)S(1)}, u32[]{:S(2)}, u32[]{:S(2)}) collective-permute-start(bf16[256,768]{1,0:T(8,128)(2,1)S(1)} %constant_dynamic-update-slice_fusion.refs_2_), channel_id=1, source_target_pairs={{0,8},{8,0},{1,9},{9,1},{2,10},{10,2},{3,11},{11,3},{4,12},{12,4},... | collective-permute-start | bytes 1179656 | tf_op jit(solution)/shard_map/ppermute | solution.py:47
  95.0 12.5 %collective-permute-start.21 = (bf16[256,768]{1,0:T(8,128)(2,1)S(1)}, bf16[256,768]{1,0:T(8,128)(2,1)S(1)}, u32[]{:S(2)}, u32[]{:S(2)}) collective-permute-start(bf16[256,768]{1,0:T(8,128)(2,1)S(1)} %constant_dynamic-update-slice_fusion.2.refs_1_), channel_id=1, source_target_pairs={{0,8},{8,0},{1,9},{9,1},{2,10},{10,2},{3,11},{11,3},{4,12},{12,4},... | collective-permute-start | bytes 1179656 | tf_op jit(solution)/shard_map/ppermute | solution.py:47
  96.7 8.3 %collective-permute-start.18 = (bf16[128,768]{1,0:T(8,128)(2,1)S(1)}, bf16[128,768]{1,0:T(8,128)(2,1)S(1)}, u32[]{:S(2)}, u32[]{:S(2)}) collective-permute-start(bf16[128,768]{1,0:T(8,128)(2,1)S(1)} %collective-permute-done.14), channel_id=1, source_target_pairs={{0,1},{1,2},{2,3},{3,4},{4,5},{5,6},{6,7},{7,0},{16,23},{17,16},{1... | collective-permute-start | bytes 589832 | tf_op jit(solution)/shard_map/ppermute | solution.py:53
  96.7 8.3 %collective-permute-start.19 = (bf16[128,768]{1,0:T(8,128)(2,1)S(1)}, bf16[128,768]{1,0:T(8,128)(2,1)S(1)}, u32[]{:S(2)}, u32[]{:S(2)}) collective-permute-start(bf16[128,768]{1,0:T(8,128)(2,1)S(1)} %collective-permute-done.16), channel_id=1, source_target_pairs={{0,7},{1,0},{2,1},{3,2},{4,3},{5,4},{6,5},{7,6},{16,17},{17,18},{1... | collective-permute-start | bytes 589832 | tf_op jit(solution)/shard_map/ppermute | solution.py:53
  107.5 10.7 %collective-permute-start.22 = (bf16[256,768]{1,0:T(8,128)(2,1)S(1)}, bf16[256,768]{1,0:T(8,128)(2,1)S(1)}, u32[]{:S(2)}, u32[]{:S(2)}) collective-permute-start(bf16[256,768]{1,0:T(8,128)(2,1)S(1)} %constant_dynamic-update-slice_fusion.4.refs_0_), channel_id=1, source_target_pairs={{0,8},{8,0},{1,9},{9,1},{2,10},{10,2},{3,11},{11,3},{4,12},{12,4},... | collective-permute-start | bytes 1179656 | tf_op jit(solution)/shard_map/ppermute | solution.py:47
  109.0 7.0 %collective-permute-start.24 = (bf16[128,768]{1,0:T(8,128)(2,1)S(1)}, bf16[128,768]{1,0:T(8,128)(2,1)S(1)}, u32[]{:S(2)}, u32[]{:S(2)}) collective-permute-start(bf16[128,768]{1,0:T(8,128)(2,1)S(1)} %collective-permute-done.18), channel_id=1, source_target_pairs={{0,9},{1,10},{2,11},{3,12},{4,13},{5,14},{6,15},{7,8},{8,1},{9,2},... | collective-permute-start | bytes 589832 | tf_op jit(solution)/shard_map/ppermute | solution.py:64
  109.0 8.6 %collective-permute-start.23 = (bf16[128,768]{1,0:T(8,128)(2,1)S(1)}, bf16[128,768]{1,0:T(8,128)(2,1)S(1)}, u32[]{:S(2)}, u32[]{:S(2)}) collective-permute-start(bf16[128,768]{1,0:T(8,128)(2,1)S(1)} %collective-permute-done.18), channel_id=1, source_target_pairs={{0,1},{1,2},{2,3},{3,4},{4,5},{5,6},{6,7},{7,0},{16,23},{17,16},{1... | collective-permute-start | bytes 589832 | tf_op jit(solution)/shard_map/ppermute | solution.py:53
  125.8 10.2 %collective-permute-start.25 = (bf16[8,80,640]{2,1,0:T(8,128)(2,1)}, bf16[8,80,640]{2,1,0:T(8,128)(2,1)S(1)}, u32[]{:S(2)}, u32[]{:S(2)}) collective-permute-start(bf16[8,80,640]{2,1,0:T(8,128)(2,1)} %get-tuple-element.87), channel_id=1, source_target_pairs={{0,16},{16,0},{1,17},{17,1},{2,18},{18,2},{3,19},{19,3},{4,20},{20... | collective-permute-start | bytes 2457608 | tf_op jit(solution)/shard_map/ppermute | solution.py:47
  (17 other events, 67.9 us)
Sparse Core Ops, SparseCore 0:
  9.8 42.4 all-gather.1
  107.6 41.6 reduce-scatter.1
